TPU v7x, 32 devices: a whole 2x2x4 slice. The times are simulated.
32 devices in a mesh: loop: 8 (over y, x, core), cross: 4 (over z).
Axes of the slice: x: 2, y: 2, z: 4, core: 2. Of those that a mesh axis runs over, the one named last changes fastest.
Arguments:
- populations: float32 [27, 64, 128, 128], P(None, 'loop', 'cross'), may hold values from 0 to 1, as said below
- scalars: float32 [14, 64, 128, 128], P(None, 'loop', 'cross'), may hold values from 0 to 1, as said below
- node_flags: int32 [64, 128, 128], P('loop', 'cross'), may hold values from 0 to 4, as said below
Outputs:
- new_populations: float32 [27, 64, 128, 128], P(None, 'loop', 'cross')
- new_scalars: float32 [14, 64, 128, 128], P(None, 'loop', 'cross')
Inputs may be any that keep to these rules, and one draw needn't show every extreme that they name: `node_flags`: every cell in the first or last layer along either cross-section dimension is a wall. `populations`: all entries positive. `scalars`: all entries positive.
All inputs are finite; a program needn't handle non-finite values.
Results may differ from a plain program's by a relative error of at most 0.0001.
Values sent between devices are 32-bit elements; how exact they have to be, the bound alone decides.
No kernel may reach another device: no remote copies, remote signals or barrier semaphores. Data moves between devices by JAX's collectives and lax.ppermute only.
A program may use at most 128 MiB of HBM per device.

v0:
```python
import jax
import jax.numpy as jnp
from jax import lax
from jax.sharding import PartitionSpec as P

relax_flow = 0.8
relax_heat = 0.9
relax_solvent = 1.1
fan_speed = 0.05
heater_temp = 2.0


def padded_2(cells, sides, width, closed):
    for axis, dim in sides:
        count = lax.axis_size(axis)
        ends = count if closed else count - 1
        head = lax.slice_in_dim(cells, 0, width, axis=dim)
        tail = lax.slice_in_dim(cells, cells.shape[dim] - width, cells.shape[dim], axis=dim)
        cells = jnp.concatenate(
            [
                lax.ppermute(tail, axis, [(i, (i + 1) % count) for i in range(ends)]),
                cells,
                lax.ppermute(head, axis, [((i + 1) % count, i) for i in range(ends)]),
            ],
            axis=dim,
        )
    return cells


def flow_dirs():
    return [(a, b, c) for a in (-1, 0, 1) for b in (-1, 0, 1) for c in (-1, 0, 1)]


def flow_weights():
    table = {0: 8.0 / 27.0, 1: 2.0 / 27.0, 2: 1.0 / 54.0, 3: 1.0 / 216.0}
    return [table[abs(a) + abs(b) + abs(c)] for a, b, c in flow_dirs()]


def scalar_dirs():
    return [(0, 0, 0), (1, 0, 0), (-1, 0, 0), (0, 1, 0), (0, -1, 0), (0, 0, 1), (0, 0, -1)]


def scalar_opposite():
    return [0, 2, 1, 4, 3, 6, 5]


def scalar_weights():
    return [0.25, 0.125, 0.125, 0.125, 0.125, 0.125, 0.125]


def state_dirs():
    return flow_dirs() + scalar_dirs() + scalar_dirs()


def collide(pops, scal, flags):
    flow = flow_dirs()
    weights = flow_weights()
    wall = flags == 1
    fan = flags == 2
    heater = flags == 3
    exhaust = flags == 4
    density = jnp.sum(pops, axis=0)
    denom = jnp.where(wall, 1.0, density)
    table = jnp.array(flow, dtype=jnp.float32)
    mom_x = jnp.sum(pops * table[:, 0][:, None, None, None], axis=0)
    mom_y = jnp.sum(pops * table[:, 1][:, None, None, None], axis=0)
    mom_z = jnp.sum(pops * table[:, 2][:, None, None, None], axis=0)
    vel_x = jnp.where(fan, fan_speed, mom_x / denom)
    vel_y = jnp.where(fan, 0.0, mom_y / denom)
    vel_z = jnp.where(fan, 0.0, mom_z / denom)
    rho_eq = jnp.where(exhaust, 1.0, density)
    usq = vel_x * vel_x + vel_y * vel_y + vel_z * vel_z
    out_flow = []
    for index, (a, b, c) in enumerate(flow):
        proj = a * vel_x + b * vel_y + c * vel_z
        feq = weights[index] * rho_eq * (1.0 + 3.0 * proj + 4.5 * proj * proj - 1.5 * usq)
        relaxed = pops[index] - (pops[index] - feq) / relax_flow
        forced = jnp.where(fan | exhaust, feq, relaxed)
        out_flow.append(jnp.where(wall, pops[26 - index], forced))
    temp = jnp.sum(scal[0:7], axis=0)
    solv = jnp.sum(scal[7:14], axis=0)
    heat_out = []
    solv_out = []
    opposite = scalar_opposite()
    sweights = scalar_weights()
    for index, (a, b, c) in enumerate(scalar_dirs()):
        proj = a * vel_x + b * vel_y + c * vel_z
        factor = 1.0 + 4.0 * proj
        geq = sweights[index] * temp * factor
        hot = sweights[index] * heater_temp * factor
        relaxed = scal[index] - (scal[index] - geq) / relax_heat
        heat_out.append(jnp.where(wall, scal[opposite[index]], jnp.where(heater, hot, relaxed)))
        heq = sweights[index] * solv * factor
        relaxed = scal[7 + index] - (scal[7 + index] - heq) / relax_solvent
        solv_out.append(
            jnp.where(wall, scal[7 + opposite[index]], jnp.where(exhaust, 0.0, relaxed))
        )
    return (jnp.stack(out_flow), jnp.stack(heat_out + solv_out))


def shift_block(wide, size_x, size_y):
    padded = jnp.pad(wide, ((0, 0), (0, 0), (0, 0), (1, 1)))
    size_z = wide.shape[3]
    result = []
    for index, (a, b, c) in enumerate(state_dirs()):
        result.append(
            padded[index, 1 - a : 1 - a + size_x, 1 - b : 1 - b + size_y, 1 - c : 1 - c + size_z]
        )
    return jnp.stack(result)


def extend_once(post):
    wide = padded_2(post, (("loop", 1),), 1, True)
    return padded_2(wide, (("cross", 2),), 1, False)


def per_device(populations, scalars, node_flags):
    size_x = node_flags.shape[0]
    size_y = node_flags.shape[1]
    fields = jnp.concatenate([populations, scalars], axis=0)
    for step in range(2):
        post_flow, post_scal = collide(fields[:27], fields[27:], node_flags)
        post = jnp.concatenate([post_flow, post_scal], axis=0)
        fields = shift_block(extend_once(post), size_x, size_y)
    return (fields[:27], fields[27:])


def solution(mesh):
    in_specs = (
        P(None, "loop", "cross", None),
        P(None, "loop", "cross", None),
        P("loop", "cross", None),
    )
    out_specs = (P(None, "loop", "cross", None), P(None, "loop", "cross", None))
    return jax.shard_map(
        per_device, mesh=mesh, in_specs=in_specs, out_specs=out_specs, check_vma=False
    )
```

profile of v0, /device:TPU:0, one launch (start us, length us, event | category | flops | bytes accessed | tf_op | source)
XLA Modules:
  0.0 106.6 jit_solution(12270678409932745687)
XLA Ops:
  0.7 1.8 %slice_reduce_fusion = (f32[8,32,128]{2,1,0:T(8,128)S(1)}, f32[8,32,128]{2,1,0:T(8,128)S(1)}) fusion(f32[14,8,32,128]{3,2,1,0:T(8,128)} %param.6), kind=kLoop, calls=%fused_computation.17 | loop fusion | flops 393216 | bytes 2097152 | tf_op jit(solution)/shard_map/reduce_sum | solution.py:81
  2.5 3.0 %multiply_reduce_fusion.5 = (f32[8,32,128]{2,1,0:T(8,128)S(1)}, f32[8,32,128]{2,1,0:T(8,128)S(1)}, f32[8,32,128]{2,1,0:T(8,128)S(1)}, f32[8,32,128]{2,1,0:T(8,128)S(1)}) fusion(f32[27,8,32,128]{3,2,1,0:T(8,128)} %param.5, f32[27]{0:T(128)} %constant.138, f32[27]{0:T(128)} %constant.142, f32[27]{0:T(128)} %constant.140), kind=kLoop, calls=%fused_computation.16 | loop fusion | flops 6062080 | bytes 4063556 | tf_op jit(solution)/shard_map/reduce_sum | solution.py:65
  5.5 0.2 constant_dynamic-update-slice_fusion.40
  5.7 0.1 constant_dynamic-update-slice_fusion.39
  5.8 0.1 constant_dynamic-update-slice_fusion.38
  6.0 0.1 constant_dynamic-update-slice_fusion.37
  6.3 0.1 constant_dynamic-update-slice_fusion.34
  6.4 0.1 constant_dynamic-update-slice_fusion.33
  6.5 0.1 constant_dynamic-update-slice_fusion.32
  6.6 0.1 constant_dynamic-update-slice_fusion.31
  7.0 0.1 constant_dynamic-update-slice_fusion.28
  7.3 0.1 constant_dynamic-update-slice_fusion.25
  7.6 0.1 constant_dynamic-update-slice_fusion.22
  7.7 0.1 constant_dynamic-update-slice_fusion.21
  7.9 0.1 constant_dynamic-update-slice_fusion.20
  8.0 0.1 constant_dynamic-update-slice_fusion.19
  8.6 0.4 copy-done.1
  10.3 0.5 collective-permute-start
  10.8 2.9 %collective-permute-start.1 = (f32[41,1,32,128]{3,2,1,0:T(8,128)S(1)}, f32[41,1,32,128]{3,2,1,0:T(8,128)S(1)}, u32[]{:S(2)}, u32[]{:S(2)}) collective-permute-start(f32[41,1,32,128]{3,2,1,0:T(8,128)S(1)} %get-tuple-element.111), channel_id=1, source_target_pairs={{4,0},{8,4},{12,8},{16,12},{20,16},{24,20},{28,24},{0,28},{5,1},{9... | collective-permute-start | bytes 2015240 | tf_op jit(solution)/shard_map/ppermute | solution.py:23
  13.8 12.9 %collective-permute-done = f32[41,1,32,128]{3,2,1,0:T(8,128)S(1)} collective-permute-done((f32[41,1,32,128]{3,2,1,0:T(8,128)S(1)}, f32[41,1,32,128]{3,2,1,0:T(8,128)S(1)}, u32[]{:S(2)}, u32[]{:S(2)}) %collective-permute-start) | collective-permute-done | bytes 671776 | tf_op jit(solution)/shard_map/ppermute | solution.py:21
  26.7 1.5 %collective-permute-done.1 = f32[41,1,32,128]{3,2,1,0:T(8,128)S(1)} collective-permute-done((f32[41,1,32,128]{3,2,1,0:T(8,128)S(1)}, f32[41,1,32,128]{3,2,1,0:T(8,128)S(1)}, u32[]{:S(2)}, u32[]{:S(2)}) %collective-permute-start.1) | collective-permute-done | bytes 671776 | tf_op jit(solution)/shard_map/ppermute | solution.py:23
  28.2 0.3 pad_maximum_fusion.5
  28.5 3.5 %collective-permute-start.2 = (f32[41,10,1,128]{3,2,1,0:T(1,128)S(1)}, f32[41,10,1,128]{3,2,1,0:T(1,128)S(1)}, u32[]{:S(2)}, u32[]{:S(2)}) collective-permute-start(f32[41,10,1,128]{3,2,1,0:T(1,128)S(1)} %get-tuple-element.102), channel_id=1, source_target_pairs={{0,1},{1,2},{2,3},{4,5},{5,6},{6,7},{8,9},{9,10},{10,11},{12,13},{... | collective-permute-start | bytes 629768 | tf_op jit(solution)/shard_map/ppermute | solution.py:21
  32.0 1.5 %collective-permute-start.3 = (f32[41,10,1,128]{3,2,1,0:T(1,128)S(1)}, f32[41,10,1,128]{3,2,1,0:T(1,128)S(1)}, u32[]{:S(2)}, u32[]{:S(2)}) collective-permute-start(f32[41,10,1,128]{3,2,1,0:T(1,128)S(1)} %get-tuple-element.103), channel_id=1, source_target_pairs={{1,0},{2,1},{3,2},{5,4},{6,5},{7,6},{9,8},{10,9},{11,10},{13,12},{... | collective-permute-start | bytes 629768 | tf_op jit(solution)/shard_map/ppermute | solution.py:23
  33.5 3.3 %collective-permute-done.2 = f32[41,10,1,128]{3,2,1,0:T(1,128)S(1)} collective-permute-done((f32[41,10,1,128]{3,2,1,0:T(1,128)S(1)}, f32[41,10,1,128]{3,2,1,0:T(1,128)S(1)}, u32[]{:S(2)}, u32[]{:S(2)}) %collective-permute-start.2) | collective-permute-done | bytes 209952 | tf_op jit(solution)/shard_map/ppermute | solution.py:21
  36.8 4.7 %collective-permute-done.3 = f32[41,10,1,128]{3,2,1,0:T(1,128)S(1)} collective-permute-done((f32[41,10,1,128]{3,2,1,0:T(1,128)S(1)}, f32[41,10,1,128]{3,2,1,0:T(1,128)S(1)}, u32[]{:S(2)}, u32[]{:S(2)}) %collective-permute-start.3) | collective-permute-done | bytes 209952 | tf_op jit(solution)/shard_map/ppermute | solution.py:23
  41.5 11.4 %select_maximum_fusion.4 = f32[41,10,34,130]{3,2,1,0:T(8,128)S(1)} fusion(f32[41,10,1,128]{3,2,1,0:T(1,128)S(1)} %collective-permute-done.3, f32[41,10,1,128]{3,2,1,0:T(1,128)S(1)} %collective-permute-done.2, f32[41,1,32,128]{3,2,1,0:T(8,128)S(1)} %collective-permute-done.1, f32[41,8,32,128]{3,2,1,0:T(8,128)S(1)} %constant_dynamic-update-slice_fusion, ...), kind=kLoop, calls=%fused_computation.6 | loop fusion | flops 21746400 | bytes 14386080 | tf_op jit(solution)/shard_map/concatenate | solution.py:19
  54.4 0.4 copy-done.5
  54.8 0.9 multiply_reduce_fusion.2
  55.8 0.6 constant_dynamic-update-slice_fusion.149
  56.4 0.2 constant_dynamic-update-slice_fusion.108
  56.7 0.1 constant_dynamic-update-slice_fusion.106
  56.8 0.1 constant_dynamic-update-slice_fusion.105
  57.1 0.1 constant_dynamic-update-slice_fusion.103
  57.2 0.1 constant_dynamic-update-slice_fusion.102
  57.5 0.1 constant_dynamic-update-slice_fusion.100
  57.6 0.1 constant_dynamic-update-slice_fusion.99
  57.8 0.1 constant_dynamic-update-slice_fusion.97
  58.0 0.1 constant_dynamic-update-slice_fusion.96
  58.2 0.1 constant_dynamic-update-slice_fusion.94
  58.3 0.1 constant_dynamic-update-slice_fusion.93
  58.6 0.1 constant_dynamic-update-slice_fusion.91
  58.7 0.1 constant_dynamic-update-slice_fusion.90
  58.9 0.1 constant_dynamic-update-slice_fusion.88
  59.1 0.1 constant_dynamic-update-slice_fusion.87
  59.3 0.1 constant_dynamic-update-slice_fusion.85
  59.4 0.1 constant_dynamic-update-slice_fusion.84
  59.7 0.1 constant_dynamic-update-slice_fusion.82
  60.3 0.1 constant_dynamic-update-slice_fusion.75
  60.4 0.2 constant_dynamic-update-slice_fusion.74
  61.0 0.1 constant_dynamic-update-slice_fusion.68
  61.3 0.3 collective-permute-start.4
  61.6 2.4 %collective-permute-start.5 = (f32[41,1,32,128]{3,2,1,0:T(8,128)S(1)}, f32[41,1,32,128]{3,2,1,0:T(8,128)S(1)}, u32[]{:S(2)}, u32[]{:S(2)}) collective-permute-start(f32[41,1,32,128]{3,2,1,0:T(8,128)S(1)} %get-tuple-element.109), channel_id=1, source_target_pairs={{4,0},{8,4},{12,8},{16,12},{20,16},{24,20},{28,24},{0,28},{5,1},{9... | collective-permute-start | bytes 2015240 | tf_op jit(solution)/shard_map/ppermute | solution.py:23
  64.0 14.4 %collective-permute-done.4 = f32[41,1,32,128]{3,2,1,0:T(8,128)S(1)} collective-permute-done((f32[41,1,32,128]{3,2,1,0:T(8,128)S(1)}, f32[41,1,32,128]{3,2,1,0:T(8,128)S(1)}, u32[]{:S(2)}, u32[]{:S(2)}) %collective-permute-start.4) | collective-permute-done | bytes 671776 | tf_op jit(solution)/shard_map/ppermute | solution.py:21
  78.4 0.3 pad_maximum_fusion.2
  78.7 1.3 %collective-permute-start.7 = (f32[41,10,1,128]{3,0,2,1:T(8,128)S(1)}, f32[41,10,1,128]{3,0,2,1:T(8,128)S(1)}, u32[]{:S(2)}, u32[]{:S(2)}) collective-permute-start(f32[41,10,1,128]{3,0,2,1:T(8,128)S(1)} %copy.53), channel_id=1, source_target_pairs={{1,0},{2,1},{3,2},{5,4},{6,5},{7,6},{9,8},{10,9},{11,10},{13,12},{... | collective-permute-start | bytes 629768 | tf_op jit(solution)/shard_map/ppermute | solution.py:23
  80.1 4.8 %collective-permute-start.6 = (f32[41,10,1,128]{3,0,2,1:T(8,128)S(1)}, f32[41,10,1,128]{3,0,2,1:T(8,128)S(1)}, u32[]{:S(2)}, u32[]{:S(2)}) collective-permute-start(f32[41,10,1,128]{3,0,2,1:T(8,128)S(1)} %copy.52), channel_id=1, source_target_pairs={{0,1},{1,2},{2,3},{4,5},{5,6},{6,7},{8,9},{9,10},{10,11},{12,13},{... | collective-permute-start | bytes 629768 | tf_op jit(solution)/shard_map/ppermute | solution.py:21
  84.9 4.3 %collective-permute-done.7 = f32[41,10,1,128]{3,0,2,1:T(8,128)S(1)} collective-permute-done((f32[41,10,1,128]{3,0,2,1:T(8,128)S(1)}, f32[41,10,1,128]{3,0,2,1:T(8,128)S(1)}, u32[]{:S(2)}, u32[]{:S(2)}) %collective-permute-start.7) | collective-permute-done | bytes 209952 | tf_op jit(solution)/shard_map/ppermute | solution.py:23
  89.2 0.2 copy.55
  89.4 1.5 %collective-permute-done.6 = f32[41,10,1,128]{3,0,2,1:T(8,128)S(1)} collective-permute-done((f32[41,10,1,128]{3,0,2,1:T(8,128)S(1)}, f32[41,10,1,128]{3,0,2,1:T(8,128)S(1)}, u32[]{:S(2)}, u32[]{:S(2)}) %collective-permute-start.6) | collective-permute-done | bytes 209952 | tf_op jit(solution)/shard_map/ppermute | solution.py:21
  90.9 0.2 copy.54
  91.1 11.4 %select_maximum_fusion = f32[41,10,34,130]{3,2,1,0:T(8,128)S(1)} fusion(f32[41,10,1,128]{3,2,1,0:T(1,128)S(1)} %copy.55, f32[41,10,1,128]{3,2,1,0:T(1,128)S(1)} %copy.54, f32[41,1,32,128]{3,2,1,0:T(8,128)S(1)} %collective-permute-done.5, f32[41,8,32,128]{3,2,1,0:T(8,128)S(1)} %constant_dynamic-update-slice_fusion.68, ...), kind=kLoop, calls=%fused_computation.2 | loop fusion | flops 21746400 | bytes 14386080 | tf_op jit(solution)/shard_map/concatenate | solution.py:19
  104.2 1.2 %copy-done.3 = f32[14,8,32,128]{3,2,1,0:T(8,128)} copy-done((f32[14,8,32,128]{3,2,1,0:T(8,128)}, f32[14,8,32,128]{3,2,1,0:T(8,128)S(1)}, u32[]{:S(2)}) %copy-start.3) | copy-done | bytes 1835032
  105.4 1.2 %copy-done.4 = f32[27,8,32,128]{3,2,1,0:T(8,128)} copy-done((f32[27,8,32,128]{3,2,1,0:T(8,128)}, f32[27,8,32,128]{3,2,1,0:T(8,128)S(1)}, u32[]{:S(2)}) %copy-start.4) | copy-done | bytes 3538968
  (123 shorter events, 7.2 us)
Async XLA Ops:
  0.6 4.9 %copy-start = (f32[27,8,32,128]{3,2,1,0:T(8,128)S(1)}, f32[27,8,32,128]{3,2,1,0:T(8,128)}, u32[]{:S(2)}) copy-start(f32[27,8,32,128]{3,2,1,0:T(8,128)} %param.5) | copy-start | bytes 10616836
  0.6 4.9 %copy-start.2 = (s32[8,32,128]{2,1,0:T(8,128)S(1)}, s32[8,32,128]{2,1,0:T(8,128)}, u32[]{:S(2)}) copy-start(s32[8,32,128]{2,1,0:T(8,128)} %param.7) | copy-start | bytes 393220
  7.5 1.5 %copy-start.1 = (f32[14,8,32,128]{3,2,1,0:T(8,128)S(1)}, f32[14,8,32,128]{3,2,1,0:T(8,128)}, u32[]{:S(2)}) copy-start(f32[14,8,32,128]{3,2,1,0:T(8,128)} %param.6) | copy-start | bytes 5505028
  10.3 16.4 %collective-permute-start = (f32[41,1,32,128]{3,2,1,0:T(8,128)S(1)}, f32[41,1,32,128]{3,2,1,0:T(8,128)S(1)}, u32[]{:S(2)}, u32[]{:S(2)}) collective-permute-start(f32[41,1,32,128]{3,2,1,0:T(8,128)S(1)} %get-tuple-element.110), channel_id=1, source_target_pairs={{0,4},{4,8},{8,12},{12,16},{16,20},{20,24},{24,28},{28,0},{1,5},{5... | collective-permute-start | bytes 2015240 | tf_op jit(solution)/shard_map/ppermute | solution.py:21
  10.8 17.4 %collective-permute-start.1 = (f32[41,1,32,128]{3,2,1,0:T(8,128)S(1)}, f32[41,1,32,128]{3,2,1,0:T(8,128)S(1)}, u32[]{:S(2)}, u32[]{:S(2)}) collective-permute-start(f32[41,1,32,128]{3,2,1,0:T(8,128)S(1)} %get-tuple-element.111), channel_id=1, source_target_pairs={{4,0},{8,4},{12,8},{16,12},{20,16},{24,20},{28,24},{0,28},{5,1},{9... | collective-permute-start | bytes 2015240 | tf_op jit(solution)/shard_map/ppermute | solution.py:23
  28.5 8.3 %collective-permute-start.2 = (f32[41,10,1,128]{3,2,1,0:T(1,128)S(1)}, f32[41,10,1,128]{3,2,1,0:T(1,128)S(1)}, u32[]{:S(2)}, u32[]{:S(2)}) collective-permute-start(f32[41,10,1,128]{3,2,1,0:T(1,128)S(1)} %get-tuple-element.102), channel_id=1, source_target_pairs={{0,1},{1,2},{2,3},{4,5},{5,6},{6,7},{8,9},{9,10},{10,11},{12,13},{... | collective-permute-start | bytes 629768 | tf_op jit(solution)/shard_map/ppermute | solution.py:21
  32.0 9.5 %collective-permute-start.3 = (f32[41,10,1,128]{3,2,1,0:T(1,128)S(1)}, f32[41,10,1,128]{3,2,1,0:T(1,128)S(1)}, u32[]{:S(2)}, u32[]{:S(2)}) collective-permute-start(f32[41,10,1,128]{3,2,1,0:T(1,128)S(1)} %get-tuple-element.103), channel_id=1, source_target_pairs={{1,0},{2,1},{3,2},{5,4},{6,5},{7,6},{9,8},{10,9},{11,10},{13,12},{... | collective-permute-start | bytes 629768 | tf_op jit(solution)/shard_map/ppermute | solution.py:23
  54.1 0.7 copy-start.5
  54.2 0.7 copy-start.6
  54.2 0.7 copy-start.7
  61.3 17.1 %collective-permute-start.4 = (f32[41,1,32,128]{3,2,1,0:T(8,128)S(1)}, f32[41,1,32,128]{3,2,1,0:T(8,128)S(1)}, u32[]{:S(2)}, u32[]{:S(2)}) collective-permute-start(f32[41,1,32,128]{3,2,1,0:T(8,128)S(1)} %get-tuple-element.108), channel_id=1, source_target_pairs={{0,4},{4,8},{8,12},{12,16},{16,20},{20,24},{24,28},{28,0},{1,5},{5... | collective-permute-start | bytes 2015240 | tf_op jit(solution)/shard_map/ppermute | solution.py:21
  61.6 16.8 %collective-permute-start.5 = (f32[41,1,32,128]{3,2,1,0:T(8,128)S(1)}, f32[41,1,32,128]{3,2,1,0:T(8,128)S(1)}, u32[]{:S(2)}, u32[]{:S(2)}) collective-permute-start(f32[41,1,32,128]{3,2,1,0:T(8,128)S(1)} %get-tuple-element.109), channel_id=1, source_target_pairs={{4,0},{8,4},{12,8},{16,12},{20,16},{24,20},{28,24},{0,28},{5,1},{9... | collective-permute-start | bytes 2015240 | tf_op jit(solution)/shard_map/ppermute | solution.py:23
  78.7 10.5 %collective-permute-start.7 = (f32[41,10,1,128]{3,0,2,1:T(8,128)S(1)}, f32[41,10,1,128]{3,0,2,1:T(8,128)S(1)}, u32[]{:S(2)}, u32[]{:S(2)}) collective-permute-start(f32[41,10,1,128]{3,0,2,1:T(8,128)S(1)} %copy.53), channel_id=1, source_target_pairs={{1,0},{2,1},{3,2},{5,4},{6,5},{7,6},{9,8},{10,9},{11,10},{13,12},{... | collective-permute-start | bytes 629768 | tf_op jit(solution)/shard_map/ppermute | solution.py:23
  80.1 10.8 %collective-permute-start.6 = (f32[41,10,1,128]{3,0,2,1:T(8,128)S(1)}, f32[41,10,1,128]{3,0,2,1:T(8,128)S(1)}, u32[]{:S(2)}, u32[]{:S(2)}) collective-permute-start(f32[41,10,1,128]{3,0,2,1:T(8,128)S(1)} %copy.52), channel_id=1, source_target_pairs={{0,1},{1,2},{2,3},{4,5},{5,6},{6,7},{8,9},{9,10},{10,11},{12,13},{... | collective-permute-start | bytes 629768 | tf_op jit(solution)/shard_map/ppermute | solution.py:21
  104.2 1.2 %copy-start.3 = (f32[14,8,32,128]{3,2,1,0:T(8,128)}, f32[14,8,32,128]{3,2,1,0:T(8,128)S(1)}, u32[]{:S(2)}) copy-start(f32[14,8,32,128]{3,2,1,0:T(8,128)S(1)} %get-tuple-element.88) | copy-start | bytes 5505028
  104.2 2.4 %copy-start.4 = (f32[27,8,32,128]{3,2,1,0:T(8,128)}, f32[27,8,32,128]{3,2,1,0:T(8,128)S(1)}, u32[]{:S(2)}) copy-start(f32[27,8,32,128]{3,2,1,0:T(8,128)S(1)} %get-tuple-element.89) | copy-start | bytes 10616836
where the time goes:
time: 107 us
  waiting for transfers between devices  42.7 us (40%)
  other arithmetic  38.9 us (36%)
  starting transfers between devices  17.2 us (16%)
  local copies, waits for them, and re-layouts  6.18 us (6%)
  between operations  1.58 us (1%)
    ppermute x4, waiting for transfers between devices, padded_2(): lax.ppermute(tail, axis, [(i, (i + 1) % count) for i in range(ends)])  32.1 us
    concatenate x2, other arithmetic, padded_2(): jnp.concatenate([lax.ppermute(tail, axis, [(i, (i + 1) % count) for i in...  22.8 us
    ppermute x4, waiting for transfers between devices, padded_2(): lax.ppermute(head, axis, [((i + 1) % count, i) for i in range(ends)])  10.6 us
    unnamed x100, other arithmetic  9.62 us
    ppermute x4, starting transfers between devices, padded_2(): lax.ppermute(tail, axis, [(i, (i + 1) % count) for i in range(ends)])  9.1 us
    ppermute x4, starting transfers between devices, padded_2(): lax.ppermute(head, axis, [((i + 1) % count, i) for i in range(ends)])  8.09 us
    unnamed x54, local copies, waits for them, and re-layouts  5.38 us
    reduce_sum x2, other arithmetic, collide(): mom_x = jnp.sum(pops * table[:, 0][:, None, None, None], axis=0)  3.92 us
  transfers between devices with their start and end apart: 8, of which 7 were waited for; matrix products, arithmetic and copies ran while one was open for 0% of the time, Pallas kernels for 0%

commit v1 on v0

v1 whole, which is shorter than its diff:
```python
import functools
import math

import jax
import jax.numpy as jnp
from jax import lax
from jax.experimental import pallas as pl
from jax.experimental.pallas import tpu as pltpu
from jax.sharding import PartitionSpec as P

relax_flow = 0.8
relax_heat = 0.9
relax_solvent = 1.1
fan_speed = 0.05
heater_temp = 2.0

FLOW = [(a, b, c) for a in (-1, 0, 1) for b in (-1, 0, 1) for c in (-1, 0, 1)]
SCAL = [(0, 0, 0), (1, 0, 0), (-1, 0, 0), (0, 1, 0), (0, -1, 0), (0, 0, 1), (0, 0, -1)]
DIRS = FLOW + SCAL + SCAL
FLOW_W = {0: 8.0 / 27.0, 1: 2.0 / 27.0, 2: 1.0 / 54.0, 3: 1.0 / 216.0}
NF = len(FLOW)
NS = len(SCAL)
NQ = len(DIRS)
SUB = 8
PAD = 8

X_SETS = {a: [i for i, d in enumerate(DIRS) if d[0] == a] for a in (-1, 1)}
Y_SETS = {b: [i for i, d in enumerate(DIRS) if d[1] == b] for b in (-1, 1)}
DIAGS = [(a, b) for a in (-1, 1) for b in (-1, 1)]
XY_SETS = {ab: [i for i, d in enumerate(DIRS) if d[:2] == ab] for ab in DIAGS}


def collide(load, flags, put):
    wall = flags == 1
    fan = flags == 2
    heater = flags == 3
    exhaust = flags == 4
    row_s, row_my, row_mz = [], [], []
    for a in range(3):
        sums, mz = [], None
        for b in range(3):
            lo, mid, hi = (load(9 * a + 3 * b + c) for c in range(3))
            sums.append(lo + mid + hi)
            diff = hi - lo
            mz = diff if mz is None else mz + diff
        row_s.append(sums[0] + sums[1] + sums[2])
        row_my.append(sums[2] - sums[0])
        row_mz.append(mz)
    density = row_s[0] + row_s[1] + row_s[2]
    inverse = 1.0 / jnp.where(wall, 1.0, density)
    vel_x = jnp.where(fan, fan_speed, (row_s[2] - row_s[0]) * inverse)
    vel_y = jnp.where(fan, 0.0, (row_my[0] + row_my[1] + row_my[2]) * inverse)
    vel_z = jnp.where(fan, 0.0, (row_mz[0] + row_mz[1] + row_mz[2]) * inverse)
    rho_eq = jnp.where(exhaust, 1.0, density)
    forced = fan | exhaust
    keep = jnp.where(forced, 0.0, 1.0 - 1.0 / relax_flow)
    scale = jnp.where(forced, rho_eq, rho_eq * (1.0 / relax_flow))
    root = math.sqrt(4.5)
    q = [vel_x * root, vel_y * root, vel_z * root]
    base = 1.0 - (q[0] * q[0] + q[1] * q[1] + q[2] * q[2]) * (1.0 / 3.0)
    by_w = {n: scale * w for n, w in FLOW_W.items()}
    by_w3 = {n: scale * (w * math.sqrt(2.0)) for n, w in FLOW_W.items() if n}

    def project(vector):
        total = None
        for part, comp in zip(vector, q):
            if part:
                if total is None:
                    total = comp if part > 0 else -comp
                else:
                    total = total + comp if part > 0 else total - comp
        return total

    cache = {}
    for i in range(NF // 2, NF):
        vector = FLOW[i]
        n = sum(abs(p) for p in vector)
        f_i = load(i)
        if n == 0:
            put(i, jnp.where(wall, f_i, keep * f_i + by_w[0] * base))
            continue
        first = next(p for p in vector if p)
        assert first > 0
        lead = vector[:2]
        if vector[2] and any(lead):
            if lead not in cache:
                cache[lead] = project(lead + (0,))
            proj = cache[lead] + q[2] if vector[2] > 0 else cache[lead] - q[2]
        else:
            if vector not in cache:
                cache[lead if any(lead) else vector] = project(vector)
            proj = cache[lead if any(lead) else vector]
        f_o = load(NF - 1 - i)
        even = by_w[n] * (base + proj * proj)
        odd = by_w3[n] * proj
        put(i, jnp.where(wall, f_o, keep * f_i + (even + odd)))
        put(NF - 1 - i, jnp.where(wall, f_i, keep * f_o + (even - odd)))

    for first, relax in ((NF, relax_heat), (NF + NS, relax_solvent)):
        total = load(first)
        for j in range(1, NS):
            total = total + load(first + j)
        if first == NF:
            keep_s = jnp.where(heater, 0.0, 1.0 - 1.0 / relax)
            source = jnp.where(heater, heater_temp, total * (1.0 / relax))
        else:
            keep_s = jnp.where(exhaust, 0.0, 1.0 - 1.0 / relax)
            source = jnp.where(exhaust, 0.0, total * (1.0 / relax))
        g = load(first)
        put(first, jnp.where(wall, g, keep_s * g + source * 0.25))
        eighth = source * 0.125
        half = source * 0.5
        for axis, vel in enumerate((vel_x, vel_y, vel_z)):
            odd = half * vel
            g_p, g_m = load(first + 1 + 2 * axis), load(first + 2 + 2 * axis)
            put(first + 1 + 2 * axis, jnp.where(wall, g_m, keep_s * g_p + (eighth + odd)))
            put(first + 2 + 2 * axis, jnp.where(wall, g_p, keep_s * g_m + (eighth - odd)))


def shift_lanes(value, c):
    if c == 0:
        return value
    lanes = value.shape[-1]
    lane = lax.broadcasted_iota(jnp.int32, value.shape, value.ndim - 1)
    edge = 0 if c > 0 else lanes - 1
    return jnp.where(lane == edge, 0.0, pltpu.roll(value, c % lanes, value.ndim - 1))


def push_tile(dst, x, row):
    def put(i, value):
        a, b, c = DIRS[i]
        dst[i, x + 1 + a, row + PAD + b : row + PAD + b + SUB, :] = shift_lanes(value, c)

    return put


def row_slice(x, row, rows, count):
    return pl.ds((x + 1) * rows + PAD + row, count, stride=rows)


def extract(state, size_x, size_y, x_out, y_out, d_out):
    rows = size_y + 2 * PAD
    flat = state.reshape(NQ, (size_x + 2) * rows, state.shape[-1])
    for a in (-1, 1):
        x = -1 if a < 0 else size_x
        for k, i in enumerate(X_SETS[a]):
            b = DIRS[i][1]
            for y in range(0, size_y, SUB):
                x_out[a][k, y : y + SUB, :] = state[i, x + 1, y + PAD + b : y + PAD + b + SUB, :]
    for b in (-1, 1):
        y = -1 if b < 0 else size_y
        for k, i in enumerate(Y_SETS[b]):
            y_out[b][k, :, :] = flat[i, row_slice(DIRS[i][0], y, rows, size_x), :]
    for a, b in DIAGS:
        x = -1 if a < 0 else size_x
        y = -1 if b < 0 else size_y
        for k, i in enumerate(XY_SETS[a, b]):
            d_out[a, b][k : k + 1, :] = state[i, x + 1, y + PAD : y + PAD + 1, :]


def insert(state, size_x, size_y, x_in, y_in, d_in):
    rows = size_y + 2 * PAD
    flat = state.reshape(NQ, (size_x + 2) * rows, state.shape[-1])
    for a in (-1, 1):
        x = 0 if a > 0 else size_x - 1
        for k, i in enumerate(X_SETS[a]):
            b = DIRS[i][1]
            for y in range(0, size_y, SUB):
                state[i, x + 1, y + PAD + b : y + PAD + b + SUB, :] = x_in[a][k, y : y + SUB, :]
    for b in (-1, 1):
        y = 0 if b > 0 else size_y - 1
        for k, i in enumerate(Y_SETS[b]):
            a = DIRS[i][0]
            if a == 0:
                flat[i, row_slice(0, y, rows, size_x), :] = y_in[b][k, :, :]
            else:
                lo = 0 if a > 0 else 1
                for s in range(size_x - 1):
                    x = lo + s + a
                    state[i, x + 1, y + PAD : y + PAD + 1, :] = y_in[b][k, lo + s : lo + s + 1, :]
    for a, b in DIAGS:
        x = 0 if a > 0 else size_x - 1
        y = 0 if b > 0 else size_y - 1
        for k, i in enumerate(XY_SETS[a, b]):
            state[i, x + 1, y + PAD : y + PAD + 1, :] = d_in[a, b][k : k + 1, :]


def unpack_messages(refs):
    x_refs = {-1: refs[0], 1: refs[1]}
    y_refs = {-1: refs[2], 1: refs[3]}
    d_refs = dict(zip(DIAGS, refs[4:8]))
    return x_refs, y_refs, d_refs


def first_kernel(size_x, size_y, pops, scal, flags, state, kinds, *rest):
    messages, (raw, sems) = rest[:8], rest[8:]

    def copies(x):
        return (
            pltpu.make_async_copy(pops.at[:, x], raw.at[0:NF, x], sems.at[0, x]),
            pltpu.make_async_copy(scal.at[:, x], raw.at[NF:NQ, x], sems.at[1, x]),
            pltpu.make_async_copy(flags.at[x], kinds.at[x], sems.at[2, x]),
        )

    for x in range(size_x):
        for copy in copies(x):
            copy.start()

    @pl.loop(0, size_x)
    def _(x):
        for copy in copies(x):
            copy.wait()
        for y in range(0, size_y, SUB):
            collide(
                lambda i: raw[i, x, y : y + SUB, :],
                kinds[x, y : y + SUB, :],
                push_tile(state, x, y),
            )

    extract(state, size_x, size_y, *unpack_messages(messages))


def inner_kernel(size_x, size_y, state, kinds, out):
    @pl.loop(1, size_x - 1)
    def _(x):
        for y in range(0, size_y, SUB):
            collide(
                lambda i: state[i, x + 1, y + PAD : y + PAD + SUB, :],
                kinds[x, y : y + SUB, :],
                push_tile(out, x, y),
            )


def edge_kernel(size_x, size_y, state_in, out_in, kinds, *rest):
    received, (state, out), sent = rest[:8], rest[8:10], rest[10:18]
    rows = size_y + 2 * PAD
    insert(state, size_x, size_y, *unpack_messages(received))

    @pl.loop(0, 2)
    def _(side):
        x = side * (size_x - 1)
        for y in range(0, size_y, SUB):
            collide(
                lambda i: state[i, x + 1, y + PAD : y + PAD + SUB, :],
                kinds[x, y : y + SUB, :],
                push_tile(out, x, y),
            )

    flat = state.reshape(NQ, (size_x + 2) * rows, state.shape[-1])
    flat_out = out.reshape(NQ, (size_x + 2) * rows, out.shape[-1])
    flat_kinds = kinds.reshape(size_x * size_y, kinds.shape[-1])
    for y in (0, size_y - 1):

        def put(i, value):
            a, b, c = DIRS[i]
            flat_out[i, row_slice(a, y + b, rows, size_x), :] = shift_lanes(value, c)

        collide(
            lambda i: flat[i, row_slice(0, y, rows, size_x), :],
            flat_kinds[pl.ds(y, size_x, stride=size_y), :],
            put,
        )
    extract(out, size_x, size_y, *unpack_messages(sent))


def last_kernel(size_x, size_y, out_in, *rest):
    received, (out, pops, scal), sems = rest[:8], rest[8:11], rest[11]
    insert(out, size_x, size_y, *unpack_messages(received))
    copies = []
    for x in range(size_x):
        inner = slice(PAD, PAD + size_y)
        copies.append(pltpu.make_async_copy(out.at[0:NF, x + 1, inner], pops.at[:, x], sems.at[0, x]))
        copies.append(pltpu.make_async_copy(out.at[NF:NQ, x + 1, inner], scal.at[:, x], sems.at[1, x]))
    for copy in copies:
        copy.start()
    for copy in copies:
        copy.wait()


def exchange(sent):
    loops, crosses = lax.axis_size("loop"), lax.axis_size("cross")
    received = []
    for (axis, count, closed, step), cells in zip(
        (("loop", loops, True, -1), ("loop", loops, True, 1), ("cross", crosses, False, -1), ("cross", crosses, False, 1)),
        sent,
    ):
        pairs = [(i, (i + step) % count) for i in range(count) if closed or 0 <= i + step < count]
        received.append(lax.ppermute(cells, axis, pairs))
    for (a, b), cells in zip(DIAGS, sent[4:]):
        pairs = [
            (l * crosses + c, (l + a) % loops * crosses + c + b)
            for l in range(loops)
            for c in range(crosses)
            if 0 <= c + b < crosses
        ]
        received.append(lax.ppermute(cells, ("loop", "cross"), pairs))
    return received


def per_device(populations, scalars, node_flags):
    size_x, size_y, size_z = node_flags.shape
    f32 = jnp.float32
    state_shape = pltpu.VMEM((NQ, size_x + 2, size_y + 2 * PAD, size_z), f32)
    kinds_shape = pltpu.VMEM((size_x, size_y, size_z), jnp.int32)
    message_shapes = (
        [pltpu.VMEM((len(X_SETS[a]), size_y, size_z), f32) for a in (-1, 1)]
        + [pltpu.VMEM((len(Y_SETS[b]), size_x, size_z), f32) for b in (-1, 1)]
        + [pltpu.VMEM((len(XY_SETS[ab]), size_z), f32) for ab in DIAGS]
    )
    hbm = pl.BlockSpec(memory_space=pl.ANY)
    vmem = pl.BlockSpec(memory_space=pltpu.VMEM)
    params = pltpu.CompilerParams(vmem_limit_bytes=16 * 2**20)

    def cost(tiles):
        cells = tiles * SUB * size_z
        return pl.CostEstimate(flops=500 * cells, bytes_accessed=8 * NQ * cells, transcendentals=cells)

    def here(*arrays):
        return [pltpu.with_memory_space_constraint(x, pltpu.VMEM) for x in arrays]

    state, kinds, *sent = pl.pallas_call(
        functools.partial(first_kernel, size_x, size_y),
        out_shape=[state_shape, kinds_shape] + message_shapes,
        in_specs=[hbm] * 3,
        out_specs=[vmem] * 10,
        scratch_shapes=[
            pltpu.VMEM((NQ, size_x, size_y, size_z), f32),
            pltpu.SemaphoreType.DMA((3, size_x)),
        ],
        compiler_params=params,
        cost_estimate=cost(size_x * size_y // SUB),
        name="first_step",
    )(*(pltpu.with_memory_space_constraint(x, pltpu.HBM) for x in (populations, scalars, node_flags)))
    received = exchange(sent)
    out = pl.pallas_call(
        functools.partial(inner_kernel, size_x, size_y),
        out_shape=state_shape,
        in_specs=[vmem] * 2,
        out_specs=vmem,
        compiler_params=params,
        cost_estimate=cost((size_x - 2) * size_y // SUB),
        name="second_step_inner",
    )(*here(state, kinds))
    state, out, *sent = pl.pallas_call(
        functools.partial(edge_kernel, size_x, size_y),
        out_shape=[state_shape, state_shape] + message_shapes,
        in_specs=[vmem] * 11,
        out_specs=[vmem] * 10,
        input_output_aliases={0: 0, 1: 1},
        compiler_params=params,
        cost_estimate=cost(2 * size_y // SUB + 2),
        name="second_step_edge",
    )(*here(state, out, kinds, *received))
    received = exchange(sent)
    out, new_pops, new_scal = pl.pallas_call(
        functools.partial(last_kernel, size_x, size_y),
        out_shape=[
            state_shape,
            jax.ShapeDtypeStruct(populations.shape, f32),
            jax.ShapeDtypeStruct(scalars.shape, f32),
        ],
        in_specs=[vmem] * 9,
        out_specs=[vmem, hbm, hbm],
        input_output_aliases={0: 0},
        scratch_shapes=[pltpu.SemaphoreType.DMA((2, size_x))],
        compiler_params=params,
        cost_estimate=pl.CostEstimate(flops=0, bytes_accessed=8 * NQ * size_x * size_y * size_z, transcendentals=0),
        name="write_out",
    )(*here(out, *received))
    return new_pops, new_scal


def solution(mesh):
    wide = P(None, "loop", "cross", None)
    return jax.shard_map(
        per_device,
        mesh=mesh,
        in_specs=(wide, wide, P("loop", "cross", None)),
        out_specs=(wide, wide),
        check_vma=False,
    )
```

time: 107 us -> 73.8 us (0.69)
  the two profiles are of different devices: /device:TPU:0 before, /device:TPU:8 now
where the time goes in v1:
time: 73.8 us; the launch traced here: 73.4 us
  starting transfers between devices  41 us (56%)
  waiting for transfers between devices  22.4 us (30%)
  Pallas kernels  9.2 us (12%)
  between operations  0.79 us (1%)
    ppermute x8, starting transfers between devices, exchange(): received.append(lax.ppermute(cells, ('loop', 'cross'), pairs))  26.8 us
    ppermute x8, waiting for transfers between devices, exchange(): received.append(lax.ppermute(cells, ('loop', 'cross'), pairs))  22.4 us
    ppermute x8, starting transfers between devices, exchange(): received.append(lax.ppermute(cells, axis, pairs))  14.2 us
    pallas_call x1, Pallas kernels, per_device(): pl.pallas_call(functools.partial(first_kernel, size_x, size_y), out_shape...  3.75 us
    pallas_call x1, Pallas kernels, per_device(): pl.pallas_call(functools.partial(last_kernel, size_x, size_y), out_shape=...  2.58 us
    pallas_call x1, Pallas kernels, per_device(): pl.pallas_call(functools.partial(inner_kernel, size_x, size_y), out_shape...  1.81 us
  transfers between devices with their start and end apart: 16, of which 8 were waited for; matrix products, arithmetic and copies ran while one was open for 0% of the time, Pallas kernels for 2%

profile of v1, /device:TPU:8, one launch (start us, length us, event | category | flops | bytes accessed | tf_op | source)
XLA Modules:
  0.0 73.4 jit_solution(10772371082960619744)
XLA Ops:
  0.6 3.7 %first_step.1 = (f32[41,10,48,128]{3,2,1,0:T(8,128)S(1)}, s32[8,32,128]{2,1,0:T(8,128)S(1)}, f32[11,32,128]{2,1,0:T(8,128)S(1)}, f32[11,32,128]{2,1,0:T(8,128)S(...) custom-call(f32[27,8,32,128]{3,2,1,0:T(8,128)} %pops.1, ...), custom_call_target="tpu_custom_call" | custom-call | flops 16384000 | bytes 10747904 | tf_op jit(solution)/shard_map/first_step/pallas_call | solution.py:321
  4.4 1.9 %collective-permute-start = (f32[11,32,128]{2,1,0:T(8,128)S(1)}, f32[11,32,128]{2,1,0:T(8,128)S(1)}, u32[]{:S(2)}, u32[]{:S(2)}) collective-permute-start(f32[11,32,128]{2,1,0:T(8,128)S(1)} %get-tuple-element.25), channel_id=1, source_target_pairs={{0,28},{4,0},{8,4},{12,8},{16,12},{20,16},{24,20},{28,24},{1,29},{... | collective-permute-start | bytes 540680 | tf_op jit(solution)/shard_map/ppermute | solution.py:288
  6.3 0.0 collective-permute-start.1
  6.3 2.3 %collective-permute-start.2 = (f32[11,8,128]{2,1,0:T(8,128)S(1)}, f32[11,8,128]{2,1,0:T(8,128)S(1)}, u32[]{:S(2)}, u32[]{:S(2)}) collective-permute-start(f32[11,8,128]{2,1,0:T(8,128)S(1)} %get-tuple-element.27), channel_id=1, source_target_pairs={{1,0},{2,1},{3,2},{5,4},{6,5},{7,6},{9,8},{10,9},{11,10},{13,12},{... | collective-permute-start | bytes 135176 | tf_op jit(solution)/shard_map/ppermute | solution.py:288
  8.7 3.5 %collective-permute-start.3 = (f32[11,8,128]{2,1,0:T(8,128)S(1)}, f32[11,8,128]{2,1,0:T(8,128)S(1)}, u32[]{:S(2)}, u32[]{:S(2)}) collective-permute-start(f32[11,8,128]{2,1,0:T(8,128)S(1)} %get-tuple-element.28), channel_id=1, source_target_pairs={{0,1},{1,2},{2,3},{4,5},{5,6},{6,7},{8,9},{9,10},{10,11},{12,13},{... | collective-permute-start | bytes 135176 | tf_op jit(solution)/shard_map/ppermute | solution.py:288
  12.2 3.9 %collective-permute-start.4 = (f32[3,128]{1,0:T(4,128)S(1)}, f32[3,128]{1,0:T(4,128)S(1)}, u32[]{:S(2)}, u32[]{:S(2)}) collective-permute-start(f32[3,128]{1,0:T(4,128)S(1)} %get-tuple-element.29), channel_id=1, source_target_pairs={{1,28},{2,29},{3,30},{5,0},{6,1},{7,2},{9,4},{10,5},{11,6},{13,8},... | collective-permute-start | bytes 4616 | tf_op jit(solution)/shard_map/ppermute | solution.py:296
  16.1 1.3 %collective-permute-done.4.rest_4_ = f32[3,128]{1,0:T(4,128)S(1)} collective-permute-done((f32[3,128]{1,0:T(4,128)S(1)}, f32[3,128]{1,0:T(4,128)S(1)}, u32[]{:S(2)}, u32[]{:S(2)}) %collective-permute-start.4) | collective-permute-done | bytes 1568 | tf_op jit(solution)/shard_map/ppermute | solution.py:296
  17.3 6.5 %collective-permute-start.5 = (f32[3,128]{1,0:T(4,128)S(1)}, f32[3,128]{1,0:T(4,128)S(1)}, u32[]{:S(2)}, u32[]{:S(2)}) collective-permute-start(f32[3,128]{1,0:T(4,128)S(1)} %get-tuple-element.30), channel_id=1, source_target_pairs={{0,29},{1,30},{2,31},{4,1},{5,2},{6,3},{8,5},{9,6},{10,7},{12,9},{... | collective-permute-start | bytes 4616 | tf_op jit(solution)/shard_map/ppermute | solution.py:296
  23.9 1.3 %collective-permute-done.5.rest_5_ = f32[3,128]{1,0:T(4,128)S(1)} collective-permute-done((f32[3,128]{1,0:T(4,128)S(1)}, f32[3,128]{1,0:T(4,128)S(1)}, u32[]{:S(2)}, u32[]{:S(2)}) %collective-permute-start.5) | collective-permute-done | bytes 1568 | tf_op jit(solution)/shard_map/ppermute | solution.py:296
  25.2 1.9 %collective-permute-start.6 = (f32[3,128]{1,0:T(4,128)S(1)}, f32[3,128]{1,0:T(4,128)S(1)}, u32[]{:S(2)}, u32[]{:S(2)}) collective-permute-start(f32[3,128]{1,0:T(4,128)S(1)} %get-tuple-element.31), channel_id=1, source_target_pairs={{1,4},{2,5},{3,6},{5,8},{6,9},{7,10},{9,12},{10,13},{11,14},{13,16... | collective-permute-start | bytes 4616 | tf_op jit(solution)/shard_map/ppermute | solution.py:296
  27.1 4.8 %collective-permute-done.6.rest_6_ = f32[3,128]{1,0:T(4,128)S(1)} collective-permute-done((f32[3,128]{1,0:T(4,128)S(1)}, f32[3,128]{1,0:T(4,128)S(1)}, u32[]{:S(2)}, u32[]{:S(2)}) %collective-permute-start.6) | collective-permute-done | bytes 1568 | tf_op jit(solution)/shard_map/ppermute | solution.py:296
  31.9 1.9 %collective-permute-start.7 = (f32[3,128]{1,0:T(4,128)S(1)}, f32[3,128]{1,0:T(4,128)S(1)}, u32[]{:S(2)}, u32[]{:S(2)}) collective-permute-start(f32[3,128]{1,0:T(4,128)S(1)} %get-tuple-element.32), channel_id=1, source_target_pairs={{0,5},{1,6},{2,7},{4,9},{5,10},{6,11},{8,13},{9,14},{10,15},{12,17... | collective-permute-start | bytes 4616 | tf_op jit(solution)/shard_map/ppermute | solution.py:296
  33.8 1.8 %second_step_inner.1.out_in = f32[41,10,48,128]{3,2,1,0:T(8,128)S(1)} custom-call(f32[41,10,48,128]{3,2,1,0:T(8,128)S(1)} %get-tuple-element.23.state.state_in, s32[8,32,128]{2,1,0:T(8,128)S(1)} %get-tuple-element.24.kinds), custom_call_target="tpu_custom_call" | custom-call | flops 12288000 | bytes 8060928 | tf_op jit(solution)/shard_map/second_step_inner/pallas_call | solution.py:335
  35.6 3.0 %collective-permute-done.7.rest_7_ = f32[3,128]{1,0:T(4,128)S(1)} collective-permute-done((f32[3,128]{1,0:T(4,128)S(1)}, f32[3,128]{1,0:T(4,128)S(1)}, u32[]{:S(2)}, u32[]{:S(2)}) %collective-permute-start.7) | collective-permute-done | bytes 1568 | tf_op jit(solution)/shard_map/ppermute | solution.py:296
  38.5 0.0 collective-permute-done.2.rest_2_
  38.5 0.0 collective-permute-done.3.rest_3_
  38.5 0.0 collective-permute-done.rest_0_
  38.6 0.0 collective-permute-done.1.rest_1_
  38.6 1.1 %second_step_edge.1 = (f32[41,10,48,128]{3,2,1,0:T(8,128)S(1)}, f32[41,10,48,128]{3,2,1,0:T(8,128)S(1)}, f32[11,32,128]{2,1,0:T(8,128)S(1)}, f32[11,32,128]{2,1,...) custom-call(f32[41,10,48,128]{3,2,1,0:T(8,128)S(1)} %get-tuple-eleme, ...), custom_call_target="tpu_custom_call", output_to_operand_aliasing={{0}: (0, {}), {1}: (1, {})} | custom-call | flops 5120000 | bytes 3358720 | tf_op jit(solution)/shard_map/second_step_edge/pallas_call | solution.py:344
  39.6 0.1 collective-permute-start.8
  39.7 0.5 collective-permute-start.9
  40.2 2.6 %collective-permute-start.10 = (f32[11,8,128]{2,1,0:T(8,128)S(1)}, f32[11,8,128]{2,1,0:T(8,128)S(1)}, u32[]{:S(2)}, u32[]{:S(2)}) collective-permute-start(f32[11,8,128]{2,1,0:T(8,128)S(1)} %get-tuple-element.36), channel_id=1, source_target_pairs={{1,0},{2,1},{3,2},{5,4},{6,5},{7,6},{9,8},{10,9},{11,10},{13,12},{... | collective-permute-start | bytes 135176 | tf_op jit(solution)/shard_map/ppermute | solution.py:288
  42.8 3.3 %collective-permute-start.11 = (f32[11,8,128]{2,1,0:T(8,128)S(1)}, f32[11,8,128]{2,1,0:T(8,128)S(1)}, u32[]{:S(2)}, u32[]{:S(2)}) collective-permute-start(f32[11,8,128]{2,1,0:T(8,128)S(1)} %get-tuple-element.37), channel_id=1, source_target_pairs={{0,1},{1,2},{2,3},{4,5},{5,6},{6,7},{8,9},{9,10},{10,11},{12,13},{... | collective-permute-start | bytes 135176 | tf_op jit(solution)/shard_map/ppermute | solution.py:288
  46.0 4.1 %collective-permute-start.12 = (f32[3,128]{1,0:T(4,128)S(1)}, f32[3,128]{1,0:T(4,128)S(1)}, u32[]{:S(2)}, u32[]{:S(2)}) collective-permute-start(f32[3,128]{1,0:T(4,128)S(1)} %get-tuple-element.38), channel_id=1, source_target_pairs={{1,28},{2,29},{3,30},{5,0},{6,1},{7,2},{9,4},{10,5},{11,6},{13,8},... | collective-permute-start | bytes 4616 | tf_op jit(solution)/shard_map/ppermute | solution.py:296
  50.1 1.3 %collective-permute-done.12.rest_4_ = f32[3,128]{1,0:T(4,128)S(1)} collective-permute-done((f32[3,128]{1,0:T(4,128)S(1)}, f32[3,128]{1,0:T(4,128)S(1)}, u32[]{:S(2)}, u32[]{:S(2)}) %collective-permute-start.12) | collective-permute-done | bytes 1568 | tf_op jit(solution)/shard_map/ppermute | solution.py:296
  51.4 4.7 %collective-permute-start.13 = (f32[3,128]{1,0:T(4,128)S(1)}, f32[3,128]{1,0:T(4,128)S(1)}, u32[]{:S(2)}, u32[]{:S(2)}) collective-permute-start(f32[3,128]{1,0:T(4,128)S(1)} %get-tuple-element.39), channel_id=1, source_target_pairs={{0,29},{1,30},{2,31},{4,1},{5,2},{6,3},{8,5},{9,6},{10,7},{12,9},{... | collective-permute-start | bytes 4616 | tf_op jit(solution)/shard_map/ppermute | solution.py:296
  56.1 1.3 %collective-permute-done.13.rest_5_ = f32[3,128]{1,0:T(4,128)S(1)} collective-permute-done((f32[3,128]{1,0:T(4,128)S(1)}, f32[3,128]{1,0:T(4,128)S(1)}, u32[]{:S(2)}, u32[]{:S(2)}) %collective-permute-start.13) | collective-permute-done | bytes 1568 | tf_op jit(solution)/shard_map/ppermute | solution.py:296
  57.4 1.9 %collective-permute-start.14 = (f32[3,128]{1,0:T(4,128)S(1)}, f32[3,128]{1,0:T(4,128)S(1)}, u32[]{:S(2)}, u32[]{:S(2)}) collective-permute-start(f32[3,128]{1,0:T(4,128)S(1)} %get-tuple-element.40), channel_id=1, source_target_pairs={{1,4},{2,5},{3,6},{5,8},{6,9},{7,10},{9,12},{10,13},{11,14},{13,16... | collective-permute-start | bytes 4616 | tf_op jit(solution)/shard_map/ppermute | solution.py:296
  59.3 4.8 %collective-permute-done.14.rest_6_ = f32[3,128]{1,0:T(4,128)S(1)} collective-permute-done((f32[3,128]{1,0:T(4,128)S(1)}, f32[3,128]{1,0:T(4,128)S(1)}, u32[]{:S(2)}, u32[]{:S(2)}) %collective-permute-start.14) | collective-permute-done | bytes 1568 | tf_op jit(solution)/shard_map/ppermute | solution.py:296
  64.1 1.9 %collective-permute-start.15 = (f32[3,128]{1,0:T(4,128)S(1)}, f32[3,128]{1,0:T(4,128)S(1)}, u32[]{:S(2)}, u32[]{:S(2)}) collective-permute-start(f32[3,128]{1,0:T(4,128)S(1)} %get-tuple-element.41), channel_id=1, source_target_pairs={{0,5},{1,6},{2,7},{4,9},{5,10},{6,11},{8,13},{9,14},{10,15},{12,17... | collective-permute-start | bytes 4616 | tf_op jit(solution)/shard_map/ppermute | solution.py:296
  66.0 4.8 %collective-permute-done.15.rest_7_ = f32[3,128]{1,0:T(4,128)S(1)} collective-permute-done((f32[3,128]{1,0:T(4,128)S(1)}, f32[3,128]{1,0:T(4,128)S(1)}, u32[]{:S(2)}, u32[]{:S(2)}) %collective-permute-start.15) | collective-permute-done | bytes 1568 | tf_op jit(solution)/shard_map/ppermute | solution.py:296
  70.8 0.0 collective-permute-done.10.rest_2_
  70.8 0.0 collective-permute-done.11.rest_3_
  70.8 0.0 collective-permute-done.8.rest_0_
  70.8 0.0 collective-permute-done.9.rest_1_
  70.8 2.6 %write_out.1 = (f32[41,10,48,128]{3,2,1,0:T(8,128)S(1)}, f32[27,8,32,128]{3,2,1,0:T(8,128)}, f32[14,8,32,128]{3,2,1,0:T(8,128)}) custom-call(f32[41,10,48,128]{3,2,1,0:T(8,128)S(1)} %get-tuple-element.33.out_in, f32[11,32,128]{2,1,0:T(8,128)S(1)} %collective-permute-done.8.rest_0_, ...), custom_call_target="tpu_custom_call", output_to_operand_aliasing={{0}: (0, {})} | custom-call | bytes 10747904 | tf_op jit(solution)/shard_map/write_out/pallas_call | solution.py:355
Async XLA Ops:
  4.4 34.2 %collective-permute-start = (f32[11,32,128]{2,1,0:T(8,128)S(1)}, f32[11,32,128]{2,1,0:T(8,128)S(1)}, u32[]{:S(2)}, u32[]{:S(2)}) collective-permute-start(f32[11,32,128]{2,1,0:T(8,128)S(1)} %get-tuple-element.25), channel_id=1, source_target_pairs={{0,28},{4,0},{8,4},{12,8},{16,12},{20,16},{24,20},{28,24},{1,29},{... | collective-permute-start | bytes 540680 | tf_op jit(solution)/shard_map/ppermute | solution.py:288
  6.3 32.2 %collective-permute-start.1 = (f32[11,32,128]{2,1,0:T(8,128)S(1)}, f32[11,32,128]{2,1,0:T(8,128)S(1)}, u32[]{:S(2)}, u32[]{:S(2)}) collective-permute-start(f32[11,32,128]{2,1,0:T(8,128)S(1)} %get-tuple-element.26), channel_id=1, source_target_pairs={{0,4},{4,8},{8,12},{12,16},{16,20},{20,24},{24,28},{28,0},{1,5},{5... | collective-permute-start | bytes 540680 | tf_op jit(solution)/shard_map/ppermute | solution.py:288
  6.3 32.2 %collective-permute-start.2 = (f32[11,8,128]{2,1,0:T(8,128)S(1)}, f32[11,8,128]{2,1,0:T(8,128)S(1)}, u32[]{:S(2)}, u32[]{:S(2)}) collective-permute-start(f32[11,8,128]{2,1,0:T(8,128)S(1)} %get-tuple-element.27), channel_id=1, source_target_pairs={{1,0},{2,1},{3,2},{5,4},{6,5},{7,6},{9,8},{10,9},{11,10},{13,12},{... | collective-permute-start | bytes 135176 | tf_op jit(solution)/shard_map/ppermute | solution.py:288
  8.7 29.9 %collective-permute-start.3 = (f32[11,8,128]{2,1,0:T(8,128)S(1)}, f32[11,8,128]{2,1,0:T(8,128)S(1)}, u32[]{:S(2)}, u32[]{:S(2)}) collective-permute-start(f32[11,8,128]{2,1,0:T(8,128)S(1)} %get-tuple-element.28), channel_id=1, source_target_pairs={{0,1},{1,2},{2,3},{4,5},{5,6},{6,7},{8,9},{9,10},{10,11},{12,13},{... | collective-permute-start | bytes 135176 | tf_op jit(solution)/shard_map/ppermute | solution.py:288
  12.2 5.2 %collective-permute-start.4 = (f32[3,128]{1,0:T(4,128)S(1)}, f32[3,128]{1,0:T(4,128)S(1)}, u32[]{:S(2)}, u32[]{:S(2)}) collective-permute-start(f32[3,128]{1,0:T(4,128)S(1)} %get-tuple-element.29), channel_id=1, source_target_pairs={{1,28},{2,29},{3,30},{5,0},{6,1},{7,2},{9,4},{10,5},{11,6},{13,8},... | collective-permute-start | bytes 4616 | tf_op jit(solution)/shard_map/ppermute | solution.py:296
  17.3 7.8 %collective-permute-start.5 = (f32[3,128]{1,0:T(4,128)S(1)}, f32[3,128]{1,0:T(4,128)S(1)}, u32[]{:S(2)}, u32[]{:S(2)}) collective-permute-start(f32[3,128]{1,0:T(4,128)S(1)} %get-tuple-element.30), channel_id=1, source_target_pairs={{0,29},{1,30},{2,31},{4,1},{5,2},{6,3},{8,5},{9,6},{10,7},{12,9},{... | collective-permute-start | bytes 4616 | tf_op jit(solution)/shard_map/ppermute | solution.py:296
  25.2 6.7 %collective-permute-start.6 = (f32[3,128]{1,0:T(4,128)S(1)}, f32[3,128]{1,0:T(4,128)S(1)}, u32[]{:S(2)}, u32[]{:S(2)}) collective-permute-start(f32[3,128]{1,0:T(4,128)S(1)} %get-tuple-element.31), channel_id=1, source_target_pairs={{1,4},{2,5},{3,6},{5,8},{6,9},{7,10},{9,12},{10,13},{11,14},{13,16... | collective-permute-start | bytes 4616 | tf_op jit(solution)/shard_map/ppermute | solution.py:296
  31.9 6.7 %collective-permute-start.7 = (f32[3,128]{1,0:T(4,128)S(1)}, f32[3,128]{1,0:T(4,128)S(1)}, u32[]{:S(2)}, u32[]{:S(2)}) collective-permute-start(f32[3,128]{1,0:T(4,128)S(1)} %get-tuple-element.32), channel_id=1, source_target_pairs={{0,5},{1,6},{2,7},{4,9},{5,10},{6,11},{8,13},{9,14},{10,15},{12,17... | collective-permute-start | bytes 4616 | tf_op jit(solution)/shard_map/ppermute | solution.py:296
  39.6 31.2 %collective-permute-start.8 = (f32[11,32,128]{2,1,0:T(8,128)S(1)}, f32[11,32,128]{2,1,0:T(8,128)S(1)}, u32[]{:S(2)}, u32[]{:S(2)}) collective-permute-start(f32[11,32,128]{2,1,0:T(8,128)S(1)} %get-tuple-element.34), channel_id=1, source_target_pairs={{0,28},{4,0},{8,4},{12,8},{16,12},{20,16},{24,20},{28,24},{1,29},{... | collective-permute-start | bytes 540680 | tf_op jit(solution)/shard_map/ppermute | solution.py:288
  39.7 31.1 %collective-permute-start.9 = (f32[11,32,128]{2,1,0:T(8,128)S(1)}, f32[11,32,128]{2,1,0:T(8,128)S(1)}, u32[]{:S(2)}, u32[]{:S(2)}) collective-permute-start(f32[11,32,128]{2,1,0:T(8,128)S(1)} %get-tuple-element.35), channel_id=1, source_target_pairs={{0,4},{4,8},{8,12},{12,16},{16,20},{20,24},{24,28},{28,0},{1,5},{5... | collective-permute-start | bytes 540680 | tf_op jit(solution)/shard_map/ppermute | solution.py:288
  40.2 30.6 %collective-permute-start.10 = (f32[11,8,128]{2,1,0:T(8,128)S(1)}, f32[11,8,128]{2,1,0:T(8,128)S(1)}, u32[]{:S(2)}, u32[]{:S(2)}) collective-permute-start(f32[11,8,128]{2,1,0:T(8,128)S(1)} %get-tuple-element.36), channel_id=1, source_target_pairs={{1,0},{2,1},{3,2},{5,4},{6,5},{7,6},{9,8},{10,9},{11,10},{13,12},{... | collective-permute-start | bytes 135176 | tf_op jit(solution)/shard_map/ppermute | solution.py:288
  42.8 28.0 %collective-permute-start.11 = (f32[11,8,128]{2,1,0:T(8,128)S(1)}, f32[11,8,128]{2,1,0:T(8,128)S(1)}, u32[]{:S(2)}, u32[]{:S(2)}) collective-permute-start(f32[11,8,128]{2,1,0:T(8,128)S(1)} %get-tuple-element.37), channel_id=1, source_target_pairs={{0,1},{1,2},{2,3},{4,5},{5,6},{6,7},{8,9},{9,10},{10,11},{12,13},{... | collective-permute-start | bytes 135176 | tf_op jit(solution)/shard_map/ppermute | solution.py:288
  46.0 5.4 %collective-permute-start.12 = (f32[3,128]{1,0:T(4,128)S(1)}, f32[3,128]{1,0:T(4,128)S(1)}, u32[]{:S(2)}, u32[]{:S(2)}) collective-permute-start(f32[3,128]{1,0:T(4,128)S(1)} %get-tuple-element.38), channel_id=1, source_target_pairs={{1,28},{2,29},{3,30},{5,0},{6,1},{7,2},{9,4},{10,5},{11,6},{13,8},... | collective-permute-start | bytes 4616 | tf_op jit(solution)/shard_map/ppermute | solution.py:296
  51.4 6.0 %collective-permute-start.13 = (f32[3,128]{1,0:T(4,128)S(1)}, f32[3,128]{1,0:T(4,128)S(1)}, u32[]{:S(2)}, u32[]{:S(2)}) collective-permute-start(f32[3,128]{1,0:T(4,128)S(1)} %get-tuple-element.39), channel_id=1, source_target_pairs={{0,29},{1,30},{2,31},{4,1},{5,2},{6,3},{8,5},{9,6},{10,7},{12,9},{... | collective-permute-start | bytes 4616 | tf_op jit(solution)/shard_map/ppermute | solution.py:296
  57.4 6.7 %collective-permute-start.14 = (f32[3,128]{1,0:T(4,128)S(1)}, f32[3,128]{1,0:T(4,128)S(1)}, u32[]{:S(2)}, u32[]{:S(2)}) collective-permute-start(f32[3,128]{1,0:T(4,128)S(1)} %get-tuple-element.40), channel_id=1, source_target_pairs={{1,4},{2,5},{3,6},{5,8},{6,9},{7,10},{9,12},{10,13},{11,14},{13,16... | collective-permute-start | bytes 4616 | tf_op jit(solution)/shard_map/ppermute | solution.py:296
  64.1 6.7 %collective-permute-start.15 = (f32[3,128]{1,0:T(4,128)S(1)}, f32[3,128]{1,0:T(4,128)S(1)}, u32[]{:S(2)}, u32[]{:S(2)}) collective-permute-start(f32[3,128]{1,0:T(4,128)S(1)} %get-tuple-element.41), channel_id=1, source_target_pairs={{0,5},{1,6},{2,7},{4,9},{5,10},{6,11},{8,13},{9,14},{10,15},{12,17... | collective-permute-start | bytes 4616 | tf_op jit(solution)/shard_map/ppermute | solution.py:296

commit v2 on v1

v2 whole, which is shorter than its diff:
```python
import functools
import math

import jax
import jax.numpy as jnp
from jax import lax
from jax.experimental import pallas as pl
from jax.experimental.pallas import tpu as pltpu
from jax.sharding import PartitionSpec as P

relax_flow = 0.8
relax_heat = 0.9
relax_solvent = 1.1
fan_speed = 0.05
heater_temp = 2.0

FLOW = [(a, b, c) for a in (-1, 0, 1) for b in (-1, 0, 1) for c in (-1, 0, 1)]
SCAL = [(0, 0, 0), (1, 0, 0), (-1, 0, 0), (0, 1, 0), (0, -1, 0), (0, 0, 1), (0, 0, -1)]
DIRS = FLOW + SCAL + SCAL
FLOW_W = {0: 8.0 / 27.0, 1: 2.0 / 27.0, 2: 1.0 / 54.0, 3: 1.0 / 216.0}
NF = len(FLOW)
NS = len(SCAL)
NQ = len(DIRS)
SUB = 8
PAD = 8

X_SETS = {a: [i for i, d in enumerate(DIRS) if d[0] == a] for a in (-1, 1)}
Y_SETS = {b: [i for i, d in enumerate(DIRS) if d[1] == b] for b in (-1, 1)}
SIDE_SETS = {b: [i for i, d in enumerate(DIRS) if d[1] in (0, b)] for b in (-1, 1)}
SIDES = (-1, 1)


def collide(load, flags, put):
    wall = flags == 1
    fan = flags == 2
    heater = flags == 3
    exhaust = flags == 4
    row_s, row_my, row_mz = [], [], []
    for a in range(3):
        sums, mz = [], None
        for b in range(3):
            lo, mid, hi = (load(9 * a + 3 * b + c) for c in range(3))
            sums.append(lo + mid + hi)
            diff = hi - lo
            mz = diff if mz is None else mz + diff
        row_s.append(sums[0] + sums[1] + sums[2])
        row_my.append(sums[2] - sums[0])
        row_mz.append(mz)
    density = row_s[0] + row_s[1] + row_s[2]
    inverse = 1.0 / jnp.where(wall, 1.0, density)
    vel_x = jnp.where(fan, fan_speed, (row_s[2] - row_s[0]) * inverse)
    vel_y = jnp.where(fan, 0.0, (row_my[0] + row_my[1] + row_my[2]) * inverse)
    vel_z = jnp.where(fan, 0.0, (row_mz[0] + row_mz[1] + row_mz[2]) * inverse)
    rho_eq = jnp.where(exhaust, 1.0, density)
    forced = fan | exhaust
    keep = jnp.where(forced, 0.0, 1.0 - 1.0 / relax_flow)
    scale = jnp.where(forced, rho_eq, rho_eq * (1.0 / relax_flow))
    root = math.sqrt(4.5)
    q = [vel_x * root, vel_y * root, vel_z * root]
    base = 1.0 - (q[0] * q[0] + q[1] * q[1] + q[2] * q[2]) * (1.0 / 3.0)
    by_w = {n: scale * w for n, w in FLOW_W.items()}
    by_w3 = {n: scale * (w * math.sqrt(2.0)) for n, w in FLOW_W.items() if n}

    def project(vector):
        total = None
        for part, comp in zip(vector, q):
            if part:
                if total is None:
                    total = comp if part > 0 else -comp
                else:
                    total = total + comp if part > 0 else total - comp
        return total

    cache = {}
    for i in range(NF // 2, NF):
        vector = FLOW[i]
        n = sum(abs(p) for p in vector)
        f_i = load(i)
        if n == 0:
            put(i, jnp.where(wall, f_i, keep * f_i + by_w[0] * base))
            continue
        first = next(p for p in vector if p)
        assert first > 0
        lead = vector[:2]
        if vector[2] and any(lead):
            if lead not in cache:
                cache[lead] = project(lead + (0,))
            proj = cache[lead] + q[2] if vector[2] > 0 else cache[lead] - q[2]
        else:
            if vector not in cache:
                cache[lead if any(lead) else vector] = project(vector)
            proj = cache[lead if any(lead) else vector]
        f_o = load(NF - 1 - i)
        even = by_w[n] * (base + proj * proj)
        odd = by_w3[n] * proj
        put(i, jnp.where(wall, f_o, keep * f_i + (even + odd)))
        put(NF - 1 - i, jnp.where(wall, f_i, keep * f_o + (even - odd)))

    for first, relax in ((NF, relax_heat), (NF + NS, relax_solvent)):
        total = load(first)
        for j in range(1, NS):
            total = total + load(first + j)
        if first == NF:
            keep_s = jnp.where(heater, 0.0, 1.0 - 1.0 / relax)
            source = jnp.where(heater, heater_temp, total * (1.0 / relax))
        else:
            keep_s = jnp.where(exhaust, 0.0, 1.0 - 1.0 / relax)
            source = jnp.where(exhaust, 0.0, total * (1.0 / relax))
        g = load(first)
        put(first, jnp.where(wall, g, keep_s * g + source * 0.25))
        eighth = source * 0.125
        half = source * 0.5
        for axis, vel in enumerate((vel_x, vel_y, vel_z)):
            odd = half * vel
            g_p, g_m = load(first + 1 + 2 * axis), load(first + 2 + 2 * axis)
            put(first + 1 + 2 * axis, jnp.where(wall, g_m, keep_s * g_p + (eighth + odd)))
            put(first + 2 + 2 * axis, jnp.where(wall, g_p, keep_s * g_m + (eighth - odd)))


def shift_lanes(value, c):
    if c == 0:
        return value
    lanes = value.shape[-1]
    lane = lax.broadcasted_iota(jnp.int32, value.shape, value.ndim - 1)
    edge = 0 if c > 0 else lanes - 1
    return jnp.where(lane == edge, 0.0, pltpu.roll(value, c % lanes, value.ndim - 1))


def slot(x):
    return x + 1


def push_tile(dst, x, row):
    def put(i, value):
        a, b, c = DIRS[i]
        dst[i, slot(x + a), row + PAD + b : row + PAD + b + SUB, :] = shift_lanes(value, c)

    return put


def flat_of(ref):
    shape = ref.shape
    return ref.reshape(shape[0], shape[1] * shape[2], shape[3])


def lines(x, y, rows, count, step=1):
    return pl.ds(slot(x) * rows + PAD + y, count, stride=step * rows)


def side_span(i, size_x):
    a = DIRS[i][0]
    return {-1: (-1, 1), 0: (0, size_x - 1), 1: (size_x - 1, 1)}[a]


def sizes_of(state):
    return state.shape[1] - 2, state.shape[2] - 2 * PAD


def first_cross_rows(size_x):
    ran = len(Y_SETS[1]) * size_x
    total = ran + 2 * len(SIDE_SETS[1]) + 2
    return ran, -(-total // SUB) * SUB


def send_first_cross(state, kinds, sent):
    size_x, size_y = sizes_of(state)
    rows, flat = state.shape[2], flat_of(state)
    ran, _ = first_cross_rows(size_x)
    for b, msg in zip(SIDES, sent):
        y_out, y_edge = (size_y, size_y - 1) if b > 0 else (-1, 0)
        for k, i in enumerate(Y_SETS[b]):
            msg[k * size_x : (k + 1) * size_x, :] = flat[i, lines(DIRS[i][0], y_out, rows, size_x), :]
        for k, i in enumerate(SIDE_SETS[b]):
            x, step = side_span(i, size_x)
            msg[ran + 2 * k : ran + 2 * k + 2, :] = flat[i, lines(x, y_edge, rows, 2, step), :]
        last = ran + 2 * len(SIDE_SETS[b])
        for s, x in enumerate((0, size_x - 1)):
            line = kinds[x, y_edge : y_edge + 1, :]
            msg[last + s : last + s + 1, :] = (line + 1).astype(jnp.float32)


def take_first_cross(state, halo_kinds, received):
    size_x, size_y = sizes_of(state)
    rows, flat = state.shape[2], flat_of(state)
    ran, _ = first_cross_rows(size_x)
    halo_kinds[...] = jnp.zeros(halo_kinds.shape, jnp.float32)
    for b, msg in zip(SIDES, received):
        y_in, y_halo = (0, -1) if b > 0 else (size_y - 1, size_y)
        for k, i in enumerate(Y_SETS[b]):
            flat[i, lines(DIRS[i][0], y_in, rows, size_x), :] = msg[k * size_x : (k + 1) * size_x, :]
        for k, i in enumerate(SIDE_SETS[b]):
            x, step = side_span(i, size_x)
            flat[i, lines(x, y_halo, rows, 2, step), :] = msg[ran + 2 * k : ran + 2 * k + 2, :]
        last = ran + 2 * len(SIDE_SETS[b])
        first = 0 if b > 0 else 2
        halo_kinds[first : first + 2, :] = msg[last : last + 2, :]


def first_loop_rows(size_y):
    main = len(X_SETS[1]) * size_y
    total = main + 2 * len(X_SETS[1])
    return main, -(-total // SUB) * SUB


def send_first_loop(state, sent):
    size_x, size_y = sizes_of(state)
    main, _ = first_loop_rows(size_y)
    for a, msg in zip(SIDES, sent):
        x = -1 if a < 0 else size_x
        for k, i in enumerate(X_SETS[a]):
            for y in range(0, size_y, SUB):
                msg[k * size_y + y : k * size_y + y + SUB, :] = state[i, slot(x), y + PAD : y + PAD + SUB, :]
            for s, y in enumerate((-1, size_y)):
                row = main + 2 * k + s
                msg[row : row + 1, :] = state[i, slot(x), y + PAD : y + PAD + 1, :]


def take_first_loop(state, received):
    size_x, size_y = sizes_of(state)
    main, _ = first_loop_rows(size_y)
    for a, msg in zip(SIDES, received):
        x = 0 if a > 0 else size_x - 1
        for k, i in enumerate(X_SETS[a]):
            for y in range(0, size_y, SUB):
                state[i, slot(x), y + PAD : y + PAD + SUB, :] = msg[k * size_y + y : k * size_y + y + SUB, :]
            for s, y in enumerate((-1, size_y)):
                row = main + 2 * k + s
                state[i, slot(x), y + PAD : y + PAD + 1, :] = msg[row : row + 1, :]


def load_tile(state, x, y):
    return lambda i: state[i, slot(x), y + PAD : y + PAD + SUB, :]


def first_step_tiles(size_x, tiles, pops, scal, state, kinds, raw, sems, kinds_copy=None):
    def copies(x):
        result = []
        for n, y in enumerate(tiles):
            here = pl.ds(y, SUB)
            there = pl.ds(n * SUB, SUB)
            result.append(pltpu.make_async_copy(pops.at[:, x, here], raw.at[0:NF, x, there], sems.at[2 * n, x]))
            result.append(pltpu.make_async_copy(scal.at[:, x, here], raw.at[NF:NQ, x, there], sems.at[2 * n + 1, x]))
        return result

    for x in range(size_x):
        for copy in copies(x):
            copy.start()
        if x == 0 and kinds_copy is not None:
            kinds_copy.start()
    if kinds_copy is not None:
        kinds_copy.wait()

    @pl.loop(0, size_x)
    def _(x):
        for copy in copies(x):
            copy.wait()
        for n, y in enumerate(tiles):
            collide(
                lambda i: raw[i, x, n * SUB : (n + 1) * SUB, :],
                kinds[x, y : y + SUB, :],
                push_tile(state, x, y),
            )


def side_kernel(size_x, tiles, pops, scal, flags, state, kinds, sent_a, sent_b, raw, sems, kinds_sem):
    kinds_copy = pltpu.make_async_copy(flags, kinds, kinds_sem)
    first_step_tiles(size_x, tiles, pops, scal, state, kinds, raw, sems, kinds_copy)
    send_first_cross(state, kinds, (sent_a, sent_b))


def middle_kernel(size_x, tiles, pops, scal, kinds, state_in, state, raw, sems):
    first_step_tiles(size_x, tiles, pops, scal, state, kinds, raw, sems)


def turn_kernel(state_in, got_a, got_b, state, halo_kinds, sent_a, sent_b):
    take_first_cross(state, halo_kinds, (got_a, got_b))
    send_first_loop(state, (sent_a, sent_b))


def inner_kernel(state, kinds, out, sent_a, sent_b):
    size_x, size_y = sizes_of(state)
    rows, flat = out.shape[2], flat_of(out)

    @pl.loop(1, size_x - 1)
    def _(x):
        for y in range(0, size_y, SUB):
            collide(load_tile(state, x, y), kinds[x, y : y + SUB, :], push_tile(out, x, y))

    for b, msg in zip(SIDES, (sent_a, sent_b)):
        y_out = size_y if b > 0 else -1
        for k, i in enumerate(Y_SETS[b]):
            msg[k * SUB : k * SUB + size_x - 2, :] = flat[i, lines(DIRS[i][0] + 1, y_out, rows, size_x - 2), :]


def edge_kernel(state_in, out_in, kinds, halo_kinds, loop_a, loop_b, cross_a, cross_b, state, out, sent_a, sent_b, halo):
    size_x, size_y = sizes_of(state)
    rows, flat, flat_out = state.shape[2], flat_of(state), flat_of(out)
    take_first_loop(state, (loop_a, loop_b))
    for i in range(NQ):
        halo[i, 0:2, :] = flat[i, lines(0, -1, rows, 2, size_x - 1), :]
        halo[i, 2:4, :] = flat[i, lines(0, size_y, rows, 2, size_x - 1), :]

    @pl.loop(0, 2)
    def _(side):
        x = side * (size_x - 1)
        for y in range(0, size_y, SUB):
            collide(load_tile(state, x, y), kinds[x, y : y + SUB, :], push_tile(out, x, y))

    code = halo_kinds[...].astype(jnp.int32)

    def put(i, value):
        a, b, c = DIRS[i]
        if b:
            y_in, first = (0, 0) if b > 0 else (size_y - 1, 2)
            moved = shift_lanes(jnp.where(code == 0, 0.0, value), c)
            flat_out[i, lines(a, y_in, rows, 2, size_x - 1), :] = moved[first : first + 2, :]

    collide(lambda i: halo[i], code - 1, put)
    for b, msg in zip(SIDES, (cross_a, cross_b)):
        y_in = 0 if b > 0 else size_y - 1
        for k, i in enumerate(Y_SETS[b]):
            flat_out[i, lines(DIRS[i][0] + 1, y_in, rows, size_x - 2), :] = msg[k * SUB : k * SUB + size_x - 2, :]
    for a, msg in zip(SIDES, (sent_a, sent_b)):
        x = -1 if a < 0 else size_x
        for k, i in enumerate(X_SETS[a]):
            for y in range(0, size_y, SUB):
                msg[k, y : y + SUB, :] = out[i, slot(x), y + PAD : y + PAD + SUB, :]


def write_kernel(out, pops, scal, sems):
    size_x, size_y = sizes_of(out)
    copies = []
    for x in range(size_x):
        inner = pl.ds(PAD, size_y)
        copies.append(pltpu.make_async_copy(out.at[0:NF, slot(x), inner], pops.at[:, x], sems.at[0, x]))
        copies.append(pltpu.make_async_copy(out.at[NF:NQ, slot(x), inner], scal.at[:, x], sems.at[1, x]))
    for copy in copies:
        copy.start()
    for copy in copies:
        copy.wait()


def last_kernel(pops_in, scal_in, got_a, got_b, pops, scal, sems):
    size_x = pops.shape[1]
    copies = []
    for a, msg in zip(SIDES, (got_a, got_b)):
        x = 0 if a > 0 else size_x - 1
        flow = [i for i in X_SETS[a] if i < NF]
        spans = [(0, len(flow), pops, flow[0])]
        spans += [(k, 1, scal, i - NF) for k, i in enumerate(X_SETS[a]) if i >= NF]
        for k, count, dst, first in spans:
            here = msg.at[pl.ds(k, count)]
            copies.append(pltpu.make_async_copy(here, dst.at[pl.ds(first, count), x], sems.at[len(copies)]))
    for copy in copies:
        copy.start()
    for copy in copies:
        copy.wait()


def shift_along(axis, closed, messages):
    count = lax.axis_size(axis)
    received = []
    for step, cells in zip(SIDES, messages):
        pairs = [(i, (i + step) % count) for i in range(count) if closed or 0 <= i + step < count]
        received.append(lax.ppermute(cells, axis, pairs))
    return received


def per_device(populations, scalars, node_flags):
    size_x, size_y, size_z = node_flags.shape
    f32 = jnp.float32
    state_shape = pltpu.VMEM((NQ, size_x + 2, size_y + 2 * PAD, size_z), f32)
    kinds_shape = pltpu.VMEM((size_x, size_y, size_z), jnp.int32)
    halo_kinds_shape = pltpu.VMEM((SUB, size_z), f32)
    cross_1 = [pltpu.VMEM((first_cross_rows(size_x)[1], size_z), f32)] * 2
    loop_1 = [pltpu.VMEM((first_loop_rows(size_y)[1], size_z), f32)] * 2
    cross_2 = [pltpu.VMEM((len(Y_SETS[1]) * SUB, size_z), f32)] * 2
    loop_2 = [pltpu.VMEM((len(X_SETS[1]), size_y, size_z), f32)] * 2
    hbm = pl.BlockSpec(memory_space=pl.ANY)
    vmem = pl.BlockSpec(memory_space=pltpu.VMEM)
    pops_shape = jax.ShapeDtypeStruct(populations.shape, f32)
    scal_shape = jax.ShapeDtypeStruct(scalars.shape, f32)

    def call(kernel, name, args, results, tiles=0, moved=0, scratch=(), aliases=None):
        cells = tiles * SUB * size_z
        placed, specs = [], []
        for place, array in args:
            placed.append(pltpu.with_memory_space_constraint(array, place))
            specs.append(vmem if place == pltpu.VMEM else hbm)
        return pl.pallas_call(
            kernel,
            out_shape=results,
            in_specs=specs,
            out_specs=[hbm if isinstance(r, jax.ShapeDtypeStruct) else vmem for r in results],
            scratch_shapes=list(scratch),
            input_output_aliases=aliases or {},
            compiler_params=pltpu.CompilerParams(vmem_limit_bytes=16 * 2**20),
            cost_estimate=pl.CostEstimate(
                flops=500 * cells, bytes_accessed=8 * NQ * cells + moved, transcendentals=cells
            ),
            name=name,
        )(*placed)

    def on_chip(*arrays):
        return [(pltpu.VMEM, x) for x in arrays]

    def in_hbm(*arrays):
        return [(pltpu.HBM, x) for x in arrays]

    tiles = list(range(0, size_y, SUB))
    side, middle = sorted({tiles[0], tiles[-1]}), tiles[1:-1]

    def staging(rows):
        return [
            pltpu.VMEM((NQ, size_x, len(rows) * SUB, size_z), f32),
            pltpu.SemaphoreType.DMA((2 * len(rows), size_x)),
        ]

    state, kinds, *sent = call(
        functools.partial(side_kernel, size_x, side),
        "first_step_side_rows",
        in_hbm(populations, scalars, node_flags),
        [state_shape, kinds_shape] + cross_1,
        tiles=size_x * len(side),
        scratch=staging(side) + [pltpu.SemaphoreType.DMA],
    )
    received = shift_along("cross", False, sent)
    if middle:
        (state,) = call(
            functools.partial(middle_kernel, size_x, middle),
            "first_step_middle_rows",
            in_hbm(populations, scalars) + on_chip(kinds, state),
            [state_shape],
            tiles=size_x * len(middle),
            scratch=staging(middle),
            aliases={3: 0},
        )
    state, halo_kinds, *sent = call(
        turn_kernel,
        "cross_to_loop",
        on_chip(state, *received),
        [state_shape, halo_kinds_shape] + loop_1,
        tiles=1,
        aliases={0: 0},
    )
    from_loop = shift_along("loop", True, sent)
    out, *sent = call(
        inner_kernel,
        "second_step_inner_planes",
        on_chip(state, kinds),
        [state_shape] + cross_2,
        tiles=(size_x - 2) * len(tiles),
    )
    from_cross = shift_along("cross", False, sent)
    state, out, *sent = call(
        edge_kernel,
        "second_step_edge_planes",
        on_chip(state, out, kinds, halo_kinds, *from_loop, *from_cross),
        [state_shape, state_shape] + loop_2,
        tiles=2 * len(tiles) + 1,
        scratch=[pltpu.VMEM((NQ, SUB, size_z), f32)],
        aliases={0: 0, 1: 1},
    )
    received = shift_along("loop", True, sent)
    new_pops, new_scal = call(
        write_kernel,
        "write_all_planes",
        on_chip(out),
        [pops_shape, scal_shape],
        moved=8 * NQ * size_x * size_y * size_z,
        scratch=[pltpu.SemaphoreType.DMA((2, size_x))],
    )
    new_pops, new_scal = call(
        last_kernel,
        "write_edge_planes",
        in_hbm(new_pops, new_scal) + on_chip(*received),
        [pops_shape, scal_shape],
        moved=16 * len(X_SETS[1]) * size_y * size_z,
        scratch=[pltpu.SemaphoreType.DMA((2 * len(X_SETS[1]),))],
        aliases={0: 0, 1: 1},
    )
    return new_pops, new_scal


def solution(mesh):
    wide = P(None, "loop", "cross", None)
    return jax.shard_map(
        per_device,
        mesh=mesh,
        in_specs=(wide, wide, P("loop", "cross", None)),
        out_specs=(wide, wide),
        check_vma=False,
    )
```

time: 73.8 us -> 34.9 us (0.47)
  the two profiles are of different devices: /device:TPU:8 before, /device:TPU:0 now
where the time goes in v2:
time: 34.9 us; the launch traced here: 34.7 us
  starting transfers between devices  16.3 us (47%)
  Pallas kernels  12.7 us (36%)
  waiting for transfers between devices  5.01 us (14%)
  between operations  0.73 us (2%)
    ppermute x8, starting transfers between devices, shift_along(): received.append(lax.ppermute(cells, axis, pairs))  16.3 us
    pallas_call x7, Pallas kernels, call(): pl.pallas_call(kernel, out_shape=results, in_specs=specs, out_specs=[hbm...  12.7 us
    ppermute x8, waiting for transfers between devices, shift_along(): received.append(lax.ppermute(cells, axis, pairs))  5.01 us
  transfers between devices with their start and end apart: 8, of which 4 were waited for; matrix products, arithmetic and copies ran while one was open for 0% of the time, Pallas kernels for 20%

profile of v2, /device:TPU:0, one launch (start us, length us, event | category | flops | bytes accessed | tf_op | source)
XLA Modules:
  0.0 34.7 jit_solution(9585657077058035963)
XLA Ops:
  0.6 3.7 %first_step_side_rows.1 = (f32[41,10,48,128]{3,2,1,0:T(8,128)S(1)}, s32[8,32,128]{2,1,0:T(8,128)S(1)}, f32[152,128]{1,0:T(8,128)S(1)}, f32[152,128]{1,0:T(8,128)S(1)}) custom-call(f32[27,8,32,128]{3,2,1,0:T(8,128)} %pops.3, f32[14,8,32,128]{3,2,1,0:T(8,128)} %scal.3, s32[8,32,128]{2,1,0:T(8,128)} %flags.1), custom_call_target="tpu_custom_call" | custom-call | flops 8192000 | bytes 5373952 | tf_op jit(solution)/shard_map/first_step_side_rows/pallas_call | solution.py:390
  4.4 1.3 %collective-permute-start = (f32[152,128]{1,0:T(8,128)S(1)}, f32[152,128]{1,0:T(8,128)S(1)}, u32[]{:S(2)}, u32[]{:S(2)}) collective-permute-start(f32[152,128]{1,0:T(8,128)S(1)} %get-tuple-element.20), channel_id=1, source_target_pairs={{1,0},{2,1},{3,2},{5,4},{6,5},{7,6},{9,8},{10,9},{11,10},{13,12},{... | collective-permute-start | bytes 233480 | tf_op jit(solution)/shard_map/ppermute | solution.py:365
  5.7 5.6 %collective-permute-start.1 = (f32[152,128]{1,0:T(8,128)S(1)}, f32[152,128]{1,0:T(8,128)S(1)}, u32[]{:S(2)}, u32[]{:S(2)}) collective-permute-start(f32[152,128]{1,0:T(8,128)S(1)} %get-tuple-element.21), channel_id=1, source_target_pairs={{0,1},{1,2},{2,3},{4,5},{5,6},{6,7},{8,9},{9,10},{10,11},{12,13},{... | collective-permute-start | bytes 233480 | tf_op jit(solution)/shard_map/ppermute | solution.py:365
  11.2 2.8 %first_step_middle_rows.1.state_in = f32[41,10,48,128]{3,2,1,0:T(8,128)S(1)} custom-call(f32[27,8,32,128]{3,2,1,0:T(8,128)} %pops.3, f32[14,8,32,128]{3,2,1,0:T(8,128)} %scal.3, s32[8,32,128]{2,1,0:T(8,128)S(1)} %get-tuple-element.18.kinds, f32[41,10,48,128]{3,2,1,0:T(8,128)S(1)} %get-tuple-element.19.state_in), custom_call_target="tpu_custom_call", output_to_operand_aliasing={{}: (3, {})} | custom-call | flops 8192000 | bytes 5373952 | tf_op jit(solution)/shard_map/first_step_middle_rows/pallas_call | solution.py:390
  14.0 0.0 collective-permute-done.got_a
  14.0 0.0 collective-permute-done.1.got_b
  14.0 0.1 cross_to_loop.1
  14.1 1.8 %collective-permute-start.2 = (f32[376,128]{1,0:T(8,128)S(1)}, f32[376,128]{1,0:T(8,128)S(1)}, u32[]{:S(2)}, u32[]{:S(2)}) collective-permute-start(f32[376,128]{1,0:T(8,128)S(1)} %get-tuple-element.25), channel_id=1, source_target_pairs={{0,28},{4,0},{8,4},{12,8},{16,12},{20,16},{24,20},{28,24},{1,29},{... | collective-permute-start | bytes 577544 | tf_op jit(solution)/shard_map/ppermute | solution.py:365
  15.9 0.0 collective-permute-start.3
  16.0 1.9 %second_step_inner_planes.1 = (f32[41,10,48,128]{3,2,1,0:T(8,128)S(1)}, f32[88,128]{1,0:T(8,128)S(1)}, f32[88,128]{1,0:T(8,128)S(1)}) custom-call(f32[41,10,48,128]{3,2,1,0:T(8,128)S(1)} %get-tuple-element.22.state.state_in, s32[8,32,128]{2,1,0:T(8,128)S(1)} %get-tuple-element.18.kinds), custom_call_target="tpu_custom_call" | custom-call | flops 12288000 | bytes 8060928 | tf_op jit(solution)/shard_map/second_step_inner_planes/pallas_call | solution.py:390
  17.8 1.3 %collective-permute-start.4 = (f32[88,128]{1,0:T(8,128)S(1)}, f32[88,128]{1,0:T(8,128)S(1)}, u32[]{:S(2)}, u32[]{:S(2)}) collective-permute-start(f32[88,128]{1,0:T(8,128)S(1)} %get-tuple-element.27), channel_id=1, source_target_pairs={{1,0},{2,1},{3,2},{5,4},{6,5},{7,6},{9,8},{10,9},{11,10},{13,12},{... | collective-permute-start | bytes 135176 | tf_op jit(solution)/shard_map/ppermute | solution.py:365
  19.1 4.5 %collective-permute-start.5 = (f32[88,128]{1,0:T(8,128)S(1)}, f32[88,128]{1,0:T(8,128)S(1)}, u32[]{:S(2)}, u32[]{:S(2)}) collective-permute-start(f32[88,128]{1,0:T(8,128)S(1)} %get-tuple-element.28), channel_id=1, source_target_pairs={{0,1},{1,2},{2,3},{4,5},{5,6},{6,7},{8,9},{9,10},{10,11},{12,13},{... | collective-permute-start | bytes 135176 | tf_op jit(solution)/shard_map/ppermute | solution.py:365
  23.7 0.1 collective-permute-done.4.cross_a
  23.7 1.6 %collective-permute-done.5.cross_b = f32[88,128]{1,0:T(8,128)S(1)} collective-permute-done((f32[88,128]{1,0:T(8,128)S(1)}, f32[88,128]{1,0:T(8,128)S(1)}, u32[]{:S(2)}, u32[]{:S(2)}) %collective-permute-start.5) | collective-permute-done | bytes 45088 | tf_op jit(solution)/shard_map/ppermute | solution.py:365
  25.4 0.0 collective-permute-done.2.loop_a
  25.4 0.0 collective-permute-done.3.loop_b
  25.4 0.8 %second_step_edge_planes.1 = (f32[41,10,48,128]{3,2,1,0:T(8,128)S(1)}, f32[41,10,48,128]{3,2,1,0:T(8,128)S(1)}, f32[11,32,128]{2,1,0:T(8,128)S(1)}, f32[11,32,128]{2,1,0:T(8,128)S(1)}) custom-call(f32[41,10,48,128]{3,2,1,0:T(8,128)S(1)} %get-tuple-element.22.state.state_in, ...), custom_call_target="tpu_custom_call", output_to_operand_aliasing={{0}: (0, {}), {1}: (1, {})} | custom-call | flops 4608000 | bytes 3022848 | tf_op jit(solution)/shard_map/second_step_edge_planes/pallas_call | solution.py:390
  26.2 1.8 %collective-permute-start.6 = (f32[11,32,128]{2,1,0:T(8,128)S(1)}, f32[11,32,128]{2,1,0:T(8,128)S(1)}, u32[]{:S(2)}, u32[]{:S(2)}) collective-permute-start(f32[11,32,128]{2,1,0:T(8,128)S(1)} %get-tuple-element.32), channel_id=1, source_target_pairs={{0,28},{4,0},{8,4},{12,8},{16,12},{20,16},{24,20},{28,24},{1,29},{... | collective-permute-start | bytes 540680 | tf_op jit(solution)/shard_map/ppermute | solution.py:365
  27.9 0.0 collective-permute-start.7
  27.9 2.5 %write_all_planes.1 = (f32[27,8,32,128]{3,2,1,0:T(8,128)}, f32[14,8,32,128]{3,2,1,0:T(8,128)}) custom-call(f32[41,10,48,128]{3,2,1,0:T(8,128)S(1)} %get-tuple-element.29.out), custom_call_target="tpu_custom_call" | custom-call | bytes 10747904 | tf_op jit(solution)/shard_map/write_all_planes/pallas_call | solution.py:390
  30.4 1.0 %collective-permute-done.6.got_a = f32[11,32,128]{2,1,0:T(8,128)S(1)} collective-permute-done((f32[11,32,128]{2,1,0:T(8,128)S(1)}, f32[11,32,128]{2,1,0:T(8,128)S(1)}, u32[]{:S(2)}, u32[]{:S(2)}) %collective-permute-start.6) | collective-permute-done | bytes 180256 | tf_op jit(solution)/shard_map/ppermute | solution.py:365
  31.5 2.3 %collective-permute-done.7.got_b = f32[11,32,128]{2,1,0:T(8,128)S(1)} collective-permute-done((f32[11,32,128]{2,1,0:T(8,128)S(1)}, f32[11,32,128]{2,1,0:T(8,128)S(1)}, u32[]{:S(2)}, u32[]{:S(2)}) %collective-permute-start.7) | collective-permute-done | bytes 180256 | tf_op jit(solution)/shard_map/ppermute | solution.py:365
  33.8 0.9 %write_edge_planes.1 = (f32[27,8,32,128]{3,2,1,0:T(8,128)}, f32[14,8,32,128]{3,2,1,0:T(8,128)}) custom-call(f32[27,8,32,128]{3,2,1,0:T(8,128)} %get-tuple-element.30.pops_in, f32[14,8,32,128]{3,2,1,0:T(8,128)} %get-tuple-element.31.scal_in, f32[11,32,128]{2,1,0:T(8,128)S(1)} %collective-permute-done.6.got_a, ...), custom_call_target="tpu_custom_call", output_to_operand_aliasing={{0}: (0, {}), {1}: (1, {})} | custom-call | bytes 720896 | tf_op jit(solution)/shard_map/write_edge_planes/pallas_call | solution.py:390
Async XLA Ops:
  4.4 9.6 %collective-permute-start = (f32[152,128]{1,0:T(8,128)S(1)}, f32[152,128]{1,0:T(8,128)S(1)}, u32[]{:S(2)}, u32[]{:S(2)}) collective-permute-start(f32[152,128]{1,0:T(8,128)S(1)} %get-tuple-element.20), channel_id=1, source_target_pairs={{1,0},{2,1},{3,2},{5,4},{6,5},{7,6},{9,8},{10,9},{11,10},{13,12},{... | collective-permute-start | bytes 233480 | tf_op jit(solution)/shard_map/ppermute | solution.py:365
  5.7 8.3 %collective-permute-start.1 = (f32[152,128]{1,0:T(8,128)S(1)}, f32[152,128]{1,0:T(8,128)S(1)}, u32[]{:S(2)}, u32[]{:S(2)}) collective-permute-start(f32[152,128]{1,0:T(8,128)S(1)} %get-tuple-element.21), channel_id=1, source_target_pairs={{0,1},{1,2},{2,3},{4,5},{5,6},{6,7},{8,9},{9,10},{10,11},{12,13},{... | collective-permute-start | bytes 233480 | tf_op jit(solution)/shard_map/ppermute | solution.py:365
  14.1 11.2 %collective-permute-start.2 = (f32[376,128]{1,0:T(8,128)S(1)}, f32[376,128]{1,0:T(8,128)S(1)}, u32[]{:S(2)}, u32[]{:S(2)}) collective-permute-start(f32[376,128]{1,0:T(8,128)S(1)} %get-tuple-element.25), channel_id=1, source_target_pairs={{0,28},{4,0},{8,4},{12,8},{16,12},{20,16},{24,20},{28,24},{1,29},{... | collective-permute-start | bytes 577544 | tf_op jit(solution)/shard_map/ppermute | solution.py:365
  15.9 9.4 %collective-permute-start.3 = (f32[376,128]{1,0:T(8,128)S(1)}, f32[376,128]{1,0:T(8,128)S(1)}, u32[]{:S(2)}, u32[]{:S(2)}) collective-permute-start(f32[376,128]{1,0:T(8,128)S(1)} %get-tuple-element.26), channel_id=1, source_target_pairs={{0,4},{4,8},{8,12},{12,16},{16,20},{20,24},{24,28},{28,0},{1,5},{5... | collective-permute-start | bytes 577544 | tf_op jit(solution)/shard_map/ppermute | solution.py:365
  17.8 5.9 %collective-permute-start.4 = (f32[88,128]{1,0:T(8,128)S(1)}, f32[88,128]{1,0:T(8,128)S(1)}, u32[]{:S(2)}, u32[]{:S(2)}) collective-permute-start(f32[88,128]{1,0:T(8,128)S(1)} %get-tuple-element.27), channel_id=1, source_target_pairs={{1,0},{2,1},{3,2},{5,4},{6,5},{7,6},{9,8},{10,9},{11,10},{13,12},{... | collective-permute-start | bytes 135176 | tf_op jit(solution)/shard_map/ppermute | solution.py:365
  19.1 6.2 %collective-permute-start.5 = (f32[88,128]{1,0:T(8,128)S(1)}, f32[88,128]{1,0:T(8,128)S(1)}, u32[]{:S(2)}, u32[]{:S(2)}) collective-permute-start(f32[88,128]{1,0:T(8,128)S(1)} %get-tuple-element.28), channel_id=1, source_target_pairs={{0,1},{1,2},{2,3},{4,5},{5,6},{6,7},{8,9},{9,10},{10,11},{12,13},{... | collective-permute-start | bytes 135176 | tf_op jit(solution)/shard_map/ppermute | solution.py:365
  26.2 5.3 %collective-permute-start.6 = (f32[11,32,128]{2,1,0:T(8,128)S(1)}, f32[11,32,128]{2,1,0:T(8,128)S(1)}, u32[]{:S(2)}, u32[]{:S(2)}) collective-permute-start(f32[11,32,128]{2,1,0:T(8,128)S(1)} %get-tuple-element.32), channel_id=1, source_target_pairs={{0,28},{4,0},{8,4},{12,8},{16,12},{20,16},{24,20},{28,24},{1,29},{... | collective-permute-start | bytes 540680 | tf_op jit(solution)/shard_map/ppermute | solution.py:365
  27.9 5.8 %collective-permute-start.7 = (f32[11,32,128]{2,1,0:T(8,128)S(1)}, f32[11,32,128]{2,1,0:T(8,128)S(1)}, u32[]{:S(2)}, u32[]{:S(2)}) collective-permute-start(f32[11,32,128]{2,1,0:T(8,128)S(1)} %get-tuple-element.33), channel_id=1, source_target_pairs={{0,4},{4,8},{8,12},{12,16},{16,20},{20,24},{24,28},{28,0},{1,5},{5... | collective-permute-start | bytes 540680 | tf_op jit(solution)/shard_map/ppermute | solution.py:365

commit v3 on v2

--- a/solution.py
+++ b/solution.py
@@ -152,6 +152,16 @@
     return {-1: (-1, 1), 0: (0, size_x - 1), 1: (size_x - 1, 1)}[a]
 
 
+def by_side_sent(axis, refs, fill):
+    odd = lax.rem(lax.axis_index(axis), 2) == 1
+    pl.when(odd)(lambda: fill((refs[0], refs[1])))
+    pl.when(jnp.logical_not(odd))(lambda: fill((refs[1], refs[0])))
+
+
+def by_side_received(axis, refs, take):
+    by_side_sent(axis, (refs[1], refs[0]), take)
+
+
 def sizes_of(state):
     return state.shape[1] - 2, state.shape[2] - 2 * PAD
 
@@ -265,7 +275,7 @@
 def side_kernel(size_x, tiles, pops, scal, flags, state, kinds, sent_a, sent_b, raw, sems, kinds_sem):
     kinds_copy = pltpu.make_async_copy(flags, kinds, kinds_sem)
     first_step_tiles(size_x, tiles, pops, scal, state, kinds, raw, sems, kinds_copy)
-    send_first_cross(state, kinds, (sent_a, sent_b))
+    by_side_sent("cross", (sent_a, sent_b), functools.partial(send_first_cross, state, kinds))
 
 
 def middle_kernel(size_x, tiles, pops, scal, kinds, state_in, state, raw, sems):
@@ -273,7 +283,7 @@
 
 
 def turn_kernel(state_in, got_a, got_b, state, halo_kinds, sent_a, sent_b):
-    take_first_cross(state, halo_kinds, (got_a, got_b))
+    by_side_received("cross", (got_a, got_b), functools.partial(take_first_cross, state, halo_kinds))
     send_first_loop(state, (sent_a, sent_b))
 
 
@@ -286,10 +296,13 @@
         for y in range(0, size_y, SUB):
             collide(load_tile(state, x, y), kinds[x, y : y + SUB, :], push_tile(out, x, y))
 
-    for b, msg in zip(SIDES, (sent_a, sent_b)):
-        y_out = size_y if b > 0 else -1
-        for k, i in enumerate(Y_SETS[b]):
-            msg[k * SUB : k * SUB + size_x - 2, :] = flat[i, lines(DIRS[i][0] + 1, y_out, rows, size_x - 2), :]
+    def send(sent):
+        for b, msg in zip(SIDES, sent):
+            y_out = size_y if b > 0 else -1
+            for k, i in enumerate(Y_SETS[b]):
+                msg[k * SUB : k * SUB + size_x - 2, :] = flat[i, lines(DIRS[i][0] + 1, y_out, rows, size_x - 2), :]
+
+    by_side_sent("cross", (sent_a, sent_b), send)
 
 
 def edge_kernel(state_in, out_in, kinds, halo_kinds, loop_a, loop_b, cross_a, cross_b, state, out, sent_a, sent_b, halo):
@@ -316,10 +329,14 @@
             flat_out[i, lines(a, y_in, rows, 2, size_x - 1), :] = moved[first : first + 2, :]
 
     collide(lambda i: halo[i], code - 1, put)
-    for b, msg in zip(SIDES, (cross_a, cross_b)):
-        y_in = 0 if b > 0 else size_y - 1
-        for k, i in enumerate(Y_SETS[b]):
-            flat_out[i, lines(DIRS[i][0] + 1, y_in, rows, size_x - 2), :] = msg[k * SUB : k * SUB + size_x - 2, :]
+
+    def take(received):
+        for b, msg in zip(SIDES, received):
+            y_in = 0 if b > 0 else size_y - 1
+            for k, i in enumerate(Y_SETS[b]):
+                flat_out[i, lines(DIRS[i][0] + 1, y_in, rows, size_x - 2), :] = msg[k * SUB : k * SUB + size_x - 2, :]
+
+    by_side_received("cross", (cross_a, cross_b), take)
     for a, msg in zip(SIDES, (sent_a, sent_b)):
         x = -1 if a < 0 else size_x
         for k, i in enumerate(X_SETS[a]):
@@ -362,6 +379,17 @@
     received = []
     for step, cells in zip(SIDES, messages):
         pairs = [(i, (i + step) % count) for i in range(count) if closed or 0 <= i + step < count]
+        received.append(lax.ppermute(cells, axis, pairs))
+    return received
+
+
+def swap_along(axis, messages):
+    count = lax.axis_size(axis)
+    received = []
+    for first, cells in enumerate(messages):
+        pairs = []
+        for i in range(first, count - 1, 2):
+            pairs += [(i, i + 1), (i + 1, i)]
         received.append(lax.ppermute(cells, axis, pairs))
     return received
 
@@ -424,7 +452,7 @@
         tiles=size_x * len(side),
         scratch=staging(side) + [pltpu.SemaphoreType.DMA],
     )
-    received = shift_along("cross", False, sent)
+    received = swap_along("cross", sent)
     if middle:
         (state,) = call(
             functools.partial(middle_kernel, size_x, middle),
@@ -451,7 +479,7 @@
         [state_shape] + cross_2,
         tiles=(size_x - 2) * len(tiles),
     )
-    from_cross = shift_along("cross", False, sent)
+    from_cross = swap_along("cross", sent)
     state, out, *sent = call(
         edge_kernel,
         "second_step_edge_planes",

time: 34.9 us -> 31.3 us (0.90)
  the two profiles are of different devices: /device:TPU:0 before, /device:TPU:16 now
where the time goes in v3:
time: 31.3 us; the launch traced here: 31.1 us
  Pallas kernels  12.7 us (41%)
  starting transfers between devices  9 us (29%)
  waiting for transfers between devices  8.64 us (28%)
  between operations  0.71 us (2%)
    pallas_call x7, Pallas kernels, call(): pl.pallas_call(kernel, out_shape=results, in_specs=specs, out_specs=[hbm...  12.7 us
    ppermute x4, starting transfers between devices, swap_along(): received.append(lax.ppermute(cells, axis, pairs))  6.8 us
    ppermute x4, waiting for transfers between devices, swap_along(): received.append(lax.ppermute(cells, axis, pairs))  4.63 us
    ppermute x4, waiting for transfers between devices, shift_along(): received.append(lax.ppermute(cells, axis, pairs))  4.01 us
    ppermute x4, starting transfers between devices, shift_along(): received.append(lax.ppermute(cells, axis, pairs))  2.2 us
  transfers between devices with their start and end apart: 8, of which 5 were waited for; matrix products, arithmetic and copies ran while one was open for 0% of the time, Pallas kernels for 23%

profile of v3, /device:TPU:16, one launch (start us, length us, event | category | flops | bytes accessed | tf_op | source)
XLA Modules:
  0.0 31.1 jit_solution(10896644976070132059)
XLA Ops:
  0.6 3.7 %first_step_side_rows.1 = (f32[41,10,48,128]{3,2,1,0:T(8,128)S(1)}, s32[8,32,128]{2,1,0:T(8,128)S(1)}, f32[152,128]{1,0:T(8,128)S(1)}, f32[152,128]{1,0:T(8,128)S(1)}) custom-call(f32[27,8,32,128]{3,2,1,0:T(8,128)} %pops.3, f32[14,8,32,128]{3,2,1,0:T(8,128)} %scal.3, s32[8,32,128]{2,1,0:T(8,128)} %flags.1), custom_call_target="tpu_custom_call" | custom-call | flops 8192000 | bytes 5373952 | tf_op jit(solution)/shard_map/first_step_side_rows/pallas_call | solution.py:418
  4.4 1.6 %collective-permute-start = (f32[152,128]{1,0:T(8,128)S(1)}, f32[152,128]{1,0:T(8,128)S(1)}, u32[]{:S(2)}, u32[]{:S(2)}) collective-permute-start(f32[152,128]{1,0:T(8,128)S(1)} %get-tuple-element.20), channel_id=1, source_target_pairs={{0,1},{1,0},{2,3},{3,2},{4,5},{5,4},{6,7},{7,6},{8,9},{9,8},{10,11... | collective-permute-start | bytes 233480 | tf_op jit(solution)/shard_map/ppermute | solution.py:393
  6.0 1.9 %collective-permute-start.1 = (f32[152,128]{1,0:T(8,128)S(1)}, f32[152,128]{1,0:T(8,128)S(1)}, u32[]{:S(2)}, u32[]{:S(2)}) collective-permute-start(f32[152,128]{1,0:T(8,128)S(1)} %get-tuple-element.21), channel_id=1, source_target_pairs={{1,2},{2,1},{5,6},{6,5},{9,10},{10,9},{13,14},{14,13},{17,18},{18,... | collective-permute-start | bytes 233480 | tf_op jit(solution)/shard_map/ppermute | solution.py:393
  7.9 2.8 %first_step_middle_rows.1.state_in = f32[41,10,48,128]{3,2,1,0:T(8,128)S(1)} custom-call(f32[27,8,32,128]{3,2,1,0:T(8,128)} %pops.3, f32[14,8,32,128]{3,2,1,0:T(8,128)} %scal.3, s32[8,32,128]{2,1,0:T(8,128)S(1)} %get-tuple-element.18.kinds, f32[41,10,48,128]{3,2,1,0:T(8,128)S(1)} %get-tuple-element.19.state_in), custom_call_target="tpu_custom_call", output_to_operand_aliasing={{}: (3, {})} | custom-call | flops 8192000 | bytes 5373952 | tf_op jit(solution)/shard_map/first_step_middle_rows/pallas_call | solution.py:418
  10.7 0.0 collective-permute-done.got_a
  10.7 1.6 %collective-permute-done.1.got_b = f32[152,128]{1,0:T(8,128)S(1)} collective-permute-done((f32[152,128]{1,0:T(8,128)S(1)}, f32[152,128]{1,0:T(8,128)S(1)}, u32[]{:S(2)}, u32[]{:S(2)}) %collective-permute-start.1) | collective-permute-done | bytes 77856 | tf_op jit(solution)/shard_map/ppermute | solution.py:393
  12.3 0.1 cross_to_loop.1
  12.4 0.5 %collective-permute-start.2 = (f32[376,128]{1,0:T(8,128)S(1)}, f32[376,128]{1,0:T(8,128)S(1)}, u32[]{:S(2)}, u32[]{:S(2)}) collective-permute-start(f32[376,128]{1,0:T(8,128)S(1)} %get-tuple-element.25), channel_id=1, source_target_pairs={{0,28},{4,0},{8,4},{12,8},{16,12},{20,16},{24,20},{28,24},{1,29},{... | collective-permute-start | bytes 577544 | tf_op jit(solution)/shard_map/ppermute | solution.py:382
  12.9 0.1 collective-permute-start.3
  13.0 1.9 %second_step_inner_planes.1 = (f32[41,10,48,128]{3,2,1,0:T(8,128)S(1)}, f32[88,128]{1,0:T(8,128)S(1)}, f32[88,128]{1,0:T(8,128)S(1)}) custom-call(f32[41,10,48,128]{3,2,1,0:T(8,128)S(1)} %get-tuple-element.22.state.state_in, s32[8,32,128]{2,1,0:T(8,128)S(1)} %get-tuple-element.18.kinds), custom_call_target="tpu_custom_call" | custom-call | flops 12288000 | bytes 8060928 | tf_op jit(solution)/shard_map/second_step_inner_planes/pallas_call | solution.py:418
  14.8 0.1 collective-permute-start.4
  14.9 3.2 %collective-permute-start.5 = (f32[88,128]{1,0:T(8,128)S(1)}, f32[88,128]{1,0:T(8,128)S(1)}, u32[]{:S(2)}, u32[]{:S(2)}) collective-permute-start(f32[88,128]{1,0:T(8,128)S(1)} %get-tuple-element.28), channel_id=1, source_target_pairs={{1,2},{2,1},{5,6},{6,5},{9,10},{10,9},{13,14},{14,13},{17,18},{18,... | collective-permute-start | bytes 135176 | tf_op jit(solution)/shard_map/ppermute | solution.py:393
  18.1 1.1 %collective-permute-done.4.cross_a = f32[88,128]{1,0:T(8,128)S(1)} collective-permute-done((f32[88,128]{1,0:T(8,128)S(1)}, f32[88,128]{1,0:T(8,128)S(1)}, u32[]{:S(2)}, u32[]{:S(2)}) %collective-permute-start.4) | collective-permute-done | bytes 45088 | tf_op jit(solution)/shard_map/ppermute | solution.py:393
  19.2 1.9 %collective-permute-done.5.cross_b = f32[88,128]{1,0:T(8,128)S(1)} collective-permute-done((f32[88,128]{1,0:T(8,128)S(1)}, f32[88,128]{1,0:T(8,128)S(1)}, u32[]{:S(2)}, u32[]{:S(2)}) %collective-permute-start.5) | collective-permute-done | bytes 45088 | tf_op jit(solution)/shard_map/ppermute | solution.py:393
  21.1 0.0 collective-permute-done.2.loop_a
  21.1 0.0 collective-permute-done.3.loop_b
  21.1 0.9 %second_step_edge_planes.1 = (f32[41,10,48,128]{3,2,1,0:T(8,128)S(1)}, f32[41,10,48,128]{3,2,1,0:T(8,128)S(1)}, f32[11,32,128]{2,1,0:T(8,128)S(1)}, f32[11,32,128]{2,1,0:T(8,128)S(1)}) custom-call(f32[41,10,48,128]{3,2,1,0:T(8,128)S(1)} %get-tuple-element.22.state.state_in, ...), custom_call_target="tpu_custom_call", output_to_operand_aliasing={{0}: (0, {}), {1}: (1, {})} | custom-call | flops 4608000 | bytes 3022848 | tf_op jit(solution)/shard_map/second_step_edge_planes/pallas_call | solution.py:418
  22.0 1.6 %collective-permute-start.6 = (f32[11,32,128]{2,1,0:T(8,128)S(1)}, f32[11,32,128]{2,1,0:T(8,128)S(1)}, u32[]{:S(2)}, u32[]{:S(2)}) collective-permute-start(f32[11,32,128]{2,1,0:T(8,128)S(1)} %get-tuple-element.32), channel_id=1, source_target_pairs={{0,28},{4,0},{8,4},{12,8},{16,12},{20,16},{24,20},{28,24},{1,29},{... | collective-permute-start | bytes 540680 | tf_op jit(solution)/shard_map/ppermute | solution.py:382
  23.6 0.0 collective-permute-start.7
  23.6 2.5 %write_all_planes.1 = (f32[27,8,32,128]{3,2,1,0:T(8,128)}, f32[14,8,32,128]{3,2,1,0:T(8,128)}) custom-call(f32[41,10,48,128]{3,2,1,0:T(8,128)S(1)} %get-tuple-element.29.out), custom_call_target="tpu_custom_call" | custom-call | bytes 10747904 | tf_op jit(solution)/shard_map/write_all_planes/pallas_call | solution.py:418
  26.1 2.0 %collective-permute-done.6.got_a = f32[11,32,128]{2,1,0:T(8,128)S(1)} collective-permute-done((f32[11,32,128]{2,1,0:T(8,128)S(1)}, f32[11,32,128]{2,1,0:T(8,128)S(1)}, u32[]{:S(2)}, u32[]{:S(2)}) %collective-permute-start.6) | collective-permute-done | bytes 180256 | tf_op jit(solution)/shard_map/ppermute | solution.py:382
  28.2 2.0 %collective-permute-done.7.got_b = f32[11,32,128]{2,1,0:T(8,128)S(1)} collective-permute-done((f32[11,32,128]{2,1,0:T(8,128)S(1)}, f32[11,32,128]{2,1,0:T(8,128)S(1)}, u32[]{:S(2)}, u32[]{:S(2)}) %collective-permute-start.7) | collective-permute-done | bytes 180256 | tf_op jit(solution)/shard_map/ppermute | solution.py:382
  30.1 0.9 %write_edge_planes.1 = (f32[27,8,32,128]{3,2,1,0:T(8,128)}, f32[14,8,32,128]{3,2,1,0:T(8,128)}) custom-call(f32[27,8,32,128]{3,2,1,0:T(8,128)} %get-tuple-element.30.pops_in, f32[14,8,32,128]{3,2,1,0:T(8,128)} %get-tuple-element.31.scal_in, f32[11,32,128]{2,1,0:T(8,128)S(1)} %collective-permute-done.6.got_a, ...), custom_call_target="tpu_custom_call", output_to_operand_aliasing={{0}: (0, {}), {1}: (1, {})} | custom-call | bytes 720896 | tf_op jit(solution)/shard_map/write_edge_planes/pallas_call | solution.py:418
Async XLA Ops:
  4.4 6.3 %collective-permute-start = (f32[152,128]{1,0:T(8,128)S(1)}, f32[152,128]{1,0:T(8,128)S(1)}, u32[]{:S(2)}, u32[]{:S(2)}) collective-permute-start(f32[152,128]{1,0:T(8,128)S(1)} %get-tuple-element.20), channel_id=1, source_target_pairs={{0,1},{1,0},{2,3},{3,2},{4,5},{5,4},{6,7},{7,6},{8,9},{9,8},{10,11... | collective-permute-start | bytes 233480 | tf_op jit(solution)/shard_map/ppermute | solution.py:393
  6.0 6.3 %collective-permute-start.1 = (f32[152,128]{1,0:T(8,128)S(1)}, f32[152,128]{1,0:T(8,128)S(1)}, u32[]{:S(2)}, u32[]{:S(2)}) collective-permute-start(f32[152,128]{1,0:T(8,128)S(1)} %get-tuple-element.21), channel_id=1, source_target_pairs={{1,2},{2,1},{5,6},{6,5},{9,10},{10,9},{13,14},{14,13},{17,18},{18,... | collective-permute-start | bytes 233480 | tf_op jit(solution)/shard_map/ppermute | solution.py:393
  12.4 8.7 %collective-permute-start.2 = (f32[376,128]{1,0:T(8,128)S(1)}, f32[376,128]{1,0:T(8,128)S(1)}, u32[]{:S(2)}, u32[]{:S(2)}) collective-permute-start(f32[376,128]{1,0:T(8,128)S(1)} %get-tuple-element.25), channel_id=1, source_target_pairs={{0,28},{4,0},{8,4},{12,8},{16,12},{20,16},{24,20},{28,24},{1,29},{... | collective-permute-start | bytes 577544 | tf_op jit(solution)/shard_map/ppermute | solution.py:382
  12.9 8.2 %collective-permute-start.3 = (f32[376,128]{1,0:T(8,128)S(1)}, f32[376,128]{1,0:T(8,128)S(1)}, u32[]{:S(2)}, u32[]{:S(2)}) collective-permute-start(f32[376,128]{1,0:T(8,128)S(1)} %get-tuple-element.26), channel_id=1, source_target_pairs={{0,4},{4,8},{8,12},{12,16},{16,20},{20,24},{24,28},{28,0},{1,5},{5... | collective-permute-start | bytes 577544 | tf_op jit(solution)/shard_map/ppermute | solution.py:382
  14.8 4.4 %collective-permute-start.4 = (f32[88,128]{1,0:T(8,128)S(1)}, f32[88,128]{1,0:T(8,128)S(1)}, u32[]{:S(2)}, u32[]{:S(2)}) collective-permute-start(f32[88,128]{1,0:T(8,128)S(1)} %get-tuple-element.27), channel_id=1, source_target_pairs={{0,1},{1,0},{2,3},{3,2},{4,5},{5,4},{6,7},{7,6},{8,9},{9,8},{10,11... | collective-permute-start | bytes 135176 | tf_op jit(solution)/shard_map/ppermute | solution.py:393
  14.9 6.2 %collective-permute-start.5 = (f32[88,128]{1,0:T(8,128)S(1)}, f32[88,128]{1,0:T(8,128)S(1)}, u32[]{:S(2)}, u32[]{:S(2)}) collective-permute-start(f32[88,128]{1,0:T(8,128)S(1)} %get-tuple-element.28), channel_id=1, source_target_pairs={{1,2},{2,1},{5,6},{6,5},{9,10},{10,9},{13,14},{14,13},{17,18},{18,... | collective-permute-start | bytes 135176 | tf_op jit(solution)/shard_map/ppermute | solution.py:393
  22.0 6.2 %collective-permute-start.6 = (f32[11,32,128]{2,1,0:T(8,128)S(1)}, f32[11,32,128]{2,1,0:T(8,128)S(1)}, u32[]{:S(2)}, u32[]{:S(2)}) collective-permute-start(f32[11,32,128]{2,1,0:T(8,128)S(1)} %get-tuple-element.32), channel_id=1, source_target_pairs={{0,28},{4,0},{8,4},{12,8},{16,12},{20,16},{24,20},{28,24},{1,29},{... | collective-permute-start | bytes 540680 | tf_op jit(solution)/shard_map/ppermute | solution.py:382
  23.6 6.5 %collective-permute-start.7 = (f32[11,32,128]{2,1,0:T(8,128)S(1)}, f32[11,32,128]{2,1,0:T(8,128)S(1)}, u32[]{:S(2)}, u32[]{:S(2)}) collective-permute-start(f32[11,32,128]{2,1,0:T(8,128)S(1)} %get-tuple-element.33), channel_id=1, source_target_pairs={{0,4},{4,8},{8,12},{12,16},{16,20},{20,24},{24,28},{28,0},{1,5},{5... | collective-permute-start | bytes 540680 | tf_op jit(solution)/shard_map/ppermute | solution.py:382

commit v4 on v3

--- a/solution.py
+++ b/solution.py
@@ -242,44 +242,40 @@
     return lambda i: state[i, slot(x), y + PAD : y + PAD + SUB, :]
 
 
-def first_step_tiles(size_x, tiles, pops, scal, state, kinds, raw, sems, kinds_copy=None):
+def collide_raw(raw, kinds, state, x, tiles):
+    for y in tiles:
+        collide(lambda i: raw[i, x, y : y + SUB, :], kinds[x, y : y + SUB, :], push_tile(state, x, y))
+
+
+def side_kernel(tiles, pops, scal, flags, state, kinds, raw, sent_a, sent_b, sems, kinds_sem):
+    size_x = kinds.shape[0]
+    kinds_copy = pltpu.make_async_copy(flags, kinds, kinds_sem)
+
     def copies(x):
-        result = []
-        for n, y in enumerate(tiles):
-            here = pl.ds(y, SUB)
-            there = pl.ds(n * SUB, SUB)
-            result.append(pltpu.make_async_copy(pops.at[:, x, here], raw.at[0:NF, x, there], sems.at[2 * n, x]))
-            result.append(pltpu.make_async_copy(scal.at[:, x, here], raw.at[NF:NQ, x, there], sems.at[2 * n + 1, x]))
-        return result
-
+        return (
+            pltpu.make_async_copy(pops.at[:, x], raw.at[0:NF, x], sems.at[0, x]),
+            pltpu.make_async_copy(scal.at[:, x], raw.at[NF:NQ, x], sems.at[1, x]),
+        )
+
+    kinds_copy.start()
     for x in range(size_x):
         for copy in copies(x):
             copy.start()
-        if x == 0 and kinds_copy is not None:
-            kinds_copy.start()
-    if kinds_copy is not None:
-        kinds_copy.wait()
+    kinds_copy.wait()
 
     @pl.loop(0, size_x)
     def _(x):
         for copy in copies(x):
             copy.wait()
-        for n, y in enumerate(tiles):
-            collide(
-                lambda i: raw[i, x, n * SUB : (n + 1) * SUB, :],
-                kinds[x, y : y + SUB, :],
-                push_tile(state, x, y),
-            )
-
-
-def side_kernel(size_x, tiles, pops, scal, flags, state, kinds, sent_a, sent_b, raw, sems, kinds_sem):
-    kinds_copy = pltpu.make_async_copy(flags, kinds, kinds_sem)
-    first_step_tiles(size_x, tiles, pops, scal, state, kinds, raw, sems, kinds_copy)
+        collide_raw(raw, kinds, state, x, tiles)
+
     by_side_sent("cross", (sent_a, sent_b), functools.partial(send_first_cross, state, kinds))
 
 
-def middle_kernel(size_x, tiles, pops, scal, kinds, state_in, state, raw, sems):
-    first_step_tiles(size_x, tiles, pops, scal, state, kinds, raw, sems)
+def middle_kernel(tiles, raw, kinds, state_in, state):
+    @pl.loop(0, kinds.shape[0])
+    def _(x):
+        collide_raw(raw, kinds, state, x, tiles)
 
 
 def turn_kernel(state_in, got_a, got_b, state, halo_kinds, sent_a, sent_b):
@@ -305,7 +301,7 @@
     by_side_sent("cross", (sent_a, sent_b), send)
 
 
-def edge_kernel(state_in, out_in, kinds, halo_kinds, loop_a, loop_b, cross_a, cross_b, state, out, sent_a, sent_b, halo):
+def edge_kernel(state_in, out_in, kinds, halo_kinds, loop_a, loop_b, state, out, sent_a, sent_b, halo):
     size_x, size_y = sizes_of(state)
     rows, flat, flat_out = state.shape[2], flat_of(state), flat_of(out)
     take_first_loop(state, (loop_a, loop_b))
@@ -329,14 +325,6 @@
             flat_out[i, lines(a, y_in, rows, 2, size_x - 1), :] = moved[first : first + 2, :]
 
     collide(lambda i: halo[i], code - 1, put)
-
-    def take(received):
-        for b, msg in zip(SIDES, received):
-            y_in = 0 if b > 0 else size_y - 1
-            for k, i in enumerate(Y_SETS[b]):
-                flat_out[i, lines(DIRS[i][0] + 1, y_in, rows, size_x - 2), :] = msg[k * SUB : k * SUB + size_x - 2, :]
-
-    by_side_received("cross", (cross_a, cross_b), take)
     for a, msg in zip(SIDES, (sent_a, sent_b)):
         x = -1 if a < 0 else size_x
         for k, i in enumerate(X_SETS[a]):
@@ -344,8 +332,17 @@
                 msg[k, y : y + SUB, :] = out[i, slot(x), y + PAD : y + PAD + SUB, :]
 
 
-def write_kernel(out, pops, scal, sems):
+def write_kernel(out_in, cross_a, cross_b, out, pops, scal, sems):
     size_x, size_y = sizes_of(out)
+    rows, flat = out.shape[2], flat_of(out)
+
+    def take(received):
+        for b, msg in zip(SIDES, received):
+            y_in = 0 if b > 0 else size_y - 1
+            for k, i in enumerate(Y_SETS[b]):
+                flat[i, lines(DIRS[i][0] + 1, y_in, rows, size_x - 2), :] = msg[k * SUB : k * SUB + size_x - 2, :]
+
+    by_side_received("cross", (cross_a, cross_b), take)
     copies = []
     for x in range(size_x):
         inner = pl.ds(PAD, size_y)
@@ -398,6 +395,7 @@
     size_x, size_y, size_z = node_flags.shape
     f32 = jnp.float32
     state_shape = pltpu.VMEM((NQ, size_x + 2, size_y + 2 * PAD, size_z), f32)
+    raw_shape = pltpu.VMEM((NQ, size_x, size_y, size_z), f32)
     kinds_shape = pltpu.VMEM((size_x, size_y, size_z), jnp.int32)
     halo_kinds_shape = pltpu.VMEM((SUB, size_z), f32)
     cross_1 = [pltpu.VMEM((first_cross_rows(size_x)[1], size_z), f32)] * 2
@@ -438,30 +436,23 @@
     tiles = list(range(0, size_y, SUB))
     side, middle = sorted({tiles[0], tiles[-1]}), tiles[1:-1]
 
-    def staging(rows):
-        return [
-            pltpu.VMEM((NQ, size_x, len(rows) * SUB, size_z), f32),
-            pltpu.SemaphoreType.DMA((2 * len(rows), size_x)),
-        ]
-
-    state, kinds, *sent = call(
-        functools.partial(side_kernel, size_x, side),
+    state, kinds, raw, *sent = call(
+        functools.partial(side_kernel, side),
         "first_step_side_rows",
         in_hbm(populations, scalars, node_flags),
-        [state_shape, kinds_shape] + cross_1,
+        [state_shape, kinds_shape, raw_shape] + cross_1,
         tiles=size_x * len(side),
-        scratch=staging(side) + [pltpu.SemaphoreType.DMA],
+        scratch=[pltpu.SemaphoreType.DMA((2, size_x)), pltpu.SemaphoreType.DMA],
     )
     received = swap_along("cross", sent)
     if middle:
         (state,) = call(
-            functools.partial(middle_kernel, size_x, middle),
+            functools.partial(middle_kernel, middle),
             "first_step_middle_rows",
-            in_hbm(populations, scalars) + on_chip(kinds, state),
+            on_chip(raw, kinds, state),
             [state_shape],
             tiles=size_x * len(middle),
-            scratch=staging(middle),
-            aliases={3: 0},
+            aliases={2: 0},
         )
     state, halo_kinds, *sent = call(
         turn_kernel,
@@ -483,20 +474,21 @@
     state, out, *sent = call(
         edge_kernel,
         "second_step_edge_planes",
-        on_chip(state, out, kinds, halo_kinds, *from_loop, *from_cross),
+        on_chip(state, out, kinds, halo_kinds, *from_loop),
         [state_shape, state_shape] + loop_2,
         tiles=2 * len(tiles) + 1,
         scratch=[pltpu.VMEM((NQ, SUB, size_z), f32)],
         aliases={0: 0, 1: 1},
     )
     received = shift_along("loop", True, sent)
-    new_pops, new_scal = call(
+    _, new_pops, new_scal = call(
         write_kernel,
         "write_all_planes",
-        on_chip(out),
-        [pops_shape, scal_shape],
+        on_chip(out, *from_cross),
+        [state_shape, pops_shape, scal_shape],
         moved=8 * NQ * size_x * size_y * size_z,
         scratch=[pltpu.SemaphoreType.DMA((2, size_x))],
+        aliases={0: 0},
     )
     new_pops, new_scal = call(
         last_kernel,

time: 31.3 us -> 32 us (1.022)
  waiting for transfers between devices: 8.64 us -> 12.7 us
  starting transfers between devices: 9 us -> 6.58 us
  Pallas kernels: 12.7 us -> 11.9 us
    ppermute x4, waiting for transfers between devices: 4.63 us -> 6.91 us  [swap_along(): received.append(lax.ppermute(cells, axis, pairs))]
    ppermute x4, waiting for transfers between devices: 4.01 us -> 5.74 us  [shift_along(): received.append(lax.ppermute(cells, axis, pairs))]
    ppermute x4, starting transfers between devices: 6.8 us -> 5.46 us  [swap_along(): received.append(lax.ppermute(cells, axis, pairs))]
    ppermute x4, starting transfers between devices: 2.2 us -> 1.12 us  [shift_along(): received.append(lax.ppermute(cells, axis, pairs))]
    pallas_call x7, Pallas kernels: 12.7 us -> 11.9 us  [call(): pl.pallas_call(kernel, out_shape=results, in_specs=specs, out_specs=[hbm...]
  transfers between devices with their start and end apart: 8 -> 8, of which waited for: 5 -> 5; matrix products, arithmetic and copies ran while one was open for 0% -> 0% of each run, Pallas kernels for 23% -> 18%
where the time goes in v4:
time: 32 us; the launch traced here: 31.8 us
  waiting for transfers between devices  12.7 us (40%)
  Pallas kernels  11.9 us (37%)
  starting transfers between devices  6.58 us (21%)
  between operations  0.72 us (2%)
    pallas_call x7, Pallas kernels, call(): pl.pallas_call(kernel, out_shape=results, in_specs=specs, out_specs=[hbm...  11.9 us
    ppermute x4, waiting for transfers between devices, swap_along(): received.append(lax.ppermute(cells, axis, pairs))  6.91 us
    ppermute x4, waiting for transfers between devices, shift_along(): received.append(lax.ppermute(cells, axis, pairs))  5.74 us
    ppermute x4, starting transfers between devices, swap_along(): received.append(lax.ppermute(cells, axis, pairs))  5.46 us
    ppermute x4, starting transfers between devices, shift_along(): received.append(lax.ppermute(cells, axis, pairs))  1.12 us
  transfers between devices with their start and end apart: 8, of which 5 were waited for; matrix products, arithmetic and copies ran while one was open for 0% of the time, Pallas kernels for 18%

profile of v4, /device:TPU:16, one launch (start us, length us, event | category | flops | bytes accessed | tf_op | source)
XLA Modules:
  0.0 31.8 jit_solution(6647051682844887658)
XLA Ops:
  0.6 4.2 %first_step_side_rows.1 = (f32[41,10,48,128]{3,2,1,0:T(8,128)S(1)}, s32[8,32,128]{2,1,0:T(8,128)S(1)}, f32[41,8,32,128]{3,2,1,0:T(8,128)S(1)}, f32[152,128]{1,0:T(8,128)S(1)}, f32[152,128]{1,0:T(8,128)S(1)}) custom-call(f32[27,8,32,128]{3,2,1,0:T(8,128)} %pops.1, f32[14,8,32,128]{3,2,1,0:T(8,128)} %scal.1, s32[8,32,128]{2,1,0:T(8,128)} %flags.1), custom_call_target="tpu_custom_call" | custom-call | flops 8192000 | bytes 5373952 | tf_op jit(solution)/shard_map/first_step_side_rows/pallas_call | solution.py:416
  4.8 1.6 %collective-permute-start = (f32[152,128]{1,0:T(8,128)S(1)}, f32[152,128]{1,0:T(8,128)S(1)}, u32[]{:S(2)}, u32[]{:S(2)}) collective-permute-start(f32[152,128]{1,0:T(8,128)S(1)} %get-tuple-element.22), channel_id=1, source_target_pairs={{0,1},{1,0},{2,3},{3,2},{4,5},{5,4},{6,7},{7,6},{8,9},{9,8},{10,11... | collective-permute-start | bytes 233480 | tf_op jit(solution)/shard_map/ppermute | solution.py:390
  6.5 1.9 %collective-permute-start.1 = (f32[152,128]{1,0:T(8,128)S(1)}, f32[152,128]{1,0:T(8,128)S(1)}, u32[]{:S(2)}, u32[]{:S(2)}) collective-permute-start(f32[152,128]{1,0:T(8,128)S(1)} %get-tuple-element.23), channel_id=1, source_target_pairs={{1,2},{2,1},{5,6},{6,5},{9,10},{10,9},{13,14},{14,13},{17,18},{18,... | collective-permute-start | bytes 233480 | tf_op jit(solution)/shard_map/ppermute | solution.py:390
  8.4 1.5 %first_step_middle_rows.1.state_in = f32[41,10,48,128]{3,2,1,0:T(8,128)S(1)} custom-call(f32[41,8,32,128]{3,2,1,0:T(8,128)S(1)} %get-tuple-element.19.raw, s32[8,32,128]{2,1,0:T(8,128)S(1)} %get-tuple-element.20.kinds, f32[41,10,48,128]{3,2,1,0:T(8,128)S(1)} %get-tuple-element.21.state_in), custom_call_target="tpu_custom_call", output_to_operand_aliasing={{}: (2, {})} | custom-call | flops 8192000 | bytes 5373952 | tf_op jit(solution)/shard_map/first_step_middle_rows/pallas_call | solution.py:416
  9.8 0.0 collective-permute-done.got_a
  9.9 2.9 %collective-permute-done.1.got_b = f32[152,128]{1,0:T(8,128)S(1)} collective-permute-done((f32[152,128]{1,0:T(8,128)S(1)}, f32[152,128]{1,0:T(8,128)S(1)}, u32[]{:S(2)}, u32[]{:S(2)}) %collective-permute-start.1) | collective-permute-done | bytes 77856 | tf_op jit(solution)/shard_map/ppermute | solution.py:390
  12.8 0.1 cross_to_loop.1
  12.9 0.5 %collective-permute-start.2 = (f32[376,128]{1,0:T(8,128)S(1)}, f32[376,128]{1,0:T(8,128)S(1)}, u32[]{:S(2)}, u32[]{:S(2)}) collective-permute-start(f32[376,128]{1,0:T(8,128)S(1)} %get-tuple-element.27), channel_id=1, source_target_pairs={{0,28},{4,0},{8,4},{12,8},{16,12},{20,16},{24,20},{28,24},{1,29},{... | collective-permute-start | bytes 577544 | tf_op jit(solution)/shard_map/ppermute | solution.py:379
  13.4 0.1 collective-permute-start.3
  13.4 1.9 %second_step_inner_planes.1 = (f32[41,10,48,128]{3,2,1,0:T(8,128)S(1)}, f32[88,128]{1,0:T(8,128)S(1)}, f32[88,128]{1,0:T(8,128)S(1)}) custom-call(f32[41,10,48,128]{3,2,1,0:T(8,128)S(1)} %get-tuple-element.24.state.state_in, s32[8,32,128]{2,1,0:T(8,128)S(1)} %get-tuple-element.20.kinds), custom_call_target="tpu_custom_call" | custom-call | flops 12288000 | bytes 8060928 | tf_op jit(solution)/shard_map/second_step_inner_planes/pallas_call | solution.py:416
  15.3 2.8 %collective-permute-done.2.loop_a = f32[376,128]{1,0:T(8,128)S(1)} collective-permute-done((f32[376,128]{1,0:T(8,128)S(1)}, f32[376,128]{1,0:T(8,128)S(1)}, u32[]{:S(2)}, u32[]{:S(2)}) %collective-permute-start.2) | collective-permute-done | bytes 192544 | tf_op jit(solution)/shard_map/ppermute | solution.py:379
  18.1 2.9 %collective-permute-done.3.loop_b = f32[376,128]{1,0:T(8,128)S(1)} collective-permute-done((f32[376,128]{1,0:T(8,128)S(1)}, f32[376,128]{1,0:T(8,128)S(1)}, u32[]{:S(2)}, u32[]{:S(2)}) %collective-permute-start.3) | collective-permute-done | bytes 192544 | tf_op jit(solution)/shard_map/ppermute | solution.py:379
  21.0 0.8 %second_step_edge_planes.1 = (f32[41,10,48,128]{3,2,1,0:T(8,128)S(1)}, f32[41,10,48,128]{3,2,1,0:T(8,128)S(1)}, f32[11,32,128]{2,1,0:T(8,128)S(1)}, f32[11,32,128]{2,1,0:T(8,128)S(1)}) custom-call(f32[41,10,48,128]{3,2,1,0:T(8,128)S(1)} %get-tuple-element.24.state.state_in, ...), custom_call_target="tpu_custom_call", output_to_operand_aliasing={{0}: (0, {}), {1}: (1, {})} | custom-call | flops 4608000 | bytes 3022848 | tf_op jit(solution)/shard_map/second_step_edge_planes/pallas_call | solution.py:416
  21.8 0.1 collective-permute-start.6
  21.9 0.5 %collective-permute-start.7 = (f32[11,32,128]{2,1,0:T(8,128)S(1)}, f32[11,32,128]{2,1,0:T(8,128)S(1)}, u32[]{:S(2)}, u32[]{:S(2)}) collective-permute-start(f32[11,32,128]{2,1,0:T(8,128)S(1)} %get-tuple-element.35), channel_id=1, source_target_pairs={{0,4},{4,8},{8,12},{12,16},{16,20},{20,24},{24,28},{28,0},{1,5},{5... | collective-permute-start | bytes 540680 | tf_op jit(solution)/shard_map/ppermute | solution.py:379
  22.4 0.0 collective-permute-start.4
  22.4 1.9 %collective-permute-start.5 = (f32[88,128]{1,0:T(8,128)S(1)}, f32[88,128]{1,0:T(8,128)S(1)}, u32[]{:S(2)}, u32[]{:S(2)}) collective-permute-start(f32[88,128]{1,0:T(8,128)S(1)} %get-tuple-element.31), channel_id=1, source_target_pairs={{1,2},{2,1},{5,6},{6,5},{9,10},{10,9},{13,14},{14,13},{17,18},{18,... | collective-permute-start | bytes 135176 | tf_op jit(solution)/shard_map/ppermute | solution.py:390
  24.3 2.1 %collective-permute-done.4.cross_a = f32[88,128]{1,0:T(8,128)S(1)} collective-permute-done((f32[88,128]{1,0:T(8,128)S(1)}, f32[88,128]{1,0:T(8,128)S(1)}, u32[]{:S(2)}, u32[]{:S(2)}) %collective-permute-start.4) | collective-permute-done | bytes 45088 | tf_op jit(solution)/shard_map/ppermute | solution.py:390
  26.5 1.9 %collective-permute-done.5.cross_b = f32[88,128]{1,0:T(8,128)S(1)} collective-permute-done((f32[88,128]{1,0:T(8,128)S(1)}, f32[88,128]{1,0:T(8,128)S(1)}, u32[]{:S(2)}, u32[]{:S(2)}) %collective-permute-start.5) | collective-permute-done | bytes 45088 | tf_op jit(solution)/shard_map/ppermute | solution.py:390
  28.3 2.5 %write_all_planes.1 = (f32[41,10,48,128]{3,2,1,0:T(8,128)S(1)}, f32[27,8,32,128]{3,2,1,0:T(8,128)}, f32[14,8,32,128]{3,2,1,0:T(8,128)}) custom-call(f32[41,10,48,128]{3,2,1,0:T(8,128)S(1)} %get-tuple-element.29.out_in, f32[88,128]{1,0:T(8,128)S(1)} %collective-permute-done.4.cross_a, ...), custom_call_target="tpu_custom_call", output_to_operand_aliasing={{0}: (0, {})} | custom-call | bytes 10747904 | tf_op jit(solution)/shard_map/write_all_planes/pallas_call | solution.py:416
  30.9 0.0 collective-permute-done.6.got_a
  30.9 0.0 collective-permute-done.7.got_b
  30.9 0.9 %write_edge_planes.1 = (f32[27,8,32,128]{3,2,1,0:T(8,128)}, f32[14,8,32,128]{3,2,1,0:T(8,128)}) custom-call(f32[27,8,32,128]{3,2,1,0:T(8,128)} %get-tuple-element.32.pops_in, f32[14,8,32,128]{3,2,1,0:T(8,128)} %get-tuple-element.33.scal_in, f32[11,32,128]{2,1,0:T(8,128)S(1)} %collective-permute-done.6.got_a, ...), custom_call_target="tpu_custom_call", output_to_operand_aliasing={{0}: (0, {}), {1}: (1, {})} | custom-call | bytes 720896 | tf_op jit(solution)/shard_map/write_edge_planes/pallas_call | solution.py:416
Async XLA Ops:
  4.8 5.0 %collective-permute-start = (f32[152,128]{1,0:T(8,128)S(1)}, f32[152,128]{1,0:T(8,128)S(1)}, u32[]{:S(2)}, u32[]{:S(2)}) collective-permute-start(f32[152,128]{1,0:T(8,128)S(1)} %get-tuple-element.22), channel_id=1, source_target_pairs={{0,1},{1,0},{2,3},{3,2},{4,5},{5,4},{6,7},{7,6},{8,9},{9,8},{10,11... | collective-permute-start | bytes 233480 | tf_op jit(solution)/shard_map/ppermute | solution.py:390
  6.5 6.3 %collective-permute-start.1 = (f32[152,128]{1,0:T(8,128)S(1)}, f32[152,128]{1,0:T(8,128)S(1)}, u32[]{:S(2)}, u32[]{:S(2)}) collective-permute-start(f32[152,128]{1,0:T(8,128)S(1)} %get-tuple-element.23), channel_id=1, source_target_pairs={{1,2},{2,1},{5,6},{6,5},{9,10},{10,9},{13,14},{14,13},{17,18},{18,... | collective-permute-start | bytes 233480 | tf_op jit(solution)/shard_map/ppermute | solution.py:390
  12.9 5.3 %collective-permute-start.2 = (f32[376,128]{1,0:T(8,128)S(1)}, f32[376,128]{1,0:T(8,128)S(1)}, u32[]{:S(2)}, u32[]{:S(2)}) collective-permute-start(f32[376,128]{1,0:T(8,128)S(1)} %get-tuple-element.27), channel_id=1, source_target_pairs={{0,28},{4,0},{8,4},{12,8},{16,12},{20,16},{24,20},{28,24},{1,29},{... | collective-permute-start | bytes 577544 | tf_op jit(solution)/shard_map/ppermute | solution.py:379
  13.4 7.7 %collective-permute-start.3 = (f32[376,128]{1,0:T(8,128)S(1)}, f32[376,128]{1,0:T(8,128)S(1)}, u32[]{:S(2)}, u32[]{:S(2)}) collective-permute-start(f32[376,128]{1,0:T(8,128)S(1)} %get-tuple-element.28), channel_id=1, source_target_pairs={{0,4},{4,8},{8,12},{12,16},{16,20},{20,24},{24,28},{28,0},{1,5},{5... | collective-permute-start | bytes 577544 | tf_op jit(solution)/shard_map/ppermute | solution.py:379
  21.8 9.0 %collective-permute-start.6 = (f32[11,32,128]{2,1,0:T(8,128)S(1)}, f32[11,32,128]{2,1,0:T(8,128)S(1)}, u32[]{:S(2)}, u32[]{:S(2)}) collective-permute-start(f32[11,32,128]{2,1,0:T(8,128)S(1)} %get-tuple-element.34), channel_id=1, source_target_pairs={{0,28},{4,0},{8,4},{12,8},{16,12},{20,16},{24,20},{28,24},{1,29},{... | collective-permute-start | bytes 540680 | tf_op jit(solution)/shard_map/ppermute | solution.py:379
  21.9 9.0 %collective-permute-start.7 = (f32[11,32,128]{2,1,0:T(8,128)S(1)}, f32[11,32,128]{2,1,0:T(8,128)S(1)}, u32[]{:S(2)}, u32[]{:S(2)}) collective-permute-start(f32[11,32,128]{2,1,0:T(8,128)S(1)} %get-tuple-element.35), channel_id=1, source_target_pairs={{0,4},{4,8},{8,12},{12,16},{16,20},{20,24},{24,28},{28,0},{1,5},{5... | collective-permute-start | bytes 540680 | tf_op jit(solution)/shard_map/ppermute | solution.py:379
  22.4 4.0 %collective-permute-start.4 = (f32[88,128]{1,0:T(8,128)S(1)}, f32[88,128]{1,0:T(8,128)S(1)}, u32[]{:S(2)}, u32[]{:S(2)}) collective-permute-start(f32[88,128]{1,0:T(8,128)S(1)} %get-tuple-element.30), channel_id=1, source_target_pairs={{0,1},{1,0},{2,3},{3,2},{4,5},{5,4},{6,7},{7,6},{8,9},{9,8},{10,11... | collective-permute-start | bytes 135176 | tf_op jit(solution)/shard_map/ppermute | solution.py:390
  22.4 5.9 %collective-permute-start.5 = (f32[88,128]{1,0:T(8,128)S(1)}, f32[88,128]{1,0:T(8,128)S(1)}, u32[]{:S(2)}, u32[]{:S(2)}) collective-permute-start(f32[88,128]{1,0:T(8,128)S(1)} %get-tuple-element.31), channel_id=1, source_target_pairs={{1,2},{2,1},{5,6},{6,5},{9,10},{10,9},{13,14},{14,13},{17,18},{18,... | collective-permute-start | bytes 135176 | tf_op jit(solution)/shard_map/ppermute | solution.py:390

commit v5 on v3

--- a/solution.py
+++ b/solution.py
@@ -152,14 +152,19 @@
     return {-1: (-1, 1), 0: (0, size_x - 1), 1: (size_x - 1, 1)}[a]
 
 
+def by_swap(axis, swap, fill):
+    odd = lax.rem(lax.axis_index(axis), 2) == 1
+    first, second = (-1, 1) if swap == 0 else (1, -1)
+    pl.when(odd)(lambda: fill(first))
+    pl.when(jnp.logical_not(odd))(lambda: fill(second))
+
+
 def by_side_sent(axis, refs, fill):
-    odd = lax.rem(lax.axis_index(axis), 2) == 1
-    pl.when(odd)(lambda: fill((refs[0], refs[1])))
-    pl.when(jnp.logical_not(odd))(lambda: fill((refs[1], refs[0])))
+    by_swap(axis, 0, lambda side: fill(refs if side < 0 else refs[::-1]))
 
 
 def by_side_received(axis, refs, take):
-    by_side_sent(axis, (refs[1], refs[0]), take)
+    by_side_sent(axis, refs[::-1], take)
 
 
 def sizes_of(state):
@@ -172,38 +177,35 @@
     return ran, -(-total // SUB) * SUB
 
 
-def send_first_cross(state, kinds, sent):
+def send_first_cross(state, kinds, b, msg):
     size_x, size_y = sizes_of(state)
     rows, flat = state.shape[2], flat_of(state)
     ran, _ = first_cross_rows(size_x)
-    for b, msg in zip(SIDES, sent):
-        y_out, y_edge = (size_y, size_y - 1) if b > 0 else (-1, 0)
-        for k, i in enumerate(Y_SETS[b]):
-            msg[k * size_x : (k + 1) * size_x, :] = flat[i, lines(DIRS[i][0], y_out, rows, size_x), :]
-        for k, i in enumerate(SIDE_SETS[b]):
-            x, step = side_span(i, size_x)
-            msg[ran + 2 * k : ran + 2 * k + 2, :] = flat[i, lines(x, y_edge, rows, 2, step), :]
-        last = ran + 2 * len(SIDE_SETS[b])
-        for s, x in enumerate((0, size_x - 1)):
-            line = kinds[x, y_edge : y_edge + 1, :]
-            msg[last + s : last + s + 1, :] = (line + 1).astype(jnp.float32)
-
-
-def take_first_cross(state, halo_kinds, received):
+    y_out, y_edge = (size_y, size_y - 1) if b > 0 else (-1, 0)
+    for k, i in enumerate(Y_SETS[b]):
+        msg[k * size_x : (k + 1) * size_x, :] = flat[i, lines(DIRS[i][0], y_out, rows, size_x), :]
+    for k, i in enumerate(SIDE_SETS[b]):
+        x, step = side_span(i, size_x)
+        msg[ran + 2 * k : ran + 2 * k + 2, :] = flat[i, lines(x, y_edge, rows, 2, step), :]
+    last = ran + 2 * len(SIDE_SETS[b])
+    for s, x in enumerate((0, size_x - 1)):
+        line = kinds[x, y_edge : y_edge + 1, :]
+        msg[last + s : last + s + 1, :] = (line + 1).astype(jnp.float32)
+
+
+def take_first_cross(state, halo_kinds, b, msg):
     size_x, size_y = sizes_of(state)
     rows, flat = state.shape[2], flat_of(state)
     ran, _ = first_cross_rows(size_x)
-    halo_kinds[...] = jnp.zeros(halo_kinds.shape, jnp.float32)
-    for b, msg in zip(SIDES, received):
-        y_in, y_halo = (0, -1) if b > 0 else (size_y - 1, size_y)
-        for k, i in enumerate(Y_SETS[b]):
-            flat[i, lines(DIRS[i][0], y_in, rows, size_x), :] = msg[k * size_x : (k + 1) * size_x, :]
-        for k, i in enumerate(SIDE_SETS[b]):
-            x, step = side_span(i, size_x)
-            flat[i, lines(x, y_halo, rows, 2, step), :] = msg[ran + 2 * k : ran + 2 * k + 2, :]
-        last = ran + 2 * len(SIDE_SETS[b])
-        first = 0 if b > 0 else 2
-        halo_kinds[first : first + 2, :] = msg[last : last + 2, :]
+    y_in, y_halo = (0, -1) if b > 0 else (size_y - 1, size_y)
+    for k, i in enumerate(Y_SETS[b]):
+        flat[i, lines(DIRS[i][0], y_in, rows, size_x), :] = msg[k * size_x : (k + 1) * size_x, :]
+    for k, i in enumerate(SIDE_SETS[b]):
+        x, step = side_span(i, size_x)
+        flat[i, lines(x, y_halo, rows, 2, step), :] = msg[ran + 2 * k : ran + 2 * k + 2, :]
+    last = ran + 2 * len(SIDE_SETS[b])
+    first = 0 if b > 0 else 2
+    halo_kinds[first : first + 2, :] = msg[last : last + 2, :]
 
 
 def first_loop_rows(size_y):
@@ -242,48 +244,84 @@
     return lambda i: state[i, slot(x), y + PAD : y + PAD + SUB, :]
 
 
-def first_step_tiles(size_x, tiles, pops, scal, state, kinds, raw, sems, kinds_copy=None):
+def collide_raw(raw, at, kinds, state, x, y):
+    collide(lambda i: raw[i, at[0], at[1] : at[1] + SUB, :], kinds[x, y : y + SUB, :], push_tile(state, x, y))
+
+
+def side_kernel(pops, scal, flags, state, kinds, sent, raw, sems, kinds_sem):
+    size_x, size_y, size_z = flags.shape
+    flat_pops = pops.reshape(NF, size_x * size_y, size_z)
+    flat_scal = scal.reshape(NS + NS, size_x * size_y, size_z)
+    kinds_copy = pltpu.make_async_copy(flags, kinds, kinds_sem)
+
+    def copies(n):
+        first, count, row = n * size_y - SUB, 2 * SUB, 0
+        if isinstance(n, int) and n == 0:
+            first, count, row = 0, SUB, SUB
+        elif isinstance(n, int) and n == size_x:
+            count = SUB
+        here, there = pl.ds(first, count), pl.ds(row, count)
+        return (
+            pltpu.make_async_copy(flat_pops.at[:, here], raw.at[0:NF, n, there], sems.at[0, n]),
+            pltpu.make_async_copy(flat_scal.at[:, here], raw.at[NF:NQ, n, there], sems.at[1, n]),
+        )
+
+    for n in range(size_x + 1):
+        for copy in copies(n):
+            copy.start()
+        if n == 0:
+            kinds_copy.start()
+
+    for copy in copies(0):
+        copy.wait()
+    kinds_copy.wait()
+    collide_raw(raw, (0, SUB), kinds, state, 0, 0)
+
+    @pl.loop(1, size_x)
+    def _(n):
+        for copy in copies(n):
+            copy.wait()
+        collide_raw(raw, (n, 0), kinds, state, n - 1, size_y - SUB)
+        collide_raw(raw, (n, SUB), kinds, state, n, 0)
+
+    for copy in copies(size_x):
+        copy.wait()
+    collide_raw(raw, (size_x, 0), kinds, state, size_x - 1, size_y - SUB)
+    by_swap("cross", 0, lambda side: send_first_cross(state, kinds, side, sent))
+
+
+def middle_kernel(pops, scal, kinds, state_in, state, sent, raw, sems):
+    size_x, size_y, _ = kinds.shape
+    inner = pl.ds(SUB, size_y - 2 * SUB)
+
     def copies(x):
-        result = []
-        for n, y in enumerate(tiles):
-            here = pl.ds(y, SUB)
-            there = pl.ds(n * SUB, SUB)
-            result.append(pltpu.make_async_copy(pops.at[:, x, here], raw.at[0:NF, x, there], sems.at[2 * n, x]))
-            result.append(pltpu.make_async_copy(scal.at[:, x, here], raw.at[NF:NQ, x, there], sems.at[2 * n + 1, x]))
-        return result
-
-    for x in range(size_x):
-        for copy in copies(x):
-            copy.start()
-        if x == 0 and kinds_copy is not None:
-            kinds_copy.start()
-    if kinds_copy is not None:
-        kinds_copy.wait()
-
-    @pl.loop(0, size_x)
-    def _(x):
-        for copy in copies(x):
-            copy.wait()
-        for n, y in enumerate(tiles):
-            collide(
-                lambda i: raw[i, x, n * SUB : (n + 1) * SUB, :],
-                kinds[x, y : y + SUB, :],
-                push_tile(state, x, y),
-            )
-
-
-def side_kernel(size_x, tiles, pops, scal, flags, state, kinds, sent_a, sent_b, raw, sems, kinds_sem):
-    kinds_copy = pltpu.make_async_copy(flags, kinds, kinds_sem)
-    first_step_tiles(size_x, tiles, pops, scal, state, kinds, raw, sems, kinds_copy)
-    by_side_sent("cross", (sent_a, sent_b), functools.partial(send_first_cross, state, kinds))
-
-
-def middle_kernel(size_x, tiles, pops, scal, kinds, state_in, state, raw, sems):
-    first_step_tiles(size_x, tiles, pops, scal, state, kinds, raw, sems)
-
-
-def turn_kernel(state_in, got_a, got_b, state, halo_kinds, sent_a, sent_b):
-    by_side_received("cross", (got_a, got_b), functools.partial(take_first_cross, state, halo_kinds))
+        return (
+            pltpu.make_async_copy(pops.at[:, x, inner], raw.at[0:NF, x], sems.at[0, x]),
+            pltpu.make_async_copy(scal.at[:, x, inner], raw.at[NF:NQ, x], sems.at[1, x]),
+        )
+
+    if size_y > 2 * SUB:
+        for x in range(size_x):
+            for copy in copies(x):
+                copy.start()
+    by_swap("cross", 1, lambda side: send_first_cross(state, kinds, side, sent))
+    if size_y > 2 * SUB:
+
+        @pl.loop(0, size_x)
+        def _(x):
+            for copy in copies(x):
+                copy.wait()
+            for y in range(SUB, size_y - SUB, SUB):
+                collide_raw(raw, (x, y - SUB), kinds, state, x, y)
+
+
+def take_kernel(state_in, got, state, halo_kinds):
+    halo_kinds[...] = jnp.zeros(halo_kinds.shape, jnp.float32)
+    by_swap("cross", 0, lambda side: take_first_cross(state, halo_kinds, -side, got))
+
+
+def turn_kernel(state_in, halo_kinds_in, got, state, halo_kinds, sent_a, sent_b):
+    by_swap("cross", 1, lambda side: take_first_cross(state, halo_kinds, -side, got))
     send_first_loop(state, (sent_a, sent_b))
 
 
@@ -383,15 +421,11 @@
     return received
 
 
-def swap_along(axis, messages):
-    count = lax.axis_size(axis)
-    received = []
-    for first, cells in enumerate(messages):
-        pairs = []
-        for i in range(first, count - 1, 2):
-            pairs += [(i, i + 1), (i + 1, i)]
-        received.append(lax.ppermute(cells, axis, pairs))
-    return received
+def swap_along(axis, swap, cells):
+    pairs = []
+    for i in range(swap, lax.axis_size(axis) - 1, 2):
+        pairs += [(i, i + 1), (i + 1, i)]
+    return lax.ppermute(cells, axis, pairs)
 
 
 def per_device(populations, scalars, node_flags):
@@ -400,7 +434,7 @@
     state_shape = pltpu.VMEM((NQ, size_x + 2, size_y + 2 * PAD, size_z), f32)
     kinds_shape = pltpu.VMEM((size_x, size_y, size_z), jnp.int32)
     halo_kinds_shape = pltpu.VMEM((SUB, size_z), f32)
-    cross_1 = [pltpu.VMEM((first_cross_rows(size_x)[1], size_z), f32)] * 2
+    cross_1 = pltpu.VMEM((first_cross_rows(size_x)[1], size_z), f32)
     loop_1 = [pltpu.VMEM((first_loop_rows(size_y)[1], size_z), f32)] * 2
     cross_2 = [pltpu.VMEM((len(Y_SETS[1]) * SUB, size_z), f32)] * 2
     loop_2 = [pltpu.VMEM((len(X_SETS[1]), size_y, size_z), f32)] * 2
@@ -435,41 +469,48 @@
     def in_hbm(*arrays):
         return [(pltpu.HBM, x) for x in arrays]
 
-    tiles = list(range(0, size_y, SUB))
-    side, middle = sorted({tiles[0], tiles[-1]}), tiles[1:-1]
-
-    def staging(rows):
-        return [
-            pltpu.VMEM((NQ, size_x, len(rows) * SUB, size_z), f32),
-            pltpu.SemaphoreType.DMA((2 * len(rows), size_x)),
-        ]
-
-    state, kinds, *sent = call(
-        functools.partial(side_kernel, size_x, side),
+    tiles = size_y // SUB
+    state, kinds, sent_a = call(
+        side_kernel,
         "first_step_side_rows",
         in_hbm(populations, scalars, node_flags),
-        [state_shape, kinds_shape] + cross_1,
-        tiles=size_x * len(side),
-        scratch=staging(side) + [pltpu.SemaphoreType.DMA],
-    )
-    received = swap_along("cross", sent)
-    if middle:
-        (state,) = call(
-            functools.partial(middle_kernel, size_x, middle),
-            "first_step_middle_rows",
-            in_hbm(populations, scalars) + on_chip(kinds, state),
-            [state_shape],
-            tiles=size_x * len(middle),
-            scratch=staging(middle),
-            aliases={3: 0},
-        )
+        [state_shape, kinds_shape, cross_1],
+        tiles=2 * size_x,
+        scratch=[
+            pltpu.VMEM((NQ, size_x + 1, 2 * SUB, size_z), f32),
+            pltpu.SemaphoreType.DMA((2, size_x + 1)),
+            pltpu.SemaphoreType.DMA,
+        ],
+    )
+    got_a = swap_along("cross", 0, sent_a)
+    state, sent_b = call(
+        middle_kernel,
+        "first_step_middle_rows",
+        in_hbm(populations, scalars) + on_chip(kinds, state),
+        [state_shape, cross_1],
+        tiles=size_x * (tiles - 2),
+        scratch=[
+            pltpu.VMEM((NQ, size_x, max(size_y - 2 * SUB, SUB), size_z), f32),
+            pltpu.SemaphoreType.DMA((2, size_x)),
+        ],
+        aliases={3: 0},
+    )
+    got_b = swap_along("cross", 1, sent_b)
+    state, halo_kinds = call(
+        take_kernel,
+        "take_first_swap",
+        on_chip(state, got_a),
+        [state_shape, halo_kinds_shape],
+        tiles=1,
+        aliases={0: 0},
+    )
     state, halo_kinds, *sent = call(
         turn_kernel,
         "cross_to_loop",
-        on_chip(state, *received),
+        on_chip(state, halo_kinds, got_b),
         [state_shape, halo_kinds_shape] + loop_1,
         tiles=1,
-        aliases={0: 0},
+        aliases={0: 0, 1: 1},
     )
     from_loop = shift_along("loop", True, sent)
     out, *sent = call(
@@ -477,15 +518,15 @@
         "second_step_inner_planes",
         on_chip(state, kinds),
         [state_shape] + cross_2,
-        tiles=(size_x - 2) * len(tiles),
-    )
-    from_cross = swap_along("cross", sent)
+        tiles=(size_x - 2) * tiles,
+    )
+    from_cross = [swap_along("cross", swap, cells) for swap, cells in enumerate(sent)]
     state, out, *sent = call(
         edge_kernel,
         "second_step_edge_planes",
         on_chip(state, out, kinds, halo_kinds, *from_loop, *from_cross),
         [state_shape, state_shape] + loop_2,
-        tiles=2 * len(tiles) + 1,
+        tiles=2 * tiles + 1,
         scratch=[pltpu.VMEM((NQ, SUB, size_z), f32)],
         aliases={0: 0, 1: 1},
     )

time: 31.3 us -> 33.7 us (1.077)
  waiting for transfers between devices: 8.64 us -> 12.4 us
  starting transfers between devices: 9 us -> 7.95 us
    ppermute x4, waiting for transfers between devices: 4.63 us -> 8.37 us  [swap_along(): return lax.ppermute(cells, axis, pairs)]
    ppermute x4, starting transfers between devices: 6.8 us -> 5.76 us  [swap_along(): return lax.ppermute(cells, axis, pairs)]
    pallas_call x7 -> x8, Pallas kernels: 12.7 us -> 12.4 us  [call(): pl.pallas_call(kernel, out_shape=results, in_specs=specs, out_specs=[hbm...]
  transfers between devices with their start and end apart: 8 -> 8, of which waited for: 5 -> 5; matrix products, arithmetic and copies ran while one was open for 0% -> 0% of each run, Pallas kernels for 23% -> 21%
where the time goes in v5:
time: 33.7 us; the launch traced here: 33.5 us
  Pallas kernels  12.4 us (37%)
  waiting for transfers between devices  12.4 us (37%)
  starting transfers between devices  7.95 us (24%)
  between operations  0.72 us (2%)
    pallas_call x8, Pallas kernels, call(): pl.pallas_call(kernel, out_shape=results, in_specs=specs, out_specs=[hbm...  12.4 us
    ppermute x4, waiting for transfers between devices, swap_along(): return lax.ppermute(cells, axis, pairs)  8.37 us
    ppermute x4, starting transfers between devices, swap_along(): return lax.ppermute(cells, axis, pairs)  5.76 us
    ppermute x4, waiting for transfers between devices, shift_along(): received.append(lax.ppermute(cells, axis, pairs))  4.01 us
    ppermute x4, starting transfers between devices, shift_along(): received.append(lax.ppermute(cells, axis, pairs))  2.2 us
  transfers between devices with their start and end apart: 8, of which 5 were waited for; matrix products, arithmetic and copies ran while one was open for 0% of the time, Pallas kernels for 21%

profile of v5, /device:TPU:16, one launch (start us, length us, event | category | flops | bytes accessed | tf_op | source)
XLA Modules:
  0.0 33.5 jit_solution(6074547782033636561)
XLA Ops:
  0.6 3.5 %first_step_side_rows.1 = (f32[41,10,48,128]{3,2,1,0:T(8,128)S(1)}, s32[8,32,128]{2,1,0:T(8,128)S(1)}, f32[152,128]{1,0:T(8,128)S(1)}) custom-call(f32[27,8,32,128]{3,2,1,0:T(8,128)} %pops.3, f32[14,8,32,128]{3,2,1,0:T(8,128)} %scal.3, s32[8,32,128]{2,1,0:T(8,128)} %flags.1), custom_call_target="tpu_custom_call" | custom-call | flops 8192000 | bytes 5373952 | tf_op jit(solution)/shard_map/first_step_side_rows/pallas_call | solution.py:452
  4.2 1.6 %collective-permute-start = (f32[152,128]{1,0:T(8,128)S(1)}, f32[152,128]{1,0:T(8,128)S(1)}, u32[]{:S(2)}, u32[]{:S(2)}) collective-permute-start(f32[152,128]{1,0:T(8,128)S(1)} %get-tuple-element.24), channel_id=1, source_target_pairs={{0,1},{1,0},{2,3},{3,2},{4,5},{5,4},{6,7},{7,6},{8,9},{9,8},{10,11... | collective-permute-start | bytes 233480 | tf_op jit(solution)/shard_map/ppermute | solution.py:428
  5.8 2.6 %first_step_middle_rows.1 = (f32[41,10,48,128]{3,2,1,0:T(8,128)S(1)}, f32[152,128]{1,0:T(8,128)S(1)}) custom-call(f32[27,8,32,128]{3,2,1,0:T(8,128)} %pops.3, f32[14,8,32,128]{3,2,1,0:T(8,128)} %scal.3, s32[8,32,128]{2,1,0:T(8,128)S(1)} %get-tuple-element.21.kinds, f32[41,10,48,128]{3,2,1,0:T(8,128)S(1)} %get-tuple-element.22.state_in), custom_call_target="tpu_custom_call", output_to_operand_aliasing={{0}: (3, {})} | custom-call | flops 8192000 | bytes 5373952 | tf_op jit(solution)/shard_map/first_step_middle_rows/pallas_call | solution.py:452
  8.4 1.9 %collective-permute-start.1 = (f32[152,128]{1,0:T(8,128)S(1)}, f32[152,128]{1,0:T(8,128)S(1)}, u32[]{:S(2)}, u32[]{:S(2)}) collective-permute-start(f32[152,128]{1,0:T(8,128)S(1)} %get-tuple-element.27), channel_id=1, source_target_pairs={{1,2},{2,1},{5,6},{6,5},{9,10},{10,9},{13,14},{14,13},{17,18},{18,... | collective-permute-start | bytes 233480 | tf_op jit(solution)/shard_map/ppermute | solution.py:428
  10.3 0.0 collective-permute-done.got
  10.3 0.1 take_first_swap.1
  10.4 4.3 %collective-permute-done.1.got = f32[152,128]{1,0:T(8,128)S(1)} collective-permute-done((f32[152,128]{1,0:T(8,128)S(1)}, f32[152,128]{1,0:T(8,128)S(1)}, u32[]{:S(2)}, u32[]{:S(2)}) %collective-permute-start.1) | collective-permute-done | bytes 77856 | tf_op jit(solution)/shard_map/ppermute | solution.py:428
  14.7 0.1 cross_to_loop.1
  14.8 0.5 %collective-permute-start.2 = (f32[376,128]{1,0:T(8,128)S(1)}, f32[376,128]{1,0:T(8,128)S(1)}, u32[]{:S(2)}, u32[]{:S(2)}) collective-permute-start(f32[376,128]{1,0:T(8,128)S(1)} %get-tuple-element.31), channel_id=1, source_target_pairs={{0,28},{4,0},{8,4},{12,8},{16,12},{20,16},{24,20},{28,24},{1,29},{... | collective-permute-start | bytes 577544 | tf_op jit(solution)/shard_map/ppermute | solution.py:420
  15.3 0.1 collective-permute-start.3
  15.3 1.9 %second_step_inner_planes.1 = (f32[41,10,48,128]{3,2,1,0:T(8,128)S(1)}, f32[88,128]{1,0:T(8,128)S(1)}, f32[88,128]{1,0:T(8,128)S(1)}) custom-call(f32[41,10,48,128]{3,2,1,0:T(8,128)S(1)} %get-tuple-element.28.state.state_in, s32[8,32,128]{2,1,0:T(8,128)S(1)} %get-tuple-element.21.kinds), custom_call_target="tpu_custom_call" | custom-call | flops 12288000 | bytes 8060928 | tf_op jit(solution)/shard_map/second_step_inner_planes/pallas_call | solution.py:452
  17.2 0.1 collective-permute-start.4
  17.3 2.2 %collective-permute-start.5 = (f32[88,128]{1,0:T(8,128)S(1)}, f32[88,128]{1,0:T(8,128)S(1)}, u32[]{:S(2)}, u32[]{:S(2)}) collective-permute-start(f32[88,128]{1,0:T(8,128)S(1)} %get-tuple-element.34), channel_id=1, source_target_pairs={{1,2},{2,1},{5,6},{6,5},{9,10},{10,9},{13,14},{14,13},{17,18},{18,... | collective-permute-start | bytes 135176 | tf_op jit(solution)/shard_map/ppermute | solution.py:428
  19.4 2.2 %collective-permute-done.4.cross_a = f32[88,128]{1,0:T(8,128)S(1)} collective-permute-done((f32[88,128]{1,0:T(8,128)S(1)}, f32[88,128]{1,0:T(8,128)S(1)}, u32[]{:S(2)}, u32[]{:S(2)}) %collective-permute-start.4) | collective-permute-done | bytes 45088 | tf_op jit(solution)/shard_map/ppermute | solution.py:428
  21.6 1.9 %collective-permute-done.5.cross_b = f32[88,128]{1,0:T(8,128)S(1)} collective-permute-done((f32[88,128]{1,0:T(8,128)S(1)}, f32[88,128]{1,0:T(8,128)S(1)}, u32[]{:S(2)}, u32[]{:S(2)}) %collective-permute-start.5) | collective-permute-done | bytes 45088 | tf_op jit(solution)/shard_map/ppermute | solution.py:428
  23.5 0.0 collective-permute-done.2.loop_a
  23.5 0.0 collective-permute-done.3.loop_b
  23.5 0.9 %second_step_edge_planes.1 = (f32[41,10,48,128]{3,2,1,0:T(8,128)S(1)}, f32[41,10,48,128]{3,2,1,0:T(8,128)S(1)}, f32[11,32,128]{2,1,0:T(8,128)S(1)}, f32[11,32,128]{2,1,0:T(8,128)S(1)}) custom-call(f32[41,10,48,128]{3,2,1,0:T(8,128)S(1)} %get-tuple-element.28.state.state_in, ...), custom_call_target="tpu_custom_call", output_to_operand_aliasing={{0}: (0, {}), {1}: (1, {})} | custom-call | flops 4608000 | bytes 3022848 | tf_op jit(solution)/shard_map/second_step_edge_planes/pallas_call | solution.py:452
  24.4 1.6 %collective-permute-start.6 = (f32[11,32,128]{2,1,0:T(8,128)S(1)}, f32[11,32,128]{2,1,0:T(8,128)S(1)}, u32[]{:S(2)}, u32[]{:S(2)}) collective-permute-start(f32[11,32,128]{2,1,0:T(8,128)S(1)} %get-tuple-element.38), channel_id=1, source_target_pairs={{0,28},{4,0},{8,4},{12,8},{16,12},{20,16},{24,20},{28,24},{1,29},{... | collective-permute-start | bytes 540680 | tf_op jit(solution)/shard_map/ppermute | solution.py:420
  26.0 0.0 collective-permute-start.7
  26.0 2.5 %write_all_planes.1 = (f32[27,8,32,128]{3,2,1,0:T(8,128)}, f32[14,8,32,128]{3,2,1,0:T(8,128)}) custom-call(f32[41,10,48,128]{3,2,1,0:T(8,128)S(1)} %get-tuple-element.35.out), custom_call_target="tpu_custom_call" | custom-call | bytes 10747904 | tf_op jit(solution)/shard_map/write_all_planes/pallas_call | solution.py:452
  28.5 2.0 %collective-permute-done.6.got_a = f32[11,32,128]{2,1,0:T(8,128)S(1)} collective-permute-done((f32[11,32,128]{2,1,0:T(8,128)S(1)}, f32[11,32,128]{2,1,0:T(8,128)S(1)}, u32[]{:S(2)}, u32[]{:S(2)}) %collective-permute-start.6) | collective-permute-done | bytes 180256 | tf_op jit(solution)/shard_map/ppermute | solution.py:420
  30.6 2.0 %collective-permute-done.7.got_b = f32[11,32,128]{2,1,0:T(8,128)S(1)} collective-permute-done((f32[11,32,128]{2,1,0:T(8,128)S(1)}, f32[11,32,128]{2,1,0:T(8,128)S(1)}, u32[]{:S(2)}, u32[]{:S(2)}) %collective-permute-start.7) | collective-permute-done | bytes 180256 | tf_op jit(solution)/shard_map/ppermute | solution.py:420
  32.5 0.9 %write_edge_planes.1 = (f32[27,8,32,128]{3,2,1,0:T(8,128)}, f32[14,8,32,128]{3,2,1,0:T(8,128)}) custom-call(f32[27,8,32,128]{3,2,1,0:T(8,128)} %get-tuple-element.36.pops_in, f32[14,8,32,128]{3,2,1,0:T(8,128)} %get-tuple-element.37.scal_in, f32[11,32,128]{2,1,0:T(8,128)S(1)} %collective-permute-done.6.got_a, ...), custom_call_target="tpu_custom_call", output_to_operand_aliasing={{0}: (0, {}), {1}: (1, {})} | custom-call | bytes 720896 | tf_op jit(solution)/shard_map/write_edge_planes/pallas_call | solution.py:452
Async XLA Ops:
  4.2 6.2 %collective-permute-start = (f32[152,128]{1,0:T(8,128)S(1)}, f32[152,128]{1,0:T(8,128)S(1)}, u32[]{:S(2)}, u32[]{:S(2)}) collective-permute-start(f32[152,128]{1,0:T(8,128)S(1)} %get-tuple-element.24), channel_id=1, source_target_pairs={{0,1},{1,0},{2,3},{3,2},{4,5},{5,4},{6,7},{7,6},{8,9},{9,8},{10,11... | collective-permute-start | bytes 233480 | tf_op jit(solution)/shard_map/ppermute | solution.py:428
  8.4 6.3 %collective-permute-start.1 = (f32[152,128]{1,0:T(8,128)S(1)}, f32[152,128]{1,0:T(8,128)S(1)}, u32[]{:S(2)}, u32[]{:S(2)}) collective-permute-start(f32[152,128]{1,0:T(8,128)S(1)} %get-tuple-element.27), channel_id=1, source_target_pairs={{1,2},{2,1},{5,6},{6,5},{9,10},{10,9},{13,14},{14,13},{17,18},{18,... | collective-permute-start | bytes 233480 | tf_op jit(solution)/shard_map/ppermute | solution.py:428
  14.8 8.7 %collective-permute-start.2 = (f32[376,128]{1,0:T(8,128)S(1)}, f32[376,128]{1,0:T(8,128)S(1)}, u32[]{:S(2)}, u32[]{:S(2)}) collective-permute-start(f32[376,128]{1,0:T(8,128)S(1)} %get-tuple-element.31), channel_id=1, source_target_pairs={{0,28},{4,0},{8,4},{12,8},{16,12},{20,16},{24,20},{28,24},{1,29},{... | collective-permute-start | bytes 577544 | tf_op jit(solution)/shard_map/ppermute | solution.py:420
  15.3 8.2 %collective-permute-start.3 = (f32[376,128]{1,0:T(8,128)S(1)}, f32[376,128]{1,0:T(8,128)S(1)}, u32[]{:S(2)}, u32[]{:S(2)}) collective-permute-start(f32[376,128]{1,0:T(8,128)S(1)} %get-tuple-element.32), channel_id=1, source_target_pairs={{0,4},{4,8},{8,12},{12,16},{16,20},{20,24},{24,28},{28,0},{1,5},{5... | collective-permute-start | bytes 577544 | tf_op jit(solution)/shard_map/ppermute | solution.py:420
  17.2 4.4 %collective-permute-start.4 = (f32[88,128]{1,0:T(8,128)S(1)}, f32[88,128]{1,0:T(8,128)S(1)}, u32[]{:S(2)}, u32[]{:S(2)}) collective-permute-start(f32[88,128]{1,0:T(8,128)S(1)} %get-tuple-element.33), channel_id=1, source_target_pairs={{0,1},{1,0},{2,3},{3,2},{4,5},{5,4},{6,7},{7,6},{8,9},{9,8},{10,11... | collective-permute-start | bytes 135176 | tf_op jit(solution)/shard_map/ppermute | solution.py:428
  17.3 6.2 %collective-permute-start.5 = (f32[88,128]{1,0:T(8,128)S(1)}, f32[88,128]{1,0:T(8,128)S(1)}, u32[]{:S(2)}, u32[]{:S(2)}) collective-permute-start(f32[88,128]{1,0:T(8,128)S(1)} %get-tuple-element.34), channel_id=1, source_target_pairs={{1,2},{2,1},{5,6},{6,5},{9,10},{10,9},{13,14},{14,13},{17,18},{18,... | collective-permute-start | bytes 135176 | tf_op jit(solution)/shard_map/ppermute | solution.py:428
  24.4 6.2 %collective-permute-start.6 = (f32[11,32,128]{2,1,0:T(8,128)S(1)}, f32[11,32,128]{2,1,0:T(8,128)S(1)}, u32[]{:S(2)}, u32[]{:S(2)}) collective-permute-start(f32[11,32,128]{2,1,0:T(8,128)S(1)} %get-tuple-element.38), channel_id=1, source_target_pairs={{0,28},{4,0},{8,4},{12,8},{16,12},{20,16},{24,20},{28,24},{1,29},{... | collective-permute-start | bytes 540680 | tf_op jit(solution)/shard_map/ppermute | solution.py:420
  26.0 6.5 %collective-permute-start.7 = (f32[11,32,128]{2,1,0:T(8,128)S(1)}, f32[11,32,128]{2,1,0:T(8,128)S(1)}, u32[]{:S(2)}, u32[]{:S(2)}) collective-permute-start(f32[11,32,128]{2,1,0:T(8,128)S(1)} %get-tuple-element.39), channel_id=1, source_target_pairs={{0,4},{4,8},{8,12},{12,16},{16,20},{20,24},{24,28},{28,0},{1,5},{5... | collective-permute-start | bytes 540680 | tf_op jit(solution)/shard_map/ppermute | solution.py:420

commit v6 on v5

--- a/solution.py
+++ b/solution.py
@@ -159,12 +159,10 @@
     pl.when(jnp.logical_not(odd))(lambda: fill(second))
 
 
-def by_side_sent(axis, refs, fill):
-    by_swap(axis, 0, lambda side: fill(refs if side < 0 else refs[::-1]))
-
-
-def by_side_received(axis, refs, take):
-    by_side_sent(axis, refs[::-1], take)
+def has_partner(axis, swap):
+    index, count = lax.axis_index(axis), lax.axis_size(axis)
+    first = index - lax.rem(index + swap, 2)
+    return (first >= 0) & (first + 1 < count)
 
 
 def sizes_of(state):
@@ -193,19 +191,19 @@
         msg[last + s : last + s + 1, :] = (line + 1).astype(jnp.float32)
 
 
-def take_first_cross(state, halo_kinds, b, msg):
+def take_first_cross(state, halo_kinds, b, msg, partner):
     size_x, size_y = sizes_of(state)
     rows, flat = state.shape[2], flat_of(state)
     ran, _ = first_cross_rows(size_x)
     y_in, y_halo = (0, -1) if b > 0 else (size_y - 1, size_y)
     for k, i in enumerate(Y_SETS[b]):
-        flat[i, lines(DIRS[i][0], y_in, rows, size_x), :] = msg[k * size_x : (k + 1) * size_x, :]
+        flat[i, lines(DIRS[i][0], y_in, rows, size_x), :] = jnp.where(partner, msg[k * size_x : (k + 1) * size_x, :], 0.0)
     for k, i in enumerate(SIDE_SETS[b]):
         x, step = side_span(i, size_x)
-        flat[i, lines(x, y_halo, rows, 2, step), :] = msg[ran + 2 * k : ran + 2 * k + 2, :]
+        flat[i, lines(x, y_halo, rows, 2, step), :] = jnp.where(partner, msg[ran + 2 * k : ran + 2 * k + 2, :], 0.0)
     last = ran + 2 * len(SIDE_SETS[b])
     first = 0 if b > 0 else 2
-    halo_kinds[first : first + 2, :] = msg[last : last + 2, :]
+    halo_kinds[first : first + 2, :] = jnp.where(partner, msg[last : last + 2, :], 0.0)
 
 
 def first_loop_rows(size_y):
@@ -248,7 +246,7 @@
     collide(lambda i: raw[i, at[0], at[1] : at[1] + SUB, :], kinds[x, y : y + SUB, :], push_tile(state, x, y))
 
 
-def side_kernel(pops, scal, flags, state, kinds, sent, raw, sems, kinds_sem):
+def side_kernel(pops, scal, flags, state, kinds, sent_a, sent_b, raw, sems, kinds_sem):
     size_x, size_y, size_z = flags.shape
     flat_pops = pops.reshape(NF, size_x * size_y, size_z)
     flat_scal = scal.reshape(NS + NS, size_x * size_y, size_z)
@@ -287,10 +285,11 @@
     for copy in copies(size_x):
         copy.wait()
     collide_raw(raw, (size_x, 0), kinds, state, size_x - 1, size_y - SUB)
-    by_swap("cross", 0, lambda side: send_first_cross(state, kinds, side, sent))
-
-
-def middle_kernel(pops, scal, kinds, state_in, state, sent, raw, sems):
+    by_swap("cross", 0, lambda side: send_first_cross(state, kinds, side, sent_a))
+    by_swap("cross", 1, lambda side: send_first_cross(state, kinds, side, sent_b))
+
+
+def middle_kernel(pops, scal, kinds, state_in, state, raw, sems):
     size_x, size_y, _ = kinds.shape
     inner = pl.ds(SUB, size_y - 2 * SUB)
 
@@ -300,28 +299,23 @@
             pltpu.make_async_copy(scal.at[:, x, inner], raw.at[NF:NQ, x], sems.at[1, x]),
         )
 
-    if size_y > 2 * SUB:
-        for x in range(size_x):
-            for copy in copies(x):
-                copy.start()
-    by_swap("cross", 1, lambda side: send_first_cross(state, kinds, side, sent))
-    if size_y > 2 * SUB:
-
-        @pl.loop(0, size_x)
-        def _(x):
-            for copy in copies(x):
-                copy.wait()
-            for y in range(SUB, size_y - SUB, SUB):
-                collide_raw(raw, (x, y - SUB), kinds, state, x, y)
-
-
-def take_kernel(state_in, got, state, halo_kinds):
+    for x in range(size_x):
+        for copy in copies(x):
+            copy.start()
+
+    @pl.loop(0, size_x)
+    def _(x):
+        for copy in copies(x):
+            copy.wait()
+        for y in range(SUB, size_y - SUB, SUB):
+            collide_raw(raw, (x, y - SUB), kinds, state, x, y)
+
+
+def turn_kernel(state_in, got_a, got_b, state, halo_kinds, sent_a, sent_b):
     halo_kinds[...] = jnp.zeros(halo_kinds.shape, jnp.float32)
-    by_swap("cross", 0, lambda side: take_first_cross(state, halo_kinds, -side, got))
-
-
-def turn_kernel(state_in, halo_kinds_in, got, state, halo_kinds, sent_a, sent_b):
-    by_swap("cross", 1, lambda side: take_first_cross(state, halo_kinds, -side, got))
+    for swap, got in enumerate((got_a, got_b)):
+        partner = has_partner("cross", swap)
+        by_swap("cross", swap, lambda side: take_first_cross(state, halo_kinds, -side, got, partner))
     send_first_loop(state, (sent_a, sent_b))
 
 
@@ -334,13 +328,13 @@
         for y in range(0, size_y, SUB):
             collide(load_tile(state, x, y), kinds[x, y : y + SUB, :], push_tile(out, x, y))
 
-    def send(sent):
-        for b, msg in zip(SIDES, sent):
-            y_out = size_y if b > 0 else -1
-            for k, i in enumerate(Y_SETS[b]):
-                msg[k * SUB : k * SUB + size_x - 2, :] = flat[i, lines(DIRS[i][0] + 1, y_out, rows, size_x - 2), :]
-
-    by_side_sent("cross", (sent_a, sent_b), send)
+    def send(b, msg):
+        y_out = size_y if b > 0 else -1
+        for k, i in enumerate(Y_SETS[b]):
+            msg[k * SUB : k * SUB + size_x - 2, :] = flat[i, lines(DIRS[i][0] + 1, y_out, rows, size_x - 2), :]
+
+    for swap, msg in enumerate((sent_a, sent_b)):
+        by_swap("cross", swap, lambda side: send(side, msg))
 
 
 def edge_kernel(state_in, out_in, kinds, halo_kinds, loop_a, loop_b, cross_a, cross_b, state, out, sent_a, sent_b, halo):
@@ -368,13 +362,15 @@
 
     collide(lambda i: halo[i], code - 1, put)
 
-    def take(received):
-        for b, msg in zip(SIDES, received):
-            y_in = 0 if b > 0 else size_y - 1
-            for k, i in enumerate(Y_SETS[b]):
-                flat_out[i, lines(DIRS[i][0] + 1, y_in, rows, size_x - 2), :] = msg[k * SUB : k * SUB + size_x - 2, :]
-
-    by_side_received("cross", (cross_a, cross_b), take)
+    def take(b, msg, partner):
+        y_in = 0 if b > 0 else size_y - 1
+        for k, i in enumerate(Y_SETS[b]):
+            got = jnp.where(partner, msg[k * SUB : k * SUB + size_x - 2, :], 0.0)
+            flat_out[i, lines(DIRS[i][0] + 1, y_in, rows, size_x - 2), :] = got
+
+    for swap, msg in enumerate((cross_a, cross_b)):
+        partner = has_partner("cross", swap)
+        by_swap("cross", swap, lambda side: take(-side, msg, partner))
     for a, msg in zip(SIDES, (sent_a, sent_b)):
         x = -1 if a < 0 else size_x
         for k, i in enumerate(X_SETS[a]):
@@ -421,11 +417,15 @@
     return received
 
 
-def swap_along(axis, swap, cells):
-    pairs = []
-    for i in range(swap, lax.axis_size(axis) - 1, 2):
-        pairs += [(i, i + 1), (i + 1, i)]
-    return lax.ppermute(cells, axis, pairs)
+def swap_along(axis, messages):
+    count, received = lax.axis_size(axis), []
+    for swap, cells in enumerate(messages):
+        pairs = []
+        for i in range(count):
+            j = i + 1 if i % 2 == swap else i - 1
+            pairs.append((i, j if 0 <= j < count else i))
+        received.append(lax.ppermute(cells, axis, pairs))
+    return received
 
 
 def per_device(populations, scalars, node_flags):
@@ -434,7 +434,7 @@
     state_shape = pltpu.VMEM((NQ, size_x + 2, size_y + 2 * PAD, size_z), f32)
     kinds_shape = pltpu.VMEM((size_x, size_y, size_z), jnp.int32)
     halo_kinds_shape = pltpu.VMEM((SUB, size_z), f32)
-    cross_1 = pltpu.VMEM((first_cross_rows(size_x)[1], size_z), f32)
+    cross_1 = [pltpu.VMEM((first_cross_rows(size_x)[1], size_z), f32)] * 2
     loop_1 = [pltpu.VMEM((first_loop_rows(size_y)[1], size_z), f32)] * 2
     cross_2 = [pltpu.VMEM((len(Y_SETS[1]) * SUB, size_z), f32)] * 2
     loop_2 = [pltpu.VMEM((len(X_SETS[1]), size_y, size_z), f32)] * 2
@@ -470,11 +470,11 @@
         return [(pltpu.HBM, x) for x in arrays]
 
     tiles = size_y // SUB
-    state, kinds, sent_a = call(
+    state, kinds, *sent = call(
         side_kernel,
         "first_step_side_rows",
         in_hbm(populations, scalars, node_flags),
-        [state_shape, kinds_shape, cross_1],
+        [state_shape, kinds_shape] + cross_1,
         tiles=2 * size_x,
         scratch=[
             pltpu.VMEM((NQ, size_x + 1, 2 * SUB, size_z), f32),
@@ -482,35 +482,27 @@
             pltpu.SemaphoreType.DMA,
         ],
     )
-    got_a = swap_along("cross", 0, sent_a)
-    state, sent_b = call(
-        middle_kernel,
-        "first_step_middle_rows",
-        in_hbm(populations, scalars) + on_chip(kinds, state),
-        [state_shape, cross_1],
-        tiles=size_x * (tiles - 2),
-        scratch=[
-            pltpu.VMEM((NQ, size_x, max(size_y - 2 * SUB, SUB), size_z), f32),
-            pltpu.SemaphoreType.DMA((2, size_x)),
-        ],
-        aliases={3: 0},
-    )
-    got_b = swap_along("cross", 1, sent_b)
-    state, halo_kinds = call(
-        take_kernel,
-        "take_first_swap",
-        on_chip(state, got_a),
-        [state_shape, halo_kinds_shape],
-        tiles=1,
-        aliases={0: 0},
-    )
+    received = swap_along("cross", sent)
+    if tiles > 2:
+        (state,) = call(
+            middle_kernel,
+            "first_step_middle_rows",
+            in_hbm(populations, scalars) + on_chip(kinds, state),
+            [state_shape],
+            tiles=size_x * (tiles - 2),
+            scratch=[
+                pltpu.VMEM((NQ, size_x, size_y - 2 * SUB, size_z), f32),
+                pltpu.SemaphoreType.DMA((2, size_x)),
+            ],
+            aliases={3: 0},
+        )
     state, halo_kinds, *sent = call(
         turn_kernel,
         "cross_to_loop",
-        on_chip(state, halo_kinds, got_b),
+        on_chip(state, *received),
         [state_shape, halo_kinds_shape] + loop_1,
         tiles=1,
-        aliases={0: 0, 1: 1},
+        aliases={0: 0},
     )
     from_loop = shift_along("loop", True, sent)
     out, *sent = call(
@@ -520,7 +512,7 @@
         [state_shape] + cross_2,
         tiles=(size_x - 2) * tiles,
     )
-    from_cross = [swap_along("cross", swap, cells) for swap, cells in enumerate(sent)]
+    from_cross = swap_along("cross", sent)
     state, out, *sent = call(
         edge_kernel,
         "second_step_edge_planes",

time: 33.7 us -> 31.1 us (0.923)
  waiting for transfers between devices: 12.4 us -> 8.91 us
  starting transfers between devices: 7.95 us -> 8.84 us
    ppermute x4, waiting for transfers between devices: 8.37 us -> 4.9 us  [swap_along(): received.append(lax.ppermute(cells, axis, pairs))]
    ppermute x4, starting transfers between devices: 5.76 us -> 6.64 us  [swap_along(): received.append(lax.ppermute(cells, axis, pairs))]
    pallas_call x8 -> x7, Pallas kernels: 12.4 us -> 12.5 us  [call(): pl.pallas_call(kernel, out_shape=results, in_specs=specs, out_specs=[hbm...]
  transfers between devices with their start and end apart: 8 -> 8, of which waited for: 5 -> 5; matrix products, arithmetic and copies ran while one was open for 0% -> 0% of each run, Pallas kernels for 21% -> 23%
where the time goes in v6:
time: 31.1 us; the launch traced here: 30.9 us
  Pallas kernels  12.5 us (40%)
  waiting for transfers between devices  8.91 us (29%)
  starting transfers between devices  8.84 us (28%)
  between operations  0.71 us (2%)
    pallas_call x7, Pallas kernels, call(): pl.pallas_call(kernel, out_shape=results, in_specs=specs, out_specs=[hbm...  12.5 us
    ppermute x4, starting transfers between devices, swap_along(): received.append(lax.ppermute(cells, axis, pairs))  6.64 us
    ppermute x4, waiting for transfers between devices, swap_along(): received.append(lax.ppermute(cells, axis, pairs))  4.9 us
    ppermute x4, waiting for transfers between devices, shift_along(): received.append(lax.ppermute(cells, axis, pairs))  4.01 us
    ppermute x4, starting transfers between devices, shift_along(): received.append(lax.ppermute(cells, axis, pairs))  2.2 us
  transfers between devices with their start and end apart: 8, of which 5 were waited for; matrix products, arithmetic and copies ran while one was open for 0% of the time, Pallas kernels for 23%

profile of v6, /device:TPU:16, one launch (start us, length us, event | category | flops | bytes accessed | tf_op | source)
XLA Modules:
  0.0 30.9 jit_solution(15788872911497372216)
XLA Ops:
  0.6 3.6 %first_step_side_rows.1 = (f32[41,10,48,128]{3,2,1,0:T(8,128)S(1)}, s32[8,32,128]{2,1,0:T(8,128)S(1)}, f32[152,128]{1,0:T(8,128)S(1)}, f32[152,128]{1,0:T(8,128)S(1)}) custom-call(f32[27,8,32,128]{3,2,1,0:T(8,128)} %pops.3, f32[14,8,32,128]{3,2,1,0:T(8,128)} %scal.3, s32[8,32,128]{2,1,0:T(8,128)} %flags.1), custom_call_target="tpu_custom_call" | custom-call | flops 8192000 | bytes 5373952 | tf_op jit(solution)/shard_map/first_step_side_rows/pallas_call | solution.py:452
  4.2 1.6 %collective-permute-start = (f32[152,128]{1,0:T(8,128)S(1)}, f32[152,128]{1,0:T(8,128)S(1)}, u32[]{:S(2)}, u32[]{:S(2)}) collective-permute-start(f32[152,128]{1,0:T(8,128)S(1)} %get-tuple-element.20), channel_id=1, source_target_pairs={{0,1},{1,0},{2,3},{3,2},{4,5},{5,4},{6,7},{7,6},{8,9},{9,8},{10,11... | collective-permute-start | bytes 233480 | tf_op jit(solution)/shard_map/ppermute | solution.py:427
  5.8 1.9 %collective-permute-start.1 = (f32[152,128]{1,0:T(8,128)S(1)}, f32[152,128]{1,0:T(8,128)S(1)}, u32[]{:S(2)}, u32[]{:S(2)}) collective-permute-start(f32[152,128]{1,0:T(8,128)S(1)} %get-tuple-element.21), channel_id=1, source_target_pairs={{0,0},{1,2},{2,1},{3,3},{4,4},{5,6},{6,5},{7,7},{8,8},{9,10},{10,9... | collective-permute-start | bytes 233480 | tf_op jit(solution)/shard_map/ppermute | solution.py:427
  7.8 2.6 %first_step_middle_rows.1.state_in = f32[41,10,48,128]{3,2,1,0:T(8,128)S(1)} custom-call(f32[27,8,32,128]{3,2,1,0:T(8,128)} %pops.3, f32[14,8,32,128]{3,2,1,0:T(8,128)} %scal.3, s32[8,32,128]{2,1,0:T(8,128)S(1)} %get-tuple-element.18.kinds, f32[41,10,48,128]{3,2,1,0:T(8,128)S(1)} %get-tuple-element.19.state_in), custom_call_target="tpu_custom_call", output_to_operand_aliasing={{}: (3, {})} | custom-call | flops 8192000 | bytes 5373952 | tf_op jit(solution)/shard_map/first_step_middle_rows/pallas_call | solution.py:452
  10.4 0.0 collective-permute-done.got_a
  10.4 1.7 %collective-permute-done.1.got_b = f32[152,128]{1,0:T(8,128)S(1)} collective-permute-done((f32[152,128]{1,0:T(8,128)S(1)}, f32[152,128]{1,0:T(8,128)S(1)}, u32[]{:S(2)}, u32[]{:S(2)}) %collective-permute-start.1) | collective-permute-done | bytes 77856 | tf_op jit(solution)/shard_map/ppermute | solution.py:427
  12.1 0.1 cross_to_loop.1
  12.2 0.5 %collective-permute-start.2 = (f32[376,128]{1,0:T(8,128)S(1)}, f32[376,128]{1,0:T(8,128)S(1)}, u32[]{:S(2)}, u32[]{:S(2)}) collective-permute-start(f32[376,128]{1,0:T(8,128)S(1)} %get-tuple-element.25), channel_id=1, source_target_pairs={{0,28},{4,0},{8,4},{12,8},{16,12},{20,16},{24,20},{28,24},{1,29},{... | collective-permute-start | bytes 577544 | tf_op jit(solution)/shard_map/ppermute | solution.py:416
  12.7 0.1 collective-permute-start.3
  12.8 1.9 %second_step_inner_planes.1 = (f32[41,10,48,128]{3,2,1,0:T(8,128)S(1)}, f32[88,128]{1,0:T(8,128)S(1)}, f32[88,128]{1,0:T(8,128)S(1)}) custom-call(f32[41,10,48,128]{3,2,1,0:T(8,128)S(1)} %get-tuple-element.22.state.state_in, s32[8,32,128]{2,1,0:T(8,128)S(1)} %get-tuple-element.18.kinds), custom_call_target="tpu_custom_call" | custom-call | flops 12288000 | bytes 8060928 | tf_op jit(solution)/shard_map/second_step_inner_planes/pallas_call | solution.py:452
  14.7 0.1 collective-permute-start.4
  14.8 3.0 %collective-permute-start.5 = (f32[88,128]{1,0:T(8,128)S(1)}, f32[88,128]{1,0:T(8,128)S(1)}, u32[]{:S(2)}, u32[]{:S(2)}) collective-permute-start(f32[88,128]{1,0:T(8,128)S(1)} %get-tuple-element.28), channel_id=1, source_target_pairs={{0,0},{1,2},{2,1},{3,3},{4,4},{5,6},{6,5},{7,7},{8,8},{9,10},{10,9... | collective-permute-start | bytes 135176 | tf_op jit(solution)/shard_map/ppermute | solution.py:427
  17.8 1.3 %collective-permute-done.4.cross_a = f32[88,128]{1,0:T(8,128)S(1)} collective-permute-done((f32[88,128]{1,0:T(8,128)S(1)}, f32[88,128]{1,0:T(8,128)S(1)}, u32[]{:S(2)}, u32[]{:S(2)}) %collective-permute-start.4) | collective-permute-done | bytes 45088 | tf_op jit(solution)/shard_map/ppermute | solution.py:427
  19.1 1.9 %collective-permute-done.5.cross_b = f32[88,128]{1,0:T(8,128)S(1)} collective-permute-done((f32[88,128]{1,0:T(8,128)S(1)}, f32[88,128]{1,0:T(8,128)S(1)}, u32[]{:S(2)}, u32[]{:S(2)}) %collective-permute-start.5) | collective-permute-done | bytes 45088 | tf_op jit(solution)/shard_map/ppermute | solution.py:427
  21.0 0.0 collective-permute-done.2.loop_a
  21.0 0.0 collective-permute-done.3.loop_b
  21.0 0.9 %second_step_edge_planes.1 = (f32[41,10,48,128]{3,2,1,0:T(8,128)S(1)}, f32[41,10,48,128]{3,2,1,0:T(8,128)S(1)}, f32[11,32,128]{2,1,0:T(8,128)S(1)}, f32[11,32,128]{2,1,0:T(8,128)S(1)}) custom-call(f32[41,10,48,128]{3,2,1,0:T(8,128)S(1)} %get-tuple-element.22.state.state_in, ...), custom_call_target="tpu_custom_call", output_to_operand_aliasing={{0}: (0, {}), {1}: (1, {})} | custom-call | flops 4608000 | bytes 3022848 | tf_op jit(solution)/shard_map/second_step_edge_planes/pallas_call | solution.py:452
  21.8 1.6 %collective-permute-start.6 = (f32[11,32,128]{2,1,0:T(8,128)S(1)}, f32[11,32,128]{2,1,0:T(8,128)S(1)}, u32[]{:S(2)}, u32[]{:S(2)}) collective-permute-start(f32[11,32,128]{2,1,0:T(8,128)S(1)} %get-tuple-element.32), channel_id=1, source_target_pairs={{0,28},{4,0},{8,4},{12,8},{16,12},{20,16},{24,20},{28,24},{1,29},{... | collective-permute-start | bytes 540680 | tf_op jit(solution)/shard_map/ppermute | solution.py:416
  23.5 0.0 collective-permute-start.7
  23.5 2.5 %write_all_planes.1 = (f32[27,8,32,128]{3,2,1,0:T(8,128)}, f32[14,8,32,128]{3,2,1,0:T(8,128)}) custom-call(f32[41,10,48,128]{3,2,1,0:T(8,128)S(1)} %get-tuple-element.29.out), custom_call_target="tpu_custom_call" | custom-call | bytes 10747904 | tf_op jit(solution)/shard_map/write_all_planes/pallas_call | solution.py:452
  26.0 2.0 %collective-permute-done.6.got_a = f32[11,32,128]{2,1,0:T(8,128)S(1)} collective-permute-done((f32[11,32,128]{2,1,0:T(8,128)S(1)}, f32[11,32,128]{2,1,0:T(8,128)S(1)}, u32[]{:S(2)}, u32[]{:S(2)}) %collective-permute-start.6) | collective-permute-done | bytes 180256 | tf_op jit(solution)/shard_map/ppermute | solution.py:416
  28.0 2.0 %collective-permute-done.7.got_b = f32[11,32,128]{2,1,0:T(8,128)S(1)} collective-permute-done((f32[11,32,128]{2,1,0:T(8,128)S(1)}, f32[11,32,128]{2,1,0:T(8,128)S(1)}, u32[]{:S(2)}, u32[]{:S(2)}) %collective-permute-start.7) | collective-permute-done | bytes 180256 | tf_op jit(solution)/shard_map/ppermute | solution.py:416
  30.0 0.9 %write_edge_planes.1 = (f32[27,8,32,128]{3,2,1,0:T(8,128)}, f32[14,8,32,128]{3,2,1,0:T(8,128)}) custom-call(f32[27,8,32,128]{3,2,1,0:T(8,128)} %get-tuple-element.30.pops_in, f32[14,8,32,128]{3,2,1,0:T(8,128)} %get-tuple-element.31.scal_in, f32[11,32,128]{2,1,0:T(8,128)S(1)} %collective-permute-done.6.got_a, ...), custom_call_target="tpu_custom_call", output_to_operand_aliasing={{0}: (0, {}), {1}: (1, {})} | custom-call | bytes 720896 | tf_op jit(solution)/shard_map/write_edge_planes/pallas_call | solution.py:452
Async XLA Ops:
  4.2 6.2 %collective-permute-start = (f32[152,128]{1,0:T(8,128)S(1)}, f32[152,128]{1,0:T(8,128)S(1)}, u32[]{:S(2)}, u32[]{:S(2)}) collective-permute-start(f32[152,128]{1,0:T(8,128)S(1)} %get-tuple-element.20), channel_id=1, source_target_pairs={{0,1},{1,0},{2,3},{3,2},{4,5},{5,4},{6,7},{7,6},{8,9},{9,8},{10,11... | collective-permute-start | bytes 233480 | tf_op jit(solution)/shard_map/ppermute | solution.py:427
  5.8 6.3 %collective-permute-start.1 = (f32[152,128]{1,0:T(8,128)S(1)}, f32[152,128]{1,0:T(8,128)S(1)}, u32[]{:S(2)}, u32[]{:S(2)}) collective-permute-start(f32[152,128]{1,0:T(8,128)S(1)} %get-tuple-element.21), channel_id=1, source_target_pairs={{0,0},{1,2},{2,1},{3,3},{4,4},{5,6},{6,5},{7,7},{8,8},{9,10},{10,9... | collective-permute-start | bytes 233480 | tf_op jit(solution)/shard_map/ppermute | solution.py:427
  12.2 8.7 %collective-permute-start.2 = (f32[376,128]{1,0:T(8,128)S(1)}, f32[376,128]{1,0:T(8,128)S(1)}, u32[]{:S(2)}, u32[]{:S(2)}) collective-permute-start(f32[376,128]{1,0:T(8,128)S(1)} %get-tuple-element.25), channel_id=1, source_target_pairs={{0,28},{4,0},{8,4},{12,8},{16,12},{20,16},{24,20},{28,24},{1,29},{... | collective-permute-start | bytes 577544 | tf_op jit(solution)/shard_map/ppermute | solution.py:416
  12.7 8.2 %collective-permute-start.3 = (f32[376,128]{1,0:T(8,128)S(1)}, f32[376,128]{1,0:T(8,128)S(1)}, u32[]{:S(2)}, u32[]{:S(2)}) collective-permute-start(f32[376,128]{1,0:T(8,128)S(1)} %get-tuple-element.26), channel_id=1, source_target_pairs={{0,4},{4,8},{8,12},{12,16},{16,20},{20,24},{24,28},{28,0},{1,5},{5... | collective-permute-start | bytes 577544 | tf_op jit(solution)/shard_map/ppermute | solution.py:416
  14.7 4.4 %collective-permute-start.4 = (f32[88,128]{1,0:T(8,128)S(1)}, f32[88,128]{1,0:T(8,128)S(1)}, u32[]{:S(2)}, u32[]{:S(2)}) collective-permute-start(f32[88,128]{1,0:T(8,128)S(1)} %get-tuple-element.27), channel_id=1, source_target_pairs={{0,1},{1,0},{2,3},{3,2},{4,5},{5,4},{6,7},{7,6},{8,9},{9,8},{10,11... | collective-permute-start | bytes 135176 | tf_op jit(solution)/shard_map/ppermute | solution.py:427
  14.8 6.2 %collective-permute-start.5 = (f32[88,128]{1,0:T(8,128)S(1)}, f32[88,128]{1,0:T(8,128)S(1)}, u32[]{:S(2)}, u32[]{:S(2)}) collective-permute-start(f32[88,128]{1,0:T(8,128)S(1)} %get-tuple-element.28), channel_id=1, source_target_pairs={{0,0},{1,2},{2,1},{3,3},{4,4},{5,6},{6,5},{7,7},{8,8},{9,10},{10,9... | collective-permute-start | bytes 135176 | tf_op jit(solution)/shard_map/ppermute | solution.py:427
  21.8 6.2 %collective-permute-start.6 = (f32[11,32,128]{2,1,0:T(8,128)S(1)}, f32[11,32,128]{2,1,0:T(8,128)S(1)}, u32[]{:S(2)}, u32[]{:S(2)}) collective-permute-start(f32[11,32,128]{2,1,0:T(8,128)S(1)} %get-tuple-element.32), channel_id=1, source_target_pairs={{0,28},{4,0},{8,4},{12,8},{16,12},{20,16},{24,20},{28,24},{1,29},{... | collective-permute-start | bytes 540680 | tf_op jit(solution)/shard_map/ppermute | solution.py:416
  23.5 6.5 %collective-permute-start.7 = (f32[11,32,128]{2,1,0:T(8,128)S(1)}, f32[11,32,128]{2,1,0:T(8,128)S(1)}, u32[]{:S(2)}, u32[]{:S(2)}) collective-permute-start(f32[11,32,128]{2,1,0:T(8,128)S(1)} %get-tuple-element.33), channel_id=1, source_target_pairs={{0,4},{4,8},{8,12},{12,16},{16,20},{20,24},{24,28},{28,0},{1,5},{5... | collective-permute-start | bytes 540680 | tf_op jit(solution)/shard_map/ppermute | solution.py:416

commit v7 on v6

--- a/solution.py
+++ b/solution.py
@@ -28,6 +28,7 @@
 Y_SETS = {b: [i for i, d in enumerate(DIRS) if d[1] == b] for b in (-1, 1)}
 SIDE_SETS = {b: [i for i, d in enumerate(DIRS) if d[1] in (0, b)] for b in (-1, 1)}
 SIDES = (-1, 1)
+SWAPS = (1, 0)
 
 
 def collide(load, flags, put):
@@ -285,8 +286,8 @@
     for copy in copies(size_x):
         copy.wait()
     collide_raw(raw, (size_x, 0), kinds, state, size_x - 1, size_y - SUB)
-    by_swap("cross", 0, lambda side: send_first_cross(state, kinds, side, sent_a))
-    by_swap("cross", 1, lambda side: send_first_cross(state, kinds, side, sent_b))
+    for swap, msg in zip(SWAPS, (sent_a, sent_b)):
+        by_swap("cross", swap, lambda side: send_first_cross(state, kinds, side, msg))
 
 
 def middle_kernel(pops, scal, kinds, state_in, state, raw, sems):
@@ -313,7 +314,7 @@
 
 def turn_kernel(state_in, got_a, got_b, state, halo_kinds, sent_a, sent_b):
     halo_kinds[...] = jnp.zeros(halo_kinds.shape, jnp.float32)
-    for swap, got in enumerate((got_a, got_b)):
+    for swap, got in zip(SWAPS, (got_a, got_b)):
         partner = has_partner("cross", swap)
         by_swap("cross", swap, lambda side: take_first_cross(state, halo_kinds, -side, got, partner))
     send_first_loop(state, (sent_a, sent_b))
@@ -333,7 +334,7 @@
         for k, i in enumerate(Y_SETS[b]):
             msg[k * SUB : k * SUB + size_x - 2, :] = flat[i, lines(DIRS[i][0] + 1, y_out, rows, size_x - 2), :]
 
-    for swap, msg in enumerate((sent_a, sent_b)):
+    for swap, msg in zip(SWAPS, (sent_a, sent_b)):
         by_swap("cross", swap, lambda side: send(side, msg))
 
 
@@ -368,7 +369,7 @@
             got = jnp.where(partner, msg[k * SUB : k * SUB + size_x - 2, :], 0.0)
             flat_out[i, lines(DIRS[i][0] + 1, y_in, rows, size_x - 2), :] = got
 
-    for swap, msg in enumerate((cross_a, cross_b)):
+    for swap, msg in zip(SWAPS, (cross_a, cross_b)):
         partner = has_partner("cross", swap)
         by_swap("cross", swap, lambda side: take(-side, msg, partner))
     for a, msg in zip(SIDES, (sent_a, sent_b)):
@@ -419,11 +420,10 @@
 
 def swap_along(axis, messages):
     count, received = lax.axis_size(axis), []
-    for swap, cells in enumerate(messages):
+    for swap, cells in zip(SWAPS, messages):
         pairs = []
-        for i in range(count):
-            j = i + 1 if i % 2 == swap else i - 1
-            pairs.append((i, j if 0 <= j < count else i))
+        for i in range(swap, count - 1, 2):
+            pairs += [(i, i + 1), (i + 1, i)]
         received.append(lax.ppermute(cells, axis, pairs))
     return received
 

time: 31.1 us -> 32.6 us (1.048)
  the two profiles are of different devices: /device:TPU:16 before, /device:TPU:0 now
where the time goes in v7:
time: 32.6 us; the launch traced here: 32.4 us
  starting transfers between devices  12.9 us (40%)
  Pallas kernels  12.5 us (38%)
  waiting for transfers between devices  6.33 us (19%)
  between operations  0.71 us (2%)
    pallas_call x7, Pallas kernels, call(): pl.pallas_call(kernel, out_shape=results, in_specs=specs, out_specs=[hbm...  12.5 us
    ppermute x4, starting transfers between devices, swap_along(): received.append(lax.ppermute(cells, axis, pairs))  9.9 us
    ppermute x4, waiting for transfers between devices, shift_along(): received.append(lax.ppermute(cells, axis, pairs))  4.01 us
    ppermute x4, starting transfers between devices, shift_along(): received.append(lax.ppermute(cells, axis, pairs))  3.02 us
    ppermute x4, waiting for transfers between devices, swap_along(): received.append(lax.ppermute(cells, axis, pairs))  2.32 us
  transfers between devices with their start and end apart: 8, of which 3 were waited for; matrix products, arithmetic and copies ran while one was open for 0% of the time, Pallas kernels for 22%

profile of v7, /device:TPU:0, one launch (start us, length us, event | category | flops | bytes accessed | tf_op | source)
XLA Modules:
  0.0 32.4 jit_solution(5429885135813161508)
XLA Ops:
  0.6 3.6 %first_step_side_rows.1 = (f32[41,10,48,128]{3,2,1,0:T(8,128)S(1)}, s32[8,32,128]{2,1,0:T(8,128)S(1)}, f32[152,128]{1,0:T(8,128)S(1)}, f32[152,128]{1,0:T(8,128)S(1)}) custom-call(f32[27,8,32,128]{3,2,1,0:T(8,128)} %pops.3, f32[14,8,32,128]{3,2,1,0:T(8,128)} %scal.3, s32[8,32,128]{2,1,0:T(8,128)} %flags.1), custom_call_target="tpu_custom_call" | custom-call | flops 8192000 | bytes 5373952 | tf_op jit(solution)/shard_map/first_step_side_rows/pallas_call | solution.py:452
  4.2 0.7 %collective-permute-start = (f32[152,128]{1,0:T(8,128)S(1)}, f32[152,128]{1,0:T(8,128)S(1)}, u32[]{:S(2)}, u32[]{:S(2)}) collective-permute-start(f32[152,128]{1,0:T(8,128)S(1)} %get-tuple-element.20), channel_id=1, source_target_pairs={{1,2},{2,1},{5,6},{6,5},{9,10},{10,9},{13,14},{14,13},{17,18},{18,... | collective-permute-start | bytes 233480 | tf_op jit(solution)/shard_map/ppermute | solution.py:427
  4.9 5.9 %collective-permute-start.1 = (f32[152,128]{1,0:T(8,128)S(1)}, f32[152,128]{1,0:T(8,128)S(1)}, u32[]{:S(2)}, u32[]{:S(2)}) collective-permute-start(f32[152,128]{1,0:T(8,128)S(1)} %get-tuple-element.21), channel_id=1, source_target_pairs={{0,1},{1,0},{2,3},{3,2},{4,5},{5,4},{6,7},{7,6},{8,9},{9,8},{10,11... | collective-permute-start | bytes 233480 | tf_op jit(solution)/shard_map/ppermute | solution.py:427
  10.8 2.6 %first_step_middle_rows.1.state_in = f32[41,10,48,128]{3,2,1,0:T(8,128)S(1)} custom-call(f32[27,8,32,128]{3,2,1,0:T(8,128)} %pops.3, f32[14,8,32,128]{3,2,1,0:T(8,128)} %scal.3, s32[8,32,128]{2,1,0:T(8,128)S(1)} %get-tuple-element.18.kinds, f32[41,10,48,128]{3,2,1,0:T(8,128)S(1)} %get-tuple-element.19.state_in), custom_call_target="tpu_custom_call", output_to_operand_aliasing={{}: (3, {})} | custom-call | flops 8192000 | bytes 5373952 | tf_op jit(solution)/shard_map/first_step_middle_rows/pallas_call | solution.py:452
  13.4 0.0 collective-permute-done.got_a
  13.4 0.0 collective-permute-done.1.got_b
  13.4 0.1 cross_to_loop.1
  13.6 1.4 %collective-permute-start.2 = (f32[376,128]{1,0:T(8,128)S(1)}, f32[376,128]{1,0:T(8,128)S(1)}, u32[]{:S(2)}, u32[]{:S(2)}) collective-permute-start(f32[376,128]{1,0:T(8,128)S(1)} %get-tuple-element.25), channel_id=1, source_target_pairs={{0,28},{4,0},{8,4},{12,8},{16,12},{20,16},{24,20},{28,24},{1,29},{... | collective-permute-start | bytes 577544 | tf_op jit(solution)/shard_map/ppermute | solution.py:417
  15.0 0.0 collective-permute-start.3
  15.0 1.9 %second_step_inner_planes.1 = (f32[41,10,48,128]{3,2,1,0:T(8,128)S(1)}, f32[88,128]{1,0:T(8,128)S(1)}, f32[88,128]{1,0:T(8,128)S(1)}) custom-call(f32[41,10,48,128]{3,2,1,0:T(8,128)S(1)} %get-tuple-element.22.state.state_in, s32[8,32,128]{2,1,0:T(8,128)S(1)} %get-tuple-element.18.kinds), custom_call_target="tpu_custom_call" | custom-call | flops 12288000 | bytes 8060928 | tf_op jit(solution)/shard_map/second_step_inner_planes/pallas_call | solution.py:452
  16.8 0.7 %collective-permute-start.4 = (f32[88,128]{1,0:T(8,128)S(1)}, f32[88,128]{1,0:T(8,128)S(1)}, u32[]{:S(2)}, u32[]{:S(2)}) collective-permute-start(f32[88,128]{1,0:T(8,128)S(1)} %get-tuple-element.27), channel_id=1, source_target_pairs={{1,2},{2,1},{5,6},{6,5},{9,10},{10,9},{13,14},{14,13},{17,18},{18,... | collective-permute-start | bytes 135176 | tf_op jit(solution)/shard_map/ppermute | solution.py:427
  17.5 2.7 %collective-permute-start.5 = (f32[88,128]{1,0:T(8,128)S(1)}, f32[88,128]{1,0:T(8,128)S(1)}, u32[]{:S(2)}, u32[]{:S(2)}) collective-permute-start(f32[88,128]{1,0:T(8,128)S(1)} %get-tuple-element.28), channel_id=1, source_target_pairs={{0,1},{1,0},{2,3},{3,2},{4,5},{5,4},{6,7},{7,6},{8,9},{9,8},{10,11... | collective-permute-start | bytes 135176 | tf_op jit(solution)/shard_map/ppermute | solution.py:427
  20.2 0.0 collective-permute-done.4.cross_a
  20.2 2.3 %collective-permute-done.5.cross_b = f32[88,128]{1,0:T(8,128)S(1)} collective-permute-done((f32[88,128]{1,0:T(8,128)S(1)}, f32[88,128]{1,0:T(8,128)S(1)}, u32[]{:S(2)}, u32[]{:S(2)}) %collective-permute-start.5) | collective-permute-done | bytes 45088 | tf_op jit(solution)/shard_map/ppermute | solution.py:427
  22.5 0.0 collective-permute-done.2.loop_a
  22.5 0.0 collective-permute-done.3.loop_b
  22.5 0.9 %second_step_edge_planes.1 = (f32[41,10,48,128]{3,2,1,0:T(8,128)S(1)}, f32[41,10,48,128]{3,2,1,0:T(8,128)S(1)}, f32[11,32,128]{2,1,0:T(8,128)S(1)}, f32[11,32,128]{2,1,0:T(8,128)S(1)}) custom-call(f32[41,10,48,128]{3,2,1,0:T(8,128)S(1)} %get-tuple-element.22.state.state_in, ...), custom_call_target="tpu_custom_call", output_to_operand_aliasing={{0}: (0, {}), {1}: (1, {})} | custom-call | flops 4608000 | bytes 3022848 | tf_op jit(solution)/shard_map/second_step_edge_planes/pallas_call | solution.py:452
  23.4 1.6 %collective-permute-start.6 = (f32[11,32,128]{2,1,0:T(8,128)S(1)}, f32[11,32,128]{2,1,0:T(8,128)S(1)}, u32[]{:S(2)}, u32[]{:S(2)}) collective-permute-start(f32[11,32,128]{2,1,0:T(8,128)S(1)} %get-tuple-element.32), channel_id=1, source_target_pairs={{0,28},{4,0},{8,4},{12,8},{16,12},{20,16},{24,20},{28,24},{1,29},{... | collective-permute-start | bytes 540680 | tf_op jit(solution)/shard_map/ppermute | solution.py:417
  25.0 0.0 collective-permute-start.7
  25.0 2.5 %write_all_planes.1 = (f32[27,8,32,128]{3,2,1,0:T(8,128)}, f32[14,8,32,128]{3,2,1,0:T(8,128)}) custom-call(f32[41,10,48,128]{3,2,1,0:T(8,128)S(1)} %get-tuple-element.29.out), custom_call_target="tpu_custom_call" | custom-call | bytes 10747904 | tf_op jit(solution)/shard_map/write_all_planes/pallas_call | solution.py:452
  27.5 2.0 %collective-permute-done.6.got_a = f32[11,32,128]{2,1,0:T(8,128)S(1)} collective-permute-done((f32[11,32,128]{2,1,0:T(8,128)S(1)}, f32[11,32,128]{2,1,0:T(8,128)S(1)}, u32[]{:S(2)}, u32[]{:S(2)}) %collective-permute-start.6) | collective-permute-done | bytes 180256 | tf_op jit(solution)/shard_map/ppermute | solution.py:417
  29.5 2.0 %collective-permute-done.7.got_b = f32[11,32,128]{2,1,0:T(8,128)S(1)} collective-permute-done((f32[11,32,128]{2,1,0:T(8,128)S(1)}, f32[11,32,128]{2,1,0:T(8,128)S(1)}, u32[]{:S(2)}, u32[]{:S(2)}) %collective-permute-start.7) | collective-permute-done | bytes 180256 | tf_op jit(solution)/shard_map/ppermute | solution.py:417
  31.5 0.9 %write_edge_planes.1 = (f32[27,8,32,128]{3,2,1,0:T(8,128)}, f32[14,8,32,128]{3,2,1,0:T(8,128)}) custom-call(f32[27,8,32,128]{3,2,1,0:T(8,128)} %get-tuple-element.30.pops_in, f32[14,8,32,128]{3,2,1,0:T(8,128)} %get-tuple-element.31.scal_in, f32[11,32,128]{2,1,0:T(8,128)S(1)} %collective-permute-done.6.got_a, ...), custom_call_target="tpu_custom_call", output_to_operand_aliasing={{0}: (0, {}), {1}: (1, {})} | custom-call | bytes 720896 | tf_op jit(solution)/shard_map/write_edge_planes/pallas_call | solution.py:452
Async XLA Ops:
  4.2 9.2 %collective-permute-start = (f32[152,128]{1,0:T(8,128)S(1)}, f32[152,128]{1,0:T(8,128)S(1)}, u32[]{:S(2)}, u32[]{:S(2)}) collective-permute-start(f32[152,128]{1,0:T(8,128)S(1)} %get-tuple-element.20), channel_id=1, source_target_pairs={{1,2},{2,1},{5,6},{6,5},{9,10},{10,9},{13,14},{14,13},{17,18},{18,... | collective-permute-start | bytes 233480 | tf_op jit(solution)/shard_map/ppermute | solution.py:427
  4.9 8.5 %collective-permute-start.1 = (f32[152,128]{1,0:T(8,128)S(1)}, f32[152,128]{1,0:T(8,128)S(1)}, u32[]{:S(2)}, u32[]{:S(2)}) collective-permute-start(f32[152,128]{1,0:T(8,128)S(1)} %get-tuple-element.21), channel_id=1, source_target_pairs={{0,1},{1,0},{2,3},{3,2},{4,5},{5,4},{6,7},{7,6},{8,9},{9,8},{10,11... | collective-permute-start | bytes 233480 | tf_op jit(solution)/shard_map/ppermute | solution.py:427
  13.6 8.9 %collective-permute-start.2 = (f32[376,128]{1,0:T(8,128)S(1)}, f32[376,128]{1,0:T(8,128)S(1)}, u32[]{:S(2)}, u32[]{:S(2)}) collective-permute-start(f32[376,128]{1,0:T(8,128)S(1)} %get-tuple-element.25), channel_id=1, source_target_pairs={{0,28},{4,0},{8,4},{12,8},{16,12},{20,16},{24,20},{28,24},{1,29},{... | collective-permute-start | bytes 577544 | tf_op jit(solution)/shard_map/ppermute | solution.py:417
  15.0 7.5 %collective-permute-start.3 = (f32[376,128]{1,0:T(8,128)S(1)}, f32[376,128]{1,0:T(8,128)S(1)}, u32[]{:S(2)}, u32[]{:S(2)}) collective-permute-start(f32[376,128]{1,0:T(8,128)S(1)} %get-tuple-element.26), channel_id=1, source_target_pairs={{0,4},{4,8},{8,12},{12,16},{16,20},{20,24},{24,28},{28,0},{1,5},{5... | collective-permute-start | bytes 577544 | tf_op jit(solution)/shard_map/ppermute | solution.py:417
  16.8 3.3 %collective-permute-start.4 = (f32[88,128]{1,0:T(8,128)S(1)}, f32[88,128]{1,0:T(8,128)S(1)}, u32[]{:S(2)}, u32[]{:S(2)}) collective-permute-start(f32[88,128]{1,0:T(8,128)S(1)} %get-tuple-element.27), channel_id=1, source_target_pairs={{1,2},{2,1},{5,6},{6,5},{9,10},{10,9},{13,14},{14,13},{17,18},{18,... | collective-permute-start | bytes 135176 | tf_op jit(solution)/shard_map/ppermute | solution.py:427
  17.5 5.0 %collective-permute-start.5 = (f32[88,128]{1,0:T(8,128)S(1)}, f32[88,128]{1,0:T(8,128)S(1)}, u32[]{:S(2)}, u32[]{:S(2)}) collective-permute-start(f32[88,128]{1,0:T(8,128)S(1)} %get-tuple-element.28), channel_id=1, source_target_pairs={{0,1},{1,0},{2,3},{3,2},{4,5},{5,4},{6,7},{7,6},{8,9},{9,8},{10,11... | collective-permute-start | bytes 135176 | tf_op jit(solution)/shard_map/ppermute | solution.py:427
  23.4 6.2 %collective-permute-start.6 = (f32[11,32,128]{2,1,0:T(8,128)S(1)}, f32[11,32,128]{2,1,0:T(8,128)S(1)}, u32[]{:S(2)}, u32[]{:S(2)}) collective-permute-start(f32[11,32,128]{2,1,0:T(8,128)S(1)} %get-tuple-element.32), channel_id=1, source_target_pairs={{0,28},{4,0},{8,4},{12,8},{16,12},{20,16},{24,20},{28,24},{1,29},{... | collective-permute-start | bytes 540680 | tf_op jit(solution)/shard_map/ppermute | solution.py:417
  25.0 6.5 %collective-permute-start.7 = (f32[11,32,128]{2,1,0:T(8,128)S(1)}, f32[11,32,128]{2,1,0:T(8,128)S(1)}, u32[]{:S(2)}, u32[]{:S(2)}) collective-permute-start(f32[11,32,128]{2,1,0:T(8,128)S(1)} %get-tuple-element.33), channel_id=1, source_target_pairs={{0,4},{4,8},{8,12},{12,16},{16,20},{20,24},{24,28},{28,0},{1,5},{5... | collective-permute-start | bytes 540680 | tf_op jit(solution)/shard_map/ppermute | solution.py:417

commit v8 on v7

--- a/solution.py
+++ b/solution.py
@@ -28,7 +28,8 @@
 Y_SETS = {b: [i for i, d in enumerate(DIRS) if d[1] == b] for b in (-1, 1)}
 SIDE_SETS = {b: [i for i, d in enumerate(DIRS) if d[1] in (0, b)] for b in (-1, 1)}
 SIDES = (-1, 1)
-SWAPS = (1, 0)
+CROSS_SWAPS = (0, 1)
+LOOP_SWAPS = (1, 0)
 
 
 def collide(load, flags, put):
@@ -160,12 +161,6 @@
     pl.when(jnp.logical_not(odd))(lambda: fill(second))
 
 
-def has_partner(axis, swap):
-    index, count = lax.axis_index(axis), lax.axis_size(axis)
-    first = index - lax.rem(index + swap, 2)
-    return (first >= 0) & (first + 1 < count)
-
-
 def sizes_of(state):
     return state.shape[1] - 2, state.shape[2] - 2 * PAD
 
@@ -192,19 +187,19 @@
         msg[last + s : last + s + 1, :] = (line + 1).astype(jnp.float32)
 
 
-def take_first_cross(state, halo_kinds, b, msg, partner):
+def take_first_cross(state, halo_kinds, b, msg):
     size_x, size_y = sizes_of(state)
     rows, flat = state.shape[2], flat_of(state)
     ran, _ = first_cross_rows(size_x)
     y_in, y_halo = (0, -1) if b > 0 else (size_y - 1, size_y)
     for k, i in enumerate(Y_SETS[b]):
-        flat[i, lines(DIRS[i][0], y_in, rows, size_x), :] = jnp.where(partner, msg[k * size_x : (k + 1) * size_x, :], 0.0)
+        flat[i, lines(DIRS[i][0], y_in, rows, size_x), :] = msg[k * size_x : (k + 1) * size_x, :]
     for k, i in enumerate(SIDE_SETS[b]):
         x, step = side_span(i, size_x)
-        flat[i, lines(x, y_halo, rows, 2, step), :] = jnp.where(partner, msg[ran + 2 * k : ran + 2 * k + 2, :], 0.0)
+        flat[i, lines(x, y_halo, rows, 2, step), :] = msg[ran + 2 * k : ran + 2 * k + 2, :]
     last = ran + 2 * len(SIDE_SETS[b])
     first = 0 if b > 0 else 2
-    halo_kinds[first : first + 2, :] = jnp.where(partner, msg[last : last + 2, :], 0.0)
+    halo_kinds[first : first + 2, :] = msg[last : last + 2, :]
 
 
 def first_loop_rows(size_y):
@@ -213,30 +208,28 @@
     return main, -(-total // SUB) * SUB
 
 
-def send_first_loop(state, sent):
+def send_first_loop(state, a, msg):
     size_x, size_y = sizes_of(state)
     main, _ = first_loop_rows(size_y)
-    for a, msg in zip(SIDES, sent):
-        x = -1 if a < 0 else size_x
-        for k, i in enumerate(X_SETS[a]):
-            for y in range(0, size_y, SUB):
-                msg[k * size_y + y : k * size_y + y + SUB, :] = state[i, slot(x), y + PAD : y + PAD + SUB, :]
-            for s, y in enumerate((-1, size_y)):
-                row = main + 2 * k + s
-                msg[row : row + 1, :] = state[i, slot(x), y + PAD : y + PAD + 1, :]
-
-
-def take_first_loop(state, received):
+    x = -1 if a < 0 else size_x
+    for k, i in enumerate(X_SETS[a]):
+        for y in range(0, size_y, SUB):
+            msg[k * size_y + y : k * size_y + y + SUB, :] = state[i, slot(x), y + PAD : y + PAD + SUB, :]
+        for s, y in enumerate((-1, size_y)):
+            row = main + 2 * k + s
+            msg[row : row + 1, :] = state[i, slot(x), y + PAD : y + PAD + 1, :]
+
+
+def take_first_loop(state, a, msg):
     size_x, size_y = sizes_of(state)
     main, _ = first_loop_rows(size_y)
-    for a, msg in zip(SIDES, received):
-        x = 0 if a > 0 else size_x - 1
-        for k, i in enumerate(X_SETS[a]):
-            for y in range(0, size_y, SUB):
-                state[i, slot(x), y + PAD : y + PAD + SUB, :] = msg[k * size_y + y : k * size_y + y + SUB, :]
-            for s, y in enumerate((-1, size_y)):
-                row = main + 2 * k + s
-                state[i, slot(x), y + PAD : y + PAD + 1, :] = msg[row : row + 1, :]
+    x = 0 if a > 0 else size_x - 1
+    for k, i in enumerate(X_SETS[a]):
+        for y in range(0, size_y, SUB):
+            state[i, slot(x), y + PAD : y + PAD + SUB, :] = msg[k * size_y + y : k * size_y + y + SUB, :]
+        for s, y in enumerate((-1, size_y)):
+            row = main + 2 * k + s
+            state[i, slot(x), y + PAD : y + PAD + 1, :] = msg[row : row + 1, :]
 
 
 def load_tile(state, x, y):
@@ -286,7 +279,7 @@
     for copy in copies(size_x):
         copy.wait()
     collide_raw(raw, (size_x, 0), kinds, state, size_x - 1, size_y - SUB)
-    for swap, msg in zip(SWAPS, (sent_a, sent_b)):
+    for swap, msg in zip(CROSS_SWAPS, (sent_a, sent_b)):
         by_swap("cross", swap, lambda side: send_first_cross(state, kinds, side, msg))
 
 
@@ -314,10 +307,10 @@
 
 def turn_kernel(state_in, got_a, got_b, state, halo_kinds, sent_a, sent_b):
     halo_kinds[...] = jnp.zeros(halo_kinds.shape, jnp.float32)
-    for swap, got in zip(SWAPS, (got_a, got_b)):
-        partner = has_partner("cross", swap)
-        by_swap("cross", swap, lambda side: take_first_cross(state, halo_kinds, -side, got, partner))
-    send_first_loop(state, (sent_a, sent_b))
+    for swap, got in zip(CROSS_SWAPS, (got_a, got_b)):
+        by_swap("cross", swap, lambda side: take_first_cross(state, halo_kinds, -side, got))
+    for swap, msg in zip(LOOP_SWAPS, (sent_a, sent_b)):
+        by_swap("loop", swap, lambda side: send_first_loop(state, side, msg))
 
 
 def inner_kernel(state, kinds, out, sent_a, sent_b):
@@ -334,14 +327,15 @@
         for k, i in enumerate(Y_SETS[b]):
             msg[k * SUB : k * SUB + size_x - 2, :] = flat[i, lines(DIRS[i][0] + 1, y_out, rows, size_x - 2), :]
 
-    for swap, msg in zip(SWAPS, (sent_a, sent_b)):
+    for swap, msg in zip(CROSS_SWAPS, (sent_a, sent_b)):
         by_swap("cross", swap, lambda side: send(side, msg))
 
 
 def edge_kernel(state_in, out_in, kinds, halo_kinds, loop_a, loop_b, cross_a, cross_b, state, out, sent_a, sent_b, halo):
     size_x, size_y = sizes_of(state)
     rows, flat, flat_out = state.shape[2], flat_of(state), flat_of(out)
-    take_first_loop(state, (loop_a, loop_b))
+    for swap, msg in zip(LOOP_SWAPS, (loop_a, loop_b)):
+        by_swap("loop", swap, lambda side: take_first_loop(state, -side, msg))
     for i in range(NQ):
         halo[i, 0:2, :] = flat[i, lines(0, -1, rows, 2, size_x - 1), :]
         halo[i, 2:4, :] = flat[i, lines(0, size_y, rows, 2, size_x - 1), :]
@@ -363,20 +357,23 @@
 
     collide(lambda i: halo[i], code - 1, put)
 
-    def take(b, msg, partner):
+    def take(b, msg):
         y_in = 0 if b > 0 else size_y - 1
         for k, i in enumerate(Y_SETS[b]):
-            got = jnp.where(partner, msg[k * SUB : k * SUB + size_x - 2, :], 0.0)
+            got = msg[k * SUB : k * SUB + size_x - 2, :]
             flat_out[i, lines(DIRS[i][0] + 1, y_in, rows, size_x - 2), :] = got
 
-    for swap, msg in zip(SWAPS, (cross_a, cross_b)):
-        partner = has_partner("cross", swap)
-        by_swap("cross", swap, lambda side: take(-side, msg, partner))
-    for a, msg in zip(SIDES, (sent_a, sent_b)):
+    for swap, msg in zip(CROSS_SWAPS, (cross_a, cross_b)):
+        by_swap("cross", swap, lambda side: take(-side, msg))
+
+    def send(a, msg):
         x = -1 if a < 0 else size_x
         for k, i in enumerate(X_SETS[a]):
             for y in range(0, size_y, SUB):
                 msg[k, y : y + SUB, :] = out[i, slot(x), y + PAD : y + PAD + SUB, :]
+
+    for swap, msg in zip(LOOP_SWAPS, (sent_a, sent_b)):
+        by_swap("loop", swap, lambda side: send(side, msg))
 
 
 def write_kernel(out, pops, scal, sems):
@@ -394,36 +391,36 @@
 
 def last_kernel(pops_in, scal_in, got_a, got_b, pops, scal, sems):
     size_x = pops.shape[1]
-    copies = []
-    for a, msg in zip(SIDES, (got_a, got_b)):
+
+    def copies(a, msg, swap):
         x = 0 if a > 0 else size_x - 1
         flow = [i for i in X_SETS[a] if i < NF]
         spans = [(0, len(flow), pops, flow[0])]
         spans += [(k, 1, scal, i - NF) for k, i in enumerate(X_SETS[a]) if i >= NF]
-        for k, count, dst, first in spans:
-            here = msg.at[pl.ds(k, count)]
-            copies.append(pltpu.make_async_copy(here, dst.at[pl.ds(first, count), x], sems.at[len(copies)]))
-    for copy in copies:
-        copy.start()
-    for copy in copies:
-        copy.wait()
-
-
-def shift_along(axis, closed, messages):
-    count = lax.axis_size(axis)
-    received = []
-    for step, cells in zip(SIDES, messages):
-        pairs = [(i, (i + step) % count) for i in range(count) if closed or 0 <= i + step < count]
-        received.append(lax.ppermute(cells, axis, pairs))
-    return received
-
-
-def swap_along(axis, messages):
+        return [
+            pltpu.make_async_copy(msg.at[pl.ds(k, count)], dst.at[pl.ds(first, count), x], sems.at[swap, n])
+            for n, (k, count, dst, first) in enumerate(spans)
+        ]
+
+    def write(side):
+        started = []
+        for swap, msg in zip(LOOP_SWAPS, (got_a, got_b)):
+            started += copies(-side if swap == 0 else side, msg, swap)
+        for copy in started:
+            copy.start()
+        for copy in started:
+            copy.wait()
+
+    by_swap("loop", 0, write)
+
+
+def swap_along(axis, swaps, closed, messages):
     count, received = lax.axis_size(axis), []
-    for swap, cells in zip(SWAPS, messages):
+    for swap, cells in zip(swaps, messages):
         pairs = []
-        for i in range(swap, count - 1, 2):
-            pairs += [(i, i + 1), (i + 1, i)]
+        for i in range(swap, count if closed else count - 1, 2):
+            j = (i + 1) % count
+            pairs += [(i, j), (j, i)]
         received.append(lax.ppermute(cells, axis, pairs))
     return received
 
@@ -482,7 +479,7 @@
             pltpu.SemaphoreType.DMA,
         ],
     )
-    received = swap_along("cross", sent)
+    received = swap_along("cross", CROSS_SWAPS, False, sent)
     if tiles > 2:
         (state,) = call(
             middle_kernel,
@@ -504,7 +501,7 @@
         tiles=1,
         aliases={0: 0},
     )
-    from_loop = shift_along("loop", True, sent)
+    from_loop = swap_along("loop", LOOP_SWAPS, True, sent)
     out, *sent = call(
         inner_kernel,
         "second_step_inner_planes",
@@ -512,7 +509,7 @@
         [state_shape] + cross_2,
         tiles=(size_x - 2) * tiles,
     )
-    from_cross = swap_along("cross", sent)
+    from_cross = swap_along("cross", CROSS_SWAPS, False, sent)
     state, out, *sent = call(
         edge_kernel,
         "second_step_edge_planes",
@@ -522,7 +519,7 @@
         scratch=[pltpu.VMEM((NQ, SUB, size_z), f32)],
         aliases={0: 0, 1: 1},
     )
-    received = shift_along("loop", True, sent)
+    received = swap_along("loop", LOOP_SWAPS, True, sent)
     new_pops, new_scal = call(
         write_kernel,
         "write_all_planes",
@@ -537,7 +534,7 @@
         in_hbm(new_pops, new_scal) + on_chip(*received),
         [pops_shape, scal_shape],
         moved=16 * len(X_SETS[1]) * size_y * size_z,
-        scratch=[pltpu.SemaphoreType.DMA((2 * len(X_SETS[1]),))],
+        scratch=[pltpu.SemaphoreType.DMA((2, len(X_SETS[1])))],
         aliases={0: 0, 1: 1},
     )
     return new_pops, new_scal

time: 32.6 us -> 30.7 us (0.942)
  the two profiles are of different devices: /device:TPU:0 before, /device:TPU:16 now
where the time goes in v8:
time: 30.7 us; the launch traced here: 30.5 us
  Pallas kernels  12.5 us (41%)
  starting transfers between devices  9.15 us (30%)
  waiting for transfers between devices  8.18 us (27%)
  between operations  0.72 us (2%)
    pallas_call x7, Pallas kernels, call(): pl.pallas_call(kernel, out_shape=results, in_specs=specs, out_specs=[hbm...  12.5 us
    ppermute x8, starting transfers between devices, swap_along(): received.append(lax.ppermute(cells, axis, pairs))  9.15 us
    ppermute x8, waiting for transfers between devices, swap_along(): received.append(lax.ppermute(cells, axis, pairs))  8.18 us
  transfers between devices with their start and end apart: 8, of which 4 were waited for; matrix products, arithmetic and copies ran while one was open for 0% of the time, Pallas kernels for 23%

profile of v8, /device:TPU:16, one launch (start us, length us, event | category | flops | bytes accessed | tf_op | source)
XLA Modules:
  0.0 30.5 jit_solution(7688566079374882048)
XLA Ops:
  0.6 3.6 %first_step_side_rows.1 = (f32[41,10,48,128]{3,2,1,0:T(8,128)S(1)}, s32[8,32,128]{2,1,0:T(8,128)S(1)}, f32[152,128]{1,0:T(8,128)S(1)}, f32[152,128]{1,0:T(8,128)S(1)}) custom-call(f32[27,8,32,128]{3,2,1,0:T(8,128)} %pops.3, f32[14,8,32,128]{3,2,1,0:T(8,128)} %scal.3, s32[8,32,128]{2,1,0:T(8,128)} %flags.1), custom_call_target="tpu_custom_call" | custom-call | flops 8192000 | bytes 5373952 | tf_op jit(solution)/shard_map/first_step_side_rows/pallas_call | solution.py:449
  4.2 1.6 %collective-permute-start = (f32[152,128]{1,0:T(8,128)S(1)}, f32[152,128]{1,0:T(8,128)S(1)}, u32[]{:S(2)}, u32[]{:S(2)}) collective-permute-start(f32[152,128]{1,0:T(8,128)S(1)} %get-tuple-element.20), channel_id=1, source_target_pairs={{0,1},{1,0},{2,3},{3,2},{4,5},{5,4},{6,7},{7,6},{8,9},{9,8},{10,11... | collective-permute-start | bytes 233480 | tf_op jit(solution)/shard_map/ppermute | solution.py:424
  5.8 1.9 %collective-permute-start.1 = (f32[152,128]{1,0:T(8,128)S(1)}, f32[152,128]{1,0:T(8,128)S(1)}, u32[]{:S(2)}, u32[]{:S(2)}) collective-permute-start(f32[152,128]{1,0:T(8,128)S(1)} %get-tuple-element.21), channel_id=1, source_target_pairs={{1,2},{2,1},{5,6},{6,5},{9,10},{10,9},{13,14},{14,13},{17,18},{18,... | collective-permute-start | bytes 233480 | tf_op jit(solution)/shard_map/ppermute | solution.py:424
  7.8 2.6 %first_step_middle_rows.1.state_in = f32[41,10,48,128]{3,2,1,0:T(8,128)S(1)} custom-call(f32[27,8,32,128]{3,2,1,0:T(8,128)} %pops.3, f32[14,8,32,128]{3,2,1,0:T(8,128)} %scal.3, s32[8,32,128]{2,1,0:T(8,128)S(1)} %get-tuple-element.18.kinds, f32[41,10,48,128]{3,2,1,0:T(8,128)S(1)} %get-tuple-element.19.state_in), custom_call_target="tpu_custom_call", output_to_operand_aliasing={{}: (3, {})} | custom-call | flops 8192000 | bytes 5373952 | tf_op jit(solution)/shard_map/first_step_middle_rows/pallas_call | solution.py:449
  10.4 0.0 collective-permute-done.got_a
  10.4 1.7 %collective-permute-done.1.got_b = f32[152,128]{1,0:T(8,128)S(1)} collective-permute-done((f32[152,128]{1,0:T(8,128)S(1)}, f32[152,128]{1,0:T(8,128)S(1)}, u32[]{:S(2)}, u32[]{:S(2)}) %collective-permute-start.1) | collective-permute-done | bytes 77856 | tf_op jit(solution)/shard_map/ppermute | solution.py:424
  12.1 0.1 cross_to_loop.1
  12.3 0.5 %collective-permute-start.2 = (f32[376,128]{1,0:T(8,128)S(1)}, f32[376,128]{1,0:T(8,128)S(1)}, u32[]{:S(2)}, u32[]{:S(2)}) collective-permute-start(f32[376,128]{1,0:T(8,128)S(1)} %get-tuple-element.25), channel_id=1, source_target_pairs={{4,8},{8,4},{12,16},{16,12},{20,24},{24,20},{28,0},{0,28},{5,9},{9... | collective-permute-start | bytes 577544 | tf_op jit(solution)/shard_map/ppermute | solution.py:424
  12.8 1.1 %collective-permute-start.3 = (f32[376,128]{1,0:T(8,128)S(1)}, f32[376,128]{1,0:T(8,128)S(1)}, u32[]{:S(2)}, u32[]{:S(2)}) collective-permute-start(f32[376,128]{1,0:T(8,128)S(1)} %get-tuple-element.26), channel_id=1, source_target_pairs={{0,4},{4,0},{8,12},{12,8},{16,20},{20,16},{24,28},{28,24},{1,5},{5... | collective-permute-start | bytes 577544 | tf_op jit(solution)/shard_map/ppermute | solution.py:424
  13.9 1.9 %second_step_inner_planes.1 = (f32[41,10,48,128]{3,2,1,0:T(8,128)S(1)}, f32[88,128]{1,0:T(8,128)S(1)}, f32[88,128]{1,0:T(8,128)S(1)}) custom-call(f32[41,10,48,128]{3,2,1,0:T(8,128)S(1)} %get-tuple-element.22.state.state_in, s32[8,32,128]{2,1,0:T(8,128)S(1)} %get-tuple-element.18.kinds), custom_call_target="tpu_custom_call" | custom-call | flops 12288000 | bytes 8060928 | tf_op jit(solution)/shard_map/second_step_inner_planes/pallas_call | solution.py:449
  15.8 0.1 collective-permute-start.4
  15.9 2.2 %collective-permute-start.5 = (f32[88,128]{1,0:T(8,128)S(1)}, f32[88,128]{1,0:T(8,128)S(1)}, u32[]{:S(2)}, u32[]{:S(2)}) collective-permute-start(f32[88,128]{1,0:T(8,128)S(1)} %get-tuple-element.28), channel_id=1, source_target_pairs={{1,2},{2,1},{5,6},{6,5},{9,10},{10,9},{13,14},{14,13},{17,18},{18,... | collective-permute-start | bytes 135176 | tf_op jit(solution)/shard_map/ppermute | solution.py:424
  18.1 1.8 %collective-permute-done.4.cross_a = f32[88,128]{1,0:T(8,128)S(1)} collective-permute-done((f32[88,128]{1,0:T(8,128)S(1)}, f32[88,128]{1,0:T(8,128)S(1)}, u32[]{:S(2)}, u32[]{:S(2)}) %collective-permute-start.4) | collective-permute-done | bytes 45088 | tf_op jit(solution)/shard_map/ppermute | solution.py:424
  19.9 1.9 %collective-permute-done.5.cross_b = f32[88,128]{1,0:T(8,128)S(1)} collective-permute-done((f32[88,128]{1,0:T(8,128)S(1)}, f32[88,128]{1,0:T(8,128)S(1)}, u32[]{:S(2)}, u32[]{:S(2)}) %collective-permute-start.5) | collective-permute-done | bytes 45088 | tf_op jit(solution)/shard_map/ppermute | solution.py:424
  21.8 0.0 collective-permute-done.2.loop_a
  21.8 0.0 collective-permute-done.3.loop_b
  21.8 0.9 %second_step_edge_planes.1 = (f32[41,10,48,128]{3,2,1,0:T(8,128)S(1)}, f32[41,10,48,128]{3,2,1,0:T(8,128)S(1)}, f32[11,32,128]{2,1,0:T(8,128)S(1)}, f32[11,32,128]{2,1,0:T(8,128)S(1)}) custom-call(f32[41,10,48,128]{3,2,1,0:T(8,128)S(1)} %get-tuple-element.22.state.state_in, ...), custom_call_target="tpu_custom_call", output_to_operand_aliasing={{0}: (0, {}), {1}: (1, {})} | custom-call | flops 4608000 | bytes 3022848 | tf_op jit(solution)/shard_map/second_step_edge_planes/pallas_call | solution.py:449
  22.7 0.1 collective-permute-start.6
  22.8 1.6 %collective-permute-start.7 = (f32[11,32,128]{2,1,0:T(8,128)S(1)}, f32[11,32,128]{2,1,0:T(8,128)S(1)}, u32[]{:S(2)}, u32[]{:S(2)}) collective-permute-start(f32[11,32,128]{2,1,0:T(8,128)S(1)} %get-tuple-element.33), channel_id=1, source_target_pairs={{0,4},{4,0},{8,12},{12,8},{16,20},{20,16},{24,28},{28,24},{1,5},{5... | collective-permute-start | bytes 540680 | tf_op jit(solution)/shard_map/ppermute | solution.py:424
  24.4 2.5 %write_all_planes.1 = (f32[27,8,32,128]{3,2,1,0:T(8,128)}, f32[14,8,32,128]{3,2,1,0:T(8,128)}) custom-call(f32[41,10,48,128]{3,2,1,0:T(8,128)S(1)} %get-tuple-element.29.out), custom_call_target="tpu_custom_call" | custom-call | bytes 10747904 | tf_op jit(solution)/shard_map/write_all_planes/pallas_call | solution.py:449
  26.9 2.7 %collective-permute-done.6.got_a = f32[11,32,128]{2,1,0:T(8,128)S(1)} collective-permute-done((f32[11,32,128]{2,1,0:T(8,128)S(1)}, f32[11,32,128]{2,1,0:T(8,128)S(1)}, u32[]{:S(2)}, u32[]{:S(2)}) %collective-permute-start.6) | collective-permute-done | bytes 180256 | tf_op jit(solution)/shard_map/ppermute | solution.py:424
  29.6 0.0 collective-permute-done.7.got_b
  29.6 0.9 %write_edge_planes.1 = (f32[27,8,32,128]{3,2,1,0:T(8,128)}, f32[14,8,32,128]{3,2,1,0:T(8,128)}) custom-call(f32[27,8,32,128]{3,2,1,0:T(8,128)} %get-tuple-element.30.pops_in, f32[14,8,32,128]{3,2,1,0:T(8,128)} %get-tuple-element.31.scal_in, f32[11,32,128]{2,1,0:T(8,128)S(1)} %collective-permute-done.6.got_a, ...), custom_call_target="tpu_custom_call", output_to_operand_aliasing={{0}: (0, {}), {1}: (1, {})} | custom-call | bytes 720896 | tf_op jit(solution)/shard_map/write_edge_planes/pallas_call | solution.py:449
Async XLA Ops:
  4.2 6.2 %collective-permute-start = (f32[152,128]{1,0:T(8,128)S(1)}, f32[152,128]{1,0:T(8,128)S(1)}, u32[]{:S(2)}, u32[]{:S(2)}) collective-permute-start(f32[152,128]{1,0:T(8,128)S(1)} %get-tuple-element.20), channel_id=1, source_target_pairs={{0,1},{1,0},{2,3},{3,2},{4,5},{5,4},{6,7},{7,6},{8,9},{9,8},{10,11... | collective-permute-start | bytes 233480 | tf_op jit(solution)/shard_map/ppermute | solution.py:424
  5.8 6.3 %collective-permute-start.1 = (f32[152,128]{1,0:T(8,128)S(1)}, f32[152,128]{1,0:T(8,128)S(1)}, u32[]{:S(2)}, u32[]{:S(2)}) collective-permute-start(f32[152,128]{1,0:T(8,128)S(1)} %get-tuple-element.21), channel_id=1, source_target_pairs={{1,2},{2,1},{5,6},{6,5},{9,10},{10,9},{13,14},{14,13},{17,18},{18,... | collective-permute-start | bytes 233480 | tf_op jit(solution)/shard_map/ppermute | solution.py:424
  12.3 9.6 %collective-permute-start.2 = (f32[376,128]{1,0:T(8,128)S(1)}, f32[376,128]{1,0:T(8,128)S(1)}, u32[]{:S(2)}, u32[]{:S(2)}) collective-permute-start(f32[376,128]{1,0:T(8,128)S(1)} %get-tuple-element.25), channel_id=1, source_target_pairs={{4,8},{8,4},{12,16},{16,12},{20,24},{24,20},{28,0},{0,28},{5,9},{9... | collective-permute-start | bytes 577544 | tf_op jit(solution)/shard_map/ppermute | solution.py:424
  12.8 9.1 %collective-permute-start.3 = (f32[376,128]{1,0:T(8,128)S(1)}, f32[376,128]{1,0:T(8,128)S(1)}, u32[]{:S(2)}, u32[]{:S(2)}) collective-permute-start(f32[376,128]{1,0:T(8,128)S(1)} %get-tuple-element.26), channel_id=1, source_target_pairs={{0,4},{4,0},{8,12},{12,8},{16,20},{20,16},{24,28},{28,24},{1,5},{5... | collective-permute-start | bytes 577544 | tf_op jit(solution)/shard_map/ppermute | solution.py:424
  15.8 4.1 %collective-permute-start.4 = (f32[88,128]{1,0:T(8,128)S(1)}, f32[88,128]{1,0:T(8,128)S(1)}, u32[]{:S(2)}, u32[]{:S(2)}) collective-permute-start(f32[88,128]{1,0:T(8,128)S(1)} %get-tuple-element.27), channel_id=1, source_target_pairs={{0,1},{1,0},{2,3},{3,2},{4,5},{5,4},{6,7},{7,6},{8,9},{9,8},{10,11... | collective-permute-start | bytes 135176 | tf_op jit(solution)/shard_map/ppermute | solution.py:424
  15.9 5.9 %collective-permute-start.5 = (f32[88,128]{1,0:T(8,128)S(1)}, f32[88,128]{1,0:T(8,128)S(1)}, u32[]{:S(2)}, u32[]{:S(2)}) collective-permute-start(f32[88,128]{1,0:T(8,128)S(1)} %get-tuple-element.28), channel_id=1, source_target_pairs={{1,2},{2,1},{5,6},{6,5},{9,10},{10,9},{13,14},{14,13},{17,18},{18,... | collective-permute-start | bytes 135176 | tf_op jit(solution)/shard_map/ppermute | solution.py:424
  22.7 6.9 %collective-permute-start.6 = (f32[11,32,128]{2,1,0:T(8,128)S(1)}, f32[11,32,128]{2,1,0:T(8,128)S(1)}, u32[]{:S(2)}, u32[]{:S(2)}) collective-permute-start(f32[11,32,128]{2,1,0:T(8,128)S(1)} %get-tuple-element.32), channel_id=1, source_target_pairs={{4,8},{8,4},{12,16},{16,12},{20,24},{24,20},{28,0},{0,28},{5,9},{9... | collective-permute-start | bytes 540680 | tf_op jit(solution)/shard_map/ppermute | solution.py:424
  22.8 6.8 %collective-permute-start.7 = (f32[11,32,128]{2,1,0:T(8,128)S(1)}, f32[11,32,128]{2,1,0:T(8,128)S(1)}, u32[]{:S(2)}, u32[]{:S(2)}) collective-permute-start(f32[11,32,128]{2,1,0:T(8,128)S(1)} %get-tuple-element.33), channel_id=1, source_target_pairs={{0,4},{4,0},{8,12},{12,8},{16,20},{20,16},{24,28},{28,24},{1,5},{5... | collective-permute-start | bytes 540680 | tf_op jit(solution)/shard_map/ppermute | solution.py:424

commit v9 on v8

--- a/solution.py
+++ b/solution.py
@@ -32,7 +32,13 @@
 LOOP_SWAPS = (1, 0)
 
 
-def collide(load, flags, put):
+def collide(load, flags, put_any, want=None):
+    want = set(range(NQ)) if want is None else set(want)
+
+    def put(i, value):
+        if i in want:
+            put_any(i, value())
+
     wall = flags == 1
     fan = flags == 2
     heater = flags == 3
@@ -77,9 +83,11 @@
     for i in range(NF // 2, NF):
         vector = FLOW[i]
         n = sum(abs(p) for p in vector)
+        if not want & {i, NF - 1 - i}:
+            continue
         f_i = load(i)
         if n == 0:
-            put(i, jnp.where(wall, f_i, keep * f_i + by_w[0] * base))
+            put(i, lambda: jnp.where(wall, f_i, keep * f_i + by_w[0] * base))
             continue
         first = next(p for p in vector if p)
         assert first > 0
@@ -95,10 +103,12 @@
         f_o = load(NF - 1 - i)
         even = by_w[n] * (base + proj * proj)
         odd = by_w3[n] * proj
-        put(i, jnp.where(wall, f_o, keep * f_i + (even + odd)))
-        put(NF - 1 - i, jnp.where(wall, f_i, keep * f_o + (even - odd)))
+        put(i, lambda: jnp.where(wall, f_o, keep * f_i + (even + odd)))
+        put(NF - 1 - i, lambda: jnp.where(wall, f_i, keep * f_o + (even - odd)))
 
     for first, relax in ((NF, relax_heat), (NF + NS, relax_solvent)):
+        if not want & set(range(first, first + NS)):
+            continue
         total = load(first)
         for j in range(1, NS):
             total = total + load(first + j)
@@ -109,14 +119,16 @@
             keep_s = jnp.where(exhaust, 0.0, 1.0 - 1.0 / relax)
             source = jnp.where(exhaust, 0.0, total * (1.0 / relax))
         g = load(first)
-        put(first, jnp.where(wall, g, keep_s * g + source * 0.25))
+        put(first, lambda: jnp.where(wall, g, keep_s * g + source * 0.25))
         eighth = source * 0.125
         half = source * 0.5
         for axis, vel in enumerate((vel_x, vel_y, vel_z)):
+            if not want & {first + 1 + 2 * axis, first + 2 + 2 * axis}:
+                continue
             odd = half * vel
             g_p, g_m = load(first + 1 + 2 * axis), load(first + 2 + 2 * axis)
-            put(first + 1 + 2 * axis, jnp.where(wall, g_m, keep_s * g_p + (eighth + odd)))
-            put(first + 2 + 2 * axis, jnp.where(wall, g_p, keep_s * g_m + (eighth - odd)))
+            put(first + 1 + 2 * axis, lambda: jnp.where(wall, g_m, keep_s * g_p + (eighth + odd)))
+            put(first + 2 + 2 * axis, lambda: jnp.where(wall, g_p, keep_s * g_m + (eighth - odd)))
 
 
 def shift_lanes(value, c):
@@ -313,14 +325,19 @@
         by_swap("loop", swap, lambda side: send_first_loop(state, side, msg))
 
 
-def inner_kernel(state, kinds, out, sent_a, sent_b):
+def collide_inner(state, kinds, out, tiles):
+    size_x, _ = sizes_of(state)
+
+    @pl.loop(1, size_x - 1)
+    def _(x):
+        for y in tiles:
+            collide(load_tile(state, x, y), kinds[x, y : y + SUB, :], push_tile(out, x, y))
+
+
+def inner_side_kernel(state, kinds, out, sent_a, sent_b):
     size_x, size_y = sizes_of(state)
     rows, flat = out.shape[2], flat_of(out)
-
-    @pl.loop(1, size_x - 1)
-    def _(x):
-        for y in range(0, size_y, SUB):
-            collide(load_tile(state, x, y), kinds[x, y : y + SUB, :], push_tile(out, x, y))
+    collide_inner(state, kinds, out, (0, size_y - SUB))
 
     def send(b, msg):
         y_out = size_y if b > 0 else -1
@@ -331,31 +348,51 @@
         by_swap("cross", swap, lambda side: send(side, msg))
 
 
-def edge_kernel(state_in, out_in, kinds, halo_kinds, loop_a, loop_b, cross_a, cross_b, state, out, sent_a, sent_b, halo):
+def inner_middle_kernel(state, kinds, out_in, out):
+    _, size_y = sizes_of(state)
+    collide_inner(state, kinds, out, range(SUB, size_y - SUB, SUB))
+
+
+def collide_edges(state, kinds, halo_kinds, out, halo, sent):
     size_x, size_y = sizes_of(state)
     rows, flat, flat_out = state.shape[2], flat_of(state), flat_of(out)
-    for swap, msg in zip(LOOP_SWAPS, (loop_a, loop_b)):
-        by_swap("loop", swap, lambda side: take_first_loop(state, -side, msg))
     for i in range(NQ):
         halo[i, 0:2, :] = flat[i, lines(0, -1, rows, 2, size_x - 1), :]
         halo[i, 2:4, :] = flat[i, lines(0, size_y, rows, 2, size_x - 1), :]
-
-    @pl.loop(0, 2)
-    def _(side):
-        x = side * (size_x - 1)
+    for a in SIDES:
+        x = 0 if a < 0 else size_x - 1
+        want = [i for i in range(NQ) if (i in X_SETS[a]) == sent]
         for y in range(0, size_y, SUB):
-            collide(load_tile(state, x, y), kinds[x, y : y + SUB, :], push_tile(out, x, y))
-
+            collide(load_tile(state, x, y), kinds[x, y : y + SUB, :], push_tile(out, x, y), want)
     code = halo_kinds[...].astype(jnp.int32)
 
     def put(i, value):
         a, b, c = DIRS[i]
-        if b:
-            y_in, first = (0, 0) if b > 0 else (size_y - 1, 2)
-            moved = shift_lanes(jnp.where(code == 0, 0.0, value), c)
-            flat_out[i, lines(a, y_in, rows, 2, size_x - 1), :] = moved[first : first + 2, :]
-
-    collide(lambda i: halo[i], code - 1, put)
+        y_in, first = (0, 0) if b > 0 else (size_y - 1, 2)
+        moved = shift_lanes(jnp.where(code == 0, 0.0, value), c)
+        flat_out[i, lines(a, y_in, rows, 2, size_x - 1), :] = moved[first : first + 2, :]
+
+    want = [i for i, d in enumerate(DIRS) if d[1] and bool(d[0]) == sent]
+    collide(lambda i: halo[i], code - 1, put, want)
+
+
+def edge_kernel(
+    state_in, out_in, kinds, halo_kinds, loop_a, loop_b, cross_a, cross_b, state, out, sent_a, sent_b, halo
+):
+    size_x, size_y = sizes_of(state)
+    rows, flat_out = state.shape[2], flat_of(out)
+    for swap, msg in zip(LOOP_SWAPS, (loop_a, loop_b)):
+        by_swap("loop", swap, lambda side: take_first_loop(state, -side, msg))
+    collide_edges(state, kinds, halo_kinds, out, halo, True)
+
+    def send(a, msg):
+        x = -1 if a < 0 else size_x
+        for k, i in enumerate(X_SETS[a]):
+            for y in range(0, size_y, SUB):
+                msg[k, y : y + SUB, :] = out[i, slot(x), y + PAD : y + PAD + SUB, :]
+
+    for swap, msg in zip(LOOP_SWAPS, (sent_a, sent_b)):
+        by_swap("loop", swap, lambda side: send(side, msg))
 
     def take(b, msg):
         y_in = 0 if b > 0 else size_y - 1
@@ -366,27 +403,29 @@
     for swap, msg in zip(CROSS_SWAPS, (cross_a, cross_b)):
         by_swap("cross", swap, lambda side: take(-side, msg))
 
-    def send(a, msg):
-        x = -1 if a < 0 else size_x
-        for k, i in enumerate(X_SETS[a]):
-            for y in range(0, size_y, SUB):
-                msg[k, y : y + SUB, :] = out[i, slot(x), y + PAD : y + PAD + SUB, :]
-
-    for swap, msg in zip(LOOP_SWAPS, (sent_a, sent_b)):
-        by_swap("loop", swap, lambda side: send(side, msg))
-
-
-def write_kernel(out, pops, scal, sems):
+
+def write_kernel(state, out_in, kinds, halo_kinds, out, pops, scal, sems, halo):
     size_x, size_y = sizes_of(out)
-    copies = []
+
+    def copies(x):
+        inner = pl.ds(PAD, size_y)
+        return [
+            pltpu.make_async_copy(out.at[0:NF, slot(x), inner], pops.at[:, x], sems.at[0, x]),
+            pltpu.make_async_copy(out.at[NF:NQ, slot(x), inner], scal.at[:, x], sems.at[1, x]),
+        ]
+
+    done = range(2, size_x - 2)
+    late = [x for x in range(size_x) if x not in done]
+    for x in done:
+        for copy in copies(x):
+            copy.start()
+    collide_edges(state, kinds, halo_kinds, out, halo, False)
+    for x in late:
+        for copy in copies(x):
+            copy.start()
     for x in range(size_x):
-        inner = pl.ds(PAD, size_y)
-        copies.append(pltpu.make_async_copy(out.at[0:NF, slot(x), inner], pops.at[:, x], sems.at[0, x]))
-        copies.append(pltpu.make_async_copy(out.at[NF:NQ, slot(x), inner], scal.at[:, x], sems.at[1, x]))
-    for copy in copies:
-        copy.start()
-    for copy in copies:
-        copy.wait()
+        for copy in copies(x):
+            copy.wait()
 
 
 def last_kernel(pops_in, scal_in, got_a, got_b, pops, scal, sems):
@@ -503,30 +542,42 @@
     )
     from_loop = swap_along("loop", LOOP_SWAPS, True, sent)
     out, *sent = call(
-        inner_kernel,
-        "second_step_inner_planes",
+        inner_side_kernel,
+        "second_step_inner_side_rows",
         on_chip(state, kinds),
         [state_shape] + cross_2,
-        tiles=(size_x - 2) * tiles,
+        tiles=(size_x - 2) * 2,
     )
     from_cross = swap_along("cross", CROSS_SWAPS, False, sent)
+    if tiles > 2:
+        (out,) = call(
+            inner_middle_kernel,
+            "second_step_inner_middle_rows",
+            on_chip(state, kinds, out),
+            [state_shape],
+            tiles=(size_x - 2) * (tiles - 2),
+            aliases={2: 0},
+        )
+    halo = pltpu.VMEM((NQ, SUB, size_z), f32)
     state, out, *sent = call(
         edge_kernel,
-        "second_step_edge_planes",
+        "second_step_edges_to_send",
         on_chip(state, out, kinds, halo_kinds, *from_loop, *from_cross),
         [state_shape, state_shape] + loop_2,
         tiles=2 * tiles + 1,
-        scratch=[pltpu.VMEM((NQ, SUB, size_z), f32)],
+        scratch=[halo],
         aliases={0: 0, 1: 1},
     )
     received = swap_along("loop", LOOP_SWAPS, True, sent)
-    new_pops, new_scal = call(
+    _, new_pops, new_scal = call(
         write_kernel,
-        "write_all_planes",
-        on_chip(out),
-        [pops_shape, scal_shape],
+        "second_step_edges_rest_and_write",
+        on_chip(state, out, kinds, halo_kinds),
+        [state_shape, pops_shape, scal_shape],
+        tiles=2 * tiles + 1,
         moved=8 * NQ * size_x * size_y * size_z,
-        scratch=[pltpu.SemaphoreType.DMA((2, size_x))],
+        scratch=[pltpu.SemaphoreType.DMA((2, size_x)), halo],
+        aliases={1: 0},
     )
     new_pops, new_scal = call(
         last_kernel,

time: 30.7 us -> 29.5 us (0.961)
  waiting for transfers between devices: 8.18 us -> 7.09 us
    ppermute x8, waiting for transfers between devices: 8.18 us -> 7.09 us  [swap_along(): received.append(lax.ppermute(cells, axis, pairs))]
    pallas_call x7 -> x8, Pallas kernels: 12.5 us -> 12.4 us  [call(): pl.pallas_call(kernel, out_shape=results, in_specs=specs, out_specs=[hbm...]
  transfers between devices with their start and end apart: 8 -> 8, of which waited for: 4 -> 4; matrix products, arithmetic and copies ran while one was open for 0% -> 0% of each run, Pallas kernels for 23% -> 25%
where the time goes in v9:
time: 29.5 us; the launch traced here: 29.3 us
  Pallas kernels  12.4 us (42%)
  starting transfers between devices  9.16 us (31%)
  waiting for transfers between devices  7.09 us (24%)
  between operations  0.72 us (2%)
    pallas_call x8, Pallas kernels, call(): pl.pallas_call(kernel, out_shape=results, in_specs=specs, out_specs=[hbm...  12.4 us
    ppermute x8, starting transfers between devices, swap_along(): received.append(lax.ppermute(cells, axis, pairs))  9.16 us
    ppermute x8, waiting for transfers between devices, swap_along(): received.append(lax.ppermute(cells, axis, pairs))  7.09 us
  transfers between devices with their start and end apart: 8, of which 4 were waited for; matrix products, arithmetic and copies ran while one was open for 0% of the time, Pallas kernels for 25%

profile of v9, /device:TPU:16, one launch (start us, length us, event | category | flops | bytes accessed | tf_op | source)
XLA Modules:
  0.0 29.3 jit_solution(10703148030972167745)
XLA Ops:
  0.6 3.6 %first_step_side_rows.1 = (f32[41,10,48,128]{3,2,1,0:T(8,128)S(1)}, s32[8,32,128]{2,1,0:T(8,128)S(1)}, f32[152,128]{1,0:T(8,128)S(1)}, f32[152,128]{1,0:T(8,128)S(1)}) custom-call(f32[27,8,32,128]{3,2,1,0:T(8,128)} %pops.3, f32[14,8,32,128]{3,2,1,0:T(8,128)} %scal.3, s32[8,32,128]{2,1,0:T(8,128)} %flags.1), custom_call_target="tpu_custom_call" | custom-call | flops 8192000 | bytes 5373952 | tf_op jit(solution)/shard_map/first_step_side_rows/pallas_call | solution.py:488
  4.2 1.6 %collective-permute-start = (f32[152,128]{1,0:T(8,128)S(1)}, f32[152,128]{1,0:T(8,128)S(1)}, u32[]{:S(2)}, u32[]{:S(2)}) collective-permute-start(f32[152,128]{1,0:T(8,128)S(1)} %get-tuple-element.21), channel_id=1, source_target_pairs={{0,1},{1,0},{2,3},{3,2},{4,5},{5,4},{6,7},{7,6},{8,9},{9,8},{10,11... | collective-permute-start | bytes 233480 | tf_op jit(solution)/shard_map/ppermute | solution.py:463
  5.8 1.9 %collective-permute-start.1 = (f32[152,128]{1,0:T(8,128)S(1)}, f32[152,128]{1,0:T(8,128)S(1)}, u32[]{:S(2)}, u32[]{:S(2)}) collective-permute-start(f32[152,128]{1,0:T(8,128)S(1)} %get-tuple-element.22), channel_id=1, source_target_pairs={{1,2},{2,1},{5,6},{6,5},{9,10},{10,9},{13,14},{14,13},{17,18},{18,... | collective-permute-start | bytes 233480 | tf_op jit(solution)/shard_map/ppermute | solution.py:463
  7.8 2.6 %first_step_middle_rows.1.state_in = f32[41,10,48,128]{3,2,1,0:T(8,128)S(1)} custom-call(f32[27,8,32,128]{3,2,1,0:T(8,128)} %pops.3, f32[14,8,32,128]{3,2,1,0:T(8,128)} %scal.3, s32[8,32,128]{2,1,0:T(8,128)S(1)} %get-tuple-element.19.kinds, f32[41,10,48,128]{3,2,1,0:T(8,128)S(1)} %get-tuple-element.20.state_in), custom_call_target="tpu_custom_call", output_to_operand_aliasing={{}: (3, {})} | custom-call | flops 8192000 | bytes 5373952 | tf_op jit(solution)/shard_map/first_step_middle_rows/pallas_call | solution.py:488
  10.4 0.0 collective-permute-done.got_a
  10.4 1.7 %collective-permute-done.1.got_b = f32[152,128]{1,0:T(8,128)S(1)} collective-permute-done((f32[152,128]{1,0:T(8,128)S(1)}, f32[152,128]{1,0:T(8,128)S(1)}, u32[]{:S(2)}, u32[]{:S(2)}) %collective-permute-start.1) | collective-permute-done | bytes 77856 | tf_op jit(solution)/shard_map/ppermute | solution.py:463
  12.1 0.1 cross_to_loop.1
  12.3 0.5 %collective-permute-start.2 = (f32[376,128]{1,0:T(8,128)S(1)}, f32[376,128]{1,0:T(8,128)S(1)}, u32[]{:S(2)}, u32[]{:S(2)}) collective-permute-start(f32[376,128]{1,0:T(8,128)S(1)} %get-tuple-element.26), channel_id=1, source_target_pairs={{4,8},{8,4},{12,16},{16,12},{20,24},{24,20},{28,0},{0,28},{5,9},{9... | collective-permute-start | bytes 577544 | tf_op jit(solution)/shard_map/ppermute | solution.py:463
  12.8 1.1 %collective-permute-start.3 = (f32[376,128]{1,0:T(8,128)S(1)}, f32[376,128]{1,0:T(8,128)S(1)}, u32[]{:S(2)}, u32[]{:S(2)}) collective-permute-start(f32[376,128]{1,0:T(8,128)S(1)} %get-tuple-element.27), channel_id=1, source_target_pairs={{0,4},{4,0},{8,12},{12,8},{16,20},{20,16},{24,28},{28,24},{1,5},{5... | collective-permute-start | bytes 577544 | tf_op jit(solution)/shard_map/ppermute | solution.py:463
  13.9 1.1 %second_step_inner_side_rows.1 = (f32[41,10,48,128]{3,2,1,0:T(8,128)S(1)}, f32[88,128]{1,0:T(8,128)S(1)}, f32[88,128]{1,0:T(8,128)S(1)}) custom-call(f32[41,10,48,128]{3,2,1,0:T(8,128)S(1)} %get-tuple-element.23.state.state_in, s32[8,32,128]{2,1,0:T(8,128)S(1)} %get-tuple-element.19.kinds), custom_call_target="tpu_custom_call" | custom-call | flops 6144000 | bytes 4030464 | tf_op jit(solution)/shard_map/second_step_inner_side_rows/pallas_call | solution.py:488
  15.0 0.1 collective-permute-start.4
  15.1 2.2 %collective-permute-start.5 = (f32[88,128]{1,0:T(8,128)S(1)}, f32[88,128]{1,0:T(8,128)S(1)}, u32[]{:S(2)}, u32[]{:S(2)}) collective-permute-start(f32[88,128]{1,0:T(8,128)S(1)} %get-tuple-element.29), channel_id=1, source_target_pairs={{1,2},{2,1},{5,6},{6,5},{9,10},{10,9},{13,14},{14,13},{17,18},{18,... | collective-permute-start | bytes 135176 | tf_op jit(solution)/shard_map/ppermute | solution.py:463
  17.3 1.1 %second_step_inner_middle_rows.1.out_in = f32[41,10,48,128]{3,2,1,0:T(8,128)S(1)} custom-call(f32[41,10,48,128]{3,2,1,0:T(8,128)S(1)} %get-tuple-element.23.state.state_in, s32[8,32,128]{2,1,0:T(8,128)S(1)} %get-tuple-element.19.kinds, f32[41,10,48,128]{3,2,1,0:T(8,128)S(1)} %get-tuple-element.24.out_in), custom_call_target="tpu_custom_call", output_to_operand_aliasing={{}: (2, {})} | custom-call | flops 6144000 | bytes 4030464 | tf_op jit(solution)/shard_map/second_step_inner_middle_rows/pallas_call | solution.py:488
  18.4 0.7 %collective-permute-done.4.cross_a = f32[88,128]{1,0:T(8,128)S(1)} collective-permute-done((f32[88,128]{1,0:T(8,128)S(1)}, f32[88,128]{1,0:T(8,128)S(1)}, u32[]{:S(2)}, u32[]{:S(2)}) %collective-permute-start.4) | collective-permute-done | bytes 45088 | tf_op jit(solution)/shard_map/ppermute | solution.py:463
  19.1 1.9 %collective-permute-done.5.cross_b = f32[88,128]{1,0:T(8,128)S(1)} collective-permute-done((f32[88,128]{1,0:T(8,128)S(1)}, f32[88,128]{1,0:T(8,128)S(1)}, u32[]{:S(2)}, u32[]{:S(2)}) %collective-permute-start.5) | collective-permute-done | bytes 45088 | tf_op jit(solution)/shard_map/ppermute | solution.py:463
  21.0 0.0 collective-permute-done.2.loop_a
  21.0 0.0 collective-permute-done.3.loop_b
  21.1 0.5 %second_step_edges_to_send.1 = (f32[41,10,48,128]{3,2,1,0:T(8,128)S(1)}, f32[41,10,48,128]{3,2,1,0:T(8,128)S(1)}, f32[11,32,128]{2,1,0:T(8,128)S(1)}, f32[11,32,128]{2,1,0:T(8,128)S(1)}) custom-call(f32[41,10,48,128]{3,2,1,0:T(8,128)S(1)} %get-tuple-element.23.state.state_in, ...), custom_call_target="tpu_custom_call", output_to_operand_aliasing={{0}: (0, {}), {1}: (1, {})} | custom-call | flops 4608000 | bytes 3022848 | tf_op jit(solution)/shard_map/second_step_edges_to_send/pallas_call | solution.py:488
  21.5 0.1 collective-permute-start.6
  21.6 1.6 %collective-permute-start.7 = (f32[11,32,128]{2,1,0:T(8,128)S(1)}, f32[11,32,128]{2,1,0:T(8,128)S(1)}, u32[]{:S(2)}, u32[]{:S(2)}) collective-permute-start(f32[11,32,128]{2,1,0:T(8,128)S(1)} %get-tuple-element.35), channel_id=1, source_target_pairs={{0,4},{4,0},{8,12},{12,8},{16,20},{20,16},{24,28},{28,24},{1,5},{5... | collective-permute-start | bytes 540680 | tf_op jit(solution)/shard_map/ppermute | solution.py:463
  23.2 2.5 %second_step_edges_rest_and_write.1 = (f32[41,10,48,128]{3,2,1,0:T(8,128)S(1)}, f32[27,8,32,128]{3,2,1,0:T(8,128)}, f32[14,8,32,128]{3,2,1,0:T(8,128)}) custom-call(f32[41,10,48,128]{3,2,1,0:T(8,128)S(1)} %get-tuple-element.30.state, f32[41,10,48,128]{3,2,1,0:T(8,128)S(1)} %get-tuple-element.31.out_in, ...), custom_call_target="tpu_custom_call", output_to_operand_aliasing={{0}: (1, {})} | custom-call | flops 4608000 | bytes 13770752 | tf_op jit(solution)/shard_map/second_step_edges_rest_and_write/pallas_call | solution.py:488
  25.7 2.7 %collective-permute-done.6.got_a = f32[11,32,128]{2,1,0:T(8,128)S(1)} collective-permute-done((f32[11,32,128]{2,1,0:T(8,128)S(1)}, f32[11,32,128]{2,1,0:T(8,128)S(1)}, u32[]{:S(2)}, u32[]{:S(2)}) %collective-permute-start.6) | collective-permute-done | bytes 180256 | tf_op jit(solution)/shard_map/ppermute | solution.py:463
  28.4 0.0 collective-permute-done.7.got_b
  28.4 0.9 %write_edge_planes.1 = (f32[27,8,32,128]{3,2,1,0:T(8,128)}, f32[14,8,32,128]{3,2,1,0:T(8,128)}) custom-call(f32[27,8,32,128]{3,2,1,0:T(8,128)} %get-tuple-element.32.pops_in, f32[14,8,32,128]{3,2,1,0:T(8,128)} %get-tuple-element.33.scal_in, f32[11,32,128]{2,1,0:T(8,128)S(1)} %collective-permute-done.6.got_a, ...), custom_call_target="tpu_custom_call", output_to_operand_aliasing={{0}: (0, {}), {1}: (1, {})} | custom-call | bytes 720896 | tf_op jit(solution)/shard_map/write_edge_planes/pallas_call | solution.py:488
Async XLA Ops:
  4.2 6.2 %collective-permute-start = (f32[152,128]{1,0:T(8,128)S(1)}, f32[152,128]{1,0:T(8,128)S(1)}, u32[]{:S(2)}, u32[]{:S(2)}) collective-permute-start(f32[152,128]{1,0:T(8,128)S(1)} %get-tuple-element.21), channel_id=1, source_target_pairs={{0,1},{1,0},{2,3},{3,2},{4,5},{5,4},{6,7},{7,6},{8,9},{9,8},{10,11... | collective-permute-start | bytes 233480 | tf_op jit(solution)/shard_map/ppermute | solution.py:463
  5.8 6.3 %collective-permute-start.1 = (f32[152,128]{1,0:T(8,128)S(1)}, f32[152,128]{1,0:T(8,128)S(1)}, u32[]{:S(2)}, u32[]{:S(2)}) collective-permute-start(f32[152,128]{1,0:T(8,128)S(1)} %get-tuple-element.22), channel_id=1, source_target_pairs={{1,2},{2,1},{5,6},{6,5},{9,10},{10,9},{13,14},{14,13},{17,18},{18,... | collective-permute-start | bytes 233480 | tf_op jit(solution)/shard_map/ppermute | solution.py:463
  12.3 8.8 %collective-permute-start.2 = (f32[376,128]{1,0:T(8,128)S(1)}, f32[376,128]{1,0:T(8,128)S(1)}, u32[]{:S(2)}, u32[]{:S(2)}) collective-permute-start(f32[376,128]{1,0:T(8,128)S(1)} %get-tuple-element.26), channel_id=1, source_target_pairs={{4,8},{8,4},{12,16},{16,12},{20,24},{24,20},{28,0},{0,28},{5,9},{9... | collective-permute-start | bytes 577544 | tf_op jit(solution)/shard_map/ppermute | solution.py:463
  12.8 8.3 %collective-permute-start.3 = (f32[376,128]{1,0:T(8,128)S(1)}, f32[376,128]{1,0:T(8,128)S(1)}, u32[]{:S(2)}, u32[]{:S(2)}) collective-permute-start(f32[376,128]{1,0:T(8,128)S(1)} %get-tuple-element.27), channel_id=1, source_target_pairs={{0,4},{4,0},{8,12},{12,8},{16,20},{20,16},{24,28},{28,24},{1,5},{5... | collective-permute-start | bytes 577544 | tf_op jit(solution)/shard_map/ppermute | solution.py:463
  15.0 4.1 %collective-permute-start.4 = (f32[88,128]{1,0:T(8,128)S(1)}, f32[88,128]{1,0:T(8,128)S(1)}, u32[]{:S(2)}, u32[]{:S(2)}) collective-permute-start(f32[88,128]{1,0:T(8,128)S(1)} %get-tuple-element.28), channel_id=1, source_target_pairs={{0,1},{1,0},{2,3},{3,2},{4,5},{5,4},{6,7},{7,6},{8,9},{9,8},{10,11... | collective-permute-start | bytes 135176 | tf_op jit(solution)/shard_map/ppermute | solution.py:463
  15.1 5.9 %collective-permute-start.5 = (f32[88,128]{1,0:T(8,128)S(1)}, f32[88,128]{1,0:T(8,128)S(1)}, u32[]{:S(2)}, u32[]{:S(2)}) collective-permute-start(f32[88,128]{1,0:T(8,128)S(1)} %get-tuple-element.29), channel_id=1, source_target_pairs={{1,2},{2,1},{5,6},{6,5},{9,10},{10,9},{13,14},{14,13},{17,18},{18,... | collective-permute-start | bytes 135176 | tf_op jit(solution)/shard_map/ppermute | solution.py:463
  21.5 6.9 %collective-permute-start.6 = (f32[11,32,128]{2,1,0:T(8,128)S(1)}, f32[11,32,128]{2,1,0:T(8,128)S(1)}, u32[]{:S(2)}, u32[]{:S(2)}) collective-permute-start(f32[11,32,128]{2,1,0:T(8,128)S(1)} %get-tuple-element.34), channel_id=1, source_target_pairs={{4,8},{8,4},{12,16},{16,12},{20,24},{24,20},{28,0},{0,28},{5,9},{9... | collective-permute-start | bytes 540680 | tf_op jit(solution)/shard_map/ppermute | solution.py:463
  21.6 6.8 %collective-permute-start.7 = (f32[11,32,128]{2,1,0:T(8,128)S(1)}, f32[11,32,128]{2,1,0:T(8,128)S(1)}, u32[]{:S(2)}, u32[]{:S(2)}) collective-permute-start(f32[11,32,128]{2,1,0:T(8,128)S(1)} %get-tuple-element.35), channel_id=1, source_target_pairs={{0,4},{4,0},{8,12},{12,8},{16,20},{20,16},{24,28},{28,24},{1,5},{5... | collective-permute-start | bytes 540680 | tf_op jit(solution)/shard_map/ppermute | solution.py:463

commit v10 on v9

--- a/solution.py
+++ b/solution.py
@@ -173,6 +173,12 @@
     pl.when(jnp.logical_not(odd))(lambda: fill(second))
 
 
+def has_partner(axis, swap):
+    index, count = lax.axis_index(axis), lax.axis_size(axis)
+    first = index - lax.rem(index + swap, 2)
+    return (first >= 0) & (first + 1 < count)
+
+
 def sizes_of(state):
     return state.shape[1] - 2, state.shape[2] - 2 * PAD
 
@@ -199,19 +205,19 @@
         msg[last + s : last + s + 1, :] = (line + 1).astype(jnp.float32)
 
 
-def take_first_cross(state, halo_kinds, b, msg):
+def take_first_cross(state, halo_kinds, b, msg, partner):
     size_x, size_y = sizes_of(state)
     rows, flat = state.shape[2], flat_of(state)
     ran, _ = first_cross_rows(size_x)
     y_in, y_halo = (0, -1) if b > 0 else (size_y - 1, size_y)
     for k, i in enumerate(Y_SETS[b]):
-        flat[i, lines(DIRS[i][0], y_in, rows, size_x), :] = msg[k * size_x : (k + 1) * size_x, :]
+        flat[i, lines(DIRS[i][0], y_in, rows, size_x), :] = jnp.where(partner, msg[k * size_x : (k + 1) * size_x, :], 0.0)
     for k, i in enumerate(SIDE_SETS[b]):
         x, step = side_span(i, size_x)
-        flat[i, lines(x, y_halo, rows, 2, step), :] = msg[ran + 2 * k : ran + 2 * k + 2, :]
+        flat[i, lines(x, y_halo, rows, 2, step), :] = jnp.where(partner, msg[ran + 2 * k : ran + 2 * k + 2, :], 0.0)
     last = ran + 2 * len(SIDE_SETS[b])
     first = 0 if b > 0 else 2
-    halo_kinds[first : first + 2, :] = msg[last : last + 2, :]
+    halo_kinds[first : first + 2, :] = jnp.where(partner, msg[last : last + 2, :], 0.0)
 
 
 def first_loop_rows(size_y):
@@ -320,7 +326,8 @@
 def turn_kernel(state_in, got_a, got_b, state, halo_kinds, sent_a, sent_b):
     halo_kinds[...] = jnp.zeros(halo_kinds.shape, jnp.float32)
     for swap, got in zip(CROSS_SWAPS, (got_a, got_b)):
-        by_swap("cross", swap, lambda side: take_first_cross(state, halo_kinds, -side, got))
+        partner = has_partner("cross", swap)
+        by_swap("cross", swap, lambda side: take_first_cross(state, halo_kinds, -side, got, partner))
     for swap, msg in zip(LOOP_SWAPS, (sent_a, sent_b)):
         by_swap("loop", swap, lambda side: send_first_loop(state, side, msg))
 
@@ -394,14 +401,15 @@
     for swap, msg in zip(LOOP_SWAPS, (sent_a, sent_b)):
         by_swap("loop", swap, lambda side: send(side, msg))
 
-    def take(b, msg):
+    def take(b, msg, partner):
         y_in = 0 if b > 0 else size_y - 1
         for k, i in enumerate(Y_SETS[b]):
-            got = msg[k * SUB : k * SUB + size_x - 2, :]
+            got = jnp.where(partner, msg[k * SUB : k * SUB + size_x - 2, :], 0.0)
             flat_out[i, lines(DIRS[i][0] + 1, y_in, rows, size_x - 2), :] = got
 
     for swap, msg in zip(CROSS_SWAPS, (cross_a, cross_b)):
-        by_swap("cross", swap, lambda side: take(-side, msg))
+        partner = has_partner("cross", swap)
+        by_swap("cross", swap, lambda side: take(-side, msg, partner))
 
 
 def write_kernel(state, out_in, kinds, halo_kinds, out, pops, scal, sems, halo):
@@ -453,14 +461,28 @@
     by_swap("loop", 0, write)
 
 
-def swap_along(axis, swaps, closed, messages):
-    count, received = lax.axis_size(axis), []
-    for swap, cells in zip(swaps, messages):
+def swap_cross(messages):
+    loops, crosses = lax.axis_size("loop"), lax.axis_size("cross")
+    received = []
+    for swap, cells in zip(CROSS_SWAPS, messages):
         pairs = []
-        for i in range(swap, count if closed else count - 1, 2):
+        for l in range(loops):
+            for c in range(crosses):
+                to = c + 1 if c % 2 == swap else c - 1
+                there = (l, to) if 0 <= to < crosses else (l + 1 if l % 2 == 0 else l - 1, c)
+                pairs.append((l * crosses + c, there[0] * crosses + there[1]))
+        received.append(lax.ppermute(cells, ("loop", "cross"), pairs))
+    return received
+
+
+def swap_loop(messages):
+    count, received = lax.axis_size("loop"), []
+    for swap, cells in zip(LOOP_SWAPS, messages):
+        pairs = []
+        for i in range(swap, count, 2):
             j = (i + 1) % count
             pairs += [(i, j), (j, i)]
-        received.append(lax.ppermute(cells, axis, pairs))
+        received.append(lax.ppermute(cells, "loop", pairs))
     return received
 
 
@@ -518,7 +540,7 @@
             pltpu.SemaphoreType.DMA,
         ],
     )
-    received = swap_along("cross", CROSS_SWAPS, False, sent)
+    received = swap_cross(sent)
     if tiles > 2:
         (state,) = call(
             middle_kernel,
@@ -540,7 +562,7 @@
         tiles=1,
         aliases={0: 0},
     )
-    from_loop = swap_along("loop", LOOP_SWAPS, True, sent)
+    from_loop = swap_loop(sent)
     out, *sent = call(
         inner_side_kernel,
         "second_step_inner_side_rows",
@@ -548,7 +570,7 @@
         [state_shape] + cross_2,
         tiles=(size_x - 2) * 2,
     )
-    from_cross = swap_along("cross", CROSS_SWAPS, False, sent)
+    from_cross = swap_cross(sent)
     if tiles > 2:
         (out,) = call(
             inner_middle_kernel,
@@ -568,7 +590,7 @@
         scratch=[halo],
         aliases={0: 0, 1: 1},
     )
-    received = swap_along("loop", LOOP_SWAPS, True, sent)
+    received = swap_loop(sent)
     _, new_pops, new_scal = call(
         write_kernel,
         "second_step_edges_rest_and_write",

time: 29.5 us -> 27.3 us (0.925)
  the two profiles are of different devices: /device:TPU:16 before, /device:TPU:0 now
where the time goes in v10:
time: 27.3 us; the launch traced here: 27.1 us
  Pallas kernels  12.4 us (45%)
  starting transfers between devices  9.61 us (35%)
  waiting for transfers between devices  4.41 us (16%)
  between operations  0.7 us (3%)
    pallas_call x8, Pallas kernels, call(): pl.pallas_call(kernel, out_shape=results, in_specs=specs, out_specs=[hbm...  12.4 us
    ppermute x4, starting transfers between devices, swap_cross(): received.append(lax.ppermute(cells, ('loop', 'cross'), pairs))  5.34 us
    ppermute x4, starting transfers between devices, swap_loop(): received.append(lax.ppermute(cells, 'loop', pairs))  4.28 us
    ppermute x4, waiting for transfers between devices, swap_loop(): received.append(lax.ppermute(cells, 'loop', pairs))  3.42 us
    ppermute x4, waiting for transfers between devices, swap_cross(): received.append(lax.ppermute(cells, ('loop', 'cross'), pairs))  0.99 us
  transfers between devices with their start and end apart: 8, of which 2 were waited for; matrix products, arithmetic and copies ran while one was open for 0% of the time, Pallas kernels for 27%

profile of v10, /device:TPU:0, one launch (start us, length us, event | category | flops | bytes accessed | tf_op | source)
XLA Modules:
  0.0 27.1 jit_solution(3462227977947053242)
XLA Ops:
  0.6 3.6 %first_step_side_rows.1 = (f32[41,10,48,128]{3,2,1,0:T(8,128)S(1)}, s32[8,32,128]{2,1,0:T(8,128)S(1)}, f32[152,128]{1,0:T(8,128)S(1)}, f32[152,128]{1,0:T(8,128)S(1)}) custom-call(f32[27,8,32,128]{3,2,1,0:T(8,128)} %pops.3, f32[14,8,32,128]{3,2,1,0:T(8,128)} %scal.3, s32[8,32,128]{2,1,0:T(8,128)} %flags.1), custom_call_target="tpu_custom_call" | custom-call | flops 8192000 | bytes 5373952 | tf_op jit(solution)/shard_map/first_step_side_rows/pallas_call | solution.py:510
  4.2 3.1 %collective-permute-start = (f32[152,128]{1,0:T(8,128)S(1)}, f32[152,128]{1,0:T(8,128)S(1)}, u32[]{:S(2)}, u32[]{:S(2)}) collective-permute-start(f32[152,128]{1,0:T(8,128)S(1)} %get-tuple-element.21), channel_id=1, source_target_pairs={{0,1},{1,0},{2,3},{3,2},{4,5},{5,4},{6,7},{7,6},{8,9},{9,8},{10,11... | collective-permute-start | bytes 233480 | tf_op jit(solution)/shard_map/ppermute | solution.py:474
  7.3 0.0 collective-permute-start.1
  7.3 2.6 %first_step_middle_rows.1.state_in = f32[41,10,48,128]{3,2,1,0:T(8,128)S(1)} custom-call(f32[27,8,32,128]{3,2,1,0:T(8,128)} %pops.3, f32[14,8,32,128]{3,2,1,0:T(8,128)} %scal.3, s32[8,32,128]{2,1,0:T(8,128)S(1)} %get-tuple-element.19.kinds, f32[41,10,48,128]{3,2,1,0:T(8,128)S(1)} %get-tuple-element.20.state_in), custom_call_target="tpu_custom_call", output_to_operand_aliasing={{}: (3, {})} | custom-call | flops 8192000 | bytes 5373952 | tf_op jit(solution)/shard_map/first_step_middle_rows/pallas_call | solution.py:510
  9.9 0.0 collective-permute-done.got_a
  9.9 0.0 collective-permute-done.1.got_b
  9.9 0.1 cross_to_loop.1
  10.1 2.6 %collective-permute-start.2 = (f32[376,128]{1,0:T(8,128)S(1)}, f32[376,128]{1,0:T(8,128)S(1)}, u32[]{:S(2)}, u32[]{:S(2)}) collective-permute-start(f32[376,128]{1,0:T(8,128)S(1)} %get-tuple-element.26), channel_id=1, source_target_pairs={{4,8},{8,4},{12,16},{16,12},{20,24},{24,20},{28,0},{0,28},{5,9},{9... | collective-permute-start | bytes 577544 | tf_op jit(solution)/shard_map/ppermute | solution.py:485
  12.7 0.0 collective-permute-start.3
  12.7 1.1 %second_step_inner_side_rows.1 = (f32[41,10,48,128]{3,2,1,0:T(8,128)S(1)}, f32[88,128]{1,0:T(8,128)S(1)}, f32[88,128]{1,0:T(8,128)S(1)}) custom-call(f32[41,10,48,128]{3,2,1,0:T(8,128)S(1)} %get-tuple-element.23.state.state_in, s32[8,32,128]{2,1,0:T(8,128)S(1)} %get-tuple-element.19.kinds), custom_call_target="tpu_custom_call" | custom-call | flops 6144000 | bytes 4030464 | tf_op jit(solution)/shard_map/second_step_inner_side_rows/pallas_call | solution.py:510
  13.8 2.3 %collective-permute-start.4 = (f32[88,128]{1,0:T(8,128)S(1)}, f32[88,128]{1,0:T(8,128)S(1)}, u32[]{:S(2)}, u32[]{:S(2)}) collective-permute-start(f32[88,128]{1,0:T(8,128)S(1)} %get-tuple-element.28), channel_id=1, source_target_pairs={{0,1},{1,0},{2,3},{3,2},{4,5},{5,4},{6,7},{7,6},{8,9},{9,8},{10,11... | collective-permute-start | bytes 135176 | tf_op jit(solution)/shard_map/ppermute | solution.py:474
  16.1 0.0 collective-permute-start.5
  16.1 1.1 %second_step_inner_middle_rows.1.out_in = f32[41,10,48,128]{3,2,1,0:T(8,128)S(1)} custom-call(f32[41,10,48,128]{3,2,1,0:T(8,128)S(1)} %get-tuple-element.23.state.state_in, s32[8,32,128]{2,1,0:T(8,128)S(1)} %get-tuple-element.19.kinds, f32[41,10,48,128]{3,2,1,0:T(8,128)S(1)} %get-tuple-element.24.out_in), custom_call_target="tpu_custom_call", output_to_operand_aliasing={{}: (2, {})} | custom-call | flops 6144000 | bytes 4030464 | tf_op jit(solution)/shard_map/second_step_inner_middle_rows/pallas_call | solution.py:510
  17.1 1.0 %collective-permute-done.4.cross_a = f32[88,128]{1,0:T(8,128)S(1)} collective-permute-done((f32[88,128]{1,0:T(8,128)S(1)}, f32[88,128]{1,0:T(8,128)S(1)}, u32[]{:S(2)}, u32[]{:S(2)}) %collective-permute-start.4) | collective-permute-done | bytes 45088 | tf_op jit(solution)/shard_map/ppermute | solution.py:474
  18.1 0.0 collective-permute-done.5.cross_b
  18.1 0.0 collective-permute-done.2.loop_a
  18.1 0.0 collective-permute-done.3.loop_b
  18.1 0.5 %second_step_edges_to_send.1 = (f32[41,10,48,128]{3,2,1,0:T(8,128)S(1)}, f32[41,10,48,128]{3,2,1,0:T(8,128)S(1)}, f32[11,32,128]{2,1,0:T(8,128)S(1)}, f32[11,32,128]{2,1,0:T(8,128)S(1)}) custom-call(f32[41,10,48,128]{3,2,1,0:T(8,128)S(1)} %get-tuple-element.23.state.state_in, ...), custom_call_target="tpu_custom_call", output_to_operand_aliasing={{0}: (0, {}), {1}: (1, {})} | custom-call | flops 4608000 | bytes 3022848 | tf_op jit(solution)/shard_map/second_step_edges_to_send/pallas_call | solution.py:510
  18.6 1.2 %collective-permute-start.6 = (f32[11,32,128]{2,1,0:T(8,128)S(1)}, f32[11,32,128]{2,1,0:T(8,128)S(1)}, u32[]{:S(2)}, u32[]{:S(2)}) collective-permute-start(f32[11,32,128]{2,1,0:T(8,128)S(1)} %get-tuple-element.34), channel_id=1, source_target_pairs={{4,8},{8,4},{12,16},{16,12},{20,24},{24,20},{28,0},{0,28},{5,9},{9... | collective-permute-start | bytes 540680 | tf_op jit(solution)/shard_map/ppermute | solution.py:485
  19.8 0.5 %collective-permute-start.7 = (f32[11,32,128]{2,1,0:T(8,128)S(1)}, f32[11,32,128]{2,1,0:T(8,128)S(1)}, u32[]{:S(2)}, u32[]{:S(2)}) collective-permute-start(f32[11,32,128]{2,1,0:T(8,128)S(1)} %get-tuple-element.35), channel_id=1, source_target_pairs={{0,4},{4,0},{8,12},{12,8},{16,20},{20,16},{24,28},{28,24},{1,5},{5... | collective-permute-start | bytes 540680 | tf_op jit(solution)/shard_map/ppermute | solution.py:485
  20.3 2.5 %second_step_edges_rest_and_write.1 = (f32[41,10,48,128]{3,2,1,0:T(8,128)S(1)}, f32[27,8,32,128]{3,2,1,0:T(8,128)}, f32[14,8,32,128]{3,2,1,0:T(8,128)}) custom-call(f32[41,10,48,128]{3,2,1,0:T(8,128)S(1)} %get-tuple-element.30.state, f32[41,10,48,128]{3,2,1,0:T(8,128)S(1)} %get-tuple-element.31.out_in, ...), custom_call_target="tpu_custom_call", output_to_operand_aliasing={{0}: (1, {})} | custom-call | flops 4608000 | bytes 13770752 | tf_op jit(solution)/shard_map/second_step_edges_rest_and_write/pallas_call | solution.py:510
  22.8 3.4 %collective-permute-done.6.got_a = f32[11,32,128]{2,1,0:T(8,128)S(1)} collective-permute-done((f32[11,32,128]{2,1,0:T(8,128)S(1)}, f32[11,32,128]{2,1,0:T(8,128)S(1)}, u32[]{:S(2)}, u32[]{:S(2)}) %collective-permute-start.6) | collective-permute-done | bytes 180256 | tf_op jit(solution)/shard_map/ppermute | solution.py:485
  26.2 0.0 collective-permute-done.7.got_b
  26.2 0.9 %write_edge_planes.1 = (f32[27,8,32,128]{3,2,1,0:T(8,128)}, f32[14,8,32,128]{3,2,1,0:T(8,128)}) custom-call(f32[27,8,32,128]{3,2,1,0:T(8,128)} %get-tuple-element.32.pops_in, f32[14,8,32,128]{3,2,1,0:T(8,128)} %get-tuple-element.33.scal_in, f32[11,32,128]{2,1,0:T(8,128)S(1)} %collective-permute-done.6.got_a, ...), custom_call_target="tpu_custom_call", output_to_operand_aliasing={{0}: (0, {}), {1}: (1, {})} | custom-call | bytes 720896 | tf_op jit(solution)/shard_map/write_edge_planes/pallas_call | solution.py:510
Async XLA Ops:
  4.2 5.7 %collective-permute-start = (f32[152,128]{1,0:T(8,128)S(1)}, f32[152,128]{1,0:T(8,128)S(1)}, u32[]{:S(2)}, u32[]{:S(2)}) collective-permute-start(f32[152,128]{1,0:T(8,128)S(1)} %get-tuple-element.21), channel_id=1, source_target_pairs={{0,1},{1,0},{2,3},{3,2},{4,5},{5,4},{6,7},{7,6},{8,9},{9,8},{10,11... | collective-permute-start | bytes 233480 | tf_op jit(solution)/shard_map/ppermute | solution.py:474
  7.3 2.6 %collective-permute-start.1 = (f32[152,128]{1,0:T(8,128)S(1)}, f32[152,128]{1,0:T(8,128)S(1)}, u32[]{:S(2)}, u32[]{:S(2)}) collective-permute-start(f32[152,128]{1,0:T(8,128)S(1)} %get-tuple-element.22), channel_id=1, source_target_pairs={{0,4},{1,2},{2,1},{3,7},{4,0},{5,6},{6,5},{7,3},{8,12},{9,10},{10,... | collective-permute-start | bytes 233480 | tf_op jit(solution)/shard_map/ppermute | solution.py:474
  10.1 8.1 %collective-permute-start.2 = (f32[376,128]{1,0:T(8,128)S(1)}, f32[376,128]{1,0:T(8,128)S(1)}, u32[]{:S(2)}, u32[]{:S(2)}) collective-permute-start(f32[376,128]{1,0:T(8,128)S(1)} %get-tuple-element.26), channel_id=1, source_target_pairs={{4,8},{8,4},{12,16},{16,12},{20,24},{24,20},{28,0},{0,28},{5,9},{9... | collective-permute-start | bytes 577544 | tf_op jit(solution)/shard_map/ppermute | solution.py:485
  12.7 5.4 %collective-permute-start.3 = (f32[376,128]{1,0:T(8,128)S(1)}, f32[376,128]{1,0:T(8,128)S(1)}, u32[]{:S(2)}, u32[]{:S(2)}) collective-permute-start(f32[376,128]{1,0:T(8,128)S(1)} %get-tuple-element.27), channel_id=1, source_target_pairs={{0,4},{4,0},{8,12},{12,8},{16,20},{20,16},{24,28},{28,24},{1,5},{5... | collective-permute-start | bytes 577544 | tf_op jit(solution)/shard_map/ppermute | solution.py:485
  13.8 4.3 %collective-permute-start.4 = (f32[88,128]{1,0:T(8,128)S(1)}, f32[88,128]{1,0:T(8,128)S(1)}, u32[]{:S(2)}, u32[]{:S(2)}) collective-permute-start(f32[88,128]{1,0:T(8,128)S(1)} %get-tuple-element.28), channel_id=1, source_target_pairs={{0,1},{1,0},{2,3},{3,2},{4,5},{5,4},{6,7},{7,6},{8,9},{9,8},{10,11... | collective-permute-start | bytes 135176 | tf_op jit(solution)/shard_map/ppermute | solution.py:474
  16.1 2.0 %collective-permute-start.5 = (f32[88,128]{1,0:T(8,128)S(1)}, f32[88,128]{1,0:T(8,128)S(1)}, u32[]{:S(2)}, u32[]{:S(2)}) collective-permute-start(f32[88,128]{1,0:T(8,128)S(1)} %get-tuple-element.29), channel_id=1, source_target_pairs={{0,4},{1,2},{2,1},{3,7},{4,0},{5,6},{6,5},{7,3},{8,12},{9,10},{10,... | collective-permute-start | bytes 135176 | tf_op jit(solution)/shard_map/ppermute | solution.py:474
  18.6 7.6 %collective-permute-start.6 = (f32[11,32,128]{2,1,0:T(8,128)S(1)}, f32[11,32,128]{2,1,0:T(8,128)S(1)}, u32[]{:S(2)}, u32[]{:S(2)}) collective-permute-start(f32[11,32,128]{2,1,0:T(8,128)S(1)} %get-tuple-element.34), channel_id=1, source_target_pairs={{4,8},{8,4},{12,16},{16,12},{20,24},{24,20},{28,0},{0,28},{5,9},{9... | collective-permute-start | bytes 540680 | tf_op jit(solution)/shard_map/ppermute | solution.py:485
  19.8 6.4 %collective-permute-start.7 = (f32[11,32,128]{2,1,0:T(8,128)S(1)}, f32[11,32,128]{2,1,0:T(8,128)S(1)}, u32[]{:S(2)}, u32[]{:S(2)}) collective-permute-start(f32[11,32,128]{2,1,0:T(8,128)S(1)} %get-tuple-element.35), channel_id=1, source_target_pairs={{0,4},{4,0},{8,12},{12,8},{16,20},{20,16},{24,28},{28,24},{1,5},{5... | collective-permute-start | bytes 540680 | tf_op jit(solution)/shard_map/ppermute | solution.py:485

commit v11 on v10

--- a/solution.py
+++ b/solution.py
@@ -179,6 +179,10 @@
     return (first >= 0) & (first + 1 < count)
 
 
+def starts_late():
+    return lax.rem((lax.axis_index("loop") + 1) // 2, 2) == 1
+
+
 def sizes_of(state):
     return state.shape[1] - 2, state.shape[2] - 2 * PAD
 
@@ -323,13 +327,13 @@
             collide_raw(raw, (x, y - SUB), kinds, state, x, y)
 
 
-def turn_kernel(state_in, got_a, got_b, state, halo_kinds, sent_a, sent_b):
+def turn_kernel(state_in, got_a, got_b, kinds, state, halo_kinds, sent, out):
     halo_kinds[...] = jnp.zeros(halo_kinds.shape, jnp.float32)
     for swap, got in zip(CROSS_SWAPS, (got_a, got_b)):
         partner = has_partner("cross", swap)
         by_swap("cross", swap, lambda side: take_first_cross(state, halo_kinds, -side, got, partner))
-    for swap, msg in zip(LOOP_SWAPS, (sent_a, sent_b)):
-        by_swap("loop", swap, lambda side: send_first_loop(state, side, msg))
+    by_swap("loop", LOOP_SWAPS[0], lambda side: send_first_loop(state, side, sent))
+    pl.when(starts_late())(lambda: collide_inner_sides(state, kinds, out))
 
 
 def collide_inner(state, kinds, out, tiles):
@@ -341,10 +345,15 @@
             collide(load_tile(state, x, y), kinds[x, y : y + SUB, :], push_tile(out, x, y))
 
 
-def inner_side_kernel(state, kinds, out, sent_a, sent_b):
+def collide_inner_sides(state, kinds, out):
+    collide_inner(state, kinds, out, (0, sizes_of(state)[1] - SUB))
+
+
+def inner_side_kernel(state, kinds, out_in, out, near, sent_a, sent_b):
     size_x, size_y = sizes_of(state)
     rows, flat = out.shape[2], flat_of(out)
-    collide_inner(state, kinds, out, (0, size_y - SUB))
+    by_swap("loop", LOOP_SWAPS[1], lambda side: send_first_loop(state, side, near))
+    pl.when(jnp.logical_not(starts_late()))(lambda: collide_inner_sides(state, kinds, out))
 
     def send(b, msg):
         y_out = size_y if b > 0 else -1
@@ -383,8 +392,38 @@
     collide(lambda i: halo[i], code - 1, put, want)
 
 
+def write_planes(out, pops, scal, sems, planes, then=None):
+    _, size_y = sizes_of(out)
+    copies = []
+    for x in planes:
+        inner = pl.ds(PAD, size_y)
+        copies.append(pltpu.make_async_copy(out.at[0:NF, slot(x), inner], pops.at[:, x], sems.at[0, x]))
+        copies.append(pltpu.make_async_copy(out.at[NF:NQ, slot(x), inner], scal.at[:, x], sems.at[1, x]))
+    for copy in copies:
+        copy.start()
+    if then is not None:
+        then()
+    for copy in copies:
+        copy.wait()
+
+
 def edge_kernel(
-    state_in, out_in, kinds, halo_kinds, loop_a, loop_b, cross_a, cross_b, state, out, sent_a, sent_b, halo
+    state_in,
+    out_in,
+    kinds,
+    halo_kinds,
+    loop_a,
+    loop_b,
+    cross_a,
+    cross_b,
+    state,
+    out,
+    sent_a,
+    sent_b,
+    pops,
+    scal,
+    halo,
+    sems,
 ):
     size_x, size_y = sizes_of(state)
     rows, flat_out = state.shape[2], flat_of(out)
@@ -411,29 +450,23 @@
         partner = has_partner("cross", swap)
         by_swap("cross", swap, lambda side: take(-side, msg, partner))
 
-
-def write_kernel(state, out_in, kinds, halo_kinds, out, pops, scal, sems, halo):
-    size_x, size_y = sizes_of(out)
-
-    def copies(x):
-        inner = pl.ds(PAD, size_y)
-        return [
-            pltpu.make_async_copy(out.at[0:NF, slot(x), inner], pops.at[:, x], sems.at[0, x]),
-            pltpu.make_async_copy(out.at[NF:NQ, slot(x), inner], scal.at[:, x], sems.at[1, x]),
-        ]
-
+    @pl.when(starts_late())
+    def _():
+        rest = functools.partial(collide_edges, state, kinds, halo_kinds, out, halo, False)
+        write_planes(out, pops, scal, sems, range(2, size_x - 2), rest)
+
+
+def write_kernel(state, out_in, kinds, halo_kinds, pops_in, scal_in, out, pops, scal, sems, halo):
+    size_x, _ = sizes_of(out)
     done = range(2, size_x - 2)
     late = [x for x in range(size_x) if x not in done]
-    for x in done:
-        for copy in copies(x):
-            copy.start()
-    collide_edges(state, kinds, halo_kinds, out, halo, False)
-    for x in late:
-        for copy in copies(x):
-            copy.start()
-    for x in range(size_x):
-        for copy in copies(x):
-            copy.wait()
+
+    @pl.when(jnp.logical_not(starts_late()))
+    def _():
+        rest = functools.partial(collide_edges, state, kinds, halo_kinds, out, halo, False)
+        write_planes(out, pops, scal, sems, done, rest)
+
+    write_planes(out, pops, scal, sems, late)
 
 
 def last_kernel(pops_in, scal_in, got_a, got_b, pops, scal, sems):
@@ -475,15 +508,12 @@
     return received
 
 
-def swap_loop(messages):
-    count, received = lax.axis_size("loop"), []
-    for swap, cells in zip(LOOP_SWAPS, messages):
-        pairs = []
-        for i in range(swap, count, 2):
-            j = (i + 1) % count
-            pairs += [(i, j), (j, i)]
-        received.append(lax.ppermute(cells, "loop", pairs))
-    return received
+def swap_loop(swap, cells):
+    count, pairs = lax.axis_size("loop"), []
+    for i in range(swap, count, 2):
+        j = (i + 1) % count
+        pairs += [(i, j), (j, i)]
+    return lax.ppermute(cells, "loop", pairs)
 
 
 def per_device(populations, scalars, node_flags):
@@ -493,7 +523,7 @@
     kinds_shape = pltpu.VMEM((size_x, size_y, size_z), jnp.int32)
     halo_kinds_shape = pltpu.VMEM((SUB, size_z), f32)
     cross_1 = [pltpu.VMEM((first_cross_rows(size_x)[1], size_z), f32)] * 2
-    loop_1 = [pltpu.VMEM((first_loop_rows(size_y)[1], size_z), f32)] * 2
+    loop_1 = pltpu.VMEM((first_loop_rows(size_y)[1], size_z), f32)
     cross_2 = [pltpu.VMEM((len(Y_SETS[1]) * SUB, size_z), f32)] * 2
     loop_2 = [pltpu.VMEM((len(X_SETS[1]), size_y, size_z), f32)] * 2
     hbm = pl.BlockSpec(memory_space=pl.ANY)
@@ -554,22 +584,24 @@
             ],
             aliases={3: 0},
         )
-    state, halo_kinds, *sent = call(
+    state, halo_kinds, far, out = call(
         turn_kernel,
         "cross_to_loop",
-        on_chip(state, *received),
-        [state_shape, halo_kinds_shape] + loop_1,
-        tiles=1,
+        on_chip(state, *received, kinds),
+        [state_shape, halo_kinds_shape, loop_1, state_shape],
+        tiles=size_x - 2,
         aliases={0: 0},
     )
-    from_loop = swap_loop(sent)
-    out, *sent = call(
+    from_far = swap_loop(LOOP_SWAPS[0], far)
+    out, near, *sent = call(
         inner_side_kernel,
         "second_step_inner_side_rows",
-        on_chip(state, kinds),
-        [state_shape] + cross_2,
-        tiles=(size_x - 2) * 2,
+        on_chip(state, kinds, out),
+        [state_shape, loop_1] + cross_2,
+        tiles=size_x - 2,
+        aliases={2: 0},
     )
+    from_near = swap_loop(LOOP_SWAPS[1], near)
     from_cross = swap_cross(sent)
     if tiles > 2:
         (out,) = call(
@@ -581,25 +613,26 @@
             aliases={2: 0},
         )
     halo = pltpu.VMEM((NQ, SUB, size_z), f32)
-    state, out, *sent = call(
+    write_sems = pltpu.SemaphoreType.DMA((2, size_x))
+    state, out, far, near, new_pops, new_scal = call(
         edge_kernel,
         "second_step_edges_to_send",
-        on_chip(state, out, kinds, halo_kinds, *from_loop, *from_cross),
-        [state_shape, state_shape] + loop_2,
+        on_chip(state, out, kinds, halo_kinds, from_far, from_near, *from_cross),
+        [state_shape, state_shape] + loop_2 + [pops_shape, scal_shape],
         tiles=2 * tiles + 1,
-        scratch=[halo],
+        scratch=[halo, write_sems],
         aliases={0: 0, 1: 1},
     )
-    received = swap_loop(sent)
+    received = [swap_loop(swap, cells) for swap, cells in zip(LOOP_SWAPS, (far, near))]
     _, new_pops, new_scal = call(
         write_kernel,
         "second_step_edges_rest_and_write",
-        on_chip(state, out, kinds, halo_kinds),
+        on_chip(state, out, kinds, halo_kinds) + in_hbm(new_pops, new_scal),
         [state_shape, pops_shape, scal_shape],
         tiles=2 * tiles + 1,
         moved=8 * NQ * size_x * size_y * size_z,
-        scratch=[pltpu.SemaphoreType.DMA((2, size_x)), halo],
-        aliases={1: 0},
+        scratch=[write_sems, halo],
+        aliases={1: 0, 4: 1, 5: 2},
     )
     new_pops, new_scal = call(
         last_kernel,

time: 27.3 us -> 27.9 us (1.022)
  the two profiles are of different devices: /device:TPU:0 before, /device:TPU:17 now
where the time goes in v11:
time: 27.9 us; the launch traced here: 27.7 us
  Pallas kernels  13.2 us (47%)
  waiting for transfers between devices  8.42 us (30%)
  starting transfers between devices  5.39 us (19%)
  between operations  0.7 us (3%)
    pallas_call x8, Pallas kernels, call(): pl.pallas_call(kernel, out_shape=results, in_specs=specs, out_specs=[hbm...  13.2 us
    ppermute x4, waiting for transfers between devices, swap_loop(): return lax.ppermute(cells, 'loop', pairs)  5.59 us
    ppermute x4, starting transfers between devices, swap_loop(): return lax.ppermute(cells, 'loop', pairs)  3.85 us
    ppermute x4, waiting for transfers between devices, swap_cross(): received.append(lax.ppermute(cells, ('loop', 'cross'), pairs))  2.84 us
    ppermute x4, starting transfers between devices, swap_cross(): received.append(lax.ppermute(cells, ('loop', 'cross'), pairs))  1.55 us
  transfers between devices with their start and end apart: 8, of which 5 were waited for; matrix products, arithmetic and copies ran while one was open for 0% of the time, Pallas kernels for 19%

profile of v11, /device:TPU:17, one launch (start us, length us, event | category | flops | bytes accessed | tf_op | source)
XLA Modules:
  0.0 27.7 jit_solution(1022330431754860294)
XLA Ops:
  0.6 3.6 %first_step_side_rows.1 = (f32[41,10,48,128]{3,2,1,0:T(8,128)S(1)}, s32[8,32,128]{2,1,0:T(8,128)S(1)}, f32[152,128]{1,0:T(8,128)S(1)}, f32[152,128]{1,0:T(8,128)S(1)}) custom-call(f32[27,8,32,128]{3,2,1,0:T(8,128)} %pops.3, f32[14,8,32,128]{3,2,1,0:T(8,128)} %scal.3, s32[8,32,128]{2,1,0:T(8,128)} %flags.1), custom_call_target="tpu_custom_call" | custom-call | flops 8192000 | bytes 5373952 | tf_op jit(solution)/shard_map/first_step_side_rows/pallas_call | solution.py:540
  4.2 1.3 %collective-permute-start = (f32[152,128]{1,0:T(8,128)S(1)}, f32[152,128]{1,0:T(8,128)S(1)}, u32[]{:S(2)}, u32[]{:S(2)}) collective-permute-start(f32[152,128]{1,0:T(8,128)S(1)} %get-tuple-element.24), channel_id=1, source_target_pairs={{0,1},{1,0},{2,3},{3,2},{4,5},{5,4},{6,7},{7,6},{8,9},{9,8},{10,11... | collective-permute-start | bytes 233480 | tf_op jit(solution)/shard_map/ppermute | solution.py:507
  5.5 0.0 collective-permute-start.1
  5.6 2.6 %first_step_middle_rows.1.state_in = f32[41,10,48,128]{3,2,1,0:T(8,128)S(1)} custom-call(f32[27,8,32,128]{3,2,1,0:T(8,128)} %pops.3, f32[14,8,32,128]{3,2,1,0:T(8,128)} %scal.3, s32[8,32,128]{2,1,0:T(8,128)S(1)} %get-tuple-element.22.kinds, f32[41,10,48,128]{3,2,1,0:T(8,128)S(1)} %get-tuple-element.23.state_in), custom_call_target="tpu_custom_call", output_to_operand_aliasing={{}: (3, {})} | custom-call | flops 8192000 | bytes 5373952 | tf_op jit(solution)/shard_map/first_step_middle_rows/pallas_call | solution.py:540
  8.2 0.0 collective-permute-done.got_a
  8.2 0.8 %collective-permute-done.1.got_b = f32[152,128]{1,0:T(8,128)S(1)} collective-permute-done((f32[152,128]{1,0:T(8,128)S(1)}, f32[152,128]{1,0:T(8,128)S(1)}, u32[]{:S(2)}, u32[]{:S(2)}) %collective-permute-start.1) | collective-permute-done | bytes 77856 | tf_op jit(solution)/shard_map/ppermute | solution.py:507
  9.0 1.2 %cross_to_loop.1 = (f32[41,10,48,128]{3,2,1,0:T(8,128)S(1)}, f32[8,128]{1,0:T(8,128)S(1)}, f32[376,128]{1,0:T(8,128)S(1)}, f32[41,10,48,128]{3,2,1,0:T(8,128)S(1)}) custom-call(f32[41,10,48,128]{3,2,1,0:T(8,128)S(1)} %first_step_middle_rows.1.state_in, f32[152,128]{1,0:T(8,128)S(1)} %collective-permute-done.got_a, ...), custom_call_target="tpu_custom_call", output_to_operand_aliasing={{0}: (0, {})} | custom-call | flops 3072000 | bytes 2015232 | tf_op jit(solution)/shard_map/cross_to_loop/pallas_call | solution.py:540
  10.1 3.1 %collective-permute-start.2 = (f32[376,128]{1,0:T(8,128)S(1)}, f32[376,128]{1,0:T(8,128)S(1)}, u32[]{:S(2)}, u32[]{:S(2)}) collective-permute-start(f32[376,128]{1,0:T(8,128)S(1)} %get-tuple-element.30), channel_id=1, source_target_pairs={{4,8},{8,4},{12,16},{16,12},{20,24},{24,20},{28,0},{0,28},{5,9},{9... | collective-permute-start | bytes 577544 | tf_op jit(solution)/shard_map/ppermute | solution.py:516
  13.2 0.1 second_step_inner_side_rows.1
  13.3 0.1 collective-permute-start.3
  13.4 0.1 collective-permute-start.4
  13.5 0.1 collective-permute-start.5
  13.6 1.1 %second_step_inner_middle_rows.1.out_in = f32[41,10,48,128]{3,2,1,0:T(8,128)S(1)} custom-call(f32[41,10,48,128]{3,2,1,0:T(8,128)S(1)} %get-tuple-element.26.state.state_in, s32[8,32,128]{2,1,0:T(8,128)S(1)} %get-tuple-element.22.kinds, f32[41,10,48,128]{3,2,1,0:T(8,128)S(1)} %get-tuple-element.28.out_in), custom_call_target="tpu_custom_call", output_to_operand_aliasing={{}: (2, {})} | custom-call | flops 6144000 | bytes 4030464 | tf_op jit(solution)/shard_map/second_step_inner_middle_rows/pallas_call | solution.py:540
  14.7 2.0 %collective-permute-done.4.cross_a = f32[88,128]{1,0:T(8,128)S(1)} collective-permute-done((f32[88,128]{1,0:T(8,128)S(1)}, f32[88,128]{1,0:T(8,128)S(1)}, u32[]{:S(2)}, u32[]{:S(2)}) %collective-permute-start.4) | collective-permute-done | bytes 45088 | tf_op jit(solution)/shard_map/ppermute | solution.py:507
  16.7 0.1 collective-permute-done.5.cross_b
  16.7 1.7 %collective-permute-done.2.loop_a = f32[376,128]{1,0:T(8,128)S(1)} collective-permute-done((f32[376,128]{1,0:T(8,128)S(1)}, f32[376,128]{1,0:T(8,128)S(1)}, u32[]{:S(2)}, u32[]{:S(2)}) %collective-permute-start.2) | collective-permute-done | bytes 192544 | tf_op jit(solution)/shard_map/ppermute | solution.py:516
  18.5 0.0 collective-permute-done.3.loop_b
  18.5 2.1 %second_step_edges_to_send.1 = (f32[41,10,48,128]{3,2,1,0:T(8,128)S(1)}, f32[41,10,48,128]{3,2,1,0:T(8,128)S(1)}, f32[11,32,128]{2,1,0:T(8,128)S(1)}, f32[11,32,...) custom-call(f32[41,10,48,128]{3,2,1,0:T(8,128)S(1)} %get-tuple-eleme, ...), custom_call_target="tpu_custom_call", output_to_operand_aliasing={{0}: (0, {}), {1}: (1, {})} | custom-call | flops 4608000 | bytes 3022848 | tf_op jit(solution)/shard_map/second_step_edges_to_send/pallas_call | solution.py:540
  20.6 0.7 %collective-permute-start.6 = (f32[11,32,128]{2,1,0:T(8,128)S(1)}, f32[11,32,128]{2,1,0:T(8,128)S(1)}, u32[]{:S(2)}, u32[]{:S(2)}) collective-permute-start(f32[11,32,128]{2,1,0:T(8,128)S(1)} %get-tuple-element.40), channel_id=1, source_target_pairs={{4,8},{8,4},{12,16},{16,12},{20,24},{24,20},{28,0},{0,28},{5,9},{9... | collective-permute-start | bytes 540680 | tf_op jit(solution)/shard_map/ppermute | solution.py:516
  21.3 0.0 collective-permute-start.7
  21.3 1.6 %second_step_edges_rest_and_write.1 = (f32[41,10,48,128]{3,2,1,0:T(8,128)S(1)}, f32[27,8,32,128]{3,2,1,0:T(8,128)}, f32[14,8,32,128]{3,2,1,0:T(8,128)}) custom-call(f32[41,10,48,128]{3,2,1,0:T(8,128)S(1)} %get-tuple-element.34.state, f32[41,10,48,128]{3,2,1,0:T(8,128)S(1)} %get-tuple-element.35.out_in, ...), custom_call_target="tpu_custom_call", output_to_operand_aliasing={{0}: (1, {}), {1}: (4, {}), {2}: (5, {})} | custom-call | flops 4608000 | bytes 13770752 | tf_op jit(solution)/shard_map/second_step_edges_rest_and_write/pallas_call | solution.py:540
  22.9 3.8 %collective-permute-done.6.got_a = f32[11,32,128]{2,1,0:T(8,128)S(1)} collective-permute-done((f32[11,32,128]{2,1,0:T(8,128)S(1)}, f32[11,32,128]{2,1,0:T(8,128)S(1)}, u32[]{:S(2)}, u32[]{:S(2)}) %collective-permute-start.6) | collective-permute-done | bytes 180256 | tf_op jit(solution)/shard_map/ppermute | solution.py:516
  26.8 0.0 collective-permute-done.7.got_b
  26.8 0.9 %write_edge_planes.1 = (f32[27,8,32,128]{3,2,1,0:T(8,128)}, f32[14,8,32,128]{3,2,1,0:T(8,128)}) custom-call(f32[27,8,32,128]{3,2,1,0:T(8,128)} %get-tuple-element.38.pops_in, f32[14,8,32,128]{3,2,1,0:T(8,128)} %get-tuple-element.39.scal_in, f32[11,32,128]{2,1,0:T(8,128)S(1)} %collective-permute-done.6.got_a, ...), custom_call_target="tpu_custom_call", output_to_operand_aliasing={{0}: (0, {}), {1}: (1, {})} | custom-call | bytes 720896 | tf_op jit(solution)/shard_map/write_edge_planes/pallas_call | solution.py:540
Async XLA Ops:
  4.2 4.0 %collective-permute-start = (f32[152,128]{1,0:T(8,128)S(1)}, f32[152,128]{1,0:T(8,128)S(1)}, u32[]{:S(2)}, u32[]{:S(2)}) collective-permute-start(f32[152,128]{1,0:T(8,128)S(1)} %get-tuple-element.24), channel_id=1, source_target_pairs={{0,1},{1,0},{2,3},{3,2},{4,5},{5,4},{6,7},{7,6},{8,9},{9,8},{10,11... | collective-permute-start | bytes 233480 | tf_op jit(solution)/shard_map/ppermute | solution.py:507
  5.5 3.4 %collective-permute-start.1 = (f32[152,128]{1,0:T(8,128)S(1)}, f32[152,128]{1,0:T(8,128)S(1)}, u32[]{:S(2)}, u32[]{:S(2)}) collective-permute-start(f32[152,128]{1,0:T(8,128)S(1)} %get-tuple-element.25), channel_id=1, source_target_pairs={{0,4},{1,2},{2,1},{3,7},{4,0},{5,6},{6,5},{7,3},{8,12},{9,10},{10,... | collective-permute-start | bytes 233480 | tf_op jit(solution)/shard_map/ppermute | solution.py:507
  10.1 8.3 %collective-permute-start.2 = (f32[376,128]{1,0:T(8,128)S(1)}, f32[376,128]{1,0:T(8,128)S(1)}, u32[]{:S(2)}, u32[]{:S(2)}) collective-permute-start(f32[376,128]{1,0:T(8,128)S(1)} %get-tuple-element.30), channel_id=1, source_target_pairs={{4,8},{8,4},{12,16},{16,12},{20,24},{24,20},{28,0},{0,28},{5,9},{9... | collective-permute-start | bytes 577544 | tf_op jit(solution)/shard_map/ppermute | solution.py:516
  13.3 5.1 %collective-permute-start.3 = (f32[376,128]{1,0:T(8,128)S(1)}, f32[376,128]{1,0:T(8,128)S(1)}, u32[]{:S(2)}, u32[]{:S(2)}) collective-permute-start(f32[376,128]{1,0:T(8,128)S(1)} %get-tuple-element.31), channel_id=1, source_target_pairs={{0,4},{4,0},{8,12},{12,8},{16,20},{20,16},{24,28},{28,24},{1,5},{5... | collective-permute-start | bytes 577544 | tf_op jit(solution)/shard_map/ppermute | solution.py:516
  13.4 3.3 %collective-permute-start.4 = (f32[88,128]{1,0:T(8,128)S(1)}, f32[88,128]{1,0:T(8,128)S(1)}, u32[]{:S(2)}, u32[]{:S(2)}) collective-permute-start(f32[88,128]{1,0:T(8,128)S(1)} %get-tuple-element.32), channel_id=1, source_target_pairs={{0,1},{1,0},{2,3},{3,2},{4,5},{5,4},{6,7},{7,6},{8,9},{9,8},{10,11... | collective-permute-start | bytes 135176 | tf_op jit(solution)/shard_map/ppermute | solution.py:507
  13.5 3.3 %collective-permute-start.5 = (f32[88,128]{1,0:T(8,128)S(1)}, f32[88,128]{1,0:T(8,128)S(1)}, u32[]{:S(2)}, u32[]{:S(2)}) collective-permute-start(f32[88,128]{1,0:T(8,128)S(1)} %get-tuple-element.33), channel_id=1, source_target_pairs={{0,4},{1,2},{2,1},{3,7},{4,0},{5,6},{6,5},{7,3},{8,12},{9,10},{10,... | collective-permute-start | bytes 135176 | tf_op jit(solution)/shard_map/ppermute | solution.py:507
  20.6 6.2 %collective-permute-start.6 = (f32[11,32,128]{2,1,0:T(8,128)S(1)}, f32[11,32,128]{2,1,0:T(8,128)S(1)}, u32[]{:S(2)}, u32[]{:S(2)}) collective-permute-start(f32[11,32,128]{2,1,0:T(8,128)S(1)} %get-tuple-element.40), channel_id=1, source_target_pairs={{4,8},{8,4},{12,16},{16,12},{20,24},{24,20},{28,0},{0,28},{5,9},{9... | collective-permute-start | bytes 540680 | tf_op jit(solution)/shard_map/ppermute | solution.py:516
  21.3 5.5 %collective-permute-start.7 = (f32[11,32,128]{2,1,0:T(8,128)S(1)}, f32[11,32,128]{2,1,0:T(8,128)S(1)}, u32[]{:S(2)}, u32[]{:S(2)}) collective-permute-start(f32[11,32,128]{2,1,0:T(8,128)S(1)} %get-tuple-element.41), channel_id=1, source_target_pairs={{0,4},{4,0},{8,12},{12,8},{16,20},{20,16},{24,28},{28,24},{1,5},{5... | collective-permute-start | bytes 540680 | tf_op jit(solution)/shard_map/ppermute | solution.py:516

commit v12 on v11

--- a/solution.py
+++ b/solution.py
@@ -333,27 +333,24 @@
         partner = has_partner("cross", swap)
         by_swap("cross", swap, lambda side: take_first_cross(state, halo_kinds, -side, got, partner))
     by_swap("loop", LOOP_SWAPS[0], lambda side: send_first_loop(state, side, sent))
-    pl.when(starts_late())(lambda: collide_inner_sides(state, kinds, out))
-
-
-def collide_inner(state, kinds, out, tiles):
-    size_x, _ = sizes_of(state)
-
-    @pl.loop(1, size_x - 1)
+    size_x, size_y = sizes_of(state)
+    pl.when(starts_late())(lambda: collide_inner(state, kinds, out, (0, size_y - SUB), 1, size_x // 2))
+
+
+def collide_inner(state, kinds, out, tiles, first, last):
+    @pl.loop(first, last)
     def _(x):
         for y in tiles:
             collide(load_tile(state, x, y), kinds[x, y : y + SUB, :], push_tile(out, x, y))
 
 
-def collide_inner_sides(state, kinds, out):
-    collide_inner(state, kinds, out, (0, sizes_of(state)[1] - SUB))
-
-
 def inner_side_kernel(state, kinds, out_in, out, near, sent_a, sent_b):
     size_x, size_y = sizes_of(state)
     rows, flat = out.shape[2], flat_of(out)
     by_swap("loop", LOOP_SWAPS[1], lambda side: send_first_loop(state, side, near))
-    pl.when(jnp.logical_not(starts_late()))(lambda: collide_inner_sides(state, kinds, out))
+    sides = 0, size_y - SUB
+    pl.when(jnp.logical_not(starts_late()))(lambda: collide_inner(state, kinds, out, sides, 1, size_x // 2))
+    collide_inner(state, kinds, out, sides, size_x // 2, size_x - 1)
 
     def send(b, msg):
         y_out = size_y if b > 0 else -1
@@ -365,8 +362,8 @@
 
 
 def inner_middle_kernel(state, kinds, out_in, out):
-    _, size_y = sizes_of(state)
-    collide_inner(state, kinds, out, range(SUB, size_y - SUB, SUB))
+    size_x, size_y = sizes_of(state)
+    collide_inner(state, kinds, out, range(SUB, size_y - SUB, SUB), 1, size_x - 1)
 
 
 def collide_edges(state, kinds, halo_kinds, out, halo, sent):
@@ -390,21 +387,6 @@
 
     want = [i for i, d in enumerate(DIRS) if d[1] and bool(d[0]) == sent]
     collide(lambda i: halo[i], code - 1, put, want)
-
-
-def write_planes(out, pops, scal, sems, planes, then=None):
-    _, size_y = sizes_of(out)
-    copies = []
-    for x in planes:
-        inner = pl.ds(PAD, size_y)
-        copies.append(pltpu.make_async_copy(out.at[0:NF, slot(x), inner], pops.at[:, x], sems.at[0, x]))
-        copies.append(pltpu.make_async_copy(out.at[NF:NQ, slot(x), inner], scal.at[:, x], sems.at[1, x]))
-    for copy in copies:
-        copy.start()
-    if then is not None:
-        then()
-    for copy in copies:
-        copy.wait()
 
 
 def edge_kernel(
@@ -420,10 +402,7 @@
     out,
     sent_a,
     sent_b,
-    pops,
-    scal,
     halo,
-    sems,
 ):
     size_x, size_y = sizes_of(state)
     rows, flat_out = state.shape[2], flat_of(out)
@@ -450,23 +429,31 @@
         partner = has_partner("cross", swap)
         by_swap("cross", swap, lambda side: take(-side, msg, partner))
 
-    @pl.when(starts_late())
-    def _():
-        rest = functools.partial(collide_edges, state, kinds, halo_kinds, out, halo, False)
-        write_planes(out, pops, scal, sems, range(2, size_x - 2), rest)
-
-
-def write_kernel(state, out_in, kinds, halo_kinds, pops_in, scal_in, out, pops, scal, sems, halo):
-    size_x, _ = sizes_of(out)
+    pl.when(starts_late())(lambda: collide_edges(state, kinds, halo_kinds, out, halo, False))
+
+
+def write_kernel(state, out_in, kinds, halo_kinds, out, pops, scal, sems, halo):
+    size_x, size_y = sizes_of(out)
+    inner = pl.ds(PAD, size_y)
+    copies = [
+        [
+            pltpu.make_async_copy(out.at[0:NF, slot(x), inner], pops.at[:, x], sems.at[0, x]),
+            pltpu.make_async_copy(out.at[NF:NQ, slot(x), inner], scal.at[:, x], sems.at[1, x]),
+        ]
+        for x in range(size_x)
+    ]
     done = range(2, size_x - 2)
     late = [x for x in range(size_x) if x not in done]
-
-    @pl.when(jnp.logical_not(starts_late()))
-    def _():
-        rest = functools.partial(collide_edges, state, kinds, halo_kinds, out, halo, False)
-        write_planes(out, pops, scal, sems, done, rest)
-
-    write_planes(out, pops, scal, sems, late)
+    for x in done:
+        for copy in copies[x]:
+            copy.start()
+    pl.when(jnp.logical_not(starts_late()))(lambda: collide_edges(state, kinds, halo_kinds, out, halo, False))
+    for x in late:
+        for copy in copies[x]:
+            copy.start()
+    for x in range(size_x):
+        for copy in copies[x]:
+            copy.wait()
 
 
 def last_kernel(pops_in, scal_in, got_a, got_b, pops, scal, sems):
@@ -613,26 +600,25 @@
             aliases={2: 0},
         )
     halo = pltpu.VMEM((NQ, SUB, size_z), f32)
-    write_sems = pltpu.SemaphoreType.DMA((2, size_x))
-    state, out, far, near, new_pops, new_scal = call(
+    state, out, far, near = call(
         edge_kernel,
         "second_step_edges_to_send",
         on_chip(state, out, kinds, halo_kinds, from_far, from_near, *from_cross),
-        [state_shape, state_shape] + loop_2 + [pops_shape, scal_shape],
+        [state_shape, state_shape] + loop_2,
         tiles=2 * tiles + 1,
-        scratch=[halo, write_sems],
+        scratch=[halo],
         aliases={0: 0, 1: 1},
     )
     received = [swap_loop(swap, cells) for swap, cells in zip(LOOP_SWAPS, (far, near))]
     _, new_pops, new_scal = call(
         write_kernel,
         "second_step_edges_rest_and_write",
-        on_chip(state, out, kinds, halo_kinds) + in_hbm(new_pops, new_scal),
+        on_chip(state, out, kinds, halo_kinds),
         [state_shape, pops_shape, scal_shape],
         tiles=2 * tiles + 1,
         moved=8 * NQ * size_x * size_y * size_z,
-        scratch=[write_sems, halo],
-        aliases={1: 0, 4: 1, 5: 2},
+        scratch=[pltpu.SemaphoreType.DMA((2, size_x)), halo],
+        aliases={1: 0},
     )
     new_pops, new_scal = call(
         last_kernel,

time: 27.9 us -> 27.2 us (0.975)
  the two profiles are of different devices: /device:TPU:17 before, /device:TPU:0 now
where the time goes in v12:
time: 27.2 us; the launch traced here: 27.1 us
  Pallas kernels  12.4 us (46%)
  starting transfers between devices  10.1 us (37%)
  waiting for transfers between devices  3.81 us (14%)
  between operations  0.71 us (3%)
    pallas_call x8, Pallas kernels, call(): pl.pallas_call(kernel, out_shape=results, in_specs=specs, out_specs=[hbm...  12.4 us
    ppermute x4, starting transfers between devices, swap_cross(): received.append(lax.ppermute(cells, ('loop', 'cross'), pairs))  5.25 us
    ppermute x4, starting transfers between devices, swap_loop(): return lax.ppermute(cells, 'loop', pairs)  4.87 us
    ppermute x4, waiting for transfers between devices, swap_loop(): return lax.ppermute(cells, 'loop', pairs)  2.81 us
    ppermute x4, waiting for transfers between devices, swap_cross(): received.append(lax.ppermute(cells, ('loop', 'cross'), pairs))  1 us
  transfers between devices with their start and end apart: 8, of which 2 were waited for; matrix products, arithmetic and copies ran while one was open for 0% of the time, Pallas kernels for 27%

profile of v12, /device:TPU:0, one launch (start us, length us, event | category | flops | bytes accessed | tf_op | source)
XLA Modules:
  0.0 27.1 jit_solution(16822719655788318259)
XLA Ops:
  0.6 3.6 %first_step_side_rows.1 = (f32[41,10,48,128]{3,2,1,0:T(8,128)S(1)}, s32[8,32,128]{2,1,0:T(8,128)S(1)}, f32[152,128]{1,0:T(8,128)S(1)}, f32[152,128]{1,0:T(8,128)S(1)}) custom-call(f32[27,8,32,128]{3,2,1,0:T(8,128)} %pops.3, f32[14,8,32,128]{3,2,1,0:T(8,128)} %scal.3, s32[8,32,128]{2,1,0:T(8,128)} %flags.1), custom_call_target="tpu_custom_call" | custom-call | flops 8192000 | bytes 5373952 | tf_op jit(solution)/shard_map/first_step_side_rows/pallas_call | solution.py:527
  4.2 3.1 %collective-permute-start = (f32[152,128]{1,0:T(8,128)S(1)}, f32[152,128]{1,0:T(8,128)S(1)}, u32[]{:S(2)}, u32[]{:S(2)}) collective-permute-start(f32[152,128]{1,0:T(8,128)S(1)} %get-tuple-element.22), channel_id=1, source_target_pairs={{0,1},{1,0},{2,3},{3,2},{4,5},{5,4},{6,7},{7,6},{8,9},{9,8},{10,11... | collective-permute-start | bytes 233480 | tf_op jit(solution)/shard_map/ppermute | solution.py:494
  7.3 0.0 collective-permute-start.1
  7.3 2.6 %first_step_middle_rows.1.state_in = f32[41,10,48,128]{3,2,1,0:T(8,128)S(1)} custom-call(f32[27,8,32,128]{3,2,1,0:T(8,128)} %pops.3, f32[14,8,32,128]{3,2,1,0:T(8,128)} %scal.3, s32[8,32,128]{2,1,0:T(8,128)S(1)} %get-tuple-element.20.kinds, f32[41,10,48,128]{3,2,1,0:T(8,128)S(1)} %get-tuple-element.21.state_in), custom_call_target="tpu_custom_call", output_to_operand_aliasing={{}: (3, {})} | custom-call | flops 8192000 | bytes 5373952 | tf_op jit(solution)/shard_map/first_step_middle_rows/pallas_call | solution.py:527
  9.9 0.0 collective-permute-done.got_a
  9.9 0.0 collective-permute-done.1.got_b
  9.9 0.1 cross_to_loop.1
  10.1 2.6 %collective-permute-start.2 = (f32[376,128]{1,0:T(8,128)S(1)}, f32[376,128]{1,0:T(8,128)S(1)}, u32[]{:S(2)}, u32[]{:S(2)}) collective-permute-start(f32[376,128]{1,0:T(8,128)S(1)} %get-tuple-element.28), channel_id=1, source_target_pairs={{4,8},{8,4},{12,16},{16,12},{20,24},{24,20},{28,0},{0,28},{5,9},{9... | collective-permute-start | bytes 577544 | tf_op jit(solution)/shard_map/ppermute | solution.py:503
  12.7 1.1 %second_step_inner_side_rows.1 = (f32[41,10,48,128]{3,2,1,0:T(8,128)S(1)}, f32[376,128]{1,0:T(8,128)S(1)}, f32[88,128]{1,0:T(8,128)S(1)}, f32[88,128]{1,0:T(8,128)S(1)}) custom-call(f32[41,10,48,128]{3,2,1,0:T(8,128)S(1)} %get-tuple-element.24.state.state_in, s32[8,32,128]{2,1,0:T(8,128)S(1)} %get-tuple-element.20.kinds, ...), custom_call_target="tpu_custom_call", output_to_operand_aliasing={{0}: (2, {})} | custom-call | flops 3072000 | bytes 2015232 | tf_op jit(solution)/shard_map/second_step_inner_side_rows/pallas_call | solution.py:527
  13.8 0.1 collective-permute-start.3
  13.9 2.2 %collective-permute-start.4 = (f32[88,128]{1,0:T(8,128)S(1)}, f32[88,128]{1,0:T(8,128)S(1)}, u32[]{:S(2)}, u32[]{:S(2)}) collective-permute-start(f32[88,128]{1,0:T(8,128)S(1)} %get-tuple-element.30), channel_id=1, source_target_pairs={{0,1},{1,0},{2,3},{3,2},{4,5},{5,4},{6,7},{7,6},{8,9},{9,8},{10,11... | collective-permute-start | bytes 135176 | tf_op jit(solution)/shard_map/ppermute | solution.py:494
  16.1 0.0 collective-permute-start.5
  16.1 1.1 %second_step_inner_middle_rows.1.out_in = f32[41,10,48,128]{3,2,1,0:T(8,128)S(1)} custom-call(f32[41,10,48,128]{3,2,1,0:T(8,128)S(1)} %get-tuple-element.24.state.state_in, s32[8,32,128]{2,1,0:T(8,128)S(1)} %get-tuple-element.20.kinds, f32[41,10,48,128]{3,2,1,0:T(8,128)S(1)} %get-tuple-element.26.out_in), custom_call_target="tpu_custom_call", output_to_operand_aliasing={{}: (2, {})} | custom-call | flops 6144000 | bytes 4030464 | tf_op jit(solution)/shard_map/second_step_inner_middle_rows/pallas_call | solution.py:527
  17.1 1.0 %collective-permute-done.4.cross_a = f32[88,128]{1,0:T(8,128)S(1)} collective-permute-done((f32[88,128]{1,0:T(8,128)S(1)}, f32[88,128]{1,0:T(8,128)S(1)}, u32[]{:S(2)}, u32[]{:S(2)}) %collective-permute-start.4) | collective-permute-done | bytes 45088 | tf_op jit(solution)/shard_map/ppermute | solution.py:494
  18.1 0.0 collective-permute-done.5.cross_b
  18.1 0.0 collective-permute-done.2.loop_a
  18.1 0.0 collective-permute-done.3.loop_b
  18.1 0.5 %second_step_edges_to_send.1 = (f32[41,10,48,128]{3,2,1,0:T(8,128)S(1)}, f32[41,10,48,128]{3,2,1,0:T(8,128)S(1)}, f32[11,32,128]{2,1,0:T(8,128)S(1)}, f32[11,32,128]{2,1,0:T(8,128)S(1)}) custom-call(f32[41,10,48,128]{3,2,1,0:T(8,128)S(1)} %get-tuple-element.24.state.state_in, ...), custom_call_target="tpu_custom_call", output_to_operand_aliasing={{0}: (0, {}), {1}: (1, {})} | custom-call | flops 4608000 | bytes 3022848 | tf_op jit(solution)/shard_map/second_step_edges_to_send/pallas_call | solution.py:527
  18.6 1.7 %collective-permute-start.6 = (f32[11,32,128]{2,1,0:T(8,128)S(1)}, f32[11,32,128]{2,1,0:T(8,128)S(1)}, u32[]{:S(2)}, u32[]{:S(2)}) collective-permute-start(f32[11,32,128]{2,1,0:T(8,128)S(1)} %get-tuple-element.36), channel_id=1, source_target_pairs={{4,8},{8,4},{12,16},{16,12},{20,24},{24,20},{28,0},{0,28},{5,9},{9... | collective-permute-start | bytes 540680 | tf_op jit(solution)/shard_map/ppermute | solution.py:503
  20.3 0.5 %collective-permute-start.7 = (f32[11,32,128]{2,1,0:T(8,128)S(1)}, f32[11,32,128]{2,1,0:T(8,128)S(1)}, u32[]{:S(2)}, u32[]{:S(2)}) collective-permute-start(f32[11,32,128]{2,1,0:T(8,128)S(1)} %get-tuple-element.37), channel_id=1, source_target_pairs={{0,4},{4,0},{8,12},{12,8},{16,20},{20,16},{24,28},{28,24},{1,5},{5... | collective-permute-start | bytes 540680 | tf_op jit(solution)/shard_map/ppermute | solution.py:503
  20.8 2.5 %second_step_edges_rest_and_write.1 = (f32[41,10,48,128]{3,2,1,0:T(8,128)S(1)}, f32[27,8,32,128]{3,2,1,0:T(8,128)}, f32[14,8,32,128]{3,2,1,0:T(8,128)}) custom-call(f32[41,10,48,128]{3,2,1,0:T(8,128)S(1)} %get-tuple-element.32.state, f32[41,10,48,128]{3,2,1,0:T(8,128)S(1)} %get-tuple-element.33.out_in, ...), custom_call_target="tpu_custom_call", output_to_operand_aliasing={{0}: (1, {})} | custom-call | flops 4608000 | bytes 13770752 | tf_op jit(solution)/shard_map/second_step_edges_rest_and_write/pallas_call | solution.py:527
  23.3 2.8 %collective-permute-done.6.got_a = f32[11,32,128]{2,1,0:T(8,128)S(1)} collective-permute-done((f32[11,32,128]{2,1,0:T(8,128)S(1)}, f32[11,32,128]{2,1,0:T(8,128)S(1)}, u32[]{:S(2)}, u32[]{:S(2)}) %collective-permute-start.6) | collective-permute-done | bytes 180256 | tf_op jit(solution)/shard_map/ppermute | solution.py:503
  26.1 0.0 collective-permute-done.7.got_b
  26.1 0.9 %write_edge_planes.1 = (f32[27,8,32,128]{3,2,1,0:T(8,128)}, f32[14,8,32,128]{3,2,1,0:T(8,128)}) custom-call(f32[27,8,32,128]{3,2,1,0:T(8,128)} %get-tuple-element.34.pops_in, f32[14,8,32,128]{3,2,1,0:T(8,128)} %get-tuple-element.35.scal_in, f32[11,32,128]{2,1,0:T(8,128)S(1)} %collective-permute-done.6.got_a, ...), custom_call_target="tpu_custom_call", output_to_operand_aliasing={{0}: (0, {}), {1}: (1, {})} | custom-call | bytes 720896 | tf_op jit(solution)/shard_map/write_edge_planes/pallas_call | solution.py:527
Async XLA Ops:
  4.2 5.7 %collective-permute-start = (f32[152,128]{1,0:T(8,128)S(1)}, f32[152,128]{1,0:T(8,128)S(1)}, u32[]{:S(2)}, u32[]{:S(2)}) collective-permute-start(f32[152,128]{1,0:T(8,128)S(1)} %get-tuple-element.22), channel_id=1, source_target_pairs={{0,1},{1,0},{2,3},{3,2},{4,5},{5,4},{6,7},{7,6},{8,9},{9,8},{10,11... | collective-permute-start | bytes 233480 | tf_op jit(solution)/shard_map/ppermute | solution.py:494
  7.3 2.6 %collective-permute-start.1 = (f32[152,128]{1,0:T(8,128)S(1)}, f32[152,128]{1,0:T(8,128)S(1)}, u32[]{:S(2)}, u32[]{:S(2)}) collective-permute-start(f32[152,128]{1,0:T(8,128)S(1)} %get-tuple-element.23), channel_id=1, source_target_pairs={{0,4},{1,2},{2,1},{3,7},{4,0},{5,6},{6,5},{7,3},{8,12},{9,10},{10,... | collective-permute-start | bytes 233480 | tf_op jit(solution)/shard_map/ppermute | solution.py:494
  10.1 8.1 %collective-permute-start.2 = (f32[376,128]{1,0:T(8,128)S(1)}, f32[376,128]{1,0:T(8,128)S(1)}, u32[]{:S(2)}, u32[]{:S(2)}) collective-permute-start(f32[376,128]{1,0:T(8,128)S(1)} %get-tuple-element.28), channel_id=1, source_target_pairs={{4,8},{8,4},{12,16},{16,12},{20,24},{24,20},{28,0},{0,28},{5,9},{9... | collective-permute-start | bytes 577544 | tf_op jit(solution)/shard_map/ppermute | solution.py:503
  13.8 4.3 %collective-permute-start.3 = (f32[376,128]{1,0:T(8,128)S(1)}, f32[376,128]{1,0:T(8,128)S(1)}, u32[]{:S(2)}, u32[]{:S(2)}) collective-permute-start(f32[376,128]{1,0:T(8,128)S(1)} %get-tuple-element.29), channel_id=1, source_target_pairs={{0,4},{4,0},{8,12},{12,8},{16,20},{20,16},{24,28},{28,24},{1,5},{5... | collective-permute-start | bytes 577544 | tf_op jit(solution)/shard_map/ppermute | solution.py:503
  13.9 4.2 %collective-permute-start.4 = (f32[88,128]{1,0:T(8,128)S(1)}, f32[88,128]{1,0:T(8,128)S(1)}, u32[]{:S(2)}, u32[]{:S(2)}) collective-permute-start(f32[88,128]{1,0:T(8,128)S(1)} %get-tuple-element.30), channel_id=1, source_target_pairs={{0,1},{1,0},{2,3},{3,2},{4,5},{5,4},{6,7},{7,6},{8,9},{9,8},{10,11... | collective-permute-start | bytes 135176 | tf_op jit(solution)/shard_map/ppermute | solution.py:494
  16.1 2.1 %collective-permute-start.5 = (f32[88,128]{1,0:T(8,128)S(1)}, f32[88,128]{1,0:T(8,128)S(1)}, u32[]{:S(2)}, u32[]{:S(2)}) collective-permute-start(f32[88,128]{1,0:T(8,128)S(1)} %get-tuple-element.31), channel_id=1, source_target_pairs={{0,4},{1,2},{2,1},{3,7},{4,0},{5,6},{6,5},{7,3},{8,12},{9,10},{10,... | collective-permute-start | bytes 135176 | tf_op jit(solution)/shard_map/ppermute | solution.py:494
  18.6 7.5 %collective-permute-start.6 = (f32[11,32,128]{2,1,0:T(8,128)S(1)}, f32[11,32,128]{2,1,0:T(8,128)S(1)}, u32[]{:S(2)}, u32[]{:S(2)}) collective-permute-start(f32[11,32,128]{2,1,0:T(8,128)S(1)} %get-tuple-element.36), channel_id=1, source_target_pairs={{4,8},{8,4},{12,16},{16,12},{20,24},{24,20},{28,0},{0,28},{5,9},{9... | collective-permute-start | bytes 540680 | tf_op jit(solution)/shard_map/ppermute | solution.py:503
  20.3 5.8 %collective-permute-start.7 = (f32[11,32,128]{2,1,0:T(8,128)S(1)}, f32[11,32,128]{2,1,0:T(8,128)S(1)}, u32[]{:S(2)}, u32[]{:S(2)}) collective-permute-start(f32[11,32,128]{2,1,0:T(8,128)S(1)} %get-tuple-element.37), channel_id=1, source_target_pairs={{0,4},{4,0},{8,12},{12,8},{16,20},{20,16},{24,28},{28,24},{1,5},{5... | collective-permute-start | bytes 540680 | tf_op jit(solution)/shard_map/ppermute | solution.py:503

commit v13 on v12

--- a/solution.py
+++ b/solution.py
@@ -224,34 +224,43 @@
     halo_kinds[first : first + 2, :] = jnp.where(partner, msg[last : last + 2, :], 0.0)
 
 
-def first_loop_rows(size_y):
-    main = len(X_SETS[1]) * size_y
-    total = main + 2 * len(X_SETS[1])
-    return main, -(-total // SUB) * SUB
-
-
-def send_first_loop(state, a, msg):
-    size_x, size_y = sizes_of(state)
-    main, _ = first_loop_rows(size_y)
+def rest_lines(a, size_y):
+    result = []
+    for i in X_SETS[a]:
+        result += [(i, -1), (i, size_y)]
+        if DIRS[i][1]:
+            result.append((i, 0 if DIRS[i][1] > 0 else size_y - 1))
+    return result
+
+
+def send_planes(state, a, msg):
+    size_x, size_y = sizes_of(state)
     x = -1 if a < 0 else size_x
     for k, i in enumerate(X_SETS[a]):
         for y in range(0, size_y, SUB):
-            msg[k * size_y + y : k * size_y + y + SUB, :] = state[i, slot(x), y + PAD : y + PAD + SUB, :]
-        for s, y in enumerate((-1, size_y)):
-            row = main + 2 * k + s
-            msg[row : row + 1, :] = state[i, slot(x), y + PAD : y + PAD + 1, :]
-
-
-def take_first_loop(state, a, msg):
-    size_x, size_y = sizes_of(state)
-    main, _ = first_loop_rows(size_y)
+            msg[k, y : y + SUB, :] = state[i, slot(x), y + PAD : y + PAD + SUB, :]
+
+
+def take_planes(state, a, msg):
+    size_x, size_y = sizes_of(state)
     x = 0 if a > 0 else size_x - 1
     for k, i in enumerate(X_SETS[a]):
         for y in range(0, size_y, SUB):
-            state[i, slot(x), y + PAD : y + PAD + SUB, :] = msg[k * size_y + y : k * size_y + y + SUB, :]
-        for s, y in enumerate((-1, size_y)):
-            row = main + 2 * k + s
-            state[i, slot(x), y + PAD : y + PAD + 1, :] = msg[row : row + 1, :]
+            state[i, slot(x), y + PAD : y + PAD + SUB, :] = msg[k, y : y + SUB, :]
+
+
+def send_rest(state, a, msg):
+    size_x, size_y = sizes_of(state)
+    x = -1 if a < 0 else size_x
+    for k, (i, y) in enumerate(rest_lines(a, size_y)):
+        msg[k : k + 1, :] = state[i, slot(x), y + PAD : y + PAD + 1, :]
+
+
+def take_rest(state, a, msg):
+    size_x, size_y = sizes_of(state)
+    x = 0 if a > 0 else size_x - 1
+    for k, (i, y) in enumerate(rest_lines(a, size_y)):
+        state[i, slot(x), y + PAD : y + PAD + 1, :] = msg[k : k + 1, :]
 
 
 def load_tile(state, x, y):
@@ -262,7 +271,7 @@
     collide(lambda i: raw[i, at[0], at[1] : at[1] + SUB, :], kinds[x, y : y + SUB, :], push_tile(state, x, y))
 
 
-def side_kernel(pops, scal, flags, state, kinds, sent_a, sent_b, raw, sems, kinds_sem):
+def side_kernel(pops, scal, flags, state, kinds, sent_a, sent_b, far, near, raw, raw_edge, sems, edge_sems, kinds_sem):
     size_x, size_y, size_z = flags.shape
     flat_pops = pops.reshape(NF, size_x * size_y, size_z)
     flat_scal = scal.reshape(NS + NS, size_x * size_y, size_z)
@@ -280,11 +289,18 @@
             pltpu.make_async_copy(flat_scal.at[:, here], raw.at[NF:NQ, n, there], sems.at[1, n]),
         )
 
+    ends, inner = (0, size_x - 1), pl.ds(SUB, size_y - 2 * SUB)
+    edge_copies = []
+    for e, x in enumerate(ends):
+        edge_copies.append(pltpu.make_async_copy(pops.at[:, x, inner], raw_edge.at[0:NF, e], edge_sems.at[0, e]))
+        edge_copies.append(pltpu.make_async_copy(scal.at[:, x, inner], raw_edge.at[NF:NQ, e], edge_sems.at[1, e]))
     for n in range(size_x + 1):
         for copy in copies(n):
             copy.start()
         if n == 0:
             kinds_copy.start()
+    for copy in edge_copies:
+        copy.start()
 
     for copy in copies(0):
         copy.wait()
@@ -303,6 +319,13 @@
     collide_raw(raw, (size_x, 0), kinds, state, size_x - 1, size_y - SUB)
     for swap, msg in zip(CROSS_SWAPS, (sent_a, sent_b)):
         by_swap("cross", swap, lambda side: send_first_cross(state, kinds, side, msg))
+    for copy in edge_copies:
+        copy.wait()
+    for e, x in enumerate(ends):
+        for y in range(SUB, size_y - SUB, SUB):
+            collide_raw(raw_edge, (e, y - SUB), kinds, state, x, y)
+    for swap, msg in zip(LOOP_SWAPS, (far, near)):
+        by_swap("loop", swap, lambda side: send_planes(state, side, msg))
 
 
 def middle_kernel(pops, scal, kinds, state_in, state, raw, sems):
@@ -315,11 +338,11 @@
             pltpu.make_async_copy(scal.at[:, x, inner], raw.at[NF:NQ, x], sems.at[1, x]),
         )
 
-    for x in range(size_x):
+    for x in range(1, size_x - 1):
         for copy in copies(x):
             copy.start()
 
-    @pl.loop(0, size_x)
+    @pl.loop(1, size_x - 1)
     def _(x):
         for copy in copies(x):
             copy.wait()
@@ -327,14 +350,13 @@
             collide_raw(raw, (x, y - SUB), kinds, state, x, y)
 
 
-def turn_kernel(state_in, got_a, got_b, kinds, state, halo_kinds, sent, out):
+def turn_kernel(state_in, got_a, got_b, state, halo_kinds, far, near):
     halo_kinds[...] = jnp.zeros(halo_kinds.shape, jnp.float32)
     for swap, got in zip(CROSS_SWAPS, (got_a, got_b)):
         partner = has_partner("cross", swap)
         by_swap("cross", swap, lambda side: take_first_cross(state, halo_kinds, -side, got, partner))
-    by_swap("loop", LOOP_SWAPS[0], lambda side: send_first_loop(state, side, sent))
-    size_x, size_y = sizes_of(state)
-    pl.when(starts_late())(lambda: collide_inner(state, kinds, out, (0, size_y - SUB), 1, size_x // 2))
+    for swap, msg in zip(LOOP_SWAPS, (far, near)):
+        by_swap("loop", swap, lambda side: send_rest(state, side, msg))
 
 
 def collide_inner(state, kinds, out, tiles, first, last):
@@ -344,13 +366,10 @@
             collide(load_tile(state, x, y), kinds[x, y : y + SUB, :], push_tile(out, x, y))
 
 
-def inner_side_kernel(state, kinds, out_in, out, near, sent_a, sent_b):
+def inner_side_kernel(state, kinds, out, sent_a, sent_b):
     size_x, size_y = sizes_of(state)
     rows, flat = out.shape[2], flat_of(out)
-    by_swap("loop", LOOP_SWAPS[1], lambda side: send_first_loop(state, side, near))
-    sides = 0, size_y - SUB
-    pl.when(jnp.logical_not(starts_late()))(lambda: collide_inner(state, kinds, out, sides, 1, size_x // 2))
-    collide_inner(state, kinds, out, sides, size_x // 2, size_x - 1)
+    collide_inner(state, kinds, out, (0, size_y - SUB), 1, size_x - 1)
 
     def send(b, msg):
         y_out = size_y if b > 0 else -1
@@ -390,45 +409,14 @@
 
 
 def edge_kernel(
-    state_in,
-    out_in,
-    kinds,
-    halo_kinds,
-    loop_a,
-    loop_b,
-    cross_a,
-    cross_b,
-    state,
-    out,
-    sent_a,
-    sent_b,
-    halo,
+    state_in, out_in, kinds, halo_kinds, far, near, far_rest, near_rest, state, out, far_sent, near_sent, halo
 ):
-    size_x, size_y = sizes_of(state)
-    rows, flat_out = state.shape[2], flat_of(out)
-    for swap, msg in zip(LOOP_SWAPS, (loop_a, loop_b)):
-        by_swap("loop", swap, lambda side: take_first_loop(state, -side, msg))
+    for swap, msg, rest in zip(LOOP_SWAPS, (far, near), (far_rest, near_rest)):
+        by_swap("loop", swap, lambda side: take_planes(state, -side, msg))
+        by_swap("loop", swap, lambda side: take_rest(state, -side, rest))
     collide_edges(state, kinds, halo_kinds, out, halo, True)
-
-    def send(a, msg):
-        x = -1 if a < 0 else size_x
-        for k, i in enumerate(X_SETS[a]):
-            for y in range(0, size_y, SUB):
-                msg[k, y : y + SUB, :] = out[i, slot(x), y + PAD : y + PAD + SUB, :]
-
-    for swap, msg in zip(LOOP_SWAPS, (sent_a, sent_b)):
-        by_swap("loop", swap, lambda side: send(side, msg))
-
-    def take(b, msg, partner):
-        y_in = 0 if b > 0 else size_y - 1
-        for k, i in enumerate(Y_SETS[b]):
-            got = jnp.where(partner, msg[k * SUB : k * SUB + size_x - 2, :], 0.0)
-            flat_out[i, lines(DIRS[i][0] + 1, y_in, rows, size_x - 2), :] = got
-
-    for swap, msg in zip(CROSS_SWAPS, (cross_a, cross_b)):
-        partner = has_partner("cross", swap)
-        by_swap("cross", swap, lambda side: take(-side, msg, partner))
-
+    for swap, msg in zip(LOOP_SWAPS, (far_sent, near_sent)):
+        by_swap("loop", swap, lambda side: send_planes(out, side, msg))
     pl.when(starts_late())(lambda: collide_edges(state, kinds, halo_kinds, out, halo, False))
 
 
@@ -456,8 +444,9 @@
             copy.wait()
 
 
-def last_kernel(pops_in, scal_in, got_a, got_b, pops, scal, sems):
-    size_x = pops.shape[1]
+def last_kernel(out_in, pops_in, scal_in, cross_a, cross_b, got_a, got_b, out, pops, scal, sems, row_sems):
+    size_x, size_y = sizes_of(out)
+    rows, flat = out.shape[2], flat_of(out)
 
     def copies(a, msg, swap):
         x = 0 if a > 0 else size_x - 1
@@ -469,15 +458,36 @@
             for n, (k, count, dst, first) in enumerate(spans)
         ]
 
+    def take(b, msg, partner):
+        y_in = 0 if b > 0 else size_y - 1
+        for k, i in enumerate(Y_SETS[b]):
+            got = jnp.where(partner, msg[k * SUB : k * SUB + size_x - 2, :], 0.0)
+            flat[i, lines(DIRS[i][0] + 1, y_in, rows, size_x - 2), :] = got
+
+    row_copies = []
+    for b in SIDES:
+        y = 0 if b > 0 else size_y - SUB
+        groups = [(9 * (a + 1) + 3 * (b + 1), 3) for a in (-1, 0, 1)] + [(i, 1) for i in Y_SETS[b] if i >= NF]
+        for first, count in groups:
+            a = DIRS[first][0]
+            x, planes = (1 if a > 0 else 0), size_x - abs(a)
+            dst, start = (pops, first) if first < NF else (scal, first - NF)
+            here = out.at[pl.ds(first, count), pl.ds(slot(x), planes), pl.ds(y + PAD, SUB)]
+            there = dst.at[pl.ds(start, count), pl.ds(x, planes), pl.ds(y, SUB)]
+            row_copies.append(pltpu.make_async_copy(here, there, row_sems.at[len(row_copies)]))
+
     def write(side):
         started = []
         for swap, msg in zip(LOOP_SWAPS, (got_a, got_b)):
             started += copies(-side if swap == 0 else side, msg, swap)
-        for copy in started:
+        for copy in started + row_copies:
             copy.start()
-        for copy in started:
+        for copy in started + row_copies:
             copy.wait()
 
+    for swap, msg in zip(CROSS_SWAPS, (cross_a, cross_b)):
+        partner = has_partner("cross", swap)
+        by_swap("cross", swap, lambda side: take(-side, msg, partner))
     by_swap("loop", 0, write)
 
 
@@ -510,9 +520,9 @@
     kinds_shape = pltpu.VMEM((size_x, size_y, size_z), jnp.int32)
     halo_kinds_shape = pltpu.VMEM((SUB, size_z), f32)
     cross_1 = [pltpu.VMEM((first_cross_rows(size_x)[1], size_z), f32)] * 2
-    loop_1 = pltpu.VMEM((first_loop_rows(size_y)[1], size_z), f32)
+    rest_shape = pltpu.VMEM((-(-len(rest_lines(1, size_y)) // SUB) * SUB, size_z), f32)
     cross_2 = [pltpu.VMEM((len(Y_SETS[1]) * SUB, size_z), f32)] * 2
-    loop_2 = [pltpu.VMEM((len(X_SETS[1]), size_y, size_z), f32)] * 2
+    planes = [pltpu.VMEM((len(X_SETS[1]), size_y, size_z), f32)] * 2
     hbm = pl.BlockSpec(memory_space=pl.ANY)
     vmem = pl.BlockSpec(memory_space=pltpu.VMEM)
     pops_shape = jax.ShapeDtypeStruct(populations.shape, f32)
@@ -545,19 +555,22 @@
         return [(pltpu.HBM, x) for x in arrays]
 
     tiles = size_y // SUB
-    state, kinds, *sent = call(
+    state, kinds, *sent, far, near = call(
         side_kernel,
         "first_step_side_rows",
         in_hbm(populations, scalars, node_flags),
-        [state_shape, kinds_shape] + cross_1,
-        tiles=2 * size_x,
+        [state_shape, kinds_shape] + cross_1 + planes,
+        tiles=2 * size_x + 2 * (tiles - 2),
         scratch=[
             pltpu.VMEM((NQ, size_x + 1, 2 * SUB, size_z), f32),
+            pltpu.VMEM((NQ, 2, size_y - 2 * SUB, size_z), f32),
             pltpu.SemaphoreType.DMA((2, size_x + 1)),
+            pltpu.SemaphoreType.DMA((2, 2)),
             pltpu.SemaphoreType.DMA,
         ],
     )
     received = swap_cross(sent)
+    from_loop = [swap_loop(swap, cells) for swap, cells in zip(LOOP_SWAPS, (far, near))]
     if tiles > 2:
         (state,) = call(
             middle_kernel,
@@ -571,24 +584,22 @@
             ],
             aliases={3: 0},
         )
-    state, halo_kinds, far, out = call(
+    state, halo_kinds, far, near = call(
         turn_kernel,
         "cross_to_loop",
-        on_chip(state, *received, kinds),
-        [state_shape, halo_kinds_shape, loop_1, state_shape],
-        tiles=size_x - 2,
+        on_chip(state, *received),
+        [state_shape, halo_kinds_shape, rest_shape, rest_shape],
+        tiles=1,
         aliases={0: 0},
     )
-    from_far = swap_loop(LOOP_SWAPS[0], far)
-    out, near, *sent = call(
+    from_rest = [swap_loop(swap, cells) for swap, cells in zip(LOOP_SWAPS, (far, near))]
+    out, *sent = call(
         inner_side_kernel,
         "second_step_inner_side_rows",
-        on_chip(state, kinds, out),
-        [state_shape, loop_1] + cross_2,
-        tiles=size_x - 2,
-        aliases={2: 0},
+        on_chip(state, kinds),
+        [state_shape] + cross_2,
+        tiles=(size_x - 2) * 2,
     )
-    from_near = swap_loop(LOOP_SWAPS[1], near)
     from_cross = swap_cross(sent)
     if tiles > 2:
         (out,) = call(
@@ -603,14 +614,14 @@
     state, out, far, near = call(
         edge_kernel,
         "second_step_edges_to_send",
-        on_chip(state, out, kinds, halo_kinds, from_far, from_near, *from_cross),
-        [state_shape, state_shape] + loop_2,
+        on_chip(state, out, kinds, halo_kinds, *from_loop, *from_rest),
+        [state_shape, state_shape] + planes,
         tiles=2 * tiles + 1,
         scratch=[halo],
         aliases={0: 0, 1: 1},
     )
     received = [swap_loop(swap, cells) for swap, cells in zip(LOOP_SWAPS, (far, near))]
-    _, new_pops, new_scal = call(
+    out, new_pops, new_scal = call(
         write_kernel,
         "second_step_edges_rest_and_write",
         on_chip(state, out, kinds, halo_kinds),
@@ -620,14 +631,14 @@
         scratch=[pltpu.SemaphoreType.DMA((2, size_x)), halo],
         aliases={1: 0},
     )
-    new_pops, new_scal = call(
+    _, new_pops, new_scal = call(
         last_kernel,
-        "write_edge_planes",
-        in_hbm(new_pops, new_scal) + on_chip(*received),
-        [pops_shape, scal_shape],
+        "write_edge_planes_and_rows",
+        on_chip(out) + in_hbm(new_pops, new_scal) + on_chip(*from_cross, *received),
+        [state_shape, pops_shape, scal_shape],
         moved=16 * len(X_SETS[1]) * size_y * size_z,
-        scratch=[pltpu.SemaphoreType.DMA((2, len(X_SETS[1])))],
-        aliases={0: 0, 1: 1},
+        scratch=[pltpu.SemaphoreType.DMA((2, len(X_SETS[1]))), pltpu.SemaphoreType.DMA((2 * len(Y_SETS[1]),))],
+        aliases={0: 0, 1: 1, 2: 2},
     )
     return new_pops, new_scal
 

time: 27.2 us -> 26.7 us (0.982)
  waiting for transfers between devices: 3.81 us -> 2.74 us
  Pallas kernels: 12.4 us -> 13 us
    ppermute x4 -> x6, starting transfers between devices: 4.87 us -> 5.69 us  [swap_loop(): return lax.ppermute(cells, 'loop', pairs)]
    ppermute x4 -> x6, waiting for transfers between devices: 2.81 us -> 2 us  [swap_loop(): return lax.ppermute(cells, 'loop', pairs)]
    ppermute x4, starting transfers between devices: 5.25 us -> 4.47 us  [swap_cross(): received.append(lax.ppermute(cells, ('loop', 'cross'), pairs))]
    pallas_call x8, Pallas kernels: 12.4 us -> 13 us  [call(): pl.pallas_call(kernel, out_shape=results, in_specs=specs, out_specs=[hbm...]
  transfers between devices with their start and end apart: 8 -> 10, of which waited for: 2 -> 3; matrix products, arithmetic and copies ran while one was open for 0% -> 0% of each run, Pallas kernels for 27% -> 26%
where the time goes in v13:
time: 26.7 us; the launch traced here: 26.6 us
  Pallas kernels  13 us (49%)
  starting transfers between devices  10.2 us (38%)
  waiting for transfers between devices  2.74 us (10%)
  between operations  0.7 us (3%)
    pallas_call x8, Pallas kernels, call(): pl.pallas_call(kernel, out_shape=results, in_specs=specs, out_specs=[hbm...  13 us
    ppermute x6, starting transfers between devices, swap_loop(): return lax.ppermute(cells, 'loop', pairs)  5.69 us
    ppermute x4, starting transfers between devices, swap_cross(): received.append(lax.ppermute(cells, ('loop', 'cross'), pairs))  4.47 us
    ppermute x6, waiting for transfers between devices, swap_loop(): return lax.ppermute(cells, 'loop', pairs)  2 us
    ppermute x4, waiting for transfers between devices, swap_cross(): received.append(lax.ppermute(cells, ('loop', 'cross'), pairs))  0.74 us
  transfers between devices with their start and end apart: 10, of which 3 were waited for; matrix products, arithmetic and copies ran while one was open for 0% of the time, Pallas kernels for 26%

profile of v13, /device:TPU:0, one launch (start us, length us, event | category | flops | bytes accessed | tf_op | source)
XLA Modules:
  0.0 26.6 jit_solution(7224212997873653961)
XLA Ops:
  0.6 4.1 %first_step_side_rows.1 = (f32[41,10,48,128]{3,2,1,0:T(8,128)S(1)}, s32[8,32,128]{2,1,0:T(8,128)S(1)}, f32[152,128]{1,0:T(8,128)S(1)}, f32[152,128]{1,0:T(8,128)...) custom-call(f32[27,8,32,128]{3,2,1,0:T(8,128)} %pops.3, f32[14,8,32,128]{3,2,1,0:T(8,128)} %scal.3, ...), custom_call_target="tpu_custom_call" | custom-call | flops 10240000 | bytes 6717440 | tf_op jit(solution)/shard_map/first_step_side_rows/pallas_call | solution.py:537
  4.7 3.4 %collective-permute-start.2 = (f32[11,32,128]{2,1,0:T(8,128)S(1)}, f32[11,32,128]{2,1,0:T(8,128)S(1)}, u32[]{:S(2)}, u32[]{:S(2)}) collective-permute-start(f32[11,32,128]{2,1,0:T(8,128)S(1)} %get-tuple-element.31), channel_id=1, source_target_pairs={{4,8},{8,4},{12,16},{16,12},{20,24},{24,20},{28,0},{0,28},{5,9},{9... | collective-permute-start | bytes 540680 | tf_op jit(solution)/shard_map/ppermute | solution.py:513
  8.1 0.0 collective-permute-start.3
  8.1 1.6 %collective-permute-start = (f32[152,128]{1,0:T(8,128)S(1)}, f32[152,128]{1,0:T(8,128)S(1)}, u32[]{:S(2)}, u32[]{:S(2)}) collective-permute-start(f32[152,128]{1,0:T(8,128)S(1)} %get-tuple-element.26), channel_id=1, source_target_pairs={{0,1},{1,0},{2,3},{3,2},{4,5},{5,4},{6,7},{7,6},{8,9},{9,8},{10,11... | collective-permute-start | bytes 233480 | tf_op jit(solution)/shard_map/ppermute | solution.py:504
  9.7 0.2 collective-permute-start.1
  9.9 2.2 %first_step_middle_rows.1.state_in = f32[41,10,48,128]{3,2,1,0:T(8,128)S(1)} custom-call(f32[27,8,32,128]{3,2,1,0:T(8,128)} %pops.3, f32[14,8,32,128]{3,2,1,0:T(8,128)} %scal.3, s32[8,32,128]{2,1,0:T(8,128)S(1)} %get-tuple-element.24.kinds, f32[41,10,48,128]{3,2,1,0:T(8,128)S(1)} %get-tuple-element.25.state_in), custom_call_target="tpu_custom_call", output_to_operand_aliasing={{}: (3, {})} | custom-call | flops 8192000 | bytes 5373952 | tf_op jit(solution)/shard_map/first_step_middle_rows/pallas_call | solution.py:537
  12.2 0.7 %collective-permute-done.got_a = f32[152,128]{1,0:T(8,128)S(1)} collective-permute-done((f32[152,128]{1,0:T(8,128)S(1)}, f32[152,128]{1,0:T(8,128)S(1)}, u32[]{:S(2)}, u32[]{:S(2)}) %collective-permute-start) | collective-permute-done | bytes 77856 | tf_op jit(solution)/shard_map/ppermute | solution.py:504
  12.9 0.0 collective-permute-done.1.got_b
  12.9 0.1 cross_to_loop.1
  13.0 0.4 %collective-permute-start.4 = (f32[32,128]{1,0:T(8,128)S(1)}, f32[32,128]{1,0:T(8,128)S(1)}, u32[]{:S(2)}, u32[]{:S(2)}) collective-permute-start(f32[32,128]{1,0:T(8,128)S(1)} %get-tuple-element.33), channel_id=1, source_target_pairs={{4,8},{8,4},{12,16},{16,12},{20,24},{24,20},{28,0},{0,28},{5,9},{9... | collective-permute-start | bytes 49160 | tf_op jit(solution)/shard_map/ppermute | solution.py:513
  13.4 0.6 %collective-permute-start.5 = (f32[32,128]{1,0:T(8,128)S(1)}, f32[32,128]{1,0:T(8,128)S(1)}, u32[]{:S(2)}, u32[]{:S(2)}) collective-permute-start(f32[32,128]{1,0:T(8,128)S(1)} %get-tuple-element.34), channel_id=1, source_target_pairs={{0,4},{4,0},{8,12},{12,8},{16,20},{20,16},{24,28},{28,24},{1,5},{5... | collective-permute-start | bytes 49160 | tf_op jit(solution)/shard_map/ppermute | solution.py:513
  14.1 1.1 %second_step_inner_side_rows.1 = (f32[41,10,48,128]{3,2,1,0:T(8,128)S(1)}, f32[88,128]{1,0:T(8,128)S(1)}, f32[88,128]{1,0:T(8,128)S(1)}) custom-call(f32[41,10,48,128]{3,2,1,0:T(8,128)S(1)} %get-tuple-element.28.state.state_in, s32[8,32,128]{2,1,0:T(8,128)S(1)} %get-tuple-element.24.kinds), custom_call_target="tpu_custom_call" | custom-call | flops 6144000 | bytes 4030464 | tf_op jit(solution)/shard_map/second_step_inner_side_rows/pallas_call | solution.py:537
  15.2 1.1 %second_step_inner_middle_rows.1.out_in = f32[41,10,48,128]{3,2,1,0:T(8,128)S(1)} custom-call(f32[41,10,48,128]{3,2,1,0:T(8,128)S(1)} %get-tuple-element.28.state.state_in, s32[8,32,128]{2,1,0:T(8,128)S(1)} %get-tuple-element.24.kinds, f32[41,10,48,128]{3,2,1,0:T(8,128)S(1)} %get-tuple-element.29.out_in), custom_call_target="tpu_custom_call", output_to_operand_aliasing={{}: (2, {})} | custom-call | flops 6144000 | bytes 4030464 | tf_op jit(solution)/shard_map/second_step_inner_middle_rows/pallas_call | solution.py:537
  16.2 0.9 %collective-permute-done.4.far_rest = f32[32,128]{1,0:T(8,128)S(1)} collective-permute-done((f32[32,128]{1,0:T(8,128)S(1)}, f32[32,128]{1,0:T(8,128)S(1)}, u32[]{:S(2)}, u32[]{:S(2)}) %collective-permute-start.4) | collective-permute-done | bytes 16416 | tf_op jit(solution)/shard_map/ppermute | solution.py:513
  17.2 0.0 collective-permute-done.5.near_rest
  17.2 0.0 collective-permute-done.2.far
  17.2 0.0 collective-permute-done.3.near
  17.2 0.5 %second_step_edges_to_send.1 = (f32[41,10,48,128]{3,2,1,0:T(8,128)S(1)}, f32[41,10,48,128]{3,2,1,0:T(8,128)S(1)}, f32[11,32,128]{2,1,0:T(8,128)S(1)}, f32[11,32,128]{2,1,0:T(8,128)S(1)}) custom-call(f32[41,10,48,128]{3,2,1,0:T(8,128)S(1)} %get-tuple-element.28.state.state_in, ...), custom_call_target="tpu_custom_call", output_to_operand_aliasing={{0}: (0, {}), {1}: (1, {})} | custom-call | flops 4608000 | bytes 3022848 | tf_op jit(solution)/shard_map/second_step_edges_to_send/pallas_call | solution.py:537
  17.7 0.8 %collective-permute-start.8 = (f32[11,32,128]{2,1,0:T(8,128)S(1)}, f32[11,32,128]{2,1,0:T(8,128)S(1)}, u32[]{:S(2)}, u32[]{:S(2)}) collective-permute-start(f32[11,32,128]{2,1,0:T(8,128)S(1)} %get-tuple-element.42), channel_id=1, source_target_pairs={{4,8},{8,4},{12,16},{16,12},{20,24},{24,20},{28,0},{0,28},{5,9},{9... | collective-permute-start | bytes 540680 | tf_op jit(solution)/shard_map/ppermute | solution.py:513
  18.5 0.4 %collective-permute-start.9 = (f32[11,32,128]{2,1,0:T(8,128)S(1)}, f32[11,32,128]{2,1,0:T(8,128)S(1)}, u32[]{:S(2)}, u32[]{:S(2)}) collective-permute-start(f32[11,32,128]{2,1,0:T(8,128)S(1)} %get-tuple-element.43), channel_id=1, source_target_pairs={{0,4},{4,0},{8,12},{12,8},{16,20},{20,16},{24,28},{28,24},{1,5},{5... | collective-permute-start | bytes 540680 | tf_op jit(solution)/shard_map/ppermute | solution.py:513
  18.9 2.7 %collective-permute-start.6 = (f32[88,128]{1,0:T(8,128)S(1)}, f32[88,128]{1,0:T(8,128)S(1)}, u32[]{:S(2)}, u32[]{:S(2)}) collective-permute-start(f32[88,128]{1,0:T(8,128)S(1)} %get-tuple-element.40), channel_id=1, source_target_pairs={{0,1},{1,0},{2,3},{3,2},{4,5},{5,4},{6,7},{7,6},{8,9},{9,8},{10,11... | collective-permute-start | bytes 135176 | tf_op jit(solution)/shard_map/ppermute | solution.py:504
  21.6 0.0 collective-permute-start.7
  21.6 2.5 %second_step_edges_rest_and_write.1 = (f32[41,10,48,128]{3,2,1,0:T(8,128)S(1)}, f32[27,8,32,128]{3,2,1,0:T(8,128)}, f32[14,8,32,128]{3,2,1,0:T(8,128)}) custom-call(f32[41,10,48,128]{3,2,1,0:T(8,128)S(1)} %get-tuple-element.35.state, f32[41,10,48,128]{3,2,1,0:T(8,128)S(1)} %get-tuple-element.36.out_in, ...), custom_call_target="tpu_custom_call", output_to_operand_aliasing={{0}: (1, {})} | custom-call | flops 4608000 | bytes 13770752 | tf_op jit(solution)/shard_map/second_step_edges_rest_and_write/pallas_call | solution.py:537
  24.1 0.0 collective-permute-done.6.cross_a
  24.1 0.0 collective-permute-done.7.cross_b
  24.2 1.0 %collective-permute-done.8.got_a = f32[11,32,128]{2,1,0:T(8,128)S(1)} collective-permute-done((f32[11,32,128]{2,1,0:T(8,128)S(1)}, f32[11,32,128]{2,1,0:T(8,128)S(1)}, u32[]{:S(2)}, u32[]{:S(2)}) %collective-permute-start.8) | collective-permute-done | bytes 180256 | tf_op jit(solution)/shard_map/ppermute | solution.py:513
  25.2 0.0 collective-permute-done.9.got_b
  25.2 1.4 %write_edge_planes_and_rows.1 = (f32[41,10,48,128]{3,2,1,0:T(8,128)S(1)}, f32[27,8,32,128]{3,2,1,0:T(8,128)}, f32[14,8,32,128]{3,2,1,0:T(8,128)}) custom-call(f32[41,10,48,128]{3,2,1,0:T(8,128)S(1)} %get-tuple-element.37.out_in, f32[27,8,32,128]{3,2,1,0:T(8,128)} %get-tuple-element.38.pops_in, ...), custom_call_target="tpu_custom_call", output_to_operand_aliasing={{0}: (0, {}), {1}: (1, {}), {2}: (2, {})} | custom-call | bytes 720896 | tf_op jit(solution)/shard_map/write_edge_planes_and_rows/pallas_call | solution.py:537
Async XLA Ops:
  4.7 12.4 %collective-permute-start.2 = (f32[11,32,128]{2,1,0:T(8,128)S(1)}, f32[11,32,128]{2,1,0:T(8,128)S(1)}, u32[]{:S(2)}, u32[]{:S(2)}) collective-permute-start(f32[11,32,128]{2,1,0:T(8,128)S(1)} %get-tuple-element.31), channel_id=1, source_target_pairs={{4,8},{8,4},{12,16},{16,12},{20,24},{24,20},{28,0},{0,28},{5,9},{9... | collective-permute-start | bytes 540680 | tf_op jit(solution)/shard_map/ppermute | solution.py:513
  8.1 9.0 %collective-permute-start.3 = (f32[11,32,128]{2,1,0:T(8,128)S(1)}, f32[11,32,128]{2,1,0:T(8,128)S(1)}, u32[]{:S(2)}, u32[]{:S(2)}) collective-permute-start(f32[11,32,128]{2,1,0:T(8,128)S(1)} %get-tuple-element.32), channel_id=1, source_target_pairs={{0,4},{4,0},{8,12},{12,8},{16,20},{20,16},{24,28},{28,24},{1,5},{5... | collective-permute-start | bytes 540680 | tf_op jit(solution)/shard_map/ppermute | solution.py:513
  8.1 4.8 %collective-permute-start = (f32[152,128]{1,0:T(8,128)S(1)}, f32[152,128]{1,0:T(8,128)S(1)}, u32[]{:S(2)}, u32[]{:S(2)}) collective-permute-start(f32[152,128]{1,0:T(8,128)S(1)} %get-tuple-element.26), channel_id=1, source_target_pairs={{0,1},{1,0},{2,3},{3,2},{4,5},{5,4},{6,7},{7,6},{8,9},{9,8},{10,11... | collective-permute-start | bytes 233480 | tf_op jit(solution)/shard_map/ppermute | solution.py:504
  9.7 3.2 %collective-permute-start.1 = (f32[152,128]{1,0:T(8,128)S(1)}, f32[152,128]{1,0:T(8,128)S(1)}, u32[]{:S(2)}, u32[]{:S(2)}) collective-permute-start(f32[152,128]{1,0:T(8,128)S(1)} %get-tuple-element.27), channel_id=1, source_target_pairs={{0,4},{1,2},{2,1},{3,7},{4,0},{5,6},{6,5},{7,3},{8,12},{9,10},{10,... | collective-permute-start | bytes 233480 | tf_op jit(solution)/shard_map/ppermute | solution.py:504
  13.0 4.1 %collective-permute-start.4 = (f32[32,128]{1,0:T(8,128)S(1)}, f32[32,128]{1,0:T(8,128)S(1)}, u32[]{:S(2)}, u32[]{:S(2)}) collective-permute-start(f32[32,128]{1,0:T(8,128)S(1)} %get-tuple-element.33), channel_id=1, source_target_pairs={{4,8},{8,4},{12,16},{16,12},{20,24},{24,20},{28,0},{0,28},{5,9},{9... | collective-permute-start | bytes 49160 | tf_op jit(solution)/shard_map/ppermute | solution.py:513
  13.4 3.7 %collective-permute-start.5 = (f32[32,128]{1,0:T(8,128)S(1)}, f32[32,128]{1,0:T(8,128)S(1)}, u32[]{:S(2)}, u32[]{:S(2)}) collective-permute-start(f32[32,128]{1,0:T(8,128)S(1)} %get-tuple-element.34), channel_id=1, source_target_pairs={{0,4},{4,0},{8,12},{12,8},{16,20},{20,16},{24,28},{28,24},{1,5},{5... | collective-permute-start | bytes 49160 | tf_op jit(solution)/shard_map/ppermute | solution.py:513
  17.7 7.5 %collective-permute-start.8 = (f32[11,32,128]{2,1,0:T(8,128)S(1)}, f32[11,32,128]{2,1,0:T(8,128)S(1)}, u32[]{:S(2)}, u32[]{:S(2)}) collective-permute-start(f32[11,32,128]{2,1,0:T(8,128)S(1)} %get-tuple-element.42), channel_id=1, source_target_pairs={{4,8},{8,4},{12,16},{16,12},{20,24},{24,20},{28,0},{0,28},{5,9},{9... | collective-permute-start | bytes 540680 | tf_op jit(solution)/shard_map/ppermute | solution.py:513
  18.5 6.7 %collective-permute-start.9 = (f32[11,32,128]{2,1,0:T(8,128)S(1)}, f32[11,32,128]{2,1,0:T(8,128)S(1)}, u32[]{:S(2)}, u32[]{:S(2)}) collective-permute-start(f32[11,32,128]{2,1,0:T(8,128)S(1)} %get-tuple-element.43), channel_id=1, source_target_pairs={{0,4},{4,0},{8,12},{12,8},{16,20},{20,16},{24,28},{28,24},{1,5},{5... | collective-permute-start | bytes 540680 | tf_op jit(solution)/shard_map/ppermute | solution.py:513
  18.9 5.2 %collective-permute-start.6 = (f32[88,128]{1,0:T(8,128)S(1)}, f32[88,128]{1,0:T(8,128)S(1)}, u32[]{:S(2)}, u32[]{:S(2)}) collective-permute-start(f32[88,128]{1,0:T(8,128)S(1)} %get-tuple-element.40), channel_id=1, source_target_pairs={{0,1},{1,0},{2,3},{3,2},{4,5},{5,4},{6,7},{7,6},{8,9},{9,8},{10,11... | collective-permute-start | bytes 135176 | tf_op jit(solution)/shard_map/ppermute | solution.py:504
  21.6 2.5 %collective-permute-start.7 = (f32[88,128]{1,0:T(8,128)S(1)}, f32[88,128]{1,0:T(8,128)S(1)}, u32[]{:S(2)}, u32[]{:S(2)}) collective-permute-start(f32[88,128]{1,0:T(8,128)S(1)} %get-tuple-element.41), channel_id=1, source_target_pairs={{0,4},{1,2},{2,1},{3,7},{4,0},{5,6},{6,5},{7,3},{8,12},{9,10},{10,... | collective-permute-start | bytes 135176 | tf_op jit(solution)/shard_map/ppermute | solution.py:504

commit v14 on v13

--- a/solution.py
+++ b/solution.py
@@ -444,9 +444,36 @@
             copy.wait()
 
 
-def last_kernel(out_in, pops_in, scal_in, cross_a, cross_b, got_a, got_b, out, pops, scal, sems, row_sems):
+def rows_kernel(out_in, pops_in, scal_in, cross_a, cross_b, out, pops, scal, sems):
     size_x, size_y = sizes_of(out)
     rows, flat = out.shape[2], flat_of(out)
+
+    def take(b, msg, partner):
+        y_in = 0 if b > 0 else size_y - 1
+        for k, i in enumerate(Y_SETS[b]):
+            got = jnp.where(partner, msg[k * SUB : k * SUB + size_x - 2, :], 0.0)
+            flat[i, lines(DIRS[i][0] + 1, y_in, rows, size_x - 2), :] = got
+
+    for swap, msg in zip(CROSS_SWAPS, (cross_a, cross_b)):
+        partner = has_partner("cross", swap)
+        by_swap("cross", swap, lambda side: take(-side, msg, partner))
+    copies = []
+    for b in SIDES:
+        y = 0 if b > 0 else size_y - SUB
+        groups = [(9 * (a + 1) + 3 * (b + 1), 3) for a in (-1, 0, 1)] + [(i, 1) for i in Y_SETS[b] if i >= NF]
+        for first, count in groups:
+            dst, start = (pops, first) if first < NF else (scal, first - NF)
+            here = out.at[pl.ds(first, count), pl.ds(slot(0), size_x), pl.ds(y + PAD, SUB)]
+            there = dst.at[pl.ds(start, count), :, pl.ds(y, SUB)]
+            copies.append(pltpu.make_async_copy(here, there, sems.at[len(copies)]))
+    for copy in copies:
+        copy.start()
+    for copy in copies:
+        copy.wait()
+
+
+def last_kernel(pops_in, scal_in, got_a, got_b, pops, scal, sems):
+    size_x = pops.shape[1]
 
     def copies(a, msg, swap):
         x = 0 if a > 0 else size_x - 1
@@ -458,36 +485,15 @@
             for n, (k, count, dst, first) in enumerate(spans)
         ]
 
-    def take(b, msg, partner):
-        y_in = 0 if b > 0 else size_y - 1
-        for k, i in enumerate(Y_SETS[b]):
-            got = jnp.where(partner, msg[k * SUB : k * SUB + size_x - 2, :], 0.0)
-            flat[i, lines(DIRS[i][0] + 1, y_in, rows, size_x - 2), :] = got
-
-    row_copies = []
-    for b in SIDES:
-        y = 0 if b > 0 else size_y - SUB
-        groups = [(9 * (a + 1) + 3 * (b + 1), 3) for a in (-1, 0, 1)] + [(i, 1) for i in Y_SETS[b] if i >= NF]
-        for first, count in groups:
-            a = DIRS[first][0]
-            x, planes = (1 if a > 0 else 0), size_x - abs(a)
-            dst, start = (pops, first) if first < NF else (scal, first - NF)
-            here = out.at[pl.ds(first, count), pl.ds(slot(x), planes), pl.ds(y + PAD, SUB)]
-            there = dst.at[pl.ds(start, count), pl.ds(x, planes), pl.ds(y, SUB)]
-            row_copies.append(pltpu.make_async_copy(here, there, row_sems.at[len(row_copies)]))
-
     def write(side):
         started = []
         for swap, msg in zip(LOOP_SWAPS, (got_a, got_b)):
             started += copies(-side if swap == 0 else side, msg, swap)
-        for copy in started + row_copies:
+        for copy in started:
             copy.start()
-        for copy in started + row_copies:
+        for copy in started:
             copy.wait()
 
-    for swap, msg in zip(CROSS_SWAPS, (cross_a, cross_b)):
-        partner = has_partner("cross", swap)
-        by_swap("cross", swap, lambda side: take(-side, msg, partner))
     by_swap("loop", 0, write)
 
 
@@ -632,13 +638,23 @@
         aliases={1: 0},
     )
     _, new_pops, new_scal = call(
+        rows_kernel,
+        "write_rows_again",
+        on_chip(out) + in_hbm(new_pops, new_scal) + on_chip(*from_cross),
+        [state_shape, pops_shape, scal_shape],
+        tiles=1,
+        moved=8 * len(Y_SETS[1]) * size_x * SUB * size_z,
+        scratch=[pltpu.SemaphoreType.DMA((2 * len(Y_SETS[1]),))],
+        aliases={0: 0, 1: 1, 2: 2},
+    )
+    new_pops, new_scal = call(
         last_kernel,
-        "write_edge_planes_and_rows",
-        on_chip(out) + in_hbm(new_pops, new_scal) + on_chip(*from_cross, *received),
-        [state_shape, pops_shape, scal_shape],
+        "write_edge_planes",
+        in_hbm(new_pops, new_scal) + on_chip(*received),
+        [pops_shape, scal_shape],
         moved=16 * len(X_SETS[1]) * size_y * size_z,
-        scratch=[pltpu.SemaphoreType.DMA((2, len(X_SETS[1]))), pltpu.SemaphoreType.DMA((2 * len(Y_SETS[1]),))],
-        aliases={0: 0, 1: 1, 2: 2},
+        scratch=[pltpu.SemaphoreType.DMA((2, len(X_SETS[1])))],
+        aliases={0: 0, 1: 1},
     )
     return new_pops, new_scal
 

time: 26.7 us -> 26.4 us (0.989)
  waiting for transfers between devices: 2.74 us -> 1.69 us
  Pallas kernels: 13 us -> 13.6 us
    ppermute x6, waiting for transfers between devices: 2 us -> 0.95 us  [swap_loop(): return lax.ppermute(cells, 'loop', pairs)]
    pallas_call x8 -> x9, Pallas kernels: 13 us -> 13.6 us  [call(): pl.pallas_call(kernel, out_shape=results, in_specs=specs, out_specs=[hbm...]
  transfers between devices with their start and end apart: 10 -> 10, of which waited for: 3 -> 2; matrix products, arithmetic and copies ran while one was open for 0% -> 0% of each run, Pallas kernels for 26% -> 31%
where the time goes in v14:
time: 26.4 us; the launch traced here: 26.2 us
  Pallas kernels  13.6 us (52%)
  starting transfers between devices  10.2 us (39%)
  waiting for transfers between devices  1.69 us (6%)
  between operations  0.73 us (3%)
    pallas_call x9, Pallas kernels, call(): pl.pallas_call(kernel, out_shape=results, in_specs=specs, out_specs=[hbm...  13.6 us
    ppermute x6, starting transfers between devices, swap_loop(): return lax.ppermute(cells, 'loop', pairs)  5.69 us
    ppermute x4, starting transfers between devices, swap_cross(): received.append(lax.ppermute(cells, ('loop', 'cross'), pairs))  4.47 us
    ppermute x6, waiting for transfers between devices, swap_loop(): return lax.ppermute(cells, 'loop', pairs)  0.95 us
    ppermute x4, waiting for transfers between devices, swap_cross(): received.append(lax.ppermute(cells, ('loop', 'cross'), pairs))  0.74 us
  transfers between devices with their start and end apart: 10, of which 2 were waited for; matrix products, arithmetic and copies ran while one was open for 0% of the time, Pallas kernels for 31%

profile of v14, /device:TPU:0, one launch (start us, length us, event | category | flops | bytes accessed | tf_op | source)
XLA Modules:
  0.0 26.2 jit_solution(3878190330165782372)
XLA Ops:
  0.6 4.1 %first_step_side_rows.1 = (f32[41,10,48,128]{3,2,1,0:T(8,128)S(1)}, s32[8,32,128]{2,1,0:T(8,128)S(1)}, f32[152,128]{1,0:T(8,128)S(1)}, f32[152,128]{1,0:T(8,128)...) custom-call(f32[27,8,32,128]{3,2,1,0:T(8,128)} %pops.3, f32[14,8,32,128]{3,2,1,0:T(8,128)} %scal.3, ...), custom_call_target="tpu_custom_call" | custom-call | flops 10240000 | bytes 6717440 | tf_op jit(solution)/shard_map/first_step_side_rows/pallas_call | solution.py:543
  4.7 3.4 %collective-permute-start.2 = (f32[11,32,128]{2,1,0:T(8,128)S(1)}, f32[11,32,128]{2,1,0:T(8,128)S(1)}, u32[]{:S(2)}, u32[]{:S(2)}) collective-permute-start(f32[11,32,128]{2,1,0:T(8,128)S(1)} %get-tuple-element.31), channel_id=1, source_target_pairs={{4,8},{8,4},{12,16},{16,12},{20,24},{24,20},{28,0},{0,28},{5,9},{9... | collective-permute-start | bytes 540680 | tf_op jit(solution)/shard_map/ppermute | solution.py:519
  8.1 0.0 collective-permute-start.3
  8.1 1.6 %collective-permute-start = (f32[152,128]{1,0:T(8,128)S(1)}, f32[152,128]{1,0:T(8,128)S(1)}, u32[]{:S(2)}, u32[]{:S(2)}) collective-permute-start(f32[152,128]{1,0:T(8,128)S(1)} %get-tuple-element.26), channel_id=1, source_target_pairs={{0,1},{1,0},{2,3},{3,2},{4,5},{5,4},{6,7},{7,6},{8,9},{9,8},{10,11... | collective-permute-start | bytes 233480 | tf_op jit(solution)/shard_map/ppermute | solution.py:510
  9.7 0.2 collective-permute-start.1
  9.9 2.2 %first_step_middle_rows.1.state_in = f32[41,10,48,128]{3,2,1,0:T(8,128)S(1)} custom-call(f32[27,8,32,128]{3,2,1,0:T(8,128)} %pops.3, f32[14,8,32,128]{3,2,1,0:T(8,128)} %scal.3, s32[8,32,128]{2,1,0:T(8,128)S(1)} %get-tuple-element.24.kinds, f32[41,10,48,128]{3,2,1,0:T(8,128)S(1)} %get-tuple-element.25.state_in), custom_call_target="tpu_custom_call", output_to_operand_aliasing={{}: (3, {})} | custom-call | flops 8192000 | bytes 5373952 | tf_op jit(solution)/shard_map/first_step_middle_rows/pallas_call | solution.py:543
  12.2 0.7 %collective-permute-done.got_a = f32[152,128]{1,0:T(8,128)S(1)} collective-permute-done((f32[152,128]{1,0:T(8,128)S(1)}, f32[152,128]{1,0:T(8,128)S(1)}, u32[]{:S(2)}, u32[]{:S(2)}) %collective-permute-start) | collective-permute-done | bytes 77856 | tf_op jit(solution)/shard_map/ppermute | solution.py:510
  12.9 0.0 collective-permute-done.1.got_b
  12.9 0.1 cross_to_loop.1
  13.0 0.4 %collective-permute-start.4 = (f32[32,128]{1,0:T(8,128)S(1)}, f32[32,128]{1,0:T(8,128)S(1)}, u32[]{:S(2)}, u32[]{:S(2)}) collective-permute-start(f32[32,128]{1,0:T(8,128)S(1)} %get-tuple-element.33), channel_id=1, source_target_pairs={{4,8},{8,4},{12,16},{16,12},{20,24},{24,20},{28,0},{0,28},{5,9},{9... | collective-permute-start | bytes 49160 | tf_op jit(solution)/shard_map/ppermute | solution.py:519
  13.4 0.6 %collective-permute-start.5 = (f32[32,128]{1,0:T(8,128)S(1)}, f32[32,128]{1,0:T(8,128)S(1)}, u32[]{:S(2)}, u32[]{:S(2)}) collective-permute-start(f32[32,128]{1,0:T(8,128)S(1)} %get-tuple-element.34), channel_id=1, source_target_pairs={{0,4},{4,0},{8,12},{12,8},{16,20},{20,16},{24,28},{28,24},{1,5},{5... | collective-permute-start | bytes 49160 | tf_op jit(solution)/shard_map/ppermute | solution.py:519
  14.1 1.1 %second_step_inner_side_rows.1 = (f32[41,10,48,128]{3,2,1,0:T(8,128)S(1)}, f32[88,128]{1,0:T(8,128)S(1)}, f32[88,128]{1,0:T(8,128)S(1)}) custom-call(f32[41,10,48,128]{3,2,1,0:T(8,128)S(1)} %get-tuple-element.28.state.state_in, s32[8,32,128]{2,1,0:T(8,128)S(1)} %get-tuple-element.24.kinds), custom_call_target="tpu_custom_call" | custom-call | flops 6144000 | bytes 4030464 | tf_op jit(solution)/shard_map/second_step_inner_side_rows/pallas_call | solution.py:543
  15.2 1.1 %second_step_inner_middle_rows.1.out_in = f32[41,10,48,128]{3,2,1,0:T(8,128)S(1)} custom-call(f32[41,10,48,128]{3,2,1,0:T(8,128)S(1)} %get-tuple-element.28.state.state_in, s32[8,32,128]{2,1,0:T(8,128)S(1)} %get-tuple-element.24.kinds, f32[41,10,48,128]{3,2,1,0:T(8,128)S(1)} %get-tuple-element.29.out_in), custom_call_target="tpu_custom_call", output_to_operand_aliasing={{}: (2, {})} | custom-call | flops 6144000 | bytes 4030464 | tf_op jit(solution)/shard_map/second_step_inner_middle_rows/pallas_call | solution.py:543
  16.2 0.9 %collective-permute-done.4.far_rest = f32[32,128]{1,0:T(8,128)S(1)} collective-permute-done((f32[32,128]{1,0:T(8,128)S(1)}, f32[32,128]{1,0:T(8,128)S(1)}, u32[]{:S(2)}, u32[]{:S(2)}) %collective-permute-start.4) | collective-permute-done | bytes 16416 | tf_op jit(solution)/shard_map/ppermute | solution.py:519
  17.2 0.0 collective-permute-done.5.near_rest
  17.2 0.0 collective-permute-done.2.far
  17.2 0.0 collective-permute-done.3.near
  17.2 0.5 %second_step_edges_to_send.1 = (f32[41,10,48,128]{3,2,1,0:T(8,128)S(1)}, f32[41,10,48,128]{3,2,1,0:T(8,128)S(1)}, f32[11,32,128]{2,1,0:T(8,128)S(1)}, f32[11,32,128]{2,1,0:T(8,128)S(1)}) custom-call(f32[41,10,48,128]{3,2,1,0:T(8,128)S(1)} %get-tuple-element.28.state.state_in, ...), custom_call_target="tpu_custom_call", output_to_operand_aliasing={{0}: (0, {}), {1}: (1, {})} | custom-call | flops 4608000 | bytes 3022848 | tf_op jit(solution)/shard_map/second_step_edges_to_send/pallas_call | solution.py:543
  17.7 0.8 %collective-permute-start.8 = (f32[11,32,128]{2,1,0:T(8,128)S(1)}, f32[11,32,128]{2,1,0:T(8,128)S(1)}, u32[]{:S(2)}, u32[]{:S(2)}) collective-permute-start(f32[11,32,128]{2,1,0:T(8,128)S(1)} %get-tuple-element.44), channel_id=1, source_target_pairs={{4,8},{8,4},{12,16},{16,12},{20,24},{24,20},{28,0},{0,28},{5,9},{9... | collective-permute-start | bytes 540680 | tf_op jit(solution)/shard_map/ppermute | solution.py:519
  18.5 0.4 %collective-permute-start.9 = (f32[11,32,128]{2,1,0:T(8,128)S(1)}, f32[11,32,128]{2,1,0:T(8,128)S(1)}, u32[]{:S(2)}, u32[]{:S(2)}) collective-permute-start(f32[11,32,128]{2,1,0:T(8,128)S(1)} %get-tuple-element.45), channel_id=1, source_target_pairs={{0,4},{4,0},{8,12},{12,8},{16,20},{20,16},{24,28},{28,24},{1,5},{5... | collective-permute-start | bytes 540680 | tf_op jit(solution)/shard_map/ppermute | solution.py:519
  18.9 2.7 %collective-permute-start.6 = (f32[88,128]{1,0:T(8,128)S(1)}, f32[88,128]{1,0:T(8,128)S(1)}, u32[]{:S(2)}, u32[]{:S(2)}) collective-permute-start(f32[88,128]{1,0:T(8,128)S(1)} %get-tuple-element.40), channel_id=1, source_target_pairs={{0,1},{1,0},{2,3},{3,2},{4,5},{5,4},{6,7},{7,6},{8,9},{9,8},{10,11... | collective-permute-start | bytes 135176 | tf_op jit(solution)/shard_map/ppermute | solution.py:510
  21.6 0.0 collective-permute-start.7
  21.6 2.5 %second_step_edges_rest_and_write.1 = (f32[41,10,48,128]{3,2,1,0:T(8,128)S(1)}, f32[27,8,32,128]{3,2,1,0:T(8,128)}, f32[14,8,32,128]{3,2,1,0:T(8,128)}) custom-call(f32[41,10,48,128]{3,2,1,0:T(8,128)S(1)} %get-tuple-element.35.state, f32[41,10,48,128]{3,2,1,0:T(8,128)S(1)} %get-tuple-element.36.out_in, ...), custom_call_target="tpu_custom_call", output_to_operand_aliasing={{0}: (1, {})} | custom-call | flops 4608000 | bytes 13770752 | tf_op jit(solution)/shard_map/second_step_edges_rest_and_write/pallas_call | solution.py:543
  24.1 0.0 collective-permute-done.6.cross_a
  24.1 0.0 collective-permute-done.7.cross_b
  24.2 1.1 %write_rows_again.1 = (f32[41,10,48,128]{3,2,1,0:T(8,128)S(1)}, f32[27,8,32,128]{3,2,1,0:T(8,128)}, f32[14,8,32,128]{3,2,1,0:T(8,128)}) custom-call(f32[41,10,48,128]{3,2,1,0:T(8,128)S(1)} %get-tuple-element.37.out_in, f32[27,8,32,128]{3,2,1,0:T(8,128)} %get-tuple-element.38.pops_in, ...), custom_call_target="tpu_custom_call", output_to_operand_aliasing={{0}: (0, {}), {1}: (1, {}), {2}: (2, {})} | custom-call | flops 512000 | bytes 1056768 | tf_op jit(solution)/shard_map/write_rows_again/pallas_call | solution.py:543
  25.3 0.0 collective-permute-done.8.got_a
  25.3 0.0 collective-permute-done.9.got_b
  25.3 0.9 %write_edge_planes.1 = (f32[27,8,32,128]{3,2,1,0:T(8,128)}, f32[14,8,32,128]{3,2,1,0:T(8,128)}) custom-call(f32[27,8,32,128]{3,2,1,0:T(8,128)} %get-tuple-element.42.pops_in, f32[14,8,32,128]{3,2,1,0:T(8,128)} %get-tuple-element.43.scal_in, f32[11,32,128]{2,1,0:T(8,128)S(1)} %collective-permute-done.8.got_a, ...), custom_call_target="tpu_custom_call", output_to_operand_aliasing={{0}: (0, {}), {1}: (1, {})} | custom-call | bytes 720896 | tf_op jit(solution)/shard_map/write_edge_planes/pallas_call | solution.py:543
Async XLA Ops:
  4.7 12.4 %collective-permute-start.2 = (f32[11,32,128]{2,1,0:T(8,128)S(1)}, f32[11,32,128]{2,1,0:T(8,128)S(1)}, u32[]{:S(2)}, u32[]{:S(2)}) collective-permute-start(f32[11,32,128]{2,1,0:T(8,128)S(1)} %get-tuple-element.31), channel_id=1, source_target_pairs={{4,8},{8,4},{12,16},{16,12},{20,24},{24,20},{28,0},{0,28},{5,9},{9... | collective-permute-start | bytes 540680 | tf_op jit(solution)/shard_map/ppermute | solution.py:519
  8.1 9.0 %collective-permute-start.3 = (f32[11,32,128]{2,1,0:T(8,128)S(1)}, f32[11,32,128]{2,1,0:T(8,128)S(1)}, u32[]{:S(2)}, u32[]{:S(2)}) collective-permute-start(f32[11,32,128]{2,1,0:T(8,128)S(1)} %get-tuple-element.32), channel_id=1, source_target_pairs={{0,4},{4,0},{8,12},{12,8},{16,20},{20,16},{24,28},{28,24},{1,5},{5... | collective-permute-start | bytes 540680 | tf_op jit(solution)/shard_map/ppermute | solution.py:519
  8.1 4.8 %collective-permute-start = (f32[152,128]{1,0:T(8,128)S(1)}, f32[152,128]{1,0:T(8,128)S(1)}, u32[]{:S(2)}, u32[]{:S(2)}) collective-permute-start(f32[152,128]{1,0:T(8,128)S(1)} %get-tuple-element.26), channel_id=1, source_target_pairs={{0,1},{1,0},{2,3},{3,2},{4,5},{5,4},{6,7},{7,6},{8,9},{9,8},{10,11... | collective-permute-start | bytes 233480 | tf_op jit(solution)/shard_map/ppermute | solution.py:510
  9.7 3.2 %collective-permute-start.1 = (f32[152,128]{1,0:T(8,128)S(1)}, f32[152,128]{1,0:T(8,128)S(1)}, u32[]{:S(2)}, u32[]{:S(2)}) collective-permute-start(f32[152,128]{1,0:T(8,128)S(1)} %get-tuple-element.27), channel_id=1, source_target_pairs={{0,4},{1,2},{2,1},{3,7},{4,0},{5,6},{6,5},{7,3},{8,12},{9,10},{10,... | collective-permute-start | bytes 233480 | tf_op jit(solution)/shard_map/ppermute | solution.py:510
  13.0 4.1 %collective-permute-start.4 = (f32[32,128]{1,0:T(8,128)S(1)}, f32[32,128]{1,0:T(8,128)S(1)}, u32[]{:S(2)}, u32[]{:S(2)}) collective-permute-start(f32[32,128]{1,0:T(8,128)S(1)} %get-tuple-element.33), channel_id=1, source_target_pairs={{4,8},{8,4},{12,16},{16,12},{20,24},{24,20},{28,0},{0,28},{5,9},{9... | collective-permute-start | bytes 49160 | tf_op jit(solution)/shard_map/ppermute | solution.py:519
  13.4 3.7 %collective-permute-start.5 = (f32[32,128]{1,0:T(8,128)S(1)}, f32[32,128]{1,0:T(8,128)S(1)}, u32[]{:S(2)}, u32[]{:S(2)}) collective-permute-start(f32[32,128]{1,0:T(8,128)S(1)} %get-tuple-element.34), channel_id=1, source_target_pairs={{0,4},{4,0},{8,12},{12,8},{16,20},{20,16},{24,28},{28,24},{1,5},{5... | collective-permute-start | bytes 49160 | tf_op jit(solution)/shard_map/ppermute | solution.py:519
  17.7 7.6 %collective-permute-start.8 = (f32[11,32,128]{2,1,0:T(8,128)S(1)}, f32[11,32,128]{2,1,0:T(8,128)S(1)}, u32[]{:S(2)}, u32[]{:S(2)}) collective-permute-start(f32[11,32,128]{2,1,0:T(8,128)S(1)} %get-tuple-element.44), channel_id=1, source_target_pairs={{4,8},{8,4},{12,16},{16,12},{20,24},{24,20},{28,0},{0,28},{5,9},{9... | collective-permute-start | bytes 540680 | tf_op jit(solution)/shard_map/ppermute | solution.py:519
  18.5 6.8 %collective-permute-start.9 = (f32[11,32,128]{2,1,0:T(8,128)S(1)}, f32[11,32,128]{2,1,0:T(8,128)S(1)}, u32[]{:S(2)}, u32[]{:S(2)}) collective-permute-start(f32[11,32,128]{2,1,0:T(8,128)S(1)} %get-tuple-element.45), channel_id=1, source_target_pairs={{0,4},{4,0},{8,12},{12,8},{16,20},{20,16},{24,28},{28,24},{1,5},{5... | collective-permute-start | bytes 540680 | tf_op jit(solution)/shard_map/ppermute | solution.py:519
  18.9 5.2 %collective-permute-start.6 = (f32[88,128]{1,0:T(8,128)S(1)}, f32[88,128]{1,0:T(8,128)S(1)}, u32[]{:S(2)}, u32[]{:S(2)}) collective-permute-start(f32[88,128]{1,0:T(8,128)S(1)} %get-tuple-element.40), channel_id=1, source_target_pairs={{0,1},{1,0},{2,3},{3,2},{4,5},{5,4},{6,7},{7,6},{8,9},{9,8},{10,11... | collective-permute-start | bytes 135176 | tf_op jit(solution)/shard_map/ppermute | solution.py:510
  21.6 2.5 %collective-permute-start.7 = (f32[88,128]{1,0:T(8,128)S(1)}, f32[88,128]{1,0:T(8,128)S(1)}, u32[]{:S(2)}, u32[]{:S(2)}) collective-permute-start(f32[88,128]{1,0:T(8,128)S(1)} %get-tuple-element.41), channel_id=1, source_target_pairs={{0,4},{1,2},{2,1},{3,7},{4,0},{5,6},{6,5},{7,3},{8,12},{9,10},{10,... | collective-permute-start | bytes 135176 | tf_op jit(solution)/shard_map/ppermute | solution.py:510

commit v15 on v14

--- a/solution.py
+++ b/solution.py
@@ -131,10 +131,12 @@
             put(first + 2 + 2 * axis, lambda: jnp.where(wall, g_p, keep_s * g_m + (eighth - odd)))
 
 
-def shift_lanes(value, c):
+def shift_lanes(value, c, closed=False):
     if c == 0:
         return value
     lanes = value.shape[-1]
+    if closed:
+        return pltpu.roll(value, c % lanes, value.ndim - 1)
     lane = lax.broadcasted_iota(jnp.int32, value.shape, value.ndim - 1)
     edge = 0 if c > 0 else lanes - 1
     return jnp.where(lane == edge, 0.0, pltpu.roll(value, c % lanes, value.ndim - 1))
@@ -144,10 +146,10 @@
     return x + 1
 
 
-def push_tile(dst, x, row):
+def push_tile(dst, x, row, closed=False):
     def put(i, value):
         a, b, c = DIRS[i]
-        dst[i, slot(x + a), row + PAD + b : row + PAD + b + SUB, :] = shift_lanes(value, c)
+        dst[i, slot(x + a), row + PAD + b : row + PAD + b + SUB, :] = shift_lanes(value, c, closed)
 
     return put
 
@@ -363,7 +365,7 @@
     @pl.loop(first, last)
     def _(x):
         for y in tiles:
-            collide(load_tile(state, x, y), kinds[x, y : y + SUB, :], push_tile(out, x, y))
+            collide(load_tile(state, x, y), kinds[x, y : y + SUB, :], push_tile(out, x, y, True))
 
 
 def inner_side_kernel(state, kinds, out, sent_a, sent_b):
@@ -395,7 +397,7 @@
         x = 0 if a < 0 else size_x - 1
         want = [i for i in range(NQ) if (i in X_SETS[a]) == sent]
         for y in range(0, size_y, SUB):
-            collide(load_tile(state, x, y), kinds[x, y : y + SUB, :], push_tile(out, x, y), want)
+            collide(load_tile(state, x, y), kinds[x, y : y + SUB, :], push_tile(out, x, y, True), want)
     code = halo_kinds[...].astype(jnp.int32)
 
     def put(i, value):

time: 26.4 us -> 26.4 us (level)
  no operation moved by 1% of the time
where the time goes in v15:
time: 26.4 us; the launch traced here: 26.2 us
  Pallas kernels  13.6 us (52%)
  starting transfers between devices  10.1 us (38%)
  waiting for transfers between devices  1.7 us (6%)
  between operations  0.73 us (3%)
    pallas_call x9, Pallas kernels, call(): pl.pallas_call(kernel, out_shape=results, in_specs=specs, out_specs=[hbm...  13.6 us
    ppermute x6, starting transfers between devices, swap_loop(): return lax.ppermute(cells, 'loop', pairs)  5.67 us
    ppermute x4, starting transfers between devices, swap_cross(): received.append(lax.ppermute(cells, ('loop', 'cross'), pairs))  4.47 us
    ppermute x6, waiting for transfers between devices, swap_loop(): return lax.ppermute(cells, 'loop', pairs)  0.96 us
    ppermute x4, waiting for transfers between devices, swap_cross(): received.append(lax.ppermute(cells, ('loop', 'cross'), pairs))  0.74 us
  transfers between devices with their start and end apart: 10, of which 2 were waited for; matrix products, arithmetic and copies ran while one was open for 0% of the time, Pallas kernels for 31%

profile of v15, /device:TPU:0, one launch (start us, length us, event | category | flops | bytes accessed | tf_op | source)
XLA Modules:
  0.0 26.2 jit_solution(5383247983400582503)
XLA Ops:
  0.6 4.1 %first_step_side_rows.1 = (f32[41,10,48,128]{3,2,1,0:T(8,128)S(1)}, s32[8,32,128]{2,1,0:T(8,128)S(1)}, f32[152,128]{1,0:T(8,128)S(1)}, f32[152,128]{1,0:T(8,128)...) custom-call(f32[27,8,32,128]{3,2,1,0:T(8,128)} %pops.3, f32[14,8,32,128]{3,2,1,0:T(8,128)} %scal.3, ...), custom_call_target="tpu_custom_call" | custom-call | flops 10240000 | bytes 6717440 | tf_op jit(solution)/shard_map/first_step_side_rows/pallas_call | solution.py:545
  4.7 3.4 %collective-permute-start.2 = (f32[11,32,128]{2,1,0:T(8,128)S(1)}, f32[11,32,128]{2,1,0:T(8,128)S(1)}, u32[]{:S(2)}, u32[]{:S(2)}) collective-permute-start(f32[11,32,128]{2,1,0:T(8,128)S(1)} %get-tuple-element.31), channel_id=1, source_target_pairs={{4,8},{8,4},{12,16},{16,12},{20,24},{24,20},{28,0},{0,28},{5,9},{9... | collective-permute-start | bytes 540680 | tf_op jit(solution)/shard_map/ppermute | solution.py:521
  8.1 0.0 collective-permute-start.3
  8.1 1.6 %collective-permute-start = (f32[152,128]{1,0:T(8,128)S(1)}, f32[152,128]{1,0:T(8,128)S(1)}, u32[]{:S(2)}, u32[]{:S(2)}) collective-permute-start(f32[152,128]{1,0:T(8,128)S(1)} %get-tuple-element.26), channel_id=1, source_target_pairs={{0,1},{1,0},{2,3},{3,2},{4,5},{5,4},{6,7},{7,6},{8,9},{9,8},{10,11... | collective-permute-start | bytes 233480 | tf_op jit(solution)/shard_map/ppermute | solution.py:512
  9.7 0.2 collective-permute-start.1
  9.9 2.2 %first_step_middle_rows.1.state_in = f32[41,10,48,128]{3,2,1,0:T(8,128)S(1)} custom-call(f32[27,8,32,128]{3,2,1,0:T(8,128)} %pops.3, f32[14,8,32,128]{3,2,1,0:T(8,128)} %scal.3, s32[8,32,128]{2,1,0:T(8,128)S(1)} %get-tuple-element.24.kinds, f32[41,10,48,128]{3,2,1,0:T(8,128)S(1)} %get-tuple-element.25.state_in), custom_call_target="tpu_custom_call", output_to_operand_aliasing={{}: (3, {})} | custom-call | flops 8192000 | bytes 5373952 | tf_op jit(solution)/shard_map/first_step_middle_rows/pallas_call | solution.py:545
  12.2 0.7 %collective-permute-done.got_a = f32[152,128]{1,0:T(8,128)S(1)} collective-permute-done((f32[152,128]{1,0:T(8,128)S(1)}, f32[152,128]{1,0:T(8,128)S(1)}, u32[]{:S(2)}, u32[]{:S(2)}) %collective-permute-start) | collective-permute-done | bytes 77856 | tf_op jit(solution)/shard_map/ppermute | solution.py:512
  12.9 0.0 collective-permute-done.1.got_b
  12.9 0.1 cross_to_loop.1
  13.0 0.4 %collective-permute-start.4 = (f32[32,128]{1,0:T(8,128)S(1)}, f32[32,128]{1,0:T(8,128)S(1)}, u32[]{:S(2)}, u32[]{:S(2)}) collective-permute-start(f32[32,128]{1,0:T(8,128)S(1)} %get-tuple-element.33), channel_id=1, source_target_pairs={{4,8},{8,4},{12,16},{16,12},{20,24},{24,20},{28,0},{0,28},{5,9},{9... | collective-permute-start | bytes 49160 | tf_op jit(solution)/shard_map/ppermute | solution.py:521
  13.4 0.6 %collective-permute-start.5 = (f32[32,128]{1,0:T(8,128)S(1)}, f32[32,128]{1,0:T(8,128)S(1)}, u32[]{:S(2)}, u32[]{:S(2)}) collective-permute-start(f32[32,128]{1,0:T(8,128)S(1)} %get-tuple-element.34), channel_id=1, source_target_pairs={{0,4},{4,0},{8,12},{12,8},{16,20},{20,16},{24,28},{28,24},{1,5},{5... | collective-permute-start | bytes 49160 | tf_op jit(solution)/shard_map/ppermute | solution.py:521
  14.1 1.1 %second_step_inner_side_rows.1 = (f32[41,10,48,128]{3,2,1,0:T(8,128)S(1)}, f32[88,128]{1,0:T(8,128)S(1)}, f32[88,128]{1,0:T(8,128)S(1)}) custom-call(f32[41,10,48,128]{3,2,1,0:T(8,128)S(1)} %get-tuple-element.28.state.state_in, s32[8,32,128]{2,1,0:T(8,128)S(1)} %get-tuple-element.24.kinds), custom_call_target="tpu_custom_call" | custom-call | flops 6144000 | bytes 4030464 | tf_op jit(solution)/shard_map/second_step_inner_side_rows/pallas_call | solution.py:545
  15.2 1.1 %second_step_inner_middle_rows.1.out_in = f32[41,10,48,128]{3,2,1,0:T(8,128)S(1)} custom-call(f32[41,10,48,128]{3,2,1,0:T(8,128)S(1)} %get-tuple-element.28.state.state_in, s32[8,32,128]{2,1,0:T(8,128)S(1)} %get-tuple-element.24.kinds, f32[41,10,48,128]{3,2,1,0:T(8,128)S(1)} %get-tuple-element.29.out_in), custom_call_target="tpu_custom_call", output_to_operand_aliasing={{}: (2, {})} | custom-call | flops 6144000 | bytes 4030464 | tf_op jit(solution)/shard_map/second_step_inner_middle_rows/pallas_call | solution.py:545
  16.2 0.9 %collective-permute-done.4.far_rest = f32[32,128]{1,0:T(8,128)S(1)} collective-permute-done((f32[32,128]{1,0:T(8,128)S(1)}, f32[32,128]{1,0:T(8,128)S(1)}, u32[]{:S(2)}, u32[]{:S(2)}) %collective-permute-start.4) | collective-permute-done | bytes 16416 | tf_op jit(solution)/shard_map/ppermute | solution.py:521
  17.2 0.0 collective-permute-done.5.near_rest
  17.2 0.0 collective-permute-done.2.far
  17.2 0.0 collective-permute-done.3.near
  17.2 0.5 %second_step_edges_to_send.1 = (f32[41,10,48,128]{3,2,1,0:T(8,128)S(1)}, f32[41,10,48,128]{3,2,1,0:T(8,128)S(1)}, f32[11,32,128]{2,1,0:T(8,128)S(1)}, f32[11,32,128]{2,1,0:T(8,128)S(1)}) custom-call(f32[41,10,48,128]{3,2,1,0:T(8,128)S(1)} %get-tuple-element.28.state.state_in, ...), custom_call_target="tpu_custom_call", output_to_operand_aliasing={{0}: (0, {}), {1}: (1, {})} | custom-call | flops 4608000 | bytes 3022848 | tf_op jit(solution)/shard_map/second_step_edges_to_send/pallas_call | solution.py:545
  17.7 0.8 %collective-permute-start.8 = (f32[11,32,128]{2,1,0:T(8,128)S(1)}, f32[11,32,128]{2,1,0:T(8,128)S(1)}, u32[]{:S(2)}, u32[]{:S(2)}) collective-permute-start(f32[11,32,128]{2,1,0:T(8,128)S(1)} %get-tuple-element.44), channel_id=1, source_target_pairs={{4,8},{8,4},{12,16},{16,12},{20,24},{24,20},{28,0},{0,28},{5,9},{9... | collective-permute-start | bytes 540680 | tf_op jit(solution)/shard_map/ppermute | solution.py:521
  18.5 0.4 %collective-permute-start.9 = (f32[11,32,128]{2,1,0:T(8,128)S(1)}, f32[11,32,128]{2,1,0:T(8,128)S(1)}, u32[]{:S(2)}, u32[]{:S(2)}) collective-permute-start(f32[11,32,128]{2,1,0:T(8,128)S(1)} %get-tuple-element.45), channel_id=1, source_target_pairs={{0,4},{4,0},{8,12},{12,8},{16,20},{20,16},{24,28},{28,24},{1,5},{5... | collective-permute-start | bytes 540680 | tf_op jit(solution)/shard_map/ppermute | solution.py:521
  18.9 2.7 %collective-permute-start.6 = (f32[88,128]{1,0:T(8,128)S(1)}, f32[88,128]{1,0:T(8,128)S(1)}, u32[]{:S(2)}, u32[]{:S(2)}) collective-permute-start(f32[88,128]{1,0:T(8,128)S(1)} %get-tuple-element.40), channel_id=1, source_target_pairs={{0,1},{1,0},{2,3},{3,2},{4,5},{5,4},{6,7},{7,6},{8,9},{9,8},{10,11... | collective-permute-start | bytes 135176 | tf_op jit(solution)/shard_map/ppermute | solution.py:512
  21.6 0.0 collective-permute-start.7
  21.6 2.5 %second_step_edges_rest_and_write.1 = (f32[41,10,48,128]{3,2,1,0:T(8,128)S(1)}, f32[27,8,32,128]{3,2,1,0:T(8,128)}, f32[14,8,32,128]{3,2,1,0:T(8,128)}) custom-call(f32[41,10,48,128]{3,2,1,0:T(8,128)S(1)} %get-tuple-element.35.state, f32[41,10,48,128]{3,2,1,0:T(8,128)S(1)} %get-tuple-element.36.out_in, ...), custom_call_target="tpu_custom_call", output_to_operand_aliasing={{0}: (1, {})} | custom-call | flops 4608000 | bytes 13770752 | tf_op jit(solution)/shard_map/second_step_edges_rest_and_write/pallas_call | solution.py:545
  24.1 0.0 collective-permute-done.6.cross_a
  24.1 0.0 collective-permute-done.7.cross_b
  24.1 1.1 %write_rows_again.1 = (f32[41,10,48,128]{3,2,1,0:T(8,128)S(1)}, f32[27,8,32,128]{3,2,1,0:T(8,128)}, f32[14,8,32,128]{3,2,1,0:T(8,128)}) custom-call(f32[41,10,48,128]{3,2,1,0:T(8,128)S(1)} %get-tuple-element.37.out_in, f32[27,8,32,128]{3,2,1,0:T(8,128)} %get-tuple-element.38.pops_in, ...), custom_call_target="tpu_custom_call", output_to_operand_aliasing={{0}: (0, {}), {1}: (1, {}), {2}: (2, {})} | custom-call | flops 512000 | bytes 1056768 | tf_op jit(solution)/shard_map/write_rows_again/pallas_call | solution.py:545
  25.2 0.0 collective-permute-done.8.got_a
  25.2 0.0 collective-permute-done.9.got_b
  25.2 0.9 %write_edge_planes.1 = (f32[27,8,32,128]{3,2,1,0:T(8,128)}, f32[14,8,32,128]{3,2,1,0:T(8,128)}) custom-call(f32[27,8,32,128]{3,2,1,0:T(8,128)} %get-tuple-element.42.pops_in, f32[14,8,32,128]{3,2,1,0:T(8,128)} %get-tuple-element.43.scal_in, f32[11,32,128]{2,1,0:T(8,128)S(1)} %collective-permute-done.8.got_a, ...), custom_call_target="tpu_custom_call", output_to_operand_aliasing={{0}: (0, {}), {1}: (1, {})} | custom-call | bytes 720896 | tf_op jit(solution)/shard_map/write_edge_planes/pallas_call | solution.py:545
Async XLA Ops:
  4.7 12.4 %collective-permute-start.2 = (f32[11,32,128]{2,1,0:T(8,128)S(1)}, f32[11,32,128]{2,1,0:T(8,128)S(1)}, u32[]{:S(2)}, u32[]{:S(2)}) collective-permute-start(f32[11,32,128]{2,1,0:T(8,128)S(1)} %get-tuple-element.31), channel_id=1, source_target_pairs={{4,8},{8,4},{12,16},{16,12},{20,24},{24,20},{28,0},{0,28},{5,9},{9... | collective-permute-start | bytes 540680 | tf_op jit(solution)/shard_map/ppermute | solution.py:521
  8.1 9.0 %collective-permute-start.3 = (f32[11,32,128]{2,1,0:T(8,128)S(1)}, f32[11,32,128]{2,1,0:T(8,128)S(1)}, u32[]{:S(2)}, u32[]{:S(2)}) collective-permute-start(f32[11,32,128]{2,1,0:T(8,128)S(1)} %get-tuple-element.32), channel_id=1, source_target_pairs={{0,4},{4,0},{8,12},{12,8},{16,20},{20,16},{24,28},{28,24},{1,5},{5... | collective-permute-start | bytes 540680 | tf_op jit(solution)/shard_map/ppermute | solution.py:521
  8.1 4.8 %collective-permute-start = (f32[152,128]{1,0:T(8,128)S(1)}, f32[152,128]{1,0:T(8,128)S(1)}, u32[]{:S(2)}, u32[]{:S(2)}) collective-permute-start(f32[152,128]{1,0:T(8,128)S(1)} %get-tuple-element.26), channel_id=1, source_target_pairs={{0,1},{1,0},{2,3},{3,2},{4,5},{5,4},{6,7},{7,6},{8,9},{9,8},{10,11... | collective-permute-start | bytes 233480 | tf_op jit(solution)/shard_map/ppermute | solution.py:512
  9.7 3.2 %collective-permute-start.1 = (f32[152,128]{1,0:T(8,128)S(1)}, f32[152,128]{1,0:T(8,128)S(1)}, u32[]{:S(2)}, u32[]{:S(2)}) collective-permute-start(f32[152,128]{1,0:T(8,128)S(1)} %get-tuple-element.27), channel_id=1, source_target_pairs={{0,4},{1,2},{2,1},{3,7},{4,0},{5,6},{6,5},{7,3},{8,12},{9,10},{10,... | collective-permute-start | bytes 233480 | tf_op jit(solution)/shard_map/ppermute | solution.py:512
  13.0 4.1 %collective-permute-start.4 = (f32[32,128]{1,0:T(8,128)S(1)}, f32[32,128]{1,0:T(8,128)S(1)}, u32[]{:S(2)}, u32[]{:S(2)}) collective-permute-start(f32[32,128]{1,0:T(8,128)S(1)} %get-tuple-element.33), channel_id=1, source_target_pairs={{4,8},{8,4},{12,16},{16,12},{20,24},{24,20},{28,0},{0,28},{5,9},{9... | collective-permute-start | bytes 49160 | tf_op jit(solution)/shard_map/ppermute | solution.py:521
  13.4 3.7 %collective-permute-start.5 = (f32[32,128]{1,0:T(8,128)S(1)}, f32[32,128]{1,0:T(8,128)S(1)}, u32[]{:S(2)}, u32[]{:S(2)}) collective-permute-start(f32[32,128]{1,0:T(8,128)S(1)} %get-tuple-element.34), channel_id=1, source_target_pairs={{0,4},{4,0},{8,12},{12,8},{16,20},{20,16},{24,28},{28,24},{1,5},{5... | collective-permute-start | bytes 49160 | tf_op jit(solution)/shard_map/ppermute | solution.py:521
  17.7 7.6 %collective-permute-start.8 = (f32[11,32,128]{2,1,0:T(8,128)S(1)}, f32[11,32,128]{2,1,0:T(8,128)S(1)}, u32[]{:S(2)}, u32[]{:S(2)}) collective-permute-start(f32[11,32,128]{2,1,0:T(8,128)S(1)} %get-tuple-element.44), channel_id=1, source_target_pairs={{4,8},{8,4},{12,16},{16,12},{20,24},{24,20},{28,0},{0,28},{5,9},{9... | collective-permute-start | bytes 540680 | tf_op jit(solution)/shard_map/ppermute | solution.py:521
  18.5 6.8 %collective-permute-start.9 = (f32[11,32,128]{2,1,0:T(8,128)S(1)}, f32[11,32,128]{2,1,0:T(8,128)S(1)}, u32[]{:S(2)}, u32[]{:S(2)}) collective-permute-start(f32[11,32,128]{2,1,0:T(8,128)S(1)} %get-tuple-element.45), channel_id=1, source_target_pairs={{0,4},{4,0},{8,12},{12,8},{16,20},{20,16},{24,28},{28,24},{1,5},{5... | collective-permute-start | bytes 540680 | tf_op jit(solution)/shard_map/ppermute | solution.py:521
  18.9 5.2 %collective-permute-start.6 = (f32[88,128]{1,0:T(8,128)S(1)}, f32[88,128]{1,0:T(8,128)S(1)}, u32[]{:S(2)}, u32[]{:S(2)}) collective-permute-start(f32[88,128]{1,0:T(8,128)S(1)} %get-tuple-element.40), channel_id=1, source_target_pairs={{0,1},{1,0},{2,3},{3,2},{4,5},{5,4},{6,7},{7,6},{8,9},{9,8},{10,11... | collective-permute-start | bytes 135176 | tf_op jit(solution)/shard_map/ppermute | solution.py:512
  21.6 2.5 %collective-permute-start.7 = (f32[88,128]{1,0:T(8,128)S(1)}, f32[88,128]{1,0:T(8,128)S(1)}, u32[]{:S(2)}, u32[]{:S(2)}) collective-permute-start(f32[88,128]{1,0:T(8,128)S(1)} %get-tuple-element.41), channel_id=1, source_target_pairs={{0,4},{1,2},{2,1},{3,7},{4,0},{5,6},{6,5},{7,3},{8,12},{9,10},{10,... | collective-permute-start | bytes 135176 | tf_op jit(solution)/shard_map/ppermute | solution.py:512
